TPU v7x, 32 devices: a whole 2x2x4 slice. The times are simulated.
32 devices in a mesh: dp: 8 (over z, y), ctx: 4 (over x, core).
Axes of the slice: x: 2, y: 2, z: 4, core: 2. Of those that a mesh axis runs over, the one named last changes fastest.
Arguments:
- tokens: bfloat16 [16, 2048, 768], P('dp', 'ctx'), may hold values from -6 to 6
- segments: int32 [16, 2048], P('dp'), may hold values from 0 to 3, as said below
- ln1_gain: bfloat16 [768], P(('dp', 'ctx')), may hold values from 0.5 to 1.5
- ln1_bias: bfloat16 [768], P(('dp', 'ctx')), may hold values from -4 to 4
- qkv_weight: bfloat16 [768, 2304], P(('dp', 'ctx')), may hold values from -0.21875 to 0.21875
- q_bias: bfloat16 [768], P(('dp', 'ctx')), may hold values from -4 to 4
- v_bias: bfloat16 [768], P(('dp', 'ctx')), may hold values from -4 to 4
- out_weight: bfloat16 [768, 768], P(('dp', 'ctx')), may hold values from -0.875 to 0.875
- out_bias: bfloat16 [768], P(('dp', 'ctx')), may hold values from -4 to 4
- ln2_gain: bfloat16 [768], P(('dp', 'ctx')), may hold values from 0.5 to 1.5
- ln2_bias: bfloat16 [768], P(('dp', 'ctx')), may hold values from -4 to 4
- up_weight: bfloat16 [768, 3072], P(('dp', 'ctx')), may hold values from -0.21875 to 0.21875
- up_bias: bfloat16 [3072], P(('dp', 'ctx')), may hold values from -4 to 4
- down_weight: bfloat16 [3072, 768], P(('dp', 'ctx')), may hold values from -0.21875 to 0.21875
- down_bias: bfloat16 [768], P(('dp', 'ctx')), may hold values from -4 to 4
- cotangent: bfloat16 [16, 2048, 768], P('dp', 'ctx'), may hold values from -6 to 6
Outputs:
- mixed: bfloat16 [16, 2048, 768], P('dp', 'ctx')
- token_grad: bfloat16 [16, 2048, 768], P('dp', 'ctx')
- grad_ln1_gain: float32 [768], P(('dp', 'ctx'))
- grad_ln1_bias: float32 [768], P(('dp', 'ctx'))
- grad_qkv_weight: float32 [768, 2304], P(('dp', 'ctx'))
- grad_q_bias: float32 [768], P(('dp', 'ctx'))
- grad_v_bias: float32 [768], P(('dp', 'ctx'))
- grad_out_weight: float32 [768, 768], P(('dp', 'ctx'))
- grad_out_bias: float32 [768], P(('dp', 'ctx'))
- grad_ln2_gain: float32 [768], P(('dp', 'ctx'))
- grad_ln2_bias: float32 [768], P(('dp', 'ctx'))
- grad_up_weight: float32 [768, 3072], P(('dp', 'ctx'))
- grad_up_bias: float32 [3072], P(('dp', 'ctx'))
- grad_down_weight: float32 [3072, 768], P(('dp', 'ctx'))
- grad_down_bias: float32 [768], P(('dp', 'ctx'))
Inputs may be any that keep to these rules, and one draw needn't show every extreme that they name: `segments`: segment numbers never fall along a sequence.
All inputs are finite; a program needn't handle non-finite values.
Results may differ from a plain program's by a relative error of at most 0.014.
Values may be sent and summed in bfloat16 or wider, within the bound.
No kernel may reach another device: no remote copies, remote signals or barrier semaphores. Data moves between devices by JAX's collectives and lax.ppermute only.
A program may use at most 256 MiB of HBM per device.

v0:
```python
import jax
import jax.numpy as jnp
from jax import lax
from jax.sharding import PartitionSpec as P

HEAD_DIM = 64


EPSILON = 1e-05


def layer_norm(source, scale_vec, shift_vec):
    average = jnp.mean(source, axis=-1, keepdims=True)
    centred = source - average
    spread = jnp.mean(centred * centred, axis=-1, keepdims=True)
    return centred * lax.rsqrt(spread + EPSILON) * scale_vec + shift_vec


def gelu_tanh(source):
    return jax.nn.gelu(source, approximate=True)


def head_pairs(matrix, seq_count):
    pair_count = matrix.shape[-1] // (2 * HEAD_DIM)
    return matrix.reshape(seq_count, -1, pair_count, 2 * HEAD_DIM).transpose(2, 0, 1, 3)


def join_pairs(stacked):
    pair_count, seq_count, row_count, pair_width = stacked.shape
    return stacked.transpose(1, 2, 0, 3).reshape(seq_count, row_count, pair_count * pair_width)


def split_heads(block):
    return block.reshape(block.shape[0], block.shape[1], 2, HEAD_DIM)


def pair_scores(query_block, key_block, key_mask):
    scores = jnp.einsum(
        "sqhd,skhd->shqk",
        split_heads(query_block),
        split_heads(key_block),
        preferred_element_type=jnp.float32,
    )
    return jnp.where(key_mask[:, None], scores, -1e30)


def forward_pair(query_block, key_block, value_block, key_mask):
    scores = pair_scores(query_block, key_block, key_mask)
    row_max = jnp.max(scores, axis=-1, keepdims=True)
    exp_terms = jnp.exp(scores - row_max)
    row_total = jnp.sum(exp_terms, axis=-1, keepdims=True)
    probs = (exp_terms / row_total).astype(jnp.bfloat16)
    attended = jnp.einsum(
        "shqk,skhd->sqhd", probs, split_heads(value_block), preferred_element_type=jnp.float32
    )
    seq_count, row_count = (query_block.shape[0], query_block.shape[1])
    log_total = (row_max + jnp.log(row_total))[..., 0]
    return (attended.reshape(seq_count, row_count, 2 * HEAD_DIM).astype(jnp.bfloat16), log_total)


def backward_pair(query_block, key_block, value_block, grad_block, log_total, key_mask):
    scores = pair_scores(query_block, key_block, key_mask)
    probs = jnp.exp(scores - log_total[..., None])
    grad_probs = jnp.einsum(
        "sqhd,skhd->shqk",
        split_heads(grad_block),
        split_heads(value_block),
        preferred_element_type=jnp.float32,
    )
    row_inner = jnp.sum(probs * grad_probs, axis=-1, keepdims=True)
    grad_scores = (probs * (grad_probs - row_inner)).astype(jnp.bfloat16)
    probs_low = probs.astype(jnp.bfloat16)
    grad_query = jnp.einsum(
        "shqk,skhd->sqhd", grad_scores, split_heads(key_block), preferred_element_type=jnp.float32
    )
    grad_key = jnp.einsum(
        "shqk,sqhd->skhd", grad_scores, split_heads(query_block), preferred_element_type=jnp.float32
    )
    grad_value = jnp.einsum(
        "shqk,sqhd->skhd", probs_low, split_heads(grad_block), preferred_element_type=jnp.float32
    )
    seq_count, query_count, key_count = (
        query_block.shape[0],
        query_block.shape[1],
        key_block.shape[1],
    )
    return (
        grad_query.reshape(seq_count, query_count, 2 * HEAD_DIM).astype(jnp.bfloat16),
        grad_key.reshape(seq_count, key_count, 2 * HEAD_DIM),
        grad_value.reshape(seq_count, key_count, 2 * HEAD_DIM),
    )


def column_sums(matrix):
    return jnp.sum(matrix.astype(jnp.float32), axis=0)


def body(
    tokens,
    segments,
    ln1_gain,
    ln1_bias,
    qkv_weight,
    q_bias,
    v_bias,
    out_weight,
    out_bias,
    ln2_gain,
    ln2_bias,
    up_weight,
    up_bias,
    down_weight,
    down_bias,
    cotangent,
):
    gathered = (
        lax.all_gather(ln1_gain, ("dp", "ctx"), axis=0, tiled=True),
        lax.all_gather(ln1_bias, ("dp", "ctx"), axis=0, tiled=True),
        lax.all_gather(qkv_weight, ("dp", "ctx"), axis=0, tiled=True),
        lax.all_gather(q_bias, ("dp", "ctx"), axis=0, tiled=True),
        lax.all_gather(v_bias, ("dp", "ctx"), axis=0, tiled=True),
        lax.all_gather(out_weight, ("dp", "ctx"), axis=0, tiled=True),
        lax.all_gather(out_bias, ("dp", "ctx"), axis=0, tiled=True),
        lax.all_gather(ln2_gain, ("dp", "ctx"), axis=0, tiled=True),
        lax.all_gather(ln2_bias, ("dp", "ctx"), axis=0, tiled=True),
        lax.all_gather(up_weight, ("dp", "ctx"), axis=0, tiled=True),
        lax.all_gather(up_bias, ("dp", "ctx"), axis=0, tiled=True),
        lax.all_gather(down_weight, ("dp", "ctx"), axis=0, tiled=True),
        lax.all_gather(down_bias, ("dp", "ctx"), axis=0, tiled=True),
    )
    (
        gain_one,
        shift_one,
        proj_qkv,
        query_shift,
        value_shift,
        proj_out,
        out_shift,
        gain_two,
        shift_two,
        proj_up,
        up_shift,
        proj_down,
        down_shift,
    ) = gathered
    seq_count, row_count, feat_width = tokens.shape
    tok_count = seq_count * row_count
    seq_length = segments.shape[1]
    offset = lax.axis_index("ctx") * row_count
    inputs = tokens.astype(jnp.float32).reshape(tok_count, feat_width)
    normed, norm_one_back = jax.vjp(
        layer_norm, inputs, gain_one.astype(jnp.float32), shift_one.astype(jnp.float32)
    )
    normed_low = normed.astype(jnp.bfloat16)
    joint = jnp.dot(normed_low, proj_qkv, preferred_element_type=jnp.float32)
    query_low = ((joint[:, :feat_width] + query_shift.astype(jnp.float32)) * 0.125).astype(
        jnp.bfloat16
    )
    key_low = joint[:, feat_width : 2 * feat_width].astype(jnp.bfloat16)
    value_low = (joint[:, 2 * feat_width :] + value_shift.astype(jnp.float32)).astype(jnp.bfloat16)
    key_full, value_full = (
        lax.all_gather(
            key_low.reshape(seq_count, row_count, feat_width), "ctx", axis=1, tiled=True
        ),
        lax.all_gather(
            value_low.reshape(seq_count, row_count, feat_width), "ctx", axis=1, tiled=True
        ),
    )
    seg_rows = lax.dynamic_slice_in_dim(segments, offset, row_count, 1)
    query_places = offset + jnp.arange(row_count)
    key_places = jnp.arange(seq_length)
    key_mask = (key_places[None, None, :] <= query_places[None, :, None]) & (
        segments[:, None, :] == seg_rows[:, :, None]
    )
    query_pairs = head_pairs(query_low, seq_count)
    key_pairs = head_pairs(key_full, seq_count)
    value_pairs = head_pairs(value_full, seq_count)

    def forward_blocks(blocks):
        return forward_pair(blocks[0], blocks[1], blocks[2], key_mask)

    attended_pairs, log_totals = lax.map(forward_blocks, (query_pairs, key_pairs, value_pairs))
    attended_low = join_pairs(attended_pairs).reshape(tok_count, feat_width)
    middle = (
        inputs
        + jnp.dot(attended_low, proj_out, preferred_element_type=jnp.float32)
        + out_shift.astype(jnp.float32)
    )
    normed_two, norm_two_back = jax.vjp(
        layer_norm, middle, gain_two.astype(jnp.float32), shift_two.astype(jnp.float32)
    )
    normed_two_low = normed_two.astype(jnp.bfloat16)
    hidden_pre = jnp.dot(
        normed_two_low, proj_up, preferred_element_type=jnp.float32
    ) + up_shift.astype(jnp.float32)
    hidden, gelu_back = jax.vjp(gelu_tanh, hidden_pre)
    hidden_low = hidden.astype(jnp.bfloat16)
    mixed = middle + (
        jnp.dot(hidden_low, proj_down, preferred_element_type=jnp.float32)
        + down_shift.astype(jnp.float32)
    )
    back_qkv, back_out, back_up, back_down = (
        lax.all_gather(qkv_weight, ("dp", "ctx"), axis=0, tiled=True),
        lax.all_gather(out_weight, ("dp", "ctx"), axis=0, tiled=True),
        lax.all_gather(up_weight, ("dp", "ctx"), axis=0, tiled=True),
        lax.all_gather(down_weight, ("dp", "ctx"), axis=0, tiled=True),
    )
    grad_out_low = cotangent.reshape(tok_count, feat_width)
    grad_mixed = grad_out_low.astype(jnp.float32)
    grad_proj_down = jnp.einsum(
        "rf,rd->fd", hidden_low, grad_out_low, preferred_element_type=jnp.float32
    )
    grad_down_shift = column_sums(grad_mixed)
    grad_hidden = jnp.einsum(
        "rd,fd->rf", grad_out_low, back_down, preferred_element_type=jnp.float32
    )
    grad_pre_low = gelu_back(grad_hidden)[0].astype(jnp.bfloat16)
    grad_proj_up = jnp.einsum(
        "rd,rf->df", normed_two_low, grad_pre_low, preferred_element_type=jnp.float32
    )
    grad_up_shift = column_sums(grad_pre_low)
    grad_normed_two = jnp.einsum(
        "rf,df->rd", grad_pre_low, back_up, preferred_element_type=jnp.float32
    )
    grad_middle_part, grad_gain_two, grad_shift_two = norm_two_back(grad_normed_two)
    grad_middle = grad_mixed + grad_middle_part
    grad_branch_low = grad_middle.astype(jnp.bfloat16)
    grad_proj_out = jnp.einsum(
        "rc,rd->cd", attended_low, grad_branch_low, preferred_element_type=jnp.float32
    )
    grad_out_shift = column_sums(grad_branch_low)
    grad_attended_low = jnp.einsum(
        "rd,cd->rc", grad_branch_low, back_out, preferred_element_type=jnp.float32
    ).astype(jnp.bfloat16)
    grad_pairs = head_pairs(grad_attended_low, seq_count)

    def backward_blocks(blocks):
        return backward_pair(blocks[0], blocks[1], blocks[2], blocks[3], blocks[4], key_mask)

    query_grad_pairs, key_grad_pairs, value_grad_pairs = lax.map(
        backward_blocks, (query_pairs, key_pairs, value_pairs, grad_pairs, log_totals)
    )
    key_grad_own, value_grad_own = (
        lax.psum_scatter(
            join_pairs(key_grad_pairs).astype(jnp.bfloat16), "ctx", scatter_dimension=1, tiled=True
        ).astype(jnp.float32),
        lax.psum_scatter(
            join_pairs(value_grad_pairs).astype(jnp.bfloat16),
            "ctx",
            scatter_dimension=1,
            tiled=True,
        ).astype(jnp.float32),
    )
    grad_key_low = key_grad_own.reshape(tok_count, feat_width).astype(jnp.bfloat16)
    grad_value_low = value_grad_own.reshape(tok_count, feat_width).astype(jnp.bfloat16)
    grad_query_low = join_pairs(query_grad_pairs).reshape(tok_count, feat_width)
    grad_query_scaled = (grad_query_low.astype(jnp.float32) * 0.125).astype(jnp.bfloat16)
    grad_joint = jnp.concatenate([grad_query_scaled, grad_key_low, grad_value_low], axis=1)
    grad_proj_qkv = jnp.einsum(
        "rd,re->de", normed_low, grad_joint, preferred_element_type=jnp.float32
    )
    grad_query_shift = column_sums(grad_query_scaled)
    grad_value_shift = column_sums(grad_value_low)
    grad_normed = jnp.einsum("re,de->rd", grad_joint, back_qkv, preferred_element_type=jnp.float32)
    grad_input_part, grad_gain_one, grad_shift_one = norm_one_back(grad_normed)
    token_grad = (
        (grad_middle + grad_input_part)
        .astype(jnp.bfloat16)
        .reshape(seq_count, row_count, feat_width)
    )
    owned = tuple(
        (
            lax.psum_scatter(grad_gain_one, ("dp", "ctx"), scatter_dimension=0, tiled=True),
            lax.psum_scatter(grad_shift_one, ("dp", "ctx"), scatter_dimension=0, tiled=True),
            lax.psum_scatter(grad_proj_qkv, ("dp", "ctx"), scatter_dimension=0, tiled=True),
            lax.psum_scatter(grad_query_shift, ("dp", "ctx"), scatter_dimension=0, tiled=True),
            lax.psum_scatter(grad_value_shift, ("dp", "ctx"), scatter_dimension=0, tiled=True),
            lax.psum_scatter(grad_proj_out, ("dp", "ctx"), scatter_dimension=0, tiled=True),
            lax.psum_scatter(grad_out_shift, ("dp", "ctx"), scatter_dimension=0, tiled=True),
            lax.psum_scatter(grad_gain_two, ("dp", "ctx"), scatter_dimension=0, tiled=True),
            lax.psum_scatter(grad_shift_two, ("dp", "ctx"), scatter_dimension=0, tiled=True),
            lax.psum_scatter(grad_proj_up, ("dp", "ctx"), scatter_dimension=0, tiled=True),
            lax.psum_scatter(grad_up_shift, ("dp", "ctx"), scatter_dimension=0, tiled=True),
            lax.psum_scatter(grad_proj_down, ("dp", "ctx"), scatter_dimension=0, tiled=True),
            lax.psum_scatter(grad_down_shift, ("dp", "ctx"), scatter_dimension=0, tiled=True),
        )
    )
    mixed_out = mixed.astype(jnp.bfloat16).reshape(seq_count, row_count, feat_width)
    return (
        mixed_out,
        token_grad,
        owned[0],
        owned[1],
        owned[2],
        owned[3],
        owned[4],
        owned[5],
        owned[6],
        owned[7],
        owned[8],
        owned[9],
        owned[10],
        owned[11],
        owned[12],
    )


def solution(mesh):
    placed = (
        P("dp", "ctx", None),
        P("dp", None),
        P(("dp", "ctx")),
        P(("dp", "ctx")),
        P(("dp", "ctx"), None),
        P(("dp", "ctx")),
        P(("dp", "ctx")),
        P(("dp", "ctx"), None),
        P(("dp", "ctx")),
        P(("dp", "ctx")),
        P(("dp", "ctx")),
        P(("dp", "ctx"), None),
        P(("dp", "ctx")),
        P(("dp", "ctx"), None),
        P(("dp", "ctx")),
        P("dp", "ctx", None),
    )
    return jax.shard_map(
        body,
        mesh=mesh,
        in_specs=placed,
        out_specs=(
            P("dp", "ctx", None),
            P("dp", "ctx", None),
            P(("dp", "ctx")),
            P(("dp", "ctx")),
            P(("dp", "ctx"), None),
            P(("dp", "ctx")),
            P(("dp", "ctx")),
            P(("dp", "ctx"), None),
            P(("dp", "ctx")),
            P(("dp", "ctx")),
            P(("dp", "ctx")),
            P(("dp", "ctx"), None),
            P(("dp", "ctx")),
            P(("dp", "ctx"), None),
            P(("dp", "ctx")),
        ),
        check_vma=False,
    )
```

profile of v0, /device:TPU:0, one launch (start us, length us, event | category | flops | bytes accessed | tf_op | source)
XLA Modules:
  0.0 1373.7 jit_solution(8888164659233295926)
XLA Ops:
  14.0 42.6 %all-reduce.19 = (bf16[768]{0:T(1024)(128)(2,1)S(1)}, bf16[768]{0:T(1024)(128)(2,1)S(1)}, bf16[768]{0:T(1024)(128)(2,1)S(1)}, bf16[768]{0:T(1024)(128)(2,1)S(1)}...) all-reduce(bf16[768]{0:T(1024)(128)(2,1)S(1)} %dynamic-update-slice, ...), channel_id=1, replica_groups=mesh['dp'=8,'ctx'=4] {'dp','ctx'}, use_global_device_ids=true, to_apply=%add.1 | all-reduce | flops 9216 | bytes 36864
  57.9 16.2 %all-gather.7.cloned.1.call-done = bf16[768,2304]{1,0:T(8,128)(2,1)} async-done(((bf16[24,2304]{1,0:T(8,128)(2,1)}), bf16[768,2304]{1,0:T(8,128)(2,1)}) %all-gather.7.cloned.1.call-update) | async-done | bytes 3538960 | tf_op jit(solution)/shard_map/all_gather | solution.py:119
  74.1 5.8 fusion.51
  85.4 4.5 fusion.23
  106.2 24.5 %all-gather.11.cloned.1.call-done = bf16[2,2048,768]{1,2,0:T(8,128)(2,1)} async-done(((bf16[2,512,768]{1,2,0:T(8,128)(2,1)}), bf16[2,2048,768]{1,2,0:T(8,128)(2,1)}) %all-gather.11.cloned.1.call-update) | async-done | bytes 6291472 | tf_op jit(solution)/shard_map/all_gather | solution.py:162
  130.7 6.5 copy.55
  137.2 42.0 %all-gather.9.cloned.1.call-done = bf16[2,2048,768]{1,2,0:T(8,128)(2,1)} async-done(((bf16[2,512,768]{1,2,0:T(8,128)(2,1)}), bf16[2,2048,768]{1,2,0:T(8,128)(2,1)}) %all-gather.9.cloned.1.call-update) | async-done | bytes 6291472 | tf_op jit(solution)/shard_map/all_gather | solution.py:165
  179.3 6.6 copy.53
  187.1 122.2 %while.28 = (s32[]{:T(128)}, bf16[6,2,512,128]{2,3,1,0:T(8,128)(2,1)}, f32[6,2,2,512]{3,2,1,0:T(2,128)}, bf16[6,2,2048,128]{2,3,1,0:T(8,128)(2,1)}, bf16[6,2,512...) while((s32[]{:T(128)}, ...), condition=%wide.region_5.6_spmd.clone, body=%wide.region_2.5_spmd.clone.sunk | while | flops 1115813888 | bytes 67719288 | solution.py:182
  194.9 4.7 fusion.107
  199.6 5.7 fusion.108
  215.2 4.7 fusion.107
  219.9 5.7 fusion.108
  235.6 4.7 fusion.107
  240.3 5.7 fusion.108
  256.0 4.7 fusion.107
  260.6 5.7 fusion.108
  276.3 4.7 fusion.107
  281.0 5.7 fusion.108
  296.7 4.7 fusion.107
  301.4 5.7 fusion.108
  320.1 11.2 fusion.43
  331.3 35.4 %all-gather.17.cloned.1.call-done = bf16[3072,768]{1,0:T(8,128)(2,1)} async-done(((bf16[96,768]{1,0:T(8,128)(2,1)}), bf16[3072,768]{1,0:T(8,128)(2,1)}) %all-gather.17.cloned.1.call-update) | async-done | bytes 4718608 | tf_op jit(solution)/shard_map/all_gather | solution.py:128
  366.7 17.0 %convert_reduce_fusion = (f32[3072]{0:T(1024)}, bf16[1024,3072]{1,0:T(8,128)(2,1)S(1)}) fusion(f32[1024,3072]{1,0:T(8,128)} %fusion.43, f32[3072]{0:T(1024)S(1)} %copy-done.37, bf16[1024,768]{1,0:T(8,128)(2,1)} %bitcast.203, bf16[3072,768]{1,0:T(8,128)(2,1)} %all-gather.17.cloned.1.call-done), kind=kOutput, calls=%fused_computation.43 | convolution fusion | flops 4904186880 | bytes 25190400 | tf_op jit(solution)/shard_map/rd,fd->rf/dot_general | solution.py:214
  383.7 10.8 multiply_reduce_fusion.1
  409.4 325.4 %while.29 = (s32[]{:T(128)}, bf16[6,2,512,128]{2,3,1,0:T(8,128)(2,1)}, bf16[6,2,2048,128]{2,3,0,1:T(8,128)(2,1)}, bf16[6,2,2048,128]{2,3,0,1:T(8,128)(2,1)}, bf1...) while((s32[]{:T(128)}, ...), condition=%wide.region_12.13_spmd.clone, body=%wide.region_10.12_spmd.clone.sunk | while | flops 2739009536 | bytes 152383664 | solution.py:240
  417.0 8.1 fusion.119
  425.1 8.2 fusion.120
  433.3 12.1 multiply_reduce_fusion.5
  445.4 12.0 multiply_convert_fusion.6
  471.2 8.1 fusion.119
  479.3 8.2 fusion.120
  487.5 12.1 multiply_reduce_fusion.5
  499.6 12.0 multiply_convert_fusion.6
  525.3 8.1 fusion.119
  533.4 8.2 fusion.120
  541.6 12.1 multiply_reduce_fusion.5
  553.7 12.0 multiply_convert_fusion.6
  579.4 8.1 fusion.119
  587.5 8.2 fusion.120
  595.7 12.1 multiply_reduce_fusion.5
  607.8 12.0 multiply_convert_fusion.6
  633.6 8.1 fusion.119
  641.7 8.2 fusion.120
  649.9 12.1 multiply_reduce_fusion.5
  662.0 12.0 multiply_convert_fusion.6
  687.7 8.1 fusion.119
  695.8 8.2 fusion.120
  704.0 12.1 multiply_reduce_fusion.5
  716.2 12.0 multiply_convert_fusion.6
  735.7 4.8 fusion.53
  740.7 12.0 fusion.42
  754.1 13.7 fusion.44
  772.8 19.3 %reduce-scatter.7.cloned.1.call-done = bf16[2,512,768]{1,2,0:T(8,128)(2,1)} async-done(((bf16[2,2048,768]{1,2,0:T(8,128)(2,1)}), bf16[2,512,768]{1,2,0:T(8,128)(2,1)}) %reduce-scatter.7.cloned.1.call-update) | async-done | bytes 1572880 | tf_op jit(solution)/shard_map/reduce_scatter | solution.py:244
  795.0 58.3 %reduce-scatter.9.cloned.1.call-done = bf16[2,512,768]{1,2,0:T(8,128)(2,1)} async-done(((bf16[2,2048,768]{1,2,0:T(8,128)(2,1)}), bf16[2,512,768]{1,2,0:T(8,128)(2,1)}) %reduce-scatter.9.cloned.1.call-update) | async-done | bytes 1572880 | tf_op jit(solution)/shard_map/reduce_scatter | solution.py:247
  857.7 8.6 fusion.52
  867.8 13.8 %add_convert_fusion.1 = bf16[1024,768]{1,0:T(8,128)(2,1)} fusion(f32[1024,768]{1,0:T(8,128)} %copy-done.2, bf16[3072,768]{1,0:T(8,128)(2,1)} %all-gather.17.cloned.1.call-done, f32[768]{0:T(1024)S(1)} %convert_element_type.183, f32[1024,3072]{1,0:T(8,128)} %fusion.43, f32[3072]{0:T(1024)S(1)} %copy-done.38), kind=kOutput, calls=%fused_computation.79 | convolution fusion | flops 4865654784 | bytes 22035456 | tf_op jit(solution)/shard_map/dot_general | solution.py:199
  882.0 4.6 fusion.45
  890.0 40.6 %all-reduce.18 = (f32[768]{0:T(1024)S(1)}, f32[768]{0:T(1024)S(1)}, f32[768]{0:T(1024)S(1)}, f32[768]{0:T(1024)S(1)}, f32[768]{0:T(1024)S(1)}, /*index=5*/f32[76...) all-reduce(f32[768]{0:T(1024)S(1)} %get-tuple-element.208, ...), channel_id=4, replica_groups=mesh['dp'=8,'ctx'=4] {'dp','ctx'}, use_global_device_ids=true, to_apply=%region_18.19.clone | all-reduce | flops 9216 | bytes 73728
  935.9 4.5 add_convert_fusion
  940.4 17.9 %reduce-scatter.13.cloned.1.call-done = f32[24,768]{1,0:T(8,128)} async-done(((f32[768,768]{1,0:T(8,128)}), f32[24,768]{1,0:T(8,128)}) %reduce-scatter.13.cloned.1.call-update) | async-done | bytes 73744 | tf_op jit(solution)/shard_map/reduce_scatter | solution.py:278
  958.3 141.8 %reduce-scatter.15.cloned.1.call-done = f32[24,3072]{1,0:T(8,128)} async-done(((f32[768,3072]{1,0:T(8,128)}), f32[24,3072]{1,0:T(8,128)}) %reduce-scatter.15.cloned.1.call-update) | async-done | bytes 294928 | tf_op jit(solution)/shard_map/reduce_scatter | solution.py:282
  1100.2 141.3 %reduce-scatter.17.cloned.1.call-done = f32[96,768]{1,0:T(8,128)} async-done(((f32[3072,768]{1,0:T(8,128)}), f32[96,768]{1,0:T(8,128)}) %reduce-scatter.17.cloned.1.call-update) | async-done | bytes 294928 | tf_op jit(solution)/shard_map/reduce_scatter | solution.py:284
  1241.4 125.2 %reduce-scatter.11.cloned.1.call-done = f32[24,2304]{1,0:T(8,128)} async-done(((f32[768,2304]{1,0:T(8,128)}), f32[24,2304]{1,0:T(8,128)}) %reduce-scatter.11.cloned.1.call-update) | async-done | bytes 221200 | tf_op jit(solution)/shard_map/reduce_scatter | solution.py:275
  (328 shorter events, 222.9 us)
Async XLA Ops:
  7.2 50.1 %copy-start = (bf16[2,512,768]{2,1,0:T(8,128)(2,1)S(1)}, bf16[2,512,768]{2,1,0:T(8,128)(2,1)}, u32[]{:S(2)}) copy-start(bf16[2,512,768]{2,1,0:T(8,128)(2,1)} %param.20) | copy-start | bytes 4718596
  7.2 4.7 copy-start.46
  7.2 4.9 copy-start.47
  7.2 5.1 copy-start.48
  7.2 5.4 copy-start.49
  7.2 5.6 copy-start.50
  7.2 5.8 copy-start.51
  7.3 6.0 copy-start.52
  7.3 6.3 copy-start.53
  7.3 6.5 copy-start.54
  7.3 66.8 %all-gather.7.cloned.1.call-start = ((), (), s32[]{:S(2)}) async-start(), calls=%async_computation.6 | async-start | bytes 3649536 | tf_op jit(solution)/shard_map/all_gather | solution.py:119
  8.0 122.7 %all-gather.11.cloned.1.call-start = ((), (), s32[]{:S(2)}) async-start(), calls=%async_computation.8 | async-start | bytes 7864320 | tf_op jit(solution)/shard_map/all_gather | solution.py:162
  9.8 70.1 %copy-start.24 = (f32[1,4,2,128]{3,1,2,0:T(4,128)}, f32[1,4,2,128]{3,1,2,0:T(4,128)S(1)}, u32[]{:S(2)}) copy-start(f32[1,4,2,128]{3,1,2,0:T(4,128)S(1)} %copy.91) | copy-start | bytes 12292
  11.8 44.8 %copy-start.34 = (f32[1,4,2,128]{3,1,2,0:T(4,128)}, f32[1,4,2,128]{3,1,2,0:T(4,128)S(1)}, u32[]{:S(2)}) copy-start(f32[1,4,2,128]{3,1,2,0:T(4,128)S(1)} %copy.92) | copy-start | bytes 12292
  11.8 68.1 %copy-start.26 = (f32[1024]{0:T(1024)}, f32[1024]{0:T(1024)S(1)}, u32[]{:S(2)}) copy-start(f32[1024]{0:T(1024)S(1)} %rsqrt.20) | copy-start | bytes 12292
  57.9 22.0 %copy-start.15 = (bf16[1024,768]{1,0:T(8,128)(2,1)}, bf16[1024,768]{1,0:T(8,128)(2,1)S(1)}, u32[]{:S(2)}) copy-start(bf16[1024,768]{1,0:T(8,128)(2,1)S(1)} %fusion.31) | copy-start | bytes 4718596
  79.9 3.7 copy-start.11
  85.4 93.9 %all-gather.9.cloned.1.call-start = ((), (), s32[]{:S(2)}) async-start(), calls=%async_computation.7 | async-start | bytes 7864320 | tf_op jit(solution)/shard_map/all_gather | solution.py:165
  89.9 6.5 copy-start.14
  91.5 222.4 %all-gather.13.cloned.1.call-start = ((), (), s32[]{:S(2)}) async-start(), calls=%async_computation.9 | async-start | bytes 1216512 | tf_op jit(solution)/shard_map/all_gather | solution.py:122
  92.1 228.0 %all-gather.15.cloned.1.call-start = ((), (), s32[]{:S(2)}) async-start(), calls=%async_computation.10 | async-start | bytes 4866048 | tf_op jit(solution)/shard_map/all_gather | solution.py:126
  92.7 274.0 %all-gather.17.cloned.1.call-start = ((), (), s32[]{:S(2)}) async-start(), calls=%async_computation.11 | async-start | bytes 4866048 | tf_op jit(solution)/shard_map/all_gather | solution.py:128
  93.3 698.9 %reduce-scatter.7.cloned.1.call-start = ((), (), s32[]{:S(2)}) async-start(), calls=%async_computation.12 | async-start | bytes 7864320 | tf_op jit(solution)/shard_map/reduce_scatter | solution.py:244
  309.3 4.6 copy-start.40
  317.9 1.7 copy-start.2
  317.9 2.2 copy-start.22
  317.9 2.2 copy-start.30
  317.9 76.6 %copy-start.18 = (f32[1024]{0:T(1024)}, f32[1024]{0:T(1024)S(1)}, u32[]{:S(2)}) copy-start(f32[1024]{0:T(1024)S(1)} %broadcast_multiply_fusion) | copy-start | bytes 12292
  320.1 74.5 %copy-start.20 = (f32[1024]{0:T(1024)}, f32[1024]{0:T(1024)S(1)}, u32[]{:S(2)}) copy-start(f32[1024]{0:T(1024)S(1)} %fusion.39) | copy-start | bytes 12292
  320.1 46.7 %copy-start.37 = (f32[3072]{0:T(1024)S(1)}, f32[3072]{0:T(1024)}, u32[]{:S(2)}) copy-start(f32[3072]{0:T(1024)} %convert_element_type.181) | copy-start | bytes 36868
  366.7 17.0 %copy-start.3 = (f32[1024,768]{1,0:T(8,128)S(1)}, f32[1024,768]{1,0:T(8,128)}, u32[]{:S(2)}) copy-start(f32[1024,768]{1,0:T(8,128)} %copy-done.2) | copy-start | bytes 9437188
  383.7 10.8 copy-start.10
  394.6 1.5 copy-start.6
  396.1 1.7 copy-start.5
  396.1 1.7 copy-start.32
  396.1 3.0 copy-start.45
  734.9 118.4 %reduce-scatter.9.cloned.1.call-start = ((), (), s32[]{:S(2)}) async-start(), calls=%async_computation.13 | async-start | bytes 7864320 | tf_op jit(solution)/shard_map/reduce_scatter | solution.py:247
  735.6 5.0 copy-start.4
  735.6 5.0 copy-start.19
  735.6 5.0 copy-start.21
  735.6 5.0 copy-start.23
  735.7 5.0 copy-start.31
  735.7 222.6 %reduce-scatter.13.cloned.1.call-start = ((), (), s32[]{:S(2)}) async-start(), calls=%async_computation.15 | async-start | bytes 2433024 | tf_op jit(solution)/shard_map/reduce_scatter | solution.py:278
  740.6 359.6 %reduce-scatter.15.cloned.1.call-start = ((), (), s32[]{:S(2)}) async-start(), calls=%async_computation.16 | async-start | bytes 9732096 | tf_op jit(solution)/shard_map/reduce_scatter | solution.py:282
  752.7 1.4 copy-start.38
  752.7 488.7 %reduce-scatter.17.cloned.1.call-start = ((), (), s32[]{:S(2)}) async-start(), calls=%async_computation.17 | async-start | bytes 9732096 | tf_op jit(solution)/shard_map/reduce_scatter | solution.py:284
  767.8 598.8 %reduce-scatter.11.cloned.1.call-start = ((), (), s32[]{:S(2)}) async-start(), calls=%async_computation.14 | async-start | bytes 7299072 | tf_op jit(solution)/shard_map/reduce_scatter | solution.py:275
  853.3 1.9 copy-start.13
  855.2 2.6 copy-start.16
  867.3 14.6 %slice-start = ((s8[4718592]{0:T(1024)(128)(4,1)}), s8[4194304]{0:T(1024)(128)(4,1)S(1)}, s32[]{:S(2)}) async-start(s8[4718592]{0:T(1024)(128)(4,1)} %bitcast.225), calls=%async_computation.18 | async-start | bytes 8388608
  867.7 13.9 %copy-start.12 = (bf16[2,512,768]{1,2,0:T(8,128)(2,1)S(1)}, bf16[2,512,768]{1,2,0:T(8,128)(2,1)}, u32[]{:S(2)}) copy-start(bf16[2,512,768]{1,2,0:T(8,128)(2,1)} %reduce-scatter.9.cloned.1.call-done) | copy-start | bytes 4718596
  867.7 14.2 %copy-start.1 = (bf16[2,512,768]{2,1,0:T(8,128)(2,1)S(1)}, bf16[2,512,768]{2,1,0:T(8,128)(2,1)}, u32[]{:S(2)}) copy-start(bf16[2,512,768]{2,1,0:T(8,128)(2,1)} %param.20) | copy-start | bytes 4718596
  867.7 14.2 %slice-start.1 = ((s8[4718592]{0:T(1024)(128)(4,1)}), s8[524288]{0:T(1024)(128)(4,1)S(1)}, s32[]{:S(2)}) async-start(s8[4718592]{0:T(1024)(128)(4,1)} %bitcast.225), calls=%async_computation.19 | async-start | bytes 1048576
  867.7 14.2 %copy-start.25 = (f32[1,4,2,128]{3,1,2,0:T(4,128)S(1)}, f32[1,4,2,128]{3,1,2,0:T(4,128)}, u32[]{:S(2)}) copy-start(f32[1,4,2,128]{3,1,2,0:T(4,128)} %copy-done.24) | copy-start | bytes 12292
  867.8 14.2 %copy-start.29 = (f32[768]{0:T(1024)S(1)}, f32[768]{0:T(1024)}, u32[]{:S(2)}) copy-start(f32[768]{0:T(1024)} %copy-done.28) | copy-start | bytes 9220
  867.8 14.2 %copy-start.44 = (bf16[768,2304]{1,0:T(8,128)(2,1)S(1)}, bf16[768,2304]{1,0:T(8,128)(2,1)}, u32[]{:S(2)}) copy-start(bf16[768,2304]{1,0:T(8,128)(2,1)} %all-gather.7.cloned.1.call-done) | copy-start | bytes 10616836
  882.0 4.7 copy-start.35
  882.0 6.3 copy-start.27
  886.6 1.6 copy-start.9
  886.6 3.4 copy-start.36
  886.6 3.4 copy-start.39
  886.6 3.4 copy-start.41
  886.6 3.4 copy-start.42
  886.7 49.2 %copy-start.33 = (f32[1024]{0:T(1024)S(1)}, f32[1024]{0:T(1024)}, u32[]{:S(2)}) copy-start(f32[1024]{0:T(1024)} %copy-done.32) | copy-start | bytes 12292
  (5 other events, 5.4 us)
Sparse Core Ops, SparseCore 0:
  11.0 63.0 all-gather.6
  85.5 45.1 all-gather.10
  132.8 46.3 all-gather.8
  182.0 54.0 all-gather.12
  238.8 62.5 all-gather.14
  304.2 62.4 all-gather.16
  735.0 57.1 reduce-scatter.6
  794.9 58.3 reduce-scatter.8
  859.1 99.1 reduce-scatter.12
  965.6 134.4 reduce-scatter.14
  1106.6 134.7 reduce-scatter.16
  1248.5 118.0 reduce-scatter.10
where the time goes:
time: 1380 us; the launch traced here: 1370 us
  waiting for transfers between devices  625 us (45%)
  matrix products  359 us (26%)
  other arithmetic  147 us (11%)
  local copies, waits for them, and re-layouts  143 us (10%)
  blocking collectives  83.2 us (6%)
  between operations  15.3 us (1%)
    reduce_scatter x1, waiting for transfers between devices, body(): lax.psum_scatter(grad_proj_up, ('dp', 'ctx'), scatter_dimension=0, tiled=...  142 us
    reduce_scatter x1, waiting for transfers between devices, body(): lax.psum_scatter(grad_proj_down, ('dp', 'ctx'), scatter_dimension=0, tile...  141 us
    reduce_scatter x1, waiting for transfers between devices, body(): lax.psum_scatter(grad_proj_qkv, ('dp', 'ctx'), scatter_dimension=0, tiled...  125 us
    unnamed x2, blocking collectives  83.2 us
    dot_general x6, matrix products, backward_pair(): jnp.einsum('sqhd,skhd->shqk', split_heads(grad_block), split_heads(value_...  72.6 us
    convert_element_type x6, other arithmetic, backward_pair(): grad_scores = (probs * (grad_probs - row_inner)).astype(jnp.bfloat16)  72.2 us
    dot_general x12, matrix products, pair_scores(): jnp.einsum('sqhd,skhd->shqk', split_heads(query_block), split_heads(key_b...  68.8 us
    reduce_scatter x1, waiting for transfers between devices, body(): lax.psum_scatter(join_pairs(value_grad_pairs).astype(jnp.bfloat16), 'ctx'...  58.3 us
  transfers between devices with their start and end apart: 12, of which 10 were waited for; matrix products, arithmetic and copies ran while one was open for 19% of the time, Pallas kernels for 0%

commit v1 on v0

v1 whole, which is shorter than its diff:
```python
import functools

import jax
import jax.numpy as jnp
from jax import lax
from jax.experimental import pallas as pl
from jax.experimental.pallas import tpu as pltpu
from jax.sharding import Mesh, PartitionSpec as P

HEAD_DIM = 64
PAIR = 2 * HEAD_DIM
EPSILON = 1e-05
NEG = -1e30
BLK = 512
F32 = jnp.float32
BF16 = jnp.bfloat16

NN = (((1,), (0,)), ((), ()))
NT = (((1,), (1,)), ((), ()))
TN = (((0,), (0,)), ((), ()))


def mm(left, right, dims=NN):
    return lax.dot_general(left, right, dims, preferred_element_type=F32)


def build_scores_operands(qkv_ref, qs_ref, ks_ref, rows, qx, kx):
    lane = lax.broadcasted_iota(jnp.int32, (BLK, PAIR), 1)
    first = lane < HEAD_DIM
    q = qkv_ref[rows, 0:PAIR].astype(F32)
    k = qkv_ref[rows, PAIR : 2 * PAIR].astype(F32)
    qs = qs_ref[rows, :].astype(F32)
    ks = ks_ref[rows, :].astype(F32)
    qx[0, rows, :] = jnp.where(first, q, qs).astype(BF16)
    qx[1, rows, :] = jnp.where(first, qs, q).astype(BF16)
    kx[0, rows, :] = jnp.where(first, k, ks).astype(BF16)
    kx[1, rows, :] = jnp.where(first, ks, k).astype(BF16)
    return first, q, k


def causal_block(scores):
    key_at = lax.broadcasted_iota(jnp.int32, scores.shape, 0)
    query_at = lax.broadcasted_iota(jnp.int32, scores.shape, 1)
    return jnp.where(key_at <= query_at, scores, NEG)


def attention_forward_kernel(qkv_ref, qs_ref, ks_ref, o_ref, lse_ref, qx, kx, vt, acc):
    length = qkv_ref.shape[0]
    blocks = length // BLK

    @pl.loop(0, blocks)
    def _(i):
        rows = pl.ds(pl.multiple_of(i * BLK, BLK), BLK)
        build_scores_operands(qkv_ref, qs_ref, ks_ref, rows, qx, kx)
        v_t = qkv_ref[rows, 2 * PAIR : 3 * PAIR].astype(F32).T
        ones = jnp.ones((16, BLK), BF16)
        for h in range(2):
            vt[h, 0:HEAD_DIM, rows] = v_t[h * HEAD_DIM : (h + 1) * HEAD_DIM].astype(BF16)
            vt[h, HEAD_DIM : HEAD_DIM + 16, rows] = ones

    @pl.loop(0, blocks)
    def _(i):
        rows = pl.ds(pl.multiple_of(i * BLK, BLK), BLK)
        queries = [qx[h, rows, :] for h in range(2)]
        tops = []
        for h in range(2):
            s = causal_block(mm(kx[h, rows, :], queries[h], NT))
            top = jnp.max(s, axis=0, keepdims=True)
            p = jnp.exp(s - top).astype(BF16)
            acc[h] = mm(vt[h, :, rows], p)
            tops.append(top)

        def step(j, carry):
            keys = pl.ds(pl.multiple_of(j * BLK, BLK), BLK)
            out = []
            for h in range(2):
                s = mm(kx[h, keys, :], qx[h, rows, :], NT)
                top = jnp.maximum(carry[h], jnp.max(s, axis=0, keepdims=True))
                p = jnp.exp(s - top).astype(BF16)
                acc[h] = acc[h] * jnp.exp(carry[h] - top) + mm(vt[h, :, keys], p)
                out.append(top)
            return tuple(out)

        tops = lax.fori_loop(0, i, step, tuple(tops))
        parts = []
        for h in range(2):
            total = acc[h, HEAD_DIM : HEAD_DIM + 1, :]
            parts.append(acc[h, 0:HEAD_DIM, :] / total)
            lse_ref[0, h : h + 1, rows] = tops[h] + jnp.log(total)
        o_ref[rows, :] = jnp.concatenate(parts, axis=0).T.astype(BF16)


def attention_backward_kernel(
    qkv_ref, qs_ref, ks_ref, o_ref, do_ref, lse_ref, d_ref, qx, kx, qm, dm, kt, delta, dqt, dk, dv
):
    length = qkv_ref.shape[0]
    blocks = length // BLK

    @pl.loop(0, blocks)
    def _(i):
        rows = pl.ds(pl.multiple_of(i * BLK, BLK), BLK)
        first, q, k = build_scores_operands(qkv_ref, qs_ref, ks_ref, rows, qx, kx)
        do = do_ref[rows, :].astype(F32)
        zero = jnp.zeros_like(q)
        qm[0, rows, :] = jnp.where(first, q, zero).astype(BF16)
        qm[1, rows, :] = jnp.where(first, zero, q).astype(BF16)
        dm[0, rows, :] = jnp.where(first, do, zero).astype(BF16)
        dm[1, rows, :] = jnp.where(first, zero, do).astype(BF16)
        kt[:, rows] = k.T.astype(BF16)
        inner = (do * o_ref[rows, :].astype(F32)).T
        for h in range(2):
            delta[h : h + 1, rows] = jnp.sum(
                inner[h * HEAD_DIM : (h + 1) * HEAD_DIM], axis=0, keepdims=True
            )
        dqt[:, rows] = jnp.zeros((PAIR, BLK), F32)

    def tile(keys, rows, masked):
        values = qkv_ref[keys, 2 * PAIR : 3 * PAIR]
        dv_part, dk_part = None, None
        for h in range(2):
            s = mm(kx[h, keys, :], qx[h, rows, :], NT)
            if masked:
                s = causal_block(s)
            p = jnp.exp(s - lse_ref[0, h : h + 1, rows])
            dp = mm(values, dm[h, rows, :], NT)
            ds = (p * (dp - delta[h : h + 1, rows])).astype(BF16)
            dv_h = mm(p.astype(BF16), dm[h, rows, :])
            dk_h = mm(ds, qm[h, rows, :])
            dv_part = dv_h if h == 0 else dv_part + dv_h
            dk_part = dk_h if h == 0 else dk_part + dk_h
            part = slice(h * HEAD_DIM, (h + 1) * HEAD_DIM)
            dqt[part, rows] += mm(kt[part, keys], ds)
        return dk_part, dv_part

    @pl.loop(0, blocks)
    def _(j):
        keys = pl.ds(pl.multiple_of(j * BLK, BLK), BLK)
        dk[...], dv[...] = tile(keys, keys, True)

        @pl.loop(j + 1, blocks)
        def _(i):
            dk_part, dv_part = tile(keys, pl.ds(pl.multiple_of(i * BLK, BLK), BLK), False)
            dk[...] += dk_part
            dv[...] += dv_part

        d_ref[keys, PAIR : 2 * PAIR] = dk[...].astype(BF16)
        d_ref[keys, 2 * PAIR : 3 * PAIR] = dv[...].astype(BF16)

    @pl.loop(0, blocks)
    def _(i):
        rows = pl.ds(pl.multiple_of(i * BLK, BLK), BLK)
        d_ref[rows, 0:PAIR] = (dqt[:, rows].T.astype(BF16).astype(F32) * 0.125).astype(BF16)


VMEM_LIMIT = 48 * 1024 * 1024


def attention_forward(qkv, query_code, key_code):
    length, width = qkv.shape
    pairs = width // (3 * PAIR)
    tiles = pairs * 2 * length * length
    return pl.pallas_call(
        attention_forward_kernel,
        grid=(pairs,),
        in_specs=[
            pl.BlockSpec((length, 3 * PAIR), lambda p: (0, p)),
            pl.BlockSpec((length, PAIR), lambda p: (0, 0)),
            pl.BlockSpec((length, PAIR), lambda p: (0, 0)),
        ],
        out_specs=[
            pl.BlockSpec((length, PAIR), lambda p: (0, p)),
            pl.BlockSpec((1, 8, length), lambda p: (p, 0, 0)),
        ],
        out_shape=[
            jax.ShapeDtypeStruct((length, pairs * PAIR), BF16),
            jax.ShapeDtypeStruct((pairs, 8, length), F32),
        ],
        scratch_shapes=[
            pltpu.VMEM((2, length, PAIR), BF16),
            pltpu.VMEM((2, length, PAIR), BF16),
            pltpu.VMEM((2, HEAD_DIM + 16, length), BF16),
            pltpu.VMEM((2, HEAD_DIM + 16, BLK), F32),
        ],
        compiler_params=pltpu.CompilerParams(vmem_limit_bytes=VMEM_LIMIT),
        cost_estimate=pl.CostEstimate(
            flops=tiles * 1024, bytes_accessed=length * width * 3, transcendentals=tiles // 2
        ),
    )(qkv, query_code, key_code)


def attention_backward(qkv, query_code, key_code, attended, grad_attended, log_total):
    length, width = qkv.shape
    pairs = width // (3 * PAIR)
    tiles = pairs * 2 * length * length
    return pl.pallas_call(
        attention_backward_kernel,
        grid=(pairs,),
        in_specs=[
            pl.BlockSpec((length, 3 * PAIR), lambda p: (0, p)),
            pl.BlockSpec((length, PAIR), lambda p: (0, 0)),
            pl.BlockSpec((length, PAIR), lambda p: (0, 0)),
            pl.BlockSpec((length, PAIR), lambda p: (0, p)),
            pl.BlockSpec((length, PAIR), lambda p: (0, p)),
            pl.BlockSpec((1, 8, length), lambda p: (p, 0, 0)),
        ],
        out_specs=pl.BlockSpec((length, 3 * PAIR), lambda p: (0, p)),
        out_shape=jax.ShapeDtypeStruct((length, width), BF16),
        scratch_shapes=[
            pltpu.VMEM((2, length, PAIR), BF16),
            pltpu.VMEM((2, length, PAIR), BF16),
            pltpu.VMEM((2, length, PAIR), BF16),
            pltpu.VMEM((2, length, PAIR), BF16),
            pltpu.VMEM((PAIR, length), BF16),
            pltpu.VMEM((8, length), F32),
            pltpu.VMEM((PAIR, length), F32),
            pltpu.VMEM((BLK, PAIR), F32),
            pltpu.VMEM((BLK, PAIR), F32),
        ],
        compiler_params=pltpu.CompilerParams(vmem_limit_bytes=VMEM_LIMIT),
        cost_estimate=pl.CostEstimate(
            flops=tiles * 2560, bytes_accessed=length * width * 6, transcendentals=tiles // 2
        ),
    )(qkv, query_code, key_code, attended, grad_attended, log_total)


def norm_forward(source):
    average = jnp.mean(source, axis=-1, keepdims=True)
    centred = source - average
    spread = jnp.mean(centred * centred, axis=-1, keepdims=True)
    scale = lax.rsqrt(spread + EPSILON)
    return centred * scale, scale


def norm_backward(normal, scale, grad):
    return scale * (
        grad
        - jnp.mean(grad, axis=-1, keepdims=True)
        - normal * jnp.mean(grad * normal, axis=-1, keepdims=True)
    )


GELU_A = 0.7978845608028654
GELU_B = 0.044715


def gelu_parts(source):
    square = source * source
    inner = jnp.tanh(GELU_A * (source + GELU_B * source * square))
    value = 0.5 * source * (1.0 + inner)
    slope = 0.5 * (1.0 + inner) + 0.5 * source * (1.0 - inner * inner) * (
        GELU_A * (1.0 + 3.0 * GELU_B * square)
    )
    return value, slope


def swap(value, axis):
    return lax.ppermute(value, axis, [(0, 1), (1, 0)])


def pick(flag, first, second):
    return jnp.where(flag == 0, first, second), jnp.where(flag == 0, second, first)


def body(
    tokens,
    segments,
    ln1_gain,
    ln1_bias,
    qkv_weight,
    q_bias,
    v_bias,
    out_weight,
    out_bias,
    ln2_gain,
    ln2_bias,
    up_weight,
    up_bias,
    down_weight,
    down_bias,
    cotangent,
):
    side = lax.axis_index("xx")
    core = lax.axis_index("core")
    chips = lax.axis_size("dp") * lax.axis_size("xx")
    seq_count, quarter, width = tokens.shape
    length = segments.shape[1]
    own = qkv_weight.shape[0]
    pair_row = 2 * own
    hidden_own = up_bias.shape[0]
    half = width // 2
    cols = 3 * half
    pairs = half // PAIR
    splits = hidden_own // pair_row
    hidden = splits * width

    def at_index(array, index):
        return lax.dynamic_index_in_dim(array, index, 0, keepdims=False)

    def to_sequence(array):
        kept = at_index(array, side)
        come = swap(at_index(array, 1 - side), "xx")
        low, high = pick(side, kept, come)
        mine = jnp.stack([low, high])
        other = swap(mine, "core")
        even, odd = pick(core, mine, other)
        return jnp.stack([even, odd], axis=1).reshape(length, width)

    def own_rows(array):
        return lax.dynamic_index_in_dim(
            array.reshape(2, 2, quarter, array.shape[-1]), core, 1, keepdims=False
        )

    def other_rows(array):
        return lax.dynamic_index_in_dim(
            array.reshape(2, 2, quarter, array.shape[-1]), 1 - core, 1, keepdims=False
        )

    def from_sequence(mine):
        come = swap(at_index(mine, 1 - side), "xx")
        first, second = pick(side, at_index(mine, side), come)
        return jnp.stack([first, second])

    qkv_cols = qkv_weight.reshape(own, 3, 2, pairs, PAIR).transpose(2, 0, 3, 1, 4).reshape(2, own, cols)
    up_cols = (
        up_weight.reshape(own, chips, 2, splits, pair_row)
        .transpose(2, 0, 3, 1, 4)
        .reshape(2, own, hidden)
    )
    vectors = jnp.stack(
        [ln1_gain, ln1_bias, q_bias, v_bias, out_bias, ln2_gain, ln2_bias, down_bias], axis=1
    )
    vectors = jnp.pad(vectors, ((0, 0), (0, PAIR - vectors.shape[1])))

    def with_partner(two):
        mine, theirs = at_index(two, core), at_index(two, 1 - core)
        first, second = pick(core, mine, swap(theirs, "core"))
        return jnp.concatenate([first, second], axis=0)

    early = with_partner(
        jnp.concatenate([qkv_cols, jnp.broadcast_to(vectors, (2, own, PAIR))], axis=2)
    )
    early = jnp.concatenate(
        [
            early[:, : cols + 8],
            up_bias.reshape(splits, pair_row).T,
            early[:, cols + 8 + splits :],
        ],
        axis=1,
    )
    late = with_partner(
        jnp.concatenate([up_cols, jnp.broadcast_to(out_weight, (2, own, width))], axis=2)
    )
    down_own = down_weight.reshape(splits, pair_row, width)
    late = jnp.concatenate([late] + [down_own[i] for i in range(splits)], axis=1)
    early = lax.all_gather(early, ("dp", "xx"), axis=0, tiled=True)
    late = lax.all_gather(late, ("dp", "xx"), axis=0, tiled=True)
    proj_qkv = early[:, :cols]
    small = early[:, cols:].astype(F32).T
    gain_one, shift_one, query_shift, value_shift, out_shift, gain_two, shift_two, down_shift = (
        small[i] for i in range(8)
    )
    up_shift = small[8 : 8 + splits].reshape(hidden)
    proj_up = late[:, :hidden]
    proj_out = lax.dynamic_slice_in_dim(late[:, hidden : hidden + width], core * half, half, 0)
    proj_down = jnp.concatenate(
        [late[:, hidden + (1 + i) * width : hidden + (2 + i) * width] for i in range(splits)], axis=0
    )

    inputs = to_sequence(tokens).astype(F32)
    grad_out_low = to_sequence(cotangent)
    seg = at_index(segments, side)
    numbers = jnp.arange(PAIR, dtype=jnp.int32) % HEAD_DIM
    same = seg[:, None] == numbers[None, :]
    coded = numbers[None, :] < 4
    query_code = jnp.where(same & coded, 1.0, 0.0).astype(BF16)
    key_code = jnp.where(same | ~coded, 0.0, NEG).astype(BF16)

    normal_one, scale_one = norm_forward(inputs)
    normed_low = (normal_one * gain_one + shift_one).astype(BF16)

    def head_cols(vector):
        return lax.dynamic_slice_in_dim(vector, core * half, half, 0).reshape(pairs, 1, PAIR)

    zeros = jnp.zeros((pairs, 1, PAIR), F32)
    qkv_shift = jnp.concatenate(
        [head_cols(query_shift), zeros, head_cols(value_shift)], axis=1
    ).reshape(1, cols)
    qkv_scale = jnp.tile(jnp.repeat(jnp.array([0.125, 1.0, 1.0], F32), PAIR), pairs)[None]
    qkv = ((mm(normed_low, proj_qkv) + qkv_shift) * qkv_scale).astype(BF16)
    attended, log_total = attention_forward(qkv, query_code, key_code)

    branch = mm(attended, proj_out).astype(BF16)
    middle = inputs + (branch.astype(F32) + swap(branch, "core").astype(F32)) + out_shift
    normal_two, scale_two = norm_forward(middle)
    normed_two_low = (normal_two * gain_two + shift_two).astype(BF16)
    hidden_value, hidden_slope = gelu_parts(mm(normed_two_low, proj_up) + up_shift)
    hidden_low = hidden_value.astype(BF16)
    ffn = mm(hidden_low, proj_down)
    ffn_own = own_rows(ffn) + swap(other_rows(ffn).astype(BF16), "core").astype(F32)
    mixed = from_sequence((own_rows(middle) + ffn_own + down_shift).astype(BF16))

    grad_mixed = grad_out_low.astype(F32)
    grad_hidden = mm(grad_out_low, proj_down, NT)
    grad_pre_low = (hidden_slope * grad_hidden).astype(BF16)
    grad_proj_down = [
        mm(hidden_low[:, i * width : (i + 1) * width], grad_out_low, TN) for i in range(splits)
    ]
    grad_proj_up = mm(normed_two_low, grad_pre_low, TN)
    partial_two = mm(grad_pre_low, proj_up, NT).astype(BF16)
    grad_normed_two = partial_two.astype(F32) + swap(partial_two, "core").astype(F32)
    grad_middle = grad_mixed + norm_backward(normal_two, scale_two, grad_normed_two * gain_two)
    branch_low = grad_middle.astype(BF16)
    grad_proj_out = mm(attended, branch_low, TN)
    grad_attended = mm(branch_low, proj_out, NT).astype(BF16)

    def as_column(vectors):
        table = jnp.stack(vectors, axis=1)
        return jnp.pad(table, ((0, 0), (0, PAIR - table.shape[1])))

    def only_mine(flag, array):
        return jnp.where(flag, array, jnp.zeros_like(array))

    small_two = as_column(
        [
            jnp.sum(branch_low.astype(F32), axis=0),
            jnp.sum(grad_normed_two * normal_two, axis=0),
            jnp.sum(grad_normed_two, axis=0),
            jnp.sum(grad_mixed, axis=0),
        ]
        + [
            jnp.sum(grad_pre_low[:, i * width : (i + 1) * width].astype(F32), axis=0)
            for i in range(splits)
        ]
    )
    grad_out_low_b = grad_proj_out.astype(BF16)
    late_grads = jnp.concatenate(
        [
            grad_proj_up.astype(BF16),
            jnp.concatenate(
                [only_mine(core == 0, grad_out_low_b), only_mine(core == 1, grad_out_low_b)], axis=0
            ),
        ]
        + [part.astype(BF16) for part in grad_proj_down]
        + [small_two.astype(BF16)],
        axis=1,
    )
    late_own = lax.psum_scatter(late_grads, ("dp", "xx"), scatter_dimension=0, tiled=True)

    grad_qkv = attention_backward(qkv, query_code, key_code, attended, grad_attended, log_total)
    grad_proj_qkv = mm(normed_low, grad_qkv, TN)
    partial_one = mm(grad_qkv, proj_qkv, NT).astype(BF16)
    grad_normed = own_rows(partial_one).astype(F32) + swap(other_rows(partial_one), "core").astype(F32)
    normal_own, scale_own = norm_forward(own_rows(inputs))
    token_grad = from_sequence(
        (
            own_rows(grad_middle) + norm_backward(normal_own, scale_own, grad_normed * gain_one)
        ).astype(BF16)
    )
    grad_by_pair = jnp.sum(grad_qkv.astype(F32), axis=0).reshape(pairs, 3, PAIR)

    def padded(vector):
        vector = vector.reshape(half)
        return jnp.concatenate([only_mine(core == 0, vector), only_mine(core == 1, vector)])

    small_one = as_column(
        [
            jnp.sum(grad_normed * normal_own, axis=(0, 1)),
            jnp.sum(grad_normed, axis=(0, 1)),
            padded(grad_by_pair[:, 0]),
            padded(grad_by_pair[:, 2]),
        ]
    )
    early_grads = jnp.concatenate([grad_proj_qkv.astype(BF16), small_one.astype(BF16)], axis=1)
    early_own = lax.psum_scatter(early_grads, ("dp", "xx"), scatter_dimension=0, tiled=True)

    def rows_of(array, index):
        return lax.dynamic_slice_in_dim(array, index * own, own, 0)

    late_mine = rows_of(late_own, core)
    late_come = swap(rows_of(late_own, 1 - core)[:, : hidden + width], "core")
    early_mine = rows_of(early_own, core)
    early_come = swap(rows_of(early_own, 1 - core), "core")

    def by_core(mine, come):
        return jnp.stack(pick(core, mine, come))

    out_grad = (late_mine[:, hidden : hidden + width] + late_come[:, hidden:]).astype(F32)
    up_grad = (
        by_core(late_mine[:, :hidden], late_come[:, :hidden])
        .reshape(2, own, splits, chips, pair_row)
        .transpose(1, 3, 0, 2, 4)
        .reshape(own, 2 * hidden)
        .astype(F32)
    )
    down_grad = jnp.concatenate(
        [late_own[:, hidden + (1 + i) * width : hidden + (2 + i) * width] for i in range(splits)],
        axis=0,
    ).astype(F32)
    tail = hidden + (1 + splits) * width
    up_shift_grad = late_own[:, tail + 4 : tail + 4 + splits].T.reshape(hidden_own).astype(F32)
    qkv_grad = (
        by_core(early_mine[:, :cols], early_come[:, :cols])
        .reshape(2, own, pairs, 3, PAIR)
        .transpose(1, 3, 0, 2, 4)
        .reshape(own, 2 * cols)
        .astype(F32)
    )
    one = early_mine[:, cols : cols + 4].astype(F32) + early_come[:, cols : cols + 4].astype(F32)
    two = late_mine[:, tail : tail + 4].astype(F32)
    return (
        mixed,
        token_grad,
        one[:, 0],
        one[:, 1],
        qkv_grad,
        one[:, 2],
        one[:, 3],
        out_grad,
        two[:, 0],
        two[:, 1],
        two[:, 2],
        up_grad,
        up_shift_grad,
        down_grad,
        two[:, 3],
    )


def solution(mesh):
    parts = (mesh.shape["dp"], mesh.shape["ctx"] // 2, 2)
    split_mesh = Mesh(mesh.devices.reshape(parts), ("dp", "xx", "core"))
    rows = ("dp", "xx", "core")
    acts = P("dp", ("xx", "core"), None)
    vec, mat = P(rows), P(rows, None)
    return jax.shard_map(
        body,
        mesh=split_mesh,
        in_specs=(
            acts, P("dp", None), vec, vec, mat, vec, vec, mat, vec, vec, vec, mat, vec, mat, vec, acts,
        ),
        out_specs=(
            acts, acts, vec, vec, mat, vec, vec, mat, vec, vec, vec, mat, vec, mat, vec,
        ),
        check_vma=False,
    )
```

time: 1380 us -> 641 us (0.46)
  waiting for transfers between devices: 625 us -> 311 us
  matrix products: 359 us -> 95.9 us
  local copies, waits for them, and re-layouts: 143 us -> 41 us
  Pallas kernels: 0 us -> 91.5 us
  blocking collectives: 83.2 us -> 0 us
  other arithmetic: 147 us -> 67.2 us
    reduce_scatter x6 -> x2, waiting for transfers between devices: 504 us -> 185 us  [the longest x1 146 us: body(): lax.psum_scatter(late_grads, ('dp', 'xx'), scatter_dimension=0, tiled=True)]
    dot_general x54 -> x13, matrix products: 359 us -> 95.9 us  [mm(): return lax.dot_general(left, right, dims, preferred_element_type=F32)]
    pallas_call x0 -> x2, Pallas kernels: none -> 91.5 us  [the longest x1 54 us: attention_backward(): pl.pallas_call(attention_backward_kernel, grid=(pairs,), in_specs=[pl.Blo...]
    unnamed x2 -> x0, blocking collectives: 83.2 us -> none
    convert_element_type x19 -> x11, other arithmetic: 84.6 us -> 12.5 us  [the longest x1 3.58 us: body(): token_grad = from_sequence((own_rows(grad_middle) + norm_backward(normal_...]
    ppermute x0 -> x14, waiting for transfers between devices: none -> 59.2 us  [swap(): return lax.ppermute(value, axis, [(0, 1), (1, 0)])]
    all_gather x6 -> x2, waiting for transfers between devices: 118 us -> 66.5 us  [the longest x1 43.7 us: body(): late = lax.all_gather(late, ('dp', 'xx'), axis=0, tiled=True)]
    dynamic_slice x43 -> x3, local copies, waits for them, and re-layouts: 44.4 us -> 1.1 us  [the longest x1 0.91 us: rows_of(): return lax.dynamic_slice_in_dim(array, index * own, own, 0)]
  transfers between devices with their start and end apart: 12 -> 18, of which waited for: 10 -> 12; matrix products, arithmetic and copies ran while one was open for 19% -> 17% of each run, Pallas kernels for 0% -> 6%
where the time goes in v1:
time: 641 us; the launch traced here: 632 us
  waiting for transfers between devices  311 us (49%)
  matrix products  95.9 us (15%)
  Pallas kernels  91.5 us (14%)
  other arithmetic  67.2 us (10%)
  local copies, waits for them, and re-layouts  41 us (6%)
  between operations  15.3 us (2%)
  starting transfers between devices  10.1 us (2%)
    reduce_scatter x1, waiting for transfers between devices, body(): lax.psum_scatter(late_grads, ('dp', 'xx'), scatter_dimension=0, tiled=True)  146 us
    dot_general x13, matrix products, mm(): return lax.dot_general(left, right, dims, preferred_element_type=F32)  95.9 us
    ppermute x14, waiting for transfers between devices, swap(): return lax.ppermute(value, axis, [(0, 1), (1, 0)])  59.2 us
    pallas_call x1, Pallas kernels, attention_backward(): pl.pallas_call(attention_backward_kernel, grid=(pairs,), in_specs=[pl.Blo...  54 us
    all_gather x1, waiting for transfers between devices, body(): late = lax.all_gather(late, ('dp', 'xx'), axis=0, tiled=True)  43.7 us
    reduce_scatter x1, waiting for transfers between devices, body(): lax.psum_scatter(early_grads, ('dp', 'xx'), scatter_dimension=0, tiled=True)  39.5 us
    pallas_call x1, Pallas kernels, attention_forward(): pl.pallas_call(attention_forward_kernel, grid=(pairs,), in_specs=[pl.Bloc...  37.4 us
    all_gather x1, waiting for transfers between devices, body(): early = lax.all_gather(early, ('dp', 'xx'), axis=0, tiled=True)  22.8 us
  transfers between devices with their start and end apart: 18, of which 12 were waited for; matrix products, arithmetic and copies ran while one was open for 17% of the time, Pallas kernels for 6%

profile of v1, /device:TPU:0, one launch (start us, length us, event | category | flops | bytes accessed | tf_op | source)
XLA Modules:
  0.0 632.1 jit_solution(1433766673084583476)
XLA Ops:
  7.3 1.0 reshape.220
  11.8 1.3 reshape.225
  14.2 0.9 collective-permute-done.3
  16.1 2.9 collective-permute-start
  19.0 18.8 %collective-permute-done = bf16[512,768]{1,0:T(8,128)(2,1)} collective-permute-done((bf16[512,768]{1,0:T(8,128)(2,1)S(1)}, bf16[512,768]{1,0:T(8,128)(2,1)}, u32[]{:S(2)}, u32[]{:S(2)}) %collective-permute-start) | collective-permute-done | bytes 786464 | tf_op jit(solution)/shard_map/ppermute | solution.py:257
  37.9 1.2 fusion.49
  39.1 1.3 pad_maximum_fusion.2
  41.4 1.7 collective-permute-start.7
  44.2 1.6 select_bitcast_fusion.1
  46.3 1.2 multiply_reduce_fusion.3
  48.0 2.6 copy-done.5
  50.6 3.2 copy.91
  53.8 22.8 %all-gather.3.cloned.1.call-done = bf16[768,1280]{1,0:T(8,128)(2,1)} async-done(((bf16[48,1280]{1,0:T(8,128)(2,1)}), bf16[768,1280]{1,0:T(8,128)(2,1)}) %all-gather.3.cloned.1.call-update) | async-done | bytes 1966096 | tf_op jit(solution)/shard_map/all_gather | solution.py:355
  76.6 1.0 convert_bitcast_fusion.1
  77.6 2.0 fusion.84
  79.8 3.5 fusion.3
  83.4 5.8 multiply_convert_fusion.2.qkv_ref
  89.3 37.4 %shard_map.280 = (bf16[2048,384]{1,0:T(8,128)(2,1)S(1)}, f32[3,8,2048]{2,1,0:T(8,128)S(1)}) custom-call(bf16[2048,1152]{1,0:T(8,128)(2,1)} %multiply_convert_fusion.2.qkv_ref, bf16[2048,128]{1,0:T(8,128)(2,1)S(1)} %get-tuple-element.87.qs_ref, bf16[2048,128]{1,0:T(8,128)(2,1)S(1)} %get-tuple-element.86.ks_ref), custom_call_target="tpu_custom_call" | custom-call | flops 25769803776 | bytes 7077888 | tf_op jit(solution)/shard_map/pallas_call | solution.py:162
  126.7 43.7 %all-gather.5.cloned.1.call-done = bf16[768,3840]{1,0:T(8,128)(2,1)} async-done(((bf16[48,3840]{1,0:T(8,128)(2,1)}), bf16[768,3840]{1,0:T(8,128)(2,1)}) %all-gather.5.cloned.1.call-update) | async-done | bytes 5898256 | tf_op jit(solution)/shard_map/all_gather | solution.py:356
  170.4 3.6 fusion.83
  174.0 3.5 convolution_convert_fusion.2
  177.5 1.2 fusion.45
  179.5 5.9 collective-permute-done.8
  186.6 1.9 copy.100
  189.3 1.1 copy.99
  190.5 6.0 fusion.81
  197.4 1.7 copy-done.2
  199.1 13.1 %multiply_convert_fusion.1 = (bf16[2048,1536]{1,0:T(8,128)(2,1)}, f32[2048,1536]{1,0:T(8,128)}) fusion(f32[1536]{0:T(1024)S(1)} %add.232, bf16[768,3840]{1,0:T(8,128)(2,1)} %all-gather.5.cloned.1.call-done, f32[2048,768]{1,0:T(8,128)S(1)} %get-tuple-element.48, f32[768]{0:T(1024)S(1)} %get-tuple-element.74, f32[768]{0:T(1024)S(1)} %get-tuple-element.73, ...), kind=kOutput, calls=%fused_computation.1 | convolution fusion | flops 4871159808 | bytes 27553792 | tf_op jit(solution)/shard_map/dot_general | solution.py:24
  212.2 16.1 %multiply_convert_fusion = bf16[2048,1536]{1,0:T(8,128)(2,1)S(1)} fusion(f32[2048,1536]{1,0:T(8,128)} %get-tuple-element.95, bf16[2048,768]{1,0:T(8,128)(2,1)S(1)} %bitcast.194, f32[1536]{0:T(1024)S(1)} %add.232, bf16[768,768]{1,0:T(8,128)(2,1)S(1)} %copy-done.25, bf16[768,768]{1,0:T(8,128)(2,1)S(1)} %copy-done.23), kind=kOutput, calls=%fused_computation | convolution fusion | flops 4896325632 | bytes 24385536 | tf_op jit(solution)/shard_map/dot_general | solution.py:24
  228.3 9.9 %convolution_convert_fusion.4 = bf16[2048,768]{1,0:T(8,128)(2,1)} fusion(bf16[2048,1536]{1,0:T(8,128)(2,1)S(1)} %multiply_convert_fusion, bf16[768,3840]{1,0:T(8,128)(2,1)} %all-gather.5.cloned.1.call-done), kind=kOutput, calls=%fused_computation.30 | convolution fusion | flops 4833411072 | bytes 11796480 | tf_op jit(solution)/shard_map/dot_general | solution.py:24
  238.9 2.3 dynamic-slice_reduce_fusion
  241.2 2.7 multiply_reduce_fusion.6
  244.2 6.0 multiply_reduce_fusion
  250.2 5.9 convert_reduce_fusion.1
  256.1 1.9 convolution_convert_fusion.5.do_ref
  258.8 54.0 %shard_map.281 = bf16[2048,1152]{1,0:T(8,128)(2,1)} custom-call(bf16[2048,1152]{1,0:T(8,128)(2,1)} %multiply_convert_fusion.2.qkv_ref, bf16[2048,128]{1,0:T(8,128)(2,1)S(1)} %get-tuple-element.87.qs_ref, bf16[2048,128]{1,0:T(8,128)(2,1)S(1)} %get-tuple-element.86.ks_ref, bf16[2048,384]{1,0:T(8,128)(2,1)S(1)} %get-tuple-element.17.o_ref, ...), custom_call_target="tpu_custom_call" | custom-call | flops 64424509440 | bytes 14155776 | tf_op jit(solution)/shard_map/pallas_call | solution.py:195
  312.8 3.0 convert_reduce_fusion
  315.9 7.3 %convolution_convert_fusion.1 = bf16[2048,768]{1,0:T(8,128)(2,1)S(1)} fusion(bf16[2048,1152]{1,0:T(8,128)(2,1)} %shard_map.281, bf16[768,1280]{1,0:T(8,128)(2,1)} %all-gather.3.cloned.1.call-done), kind=kOutput, calls=%fused_computation.27 | convolution fusion | flops 3625451520 | bytes 9633792 | tf_op jit(solution)/shard_map/dot_general | solution.py:24
  323.7 2.6 copy-done.17
  326.3 4.4 convolution_convert_fusion.3
  330.8 4.3 multiply_reduce_fusion.4
  336.6 1.5 fusion.25
  338.3 3.7 slice_reduce_fusion
  342.2 12.0 %fusion.9 = bf16[768,3968]{1,0:T(8,128)(2,1)} fusion(bf16[2048,1536]{1,0:T(8,128)(2,1)} %copy-done.13, f32[2048,768]{1,0:T(8,128)} %copy-done.2, f32[768]{0:T(1024)S(1)} %copy-done.47, f32[768]{0:T(1024)S(1)} %copy-done.37, f32[2048]{0:T(1024)S(1)} %add_rsqrt_fusion, f32[2048]{0:T(1024)S(1)} %broadcast_multiply_fusion.2), kind=kOutput, calls=%fused_computation.26 | convolution fusion | flops 4840882176 | bytes 14964736 | tf_op jit(solution)/shard_map/dot_general | solution.py:24
  354.5 4.4 broadcast_select_fusion.3
  359.0 1.2 maximum_dynamic-update-slice_fusion
  360.2 5.7 fusion.32
  365.9 4.1 fusion.38
  370.7 1.2 copy-done.24
  372.0 7.6 %fusion.41 = f32[2048,768]{1,0:T(8,128)S(1)} fusion(bf16[2048,1536]{1,0:T(8,128)(2,1)} %get-tuple-element.94, bf16[768,768]{1,0:T(8,128)(2,1)} %get-tuple-element.50, bf16[768,768]{1,0:T(8,128)(2,1)S(1)} %copy-done.24), kind=kOutput, calls=%fused_computation.78 | convolution fusion | flops 4836556800 | bytes 14942208 | tf_op jit(solution)/shard_map/dot_general | solution.py:24
  380.1 3.2 collective-permute-done.5
  384.1 1.5 collective-permute-start.6
  386.3 3.6 fusion.14
  390.0 1.5 collective-permute-start.11
  391.4 14.9 %collective-permute-done.6 = bf16[512,768]{1,0:T(8,128)(2,1)} collective-permute-done((bf16[512,768]{1,0:T(8,128)(2,1)S(1)}, bf16[512,768]{1,0:T(8,128)(2,1)}, u32[]{:S(2)}, u32[]{:S(2)}) %collective-permute-start.6) | collective-permute-done | bytes 786464 | tf_op jit(solution)/shard_map/ppermute | solution.py:257
  406.4 1.5 fusion.47
  407.9 1.3 pad_maximum_fusion.3
  409.2 14.7 %collective-permute-done.11 = bf16[512,768]{1,0:T(8,128)(2,1)} collective-permute-done((bf16[512,768]{1,0:T(8,128)(2,1)S(1)}, bf16[512,768]{1,0:T(8,128)(2,1)}, u32[]{:S(2)}, u32[]{:S(2)}) %collective-permute-start.11) | collective-permute-done | bytes 786464 | tf_op jit(solution)/shard_map/ppermute | solution.py:257
  423.8 1.2 fusion.43
  425.1 39.5 %reduce-scatter.3.cloned.1.call-done = bf16[48,1280]{1,0:T(8,128)(2,1)} async-done(((bf16[768,1280]{1,0:T(8,128)(2,1)}), bf16[48,1280]{1,0:T(8,128)(2,1)}) %reduce-scatter.3.cloned.1.call-update) | async-done | bytes 122896 | tf_op jit(solution)/shard_map/reduce_scatter | solution.py:474
  465.5 1.3 pad_maximum_fusion.5
  468.6 145.9 %reduce-scatter.5.cloned.1.call-done = bf16[48,3968]{1,0:T(8,128)(2,1)} async-done(((bf16[768,3968]{1,0:T(8,128)(2,1)}), bf16[48,3968]{1,0:T(8,128)(2,1)}) %reduce-scatter.5.cloned.1.call-update) | async-done | bytes 380944 | tf_op jit(solution)/shard_map/reduce_scatter | solution.py:447
  621.9 1.8 reshape.236
  623.7 1.4 fusion.65
  (235 shorter events, 29.4 us)
Async XLA Ops:
  7.2 36.0 %copy-start = (s32[2,2048]{1,0:T(2,128)S(1)}, s32[2,2048]{1,0:T(2,128)}, u32[]{:S(2)}) copy-start(s32[2,2048]{1,0:T(2,128)} %param.18) | copy-start | bytes 49156
  7.2 6.5 %copy-start.35 = (bf16[24,768]{1,0:T(8,128)(2,1)S(1)}, bf16[24,768]{1,0:T(8,128)(2,1)}, u32[]{:S(2)}) copy-start(bf16[24,768]{1,0:T(8,128)(2,1)} %param.24) | copy-start | bytes 110596
  7.2 7.0 %copy-start.26 = (bf16[96,768]{1,0:T(8,128)(2,1)S(1)}, bf16[96,768]{1,0:T(8,128)(2,1)}, u32[]{:S(2)}) copy-start(bf16[96,768]{1,0:T(8,128)(2,1)} %param.30) | copy-start | bytes 442372
  7.2 69.4 %all-gather.3.cloned.1.call-start = ((), (), s32[]{:S(2)}) async-start(), calls=%async_computation.2 | async-start | bytes 2088960 | tf_op jit(solution)/shard_map/all_gather | solution.py:355
  8.2 7.8 %copy-start.20 = (bf16[2,512,768]{2,1,0:T(8,128)(2,1)S(1)}, bf16[2,512,768]{2,1,0:T(8,128)(2,1)}, u32[]{:S(2)}) copy-start(bf16[2,512,768]{2,1,0:T(8,128)(2,1)} %param.17) | copy-start | bytes 4718596
  9.5 1.4 collective-permute-start.2
  11.8 158.6 %all-gather.5.cloned.1.call-start = ((), (), s32[]{:S(2)}) async-start(), calls=%async_computation.3 | async-start | bytes 6266880 | tf_op jit(solution)/shard_map/all_gather | solution.py:356
  13.8 1.4 collective-permute-start.3
  16.0 448.5 %reduce-scatter.3.cloned.1.call-start = ((), (), s32[]{:S(2)}) async-start(), calls=%async_computation.4 | async-start | bytes 2088960 | tf_op jit(solution)/shard_map/reduce_scatter | solution.py:474
  16.1 21.8 %collective-permute-start = (bf16[512,768]{1,0:T(8,128)(2,1)S(1)}, bf16[512,768]{1,0:T(8,128)(2,1)}, u32[]{:S(2)}, u32[]{:S(2)}) collective-permute-start(bf16[512,768]{1,0:T(8,128)(2,1)S(1)} %dynamic-slice_bitcast_fusion.4), channel_id=1, source_target_pairs={{0,2},{2,0},{1,3},{3,1},{4,6},{6,4},{5,7},{7,5},{8,10},{10,8},{9,1... | collective-permute-start | bytes 2359304 | tf_op jit(solution)/shard_map/ppermute | solution.py:257
  19.0 21.4 %copy-start.21 = (bf16[2,512,768]{2,1,0:T(8,128)(2,1)S(1)}, bf16[2,512,768]{2,1,0:T(8,128)(2,1)}, u32[]{:S(2)}) copy-start(bf16[2,512,768]{2,1,0:T(8,128)(2,1)} %param.32) | copy-start | bytes 4718596
  39.1 4.0 copy-start.48
  40.4 3.8 collective-permute-start.1
  41.4 136.1 %collective-permute-start.7 = (bf16[512,768]{1,0:T(8,128)(2,1)}, bf16[512,768]{1,0:T(8,128)(2,1)}, u32[]{:S(2)}, u32[]{:S(2)}) collective-permute-start(bf16[512,768]{1,0:T(8,128)(2,1)} %dynamic-slice_bitcast_fusion.2), channel_id=1, source_target_pairs={{0,2},{2,0},{1,3},{3,1},{4,6},{6,4},{5,7},{7,5},{8,10},{10,8},{9,1... | collective-permute-start | bytes 2359304 | tf_op jit(solution)/shard_map/ppermute | solution.py:257
  79.6 3.8 copy-start.30
  79.6 117.8 %copy-start.46 = (f32[768]{0:T(1024)}, f32[768]{0:T(1024)S(1)}, u32[]{:S(2)}) copy-start(f32[768]{0:T(1024)S(1)} %get-tuple-element.74) | copy-start | bytes 9220
  79.6 170.6 %copy-start.36 = (f32[768]{0:T(1024)}, f32[768]{0:T(1024)S(1)}, u32[]{:S(2)}) copy-start(f32[768]{0:T(1024)S(1)} %get-tuple-element.73) | copy-start | bytes 9220
  79.8 3.6 copy-start.38
  83.4 5.9 copy-start.16
  174.0 3.5 copy-start.18
  174.0 3.5 copy-start.22
  177.5 13.0 %collective-permute-start.4 = (bf16[2048,768]{1,0:T(8,128)(2,1)}, bf16[2048,768]{1,0:T(8,128)(2,1)}, u32[]{:S(2)}, u32[]{:S(2)}) collective-permute-start(bf16[2048,768]{1,0:T(8,128)(2,1)} %convolution_convert_fusion.2), channel_id=1, source_target_pairs={{0,1},{1,0},{2,3},{3,2},{4,5},{5,4},{6,7},{7,6},{8,9},{9,8},{10,11... | collective-permute-start | bytes 9437192 | tf_op jit(solution)/shard_map/ppermute | solution.py:257
  178.9 6.5 %collective-permute-start.8 = (bf16[2,512,768]{2,1,0:T(8,128)(2,1)S(1)}, bf16[2,512,768]{2,1,0:T(8,128)(2,1)S(1)}, u32[]{:S(2)}, u32[]{:S(2)}) collective-permute-start(bf16[2,512,768]{2,1,0:T(8,128)(2,1)S(1)} %pad_maximum_fusion.4), channel_id=1, source_target_pairs={{0,1},{1,0},{2,3},{3,2},{4,5},{5,4},{6,7},{7,6},{8,9},{9,8},{10,11... | collective-permute-start | bytes 4718600 | tf_op jit(solution)/shard_map/ppermute | solution.py:257
  199.1 13.1 %copy-start.6 = (bf16[2,2,512,768]{3,2,1,0:T(8,128)(2,1)S(1)}, bf16[2,2,512,768]{3,2,1,0:T(8,128)(2,1)}, u32[]{:S(2)}) copy-start(bf16[2,2,512,768]{3,2,1,0:T(8,128)(2,1)} %copy.100) | copy-start | bytes 9437188
  199.1 13.1 %copy-start.23 = (bf16[768,768]{1,0:T(8,128)(2,1)S(1)}, bf16[768,768]{1,0:T(8,128)(2,1)}, u32[]{:S(2)}) copy-start(bf16[768,768]{1,0:T(8,128)(2,1)} %get-tuple-element.49) | copy-start | bytes 3538948
  199.1 13.1 %copy-start.25 = (bf16[768,768]{1,0:T(8,128)(2,1)S(1)}, bf16[768,768]{1,0:T(8,128)(2,1)}, u32[]{:S(2)}) copy-start(bf16[768,768]{1,0:T(8,128)(2,1)} %get-tuple-element.50) | copy-start | bytes 3538948
  228.3 9.9 %copy-start.13 = (bf16[2048,1536]{1,0:T(8,128)(2,1)}, bf16[2048,1536]{1,0:T(8,128)(2,1)S(1)}, u32[]{:S(2)}) copy-start(bf16[2048,1536]{1,0:T(8,128)(2,1)S(1)} %multiply_convert_fusion) | copy-start | bytes 18874372
  238.2 6.0 collective-permute-start.9
  238.9 5.3 copy-start.3
  241.2 89.6 %copy-start.28 = (f32[2,512]{1,0:T(2,128)}, f32[2,512]{1,0:T(2,128)S(1)}, u32[]{:S(2)}) copy-start(f32[2,512]{1,0:T(2,128)S(1)} %broadcast_multiply_fusion.6) | copy-start | bytes 12292
  243.9 86.8 %copy-start.33 = (f32[2,512]{1,0:T(2,128)}, f32[2,512]{1,0:T(2,128)S(1)}, u32[]{:S(2)}) copy-start(f32[2,512]{1,0:T(2,128)S(1)} %add_rsqrt_fusion.2) | copy-start | bytes 12292
  243.9 6.3 copy-start.7
  250.2 5.9 copy-start.19
  256.1 2.7 copy-start.4
  315.9 7.8 %copy-start.15 = (bf16[2048,1152]{1,0:T(8,128)(2,1)S(1)}, bf16[2048,1152]{1,0:T(8,128)(2,1)}, u32[]{:S(2)}) copy-start(bf16[2048,1152]{1,0:T(8,128)(2,1)} %shard_map.281) | copy-start | bytes 14155780
  323.2 7.5 %copy-start.9 = (bf16[2048,768]{1,0:T(8,128)(2,1)}, bf16[2048,768]{1,0:T(8,128)(2,1)S(1)}, u32[]{:S(2)}) copy-start(bf16[2048,768]{1,0:T(8,128)(2,1)S(1)} %convolution_convert_fusion.1) | copy-start | bytes 9437188
  323.3 3.0 copy-start.17
  323.4 7.3 %collective-permute-start.10 = (bf16[2,512,768]{2,1,0:T(8,128)(2,1)S(1)}, bf16[2,512,768]{2,1,0:T(8,128)(2,1)S(1)}, u32[]{:S(2)}, u32[]{:S(2)}) collective-permute-start(bf16[2,512,768]{2,1,0:T(8,128)(2,1)S(1)} %dynamic-slice_bitcast_fusion), channel_id=1, source_target_pairs={{0,1},{1,0},{2,3},{3,2},{4,5},{5,4},{6,7},{7,6},{8,9},{9,8},{10,11... | collective-permute-start | bytes 4718600 | tf_op jit(solution)/shard_map/ppermute | solution.py:257
  326.3 4.5 copy-start.31
  330.8 4.3 copy-start.11
  338.1 4.1 copy-start.37
  338.1 4.1 copy-start.47
  338.1 276.4 %reduce-scatter.5.cloned.1.call-start = ((), (), s32[]{:S(2)}) async-start(), calls=%async_computation.5 | async-start | bytes 6475776 | tf_op jit(solution)/shard_map/reduce_scatter | solution.py:447
  342.1 12.1 %copy-start.43 = (bf16[768]{0:T(1024)(128)(2,1)S(1)}, bf16[768]{0:T(1024)(128)(2,1)}, u32[]{:S(2)}) copy-start(bf16[768]{0:T(1024)(128)(2,1)} %get-tuple-element.45) | copy-start | bytes 4612
  342.1 12.1 %copy-start.45 = (bf16[768]{0:T(1024)(128)(2,1)S(1)}, bf16[768]{0:T(1024)(128)(2,1)}, u32[]{:S(2)}) copy-start(bf16[768]{0:T(1024)(128)(2,1)} %get-tuple-element.19) | copy-start | bytes 4612
  342.2 12.1 %copy-start.44 = (bf16[768]{0:T(1024)(128)(2,1)S(1)}, bf16[768]{0:T(1024)(128)(2,1)}, u32[]{:S(2)}) copy-start(bf16[768]{0:T(1024)(128)(2,1)} %get-tuple-element.26) | copy-start | bytes 4612
  342.2 12.1 %copy-start.42 = (bf16[768,1]{0,1:T(2,128)(2,1)S(1)}, bf16[768,1]{0,1:T(2,128)(2,1)}, u32[]{:S(2)}) copy-start(bf16[768,1]{0,1:T(2,128)(2,1)} %stack.185) | copy-start | bytes 4612
  354.5 5.7 copy-start.8
  354.5 11.3 %slice-start.2 = ((s8[6291456]{0:T(1024)(128)(4,1)}), s8[4194304]{0:T(1024)(128)(4,1)S(1)}, s32[]{:S(2)}) async-start(s8[6291456]{0:T(1024)(128)(4,1)} %bitcast.220), calls=%async_computation.8 | async-start | bytes 8388608
  359.0 6.9 %slice-start.3 = ((s8[6291456]{0:T(1024)(128)(4,1)}), s8[2097152]{0:T(1024)(128)(4,1)S(1)}, s32[]{:S(2)}) async-start(s8[6291456]{0:T(1024)(128)(4,1)} %bitcast.220), calls=%async_computation.9 | async-start | bytes 4194304
  370.7 12.6 %slice-start = ((s8[6291456]{0:T(1024)(128)(4,1)}), s8[2097152]{0:T(1024)(128)(4,1)S(1)}, s32[]{:S(2)}) async-start(s8[6291456]{0:T(1024)(128)(4,1)} %bitcast.190), calls=%async_computation.6 | async-start | bytes 4194304
  372.0 11.3 %slice-start.1 = ((s8[6291456]{0:T(1024)(128)(4,1)}), s8[4194304]{0:T(1024)(128)(4,1)S(1)}, s32[]{:S(2)}) async-start(s8[6291456]{0:T(1024)(128)(4,1)} %bitcast.190), calls=%async_computation.7 | async-start | bytes 8388608
  379.6 3.7 copy-start.41
  379.8 3.5 collective-permute-start.5
  383.3 3.0 copy-start.12
  383.3 2.9 copy-start.29
  383.4 2.9 copy-start.32
  383.4 2.9 copy-start.34
  384.0 5.9 copy-start.14
  384.1 22.3 %collective-permute-start.6 = (bf16[512,768]{1,0:T(8,128)(2,1)S(1)}, bf16[512,768]{1,0:T(8,128)(2,1)}, u32[]{:S(2)}, u32[]{:S(2)}) collective-permute-start(bf16[512,768]{1,0:T(8,128)(2,1)S(1)} %dynamic-slice_bitcast_fusion.3), channel_id=1, source_target_pairs={{0,2},{2,0},{1,3},{3,1},{4,6},{6,4},{5,7},{7,5},{8,10},{10,8},{9,1... | collective-permute-start | bytes 2359304 | tf_op jit(solution)/shard_map/ppermute | solution.py:257
  390.0 33.9 %collective-permute-start.11 = (bf16[512,768]{1,0:T(8,128)(2,1)S(1)}, bf16[512,768]{1,0:T(8,128)(2,1)}, u32[]{:S(2)}, u32[]{:S(2)}) collective-permute-start(bf16[512,768]{1,0:T(8,128)(2,1)S(1)} %dynamic-slice_bitcast_fusion.1), channel_id=1, source_target_pairs={{0,2},{2,0},{1,3},{3,1},{4,6},{6,4},{5,7},{7,5},{8,10},{10,8},{9,1... | collective-permute-start | bytes 2359304 | tf_op jit(solution)/shard_map/ppermute | solution.py:257
  465.5 1.3 collective-permute-start.12
  466.9 158.2 %copy-start.1 = (s32[2,2048]{1,0:T(2,128)S(1)}, s32[2,2048]{1,0:T(2,128)}, u32[]{:S(2)}) copy-start(s32[2,2048]{1,0:T(2,128)} %param.18) | copy-start | bytes 49156
  615.4 4.6 collective-permute-start.13
  (7 other events, 15.7 us)
Sparse Core Ops, SparseCore 0:
  11.9 64.6 all-gather.2
  80.0 90.3 all-gather.4
  338.2 126.3 reduce-scatter.2
  470.6 143.8 reduce-scatter.4

commit v2 on v1

--- a/solution.py
+++ b/solution.py
@@ -90,9 +90,8 @@
         o_ref[rows, :] = jnp.concatenate(parts, axis=0).T.astype(BF16)
 
 
-def attention_backward_kernel(
-    qkv_ref, qs_ref, ks_ref, o_ref, do_ref, lse_ref, d_ref, qx, kx, qm, dm, kt, delta, dqt, dk, dv
-):
+def attention_backward_kernel(qkv_ref, qs_ref, ks_ref, o_ref, do_ref, lse_ref, *rest):
+    d_ref, qx, kx, qm, dm, kt, delta, dqt, dk, dv = rest[-10:]
     length = qkv_ref.shape[0]
     blocks = length // BLK
 
@@ -188,23 +187,23 @@
     )(qkv, query_code, key_code)
 
 
-def attention_backward(qkv, query_code, key_code, attended, grad_attended, log_total):
-    length, width = qkv.shape
-    pairs = width // (3 * PAIR)
-    tiles = pairs * 2 * length * length
+def attention_backward(pair, qkv, query_code, key_code, attended, grad_attended, log_total, after):
+    length = qkv.shape[0]
+    tiles = 2 * length * length
     return pl.pallas_call(
         attention_backward_kernel,
-        grid=(pairs,),
+        grid=(1,),
         in_specs=[
-            pl.BlockSpec((length, 3 * PAIR), lambda p: (0, p)),
+            pl.BlockSpec((length, 3 * PAIR), lambda p: (0, pair)),
             pl.BlockSpec((length, PAIR), lambda p: (0, 0)),
             pl.BlockSpec((length, PAIR), lambda p: (0, 0)),
-            pl.BlockSpec((length, PAIR), lambda p: (0, p)),
-            pl.BlockSpec((length, PAIR), lambda p: (0, p)),
-            pl.BlockSpec((1, 8, length), lambda p: (p, 0, 0)),
-        ],
-        out_specs=pl.BlockSpec((length, 3 * PAIR), lambda p: (0, p)),
-        out_shape=jax.ShapeDtypeStruct((length, width), BF16),
+            pl.BlockSpec((length, PAIR), lambda p: (0, pair)),
+            pl.BlockSpec((length, PAIR), lambda p: (0, pair)),
+            pl.BlockSpec((1, 8, length), lambda p: (pair, 0, 0)),
+        ]
+        + [pl.BlockSpec(memory_space=pl.ANY)] * len(after),
+        out_specs=pl.BlockSpec((length, 3 * PAIR), lambda p: (0, 0)),
+        out_shape=jax.ShapeDtypeStruct((length, 3 * PAIR), BF16),
         scratch_shapes=[
             pltpu.VMEM((2, length, PAIR), BF16),
             pltpu.VMEM((2, length, PAIR), BF16),
@@ -218,9 +217,9 @@
         ],
         compiler_params=pltpu.CompilerParams(vmem_limit_bytes=VMEM_LIMIT),
         cost_estimate=pl.CostEstimate(
-            flops=tiles * 2560, bytes_accessed=length * width * 6, transcendentals=tiles // 2
+            flops=tiles * 2560, bytes_accessed=length * PAIR * 24, transcendentals=tiles // 2
         ),
-    )(qkv, query_code, key_code, attended, grad_attended, log_total)
+    )(qkv, query_code, key_code, attended, grad_attended, log_total, *after)
 
 
 def norm_forward(source):
@@ -259,6 +258,63 @@
 
 def pick(flag, first, second):
     return jnp.where(flag == 0, first, second), jnp.where(flag == 0, second, first)
+
+
+class Links:
+    def __init__(self):
+        self.size = lax.axis_size("dp")
+        at = lax.axis_index("dp")
+        self.groups = {}
+        shift, name = 0, "y"
+        while (1 << shift) < self.size:
+            bits = 1 if shift == 0 else min(2, self.size.bit_length() - 1 - shift)
+            self.groups[name] = (shift, bits, (at >> shift) & ((1 << bits) - 1))
+            shift += bits
+            name = "z" + str(shift)
+        self.rest = [name for name in reversed(self.groups) if name != "y"]
+        self.dims = self.rest + ["y", "x"]
+        self.side = lax.axis_index("xx")
+
+    def counts(self, dims):
+        return [2 if d == "x" else 1 << self.groups[d][1] for d in dims]
+
+    def send(self, value, d, mask):
+        if d == "x":
+            return swap(value, "xx")
+        move = mask << self.groups[d][0]
+        return lax.ppermute(value, "dp", [(i, i ^ move) for i in range(self.size)])
+
+    def place(self, d):
+        return self.side if d == "x" else self.groups[d][2]
+
+    def reduce(self, state, d):
+        array, dims = state
+        axis, at = dims.index(d), self.place(d)
+        total = lax.dynamic_index_in_dim(array, at, axis, keepdims=False).astype(F32)
+        for mask in range(1, array.shape[axis]):
+            block = lax.dynamic_index_in_dim(array, at ^ mask, axis, keepdims=False)
+            total = total + self.send(block, d, mask).astype(F32)
+        return total.astype(BF16), [other for other in dims if other != d]
+
+    def gather(self, state, d):
+        array, dims = state
+        parts = [array] + [self.send(array, d, mask) for mask in range(1, self.counts([d])[0])]
+        for bit in range(len(parts).bit_length() - 1):
+            flag = (self.place(d) >> bit) & 1
+            for low in range(len(parts)):
+                if not low & (1 << bit):
+                    high = low | (1 << bit)
+                    parts[low], parts[high] = pick(flag, parts[low], parts[high])
+        dims = [other for other in self.dims if other in dims or other == d]
+        return jnp.stack(parts, axis=dims.index(d)), dims
+
+    def rows(self, array, lead=()):
+        shape = list(lead) + self.counts(self.dims)
+        count = 1
+        for size in shape:
+            count *= size
+        names = ["lead"] * len(lead) + self.dims
+        return array.reshape(shape + [array.shape[0] // count, array.shape[1]]), names
 
 
 def body(
@@ -352,7 +408,18 @@
     )
     down_own = down_weight.reshape(splits, pair_row, width)
     late = jnp.concatenate([late] + [down_own[i] for i in range(splits)], axis=1)
-    early = lax.all_gather(early, ("dp", "xx"), axis=0, tiled=True)
+    links = Links()
+    state = (early, [])
+    for d in links.rest:
+        state = links.gather(state, d)
+    middle_col = early.shape[1] // 2
+    halves = []
+    for order, part in (("yx", slice(0, middle_col)), ("xy", slice(middle_col, None))):
+        piece = (state[0][..., part], state[1])
+        for d in order:
+            piece = links.gather(piece, d)
+        halves.append(piece[0].reshape(width, middle_col))
+    early = jnp.concatenate(halves, axis=1)
     late = lax.all_gather(late, ("dp", "xx"), axis=0, tiled=True)
     proj_qkv = early[:, :cols]
     small = early[:, cols:].astype(F32).T
@@ -420,7 +487,7 @@
     def only_mine(flag, array):
         return jnp.where(flag, array, jnp.zeros_like(array))
 
-    small_two = as_column(
+    small_two = (
         [
             jnp.sum(branch_low.astype(F32), axis=0),
             jnp.sum(grad_normed_two * normal_two, axis=0),
@@ -432,23 +499,60 @@
             for i in range(splits)
         ]
     )
-    grad_out_low_b = grad_proj_out.astype(BF16)
-    late_grads = jnp.concatenate(
+    down_piece = links.rows(
+        jnp.concatenate([part.astype(BF16) for part in grad_proj_down], axis=0), (splits,)
+    )
+    up_piece = links.rows(grad_proj_up.astype(BF16))
+    out_piece = (
+        grad_proj_out.astype(BF16).reshape(chips // 8, 2, 2, pair_row, width),
+        ["rest", "y", "x"],
+    )
+
+    def reduce_rest(piece):
+        for d in links.rest:
+            piece = links.reduce(piece, d)
+        return piece
+
+    def pair_backward(pair, after):
+        grad = attention_backward(
+            pair, qkv, query_code, key_code, attended, grad_attended, log_total, after
+        )
+        return grad, links.rows(mm(normed_low, grad, TN).astype(BF16))
+
+    down_piece = links.reduce(down_piece, "x")
+    grads, pieces = [], []
+    for pair in range(pairs):
+        if pair == 0:
+            after = [down_piece[0], mixed]
+        elif pair == 1:
+            down_piece = links.reduce(down_piece, "y")
+            up_piece = links.reduce(up_piece, "y")
+            after = [down_piece[0], up_piece[0]]
+        else:
+            down_piece = reduce_rest(down_piece)
+            up_piece = links.reduce(up_piece, "x")
+            out_piece = links.reduce(out_piece, "x")
+            after = [down_piece[0], up_piece[0], out_piece[0]]
+        grad, piece = pair_backward(pair, after)
+        grads.append(grad)
+        pieces.append(piece)
+    grad_qkv = jnp.concatenate(grads, axis=1)
+    up_piece = reduce_rest(up_piece)
+    out_part = links.reduce(out_piece, "y")[0]
+    empty = jnp.zeros_like(out_part)
+    out_part = jnp.concatenate(pick(core, out_part, empty), axis=0)
+    out_piece = reduce_rest(
+        (out_part.reshape(links.counts(links.rest) + [pair_row, width]), links.rest)
+    )
+    qkv_own = jnp.concatenate(
         [
-            grad_proj_up.astype(BF16),
-            jnp.concatenate(
-                [only_mine(core == 0, grad_out_low_b), only_mine(core == 1, grad_out_low_b)], axis=0
-            ),
-        ]
-        + [part.astype(BF16) for part in grad_proj_down]
-        + [small_two.astype(BF16)],
+            reduce_rest(links.reduce(links.reduce(piece, order[0]), order[1]))[0]
+            for piece, order in zip(pieces, ("yx", "xy", "yx"))
+        ],
         axis=1,
     )
-    late_own = lax.psum_scatter(late_grads, ("dp", "xx"), scatter_dimension=0, tiled=True)
-
-    grad_qkv = attention_backward(qkv, query_code, key_code, attended, grad_attended, log_total)
-    grad_proj_qkv = mm(normed_low, grad_qkv, TN)
-    partial_one = mm(grad_qkv, proj_qkv, NT).astype(BF16)
+    partial_one_wide = mm(grad_qkv, proj_qkv, NT)
+    partial_one = partial_one_wide.astype(BF16)
     grad_normed = own_rows(partial_one).astype(F32) + swap(other_rows(partial_one), "core").astype(F32)
     normal_own, scale_own = norm_forward(own_rows(inputs))
     token_grad = from_sequence(
@@ -462,29 +566,29 @@
         vector = vector.reshape(half)
         return jnp.concatenate([only_mine(core == 0, vector), only_mine(core == 1, vector)])
 
-    small_one = as_column(
+    small = as_column(
         [
-            jnp.sum(grad_normed * normal_own, axis=(0, 1)),
-            jnp.sum(grad_normed, axis=(0, 1)),
+            jnp.sum(partial_one_wide * normal_one, axis=0),
+            jnp.sum(partial_one_wide, axis=0),
             padded(grad_by_pair[:, 0]),
             padded(grad_by_pair[:, 2]),
         ]
-    )
-    early_grads = jnp.concatenate([grad_proj_qkv.astype(BF16), small_one.astype(BF16)], axis=1)
-    early_own = lax.psum_scatter(early_grads, ("dp", "xx"), scatter_dimension=0, tiled=True)
+        + small_two
+    )
+    small_own = reduce_rest(links.reduce(links.reduce(links.rows(small.astype(BF16)), "y"), "x"))[0]
 
     def rows_of(array, index):
         return lax.dynamic_slice_in_dim(array, index * own, own, 0)
 
-    late_mine = rows_of(late_own, core)
-    late_come = swap(rows_of(late_own, 1 - core)[:, : hidden + width], "core")
-    early_mine = rows_of(early_own, core)
-    early_come = swap(rows_of(early_own, 1 - core), "core")
-
     def by_core(mine, come):
         return jnp.stack(pick(core, mine, come))
 
-    out_grad = (late_mine[:, hidden : hidden + width] + late_come[:, hidden:]).astype(F32)
+    def shared(array):
+        return rows_of(array, core), swap(rows_of(array, 1 - core), "core")
+
+    late_mine, late_come = shared(jnp.concatenate([up_piece[0], out_piece[0]], axis=1))
+    early_mine, early_come = shared(jnp.concatenate([qkv_own, small_own], axis=1))
+    out_grad = late_mine[:, hidden:].astype(F32) + late_come[:, hidden:].astype(F32)
     up_grad = (
         by_core(late_mine[:, :hidden], late_come[:, :hidden])
         .reshape(2, own, splits, chips, pair_row)
@@ -492,12 +596,8 @@
         .reshape(own, 2 * hidden)
         .astype(F32)
     )
-    down_grad = jnp.concatenate(
-        [late_own[:, hidden + (1 + i) * width : hidden + (2 + i) * width] for i in range(splits)],
-        axis=0,
-    ).astype(F32)
-    tail = hidden + (1 + splits) * width
-    up_shift_grad = late_own[:, tail + 4 : tail + 4 + splits].T.reshape(hidden_own).astype(F32)
+    down_grad = down_piece[0].reshape(hidden_own, width).astype(F32)
+    up_shift_grad = small_own[:, 8 : 8 + splits].T.reshape(hidden_own).astype(F32)
     qkv_grad = (
         by_core(early_mine[:, :cols], early_come[:, :cols])
         .reshape(2, own, pairs, 3, PAIR)
@@ -505,8 +605,9 @@
         .reshape(own, 2 * cols)
         .astype(F32)
     )
-    one = early_mine[:, cols : cols + 4].astype(F32) + early_come[:, cols : cols + 4].astype(F32)
-    two = late_mine[:, tail : tail + 4].astype(F32)
+    small_mine = early_mine[:, cols : cols + 8].astype(F32)
+    one = small_mine[:, :4] + early_come[:, cols : cols + 4].astype(F32)
+    two = small_mine[:, 4:]
     return (
         mixed,
         token_grad,

time: 641 us -> 492 us (0.77)
  waiting for transfers between devices: 311 us -> 119 us
  starting transfers between devices: 10.1 us -> 66.3 us
  matrix products: 95.9 us -> 84.3 us
  local copies, waits for them, and re-layouts: 41 us -> 49.2 us
  other arithmetic: 67.2 us -> 60.3 us
    reduce_scatter x2 -> x0, waiting for transfers between devices: 185 us -> none  [the longest x1 146 us: body(): lax.psum_scatter(late_grads, ('dp', 'xx'), scatter_dimension=0, tiled=True)]
    ppermute x0 -> x33, starting transfers between devices: none -> 48 us  [send(): return lax.ppermute(value, 'dp', [(i, i ^ move) for i in range(self.size)])]
    ppermute x0 -> x33, waiting for transfers between devices: none -> 48 us  [send(): return lax.ppermute(value, 'dp', [(i, i ^ move) for i in range(self.size)])]
    all_gather x1, waiting for transfers between devices: 43.7 us -> 0.02 us  [body(): late = lax.all_gather(late, ('dp', 'xx'), axis=0, tiled=True)]
    all_gather x1 -> x0, waiting for transfers between devices: 22.8 us -> none  [body(): early = lax.all_gather(early, ('dp', 'xx'), axis=0, tiled=True)]
    dot_general x13 -> x15, matrix products: 95.9 us -> 84.3 us  [mm(): return lax.dot_general(left, right, dims, preferred_element_type=F32)]
    ppermute x14 -> x23, waiting for transfers between devices: 59.2 us -> 70.7 us  [swap(): return lax.ppermute(value, axis, [(0, 1), (1, 0)])]
    ppermute x14 -> x23, starting transfers between devices: 9.75 us -> 18.2 us  [swap(): return lax.ppermute(value, axis, [(0, 1), (1, 0)])]
  transfers between devices with their start and end apart: 18 -> 57, of which waited for: 12 -> 22; matrix products, arithmetic and copies ran while one was open for 17% -> 23% of each run, Pallas kernels for 6% -> 19%
where the time goes in v2:
time: 492 us; the launch traced here: 488 us
  waiting for transfers between devices  119 us (24%)
  Pallas kernels  93.6 us (19%)
  matrix products  84.3 us (17%)
  starting transfers between devices  66.3 us (13%)
  other arithmetic  60.3 us (12%)
  local copies, waits for them, and re-layouts  49.2 us (10%)
  between operations  15.8 us (3%)
    dot_general x15, matrix products, mm(): return lax.dot_general(left, right, dims, preferred_element_type=F32)  84.3 us
    ppermute x23, waiting for transfers between devices, swap(): return lax.ppermute(value, axis, [(0, 1), (1, 0)])  70.7 us
    pallas_call x3, Pallas kernels, attention_backward(): pl.pallas_call(attention_backward_kernel, grid=(1,), in_specs=[pl.BlockSp...  56.2 us
    ppermute x33, starting transfers between devices, send(): return lax.ppermute(value, 'dp', [(i, i ^ move) for i in range(self.size)])  48 us
    ppermute x33, waiting for transfers between devices, send(): return lax.ppermute(value, 'dp', [(i, i ^ move) for i in range(self.size)])  48 us
    pallas_call x1, Pallas kernels, attention_forward(): pl.pallas_call(attention_forward_kernel, grid=(pairs,), in_specs=[pl.Bloc...  37.4 us
    ppermute x23, starting transfers between devices, swap(): return lax.ppermute(value, axis, [(0, 1), (1, 0)])  18.2 us
    unnamed x112, local copies, waits for them, and re-layouts  11.2 us
  transfers between devices with their start and end apart: 57, of which 22 were waited for; matrix products, arithmetic and copies ran while one was open for 23% of the time, Pallas kernels for 19%

profile of v2, /device:TPU:0, one launch (start us, length us, event | category | flops | bytes accessed | tf_op | source)
XLA Modules:
  0.0 488.1 jit_solution(13495573279642578730)
XLA Ops:
  15.0 2.7 collective-permute-start
  17.7 2.1 dynamic-slice_bitcast_fusion.2
  20.3 2.2 collective-permute-start.3
  22.4 2.6 collective-permute-start.4
  25.0 2.0 collective-permute-done.3
  27.0 11.0 %collective-permute-done.4 = bf16[48,1280]{1,0:T(8,128)(2,1)S(1)} collective-permute-done((bf16[48,1280]{1,0:T(8,128)(2,1)S(1)}, bf16[48,1280]{1,0:T(8,128)(2,1)S(1)}, u32[]{:S(2)}, u32[]{:S(2)}) %collective-permute-start.4) | collective-permute-done | bytes 122912 | tf_op jit(solution)/shard_map/ppermute | solution.py:285
  42.3 27.7 %collective-permute-done.6 = bf16[4,48,640]{2,1,0:T(8,128)(2,1)S(1)} collective-permute-done((bf16[4,48,640]{2,1,0:T(8,128)(2,1)S(1)}, bf16[4,48,640]{2,1,0:T(8,128)(2,1)S(1)}, u32[]{:S(2)}, u32[]{:S(2)}) %collective-permute-start.6) | collective-permute-done | bytes 245792 | tf_op jit(solution)/shard_map/ppermute | solution.py:256
  70.9 2.5 collective-permute-start.9
  79.1 4.5 collective-permute-done.9
  87.4 2.0 fusion.122
  89.6 2.1 select_bitcast_fusion.1
  94.5 2.0 copy-done.3
  99.5 5.9 %multiply_convert_fusion.2.qkv_ref = bf16[2048,1152]{1,0:T(8,128)(2,1)} fusion(bf16[2048,768]{1,0:T(8,128)(2,1)S(1)} %add_convert_fusion.1, f32[1152]{0:T(1024)S(1)} %mul.184, f32[1152]{0:T(1024)S(1)} %add.404, bf16[768,640]{1,0:T(8,128)(2,1)S(1)} %bitcast.416, bf16[768,640]{1,0:T(8,128)(2,1)S(1)} %bitcast.419), kind=kOutput, calls=%fused_computation.4 | convolution fusion | flops 3634495488 | bytes 9839616 | tf_op jit(solution)/shard_map/dot_general | solution.py:24
  105.4 37.4 %shard_map.280 = (bf16[2048,384]{1,0:T(8,128)(2,1)S(1)}, f32[3,8,2048]{2,1,0:T(8,128)S(1)}) custom-call(bf16[2048,1152]{1,0:T(8,128)(2,1)} %multiply_convert_fusion.2.qkv_ref, bf16[2048,128]{1,0:T(8,128)(2,1)S(1)} %get-tuple-element.129.qs_ref, bf16[2048,128]{1,0:T(8,128)(2,1)S(1)} %get-tuple-element.128.ks_ref), custom_call_target="tpu_custom_call" | custom-call | flops 25769803776 | bytes 7077888 | tf_op jit(solution)/shard_map/pallas_call | solution.py:161
  142.8 3.6 fusion.120
  146.4 3.4 convolution_convert_fusion.1
  155.9 2.2 collective-permute-done.15
  158.1 2.8 fusion.43
  161.3 1.8 copy.131
  165.5 4.1 fusion.118
  170.6 12.5 %multiply_convert_fusion.1 = (bf16[2048,1536]{1,0:T(8,128)(2,1)S(1)}, f32[2048,1536]{1,0:T(8,128)}) fusion(f32[1536]{0:T(1024)S(1)} %add.417, bf16[768,3840]{1,0:T(8,128)(2,1)} %all-gather.2.cloned.1.call-done, f32[2048,768]{1,0:T(8,128)S(1)} %get-tuple-element.48, f32[768]{0:T(1024)S(1)} %get-tuple-element.99, f32[768]{0:T(1024)S(1)} %get-tuple-element.98, ...), kind=kOutput, calls=%fused_computation.1 | convolution fusion | flops 4871159808 | bytes 27553792 | tf_op jit(solution)/shard_map/dot_general | solution.py:24
  183.1 2.7 copy-done.46
  185.7 3.8 fusion.23
  189.6 5.8 %fusion.26 = bf16[768,768]{1,0:T(8,128)(2,1)} fusion(bf16[2048,768]{1,0:T(8,128)(2,1)S(1)} %bitcast.395, bf16[2048,1536]{1,0:T(8,128)(2,1)} %copy-done.46), kind=kOutput, calls=%fused_computation.72 | convolution fusion | flops 2416508928 | bytes 7471104 | tf_op jit(solution)/shard_map/dot_general | solution.py:24
  195.3 6.9 %fusion.29 = f32[2048,768]{1,0:T(8,128)} fusion(bf16[2048,1536]{1,0:T(8,128)(2,1)S(1)} %copy-done.47, bf16[768,768]{1,0:T(8,128)(2,1)S(1)} %copy-done.24, bf16[768,768]{1,0:T(8,128)(2,1)S(1)} %copy-done.23), kind=kOutput, calls=%fused_computation.73 | convolution fusion | flops 4836556800 | bytes 14942208 | tf_op jit(solution)/shard_map/dot_general | solution.py:24
  202.2 15.1 %multiply_convert_fusion = bf16[2048,1536]{1,0:T(8,128)(2,1)S(1)} fusion(f32[2048,1536]{1,0:T(8,128)} %get-tuple-element.137, bf16[2048,768]{1,0:T(8,128)(2,1)S(1)} %bitcast.396, f32[1536]{0:T(1024)S(1)} %add.417, bf16[768,768]{1,0:T(8,128)(2,1)} %get-tuple-element.51, bf16[768,768]{1,0:T(8,128)(2,1)S(1)} %copy-done.23), kind=kOutput, calls=%fused_computation | convolution fusion | flops 4896325632 | bytes 24385536 | tf_op jit(solution)/shard_map/dot_general | solution.py:24
  217.4 5.8 %convolution_convert_fusion = bf16[768,1536]{1,0:T(8,128)(2,1)S(1)} fusion(bf16[2048,1536]{1,0:T(8,128)(2,1)S(1)} %multiply_convert_fusion, f32[2048,768]{1,0:T(8,128)S(1)} %get-tuple-element.48, f32[768]{0:T(1024)S(1)} %get-tuple-element.99, f32[768]{0:T(1024)S(1)} %get-tuple-element.98, f32[2048]{0:T(1024)S(1)} %add_rsqrt_fusion, ...), kind=kOutput, calls=%fused_computation.23 | convolution fusion | flops 4840882176 | bytes 14964736 | tf_op jit(solution)/shard_map/dot_general | solution.py:24
  226.3 1.8 collective-permute-start.17
  228.1 7.1 %convolution_convert_fusion.2 = bf16[2048,768]{1,0:T(8,128)(2,1)S(1)} fusion(bf16[2048,1536]{1,0:T(8,128)(2,1)S(1)} %bitcast.402, bf16[768,3840]{1,0:T(8,128)(2,1)} %all-gather.2.cloned.1.call-done), kind=kOutput, calls=%fused_computation.25 | convolution fusion | flops 4833411072 | bytes 11796480 | tf_op jit(solution)/shard_map/dot_general | solution.py:24
  235.3 2.1 fusion.22
  238.9 15.2 %collective-permute-done.17 = bf16[2,4,2,48,768]{4,3,0,1,2:T(8,128)(2,1)S(1)} collective-permute-done((bf16[2,4,2,48,768]{4,3,0,1,2:T(8,128)(2,1)S(1)}, bf16[2,4,2,48,768]{4,3,0,1,2:T(8,128)(2,1)S(1)}, u32[]{:S(2)}, u32[]{:S(2)}) %collective-permute-start.17) | collective-permute-done | bytes 1179680 | tf_op jit(solution)/shard_map/ppermute | solution.py:256
  256.1 1.8 collective-permute-start.23
  257.9 2.6 fusion.13
  261.0 8.4 %collective-permute-done.18 = bf16[2,4,48,768]{3,2,0,1:T(8,128)(2,1)S(1)} collective-permute-done((bf16[2,4,48,768]{3,2,0,1:T(8,128)(2,1)S(1)}, bf16[2,4,48,768]{3,2,0,1:T(8,128)(2,1)S(1)}, u32[]{:S(2)}, u32[]{:S(2)}) %collective-permute-start.18) | collective-permute-done | bytes 589856 | tf_op jit(solution)/shard_map/ppermute | solution.py:285
  269.6 1.8 collective-permute-start.20
  271.3 2.7 collective-permute-start.21
  274.1 2.2 collective-permute-start.22
  278.2 7.2 %collective-permute-done.21 = bf16[2,48,768]{2,1,0:T(8,128)(2,1)S(1)} collective-permute-done((bf16[2,48,768]{2,1,0:T(8,128)(2,1)S(1)}, bf16[2,48,768]{2,1,0:T(8,128)(2,1)S(1)}, u32[]{:S(2)}, u32[]{:S(2)}) %collective-permute-start.21) | collective-permute-done | bytes 147488 | tf_op jit(solution)/shard_map/ppermute | solution.py:285
  285.3 2.6 collective-permute-start.50
  288.7 7.7 %collective-permute-done.49 = bf16[48,1536]{1,0:T(8,128)(2,1)S(1)} collective-permute-done((bf16[48,1536]{1,0:T(8,128)(2,1)S(1)}, bf16[48,1536]{1,0:T(8,128)(2,1)S(1)}, u32[]{:S(2)}, u32[]{:S(2)}) %collective-permute-start.49) | collective-permute-done | bytes 147488 | tf_op jit(solution)/shard_map/ppermute | solution.py:285
  297.9 3.5 multiply_reduce_fusion
  301.4 3.5 convert_reduce_fusion.1
  307.6 3.0 convolution_convert_fusion.3.do_ref
  312.3 18.9 %shard_map.281 = bf16[2048,384]{1,0:T(8,128)(2,1)S(1)} custom-call(bf16[2048,1152]{1,0:T(8,128)(2,1)} %multiply_convert_fusion.2.qkv_ref, bf16[2048,128]{1,0:T(8,128)(2,1)S(1)} %get-tuple-element.129.qs_ref, bf16[2048,128]{1,0:T(8,128)(2,1)S(1)} %get-tuple-element.128.ks_ref, bf16[2048,384]{1,0:T(8,128)(2,1)S(1)} %get-tuple-element.17.o_ref, ...), custom_call_target="tpu_custom_call" | custom-call | flops 21474836480 | bytes 6291456 | tf_op jit(solution)/shard_map/pallas_call | solution.py:193
  331.3 1.8 convolution_convert_fusion.6
  335.5 18.6 %shard_map.282 = bf16[2048,384]{1,0:T(8,128)(2,1)S(1)} custom-call(bf16[2048,1152]{1,0:T(8,128)(2,1)} %multiply_convert_fusion.2.qkv_ref, bf16[2048,128]{1,0:T(8,128)(2,1)S(1)} %get-tuple-element.129.qs_ref, bf16[2048,128]{1,0:T(8,128)(2,1)S(1)} %get-tuple-element.128.ks_ref, bf16[2048,384]{1,0:T(8,128)(2,1)S(1)} %get-tuple-element.17.o_ref, ...), custom_call_target="tpu_custom_call" | custom-call | flops 21474836480 | bytes 6291456 | tf_op jit(solution)/shard_map/pallas_call | solution.py:193
  354.1 1.8 convolution_convert_fusion.5
  356.6 18.7 %shard_map.283 = bf16[2048,384]{1,0:T(8,128)(2,1)S(1)} custom-call(bf16[2048,1152]{1,0:T(8,128)(2,1)} %multiply_convert_fusion.2.qkv_ref, bf16[2048,128]{1,0:T(8,128)(2,1)S(1)} %get-tuple-element.129.qs_ref, bf16[2048,128]{1,0:T(8,128)(2,1)S(1)} %get-tuple-element.128.ks_ref, bf16[2048,384]{1,0:T(8,128)(2,1)S(1)} %get-tuple-element.17.o_ref, ...), custom_call_target="tpu_custom_call" | custom-call | flops 21474836480 | bytes 6291456 | tf_op jit(solution)/shard_map/pallas_call | solution.py:193
  375.8 8.1 %fusion.117 = (bf16[768]{0:T(1024)(128)(2,1)S(1)}, bf16[768]{0:T(1024)(128)(2,1)S(1)}, bf16[2048,768]{1,0:T(8,128)(2,1)}) fusion(f32[2048]{0:T(1024)S(1)} %bitcast.428, f32[2048]{0:T(1024)S(1)} %bitcast.430, f32[2,2,512,768]{3,2,1,0:T(8,128)} %copy-done.4, bf16[768,640]{1,0:T(8,128)(2,1)S(1)} %bitcast.417, bf16[768,640]{1,0:T(8,128)(2,1)S(1)} %bitcast.420, ...), kind=kOutput, calls=%fused_computation.344 | convolution fusion | flops 3651009024 | bytes 16141312 | tf_op jit(solution)/shard_map/dot_general | solution.py:24
  383.9 1.8 convolution_convert_fusion.4
  392.9 2.5 collective-permute-done.42
  395.9 2.7 dynamic-slice_bitcast_fusion
  399.6 3.5 collective-permute-start.44
  413.7 2.4 collective-permute-start.35
  418.9 3.0 collective-permute-start.53
  422.7 1.8 collective-permute-start.54
  425.8 3.1 collective-permute-done.54
  431.2 1.8 stack.252
  437.5 2.3 collective-permute-start.40
  439.9 2.0 collective-permute-start.41
  444.4 3.0 reshape.338
  449.8 3.5 fusion.15
  453.4 3.9 fusion.10
  461.0 17.5 %collective-permute-done.26 = bf16[512,768]{1,0:T(8,128)(2,1)S(1)} collective-permute-done((bf16[512,768]{1,0:T(8,128)(2,1)S(1)}, bf16[512,768]{1,0:T(8,128)(2,1)S(1)}, u32[]{:S(2)}, u32[]{:S(2)}) %collective-permute-start.26) | collective-permute-done | bytes 786464 | tf_op jit(solution)/shard_map/ppermute | solution.py:256
  (372 shorter events, 99.4 us)
Async XLA Ops:
  7.2 135.6 %all-gather.2.cloned.1.call-start = ((), (), s32[]{:S(2)}) async-start(), calls=%async_computation | async-start | bytes 6266880 | tf_op jit(solution)/shard_map/all_gather | solution.py:423
  9.4 10.6 %collective-permute-start.2 = (bf16[24,1280]{1,0:T(8,128)(2,1)S(1)}, bf16[24,1280]{1,0:T(8,128)(2,1)S(1)}, u32[]{:S(2)}, u32[]{:S(2)}) collective-permute-start(bf16[24,1280]{1,0:T(8,128)(2,1)S(1)} %fusion.90), channel_id=1, source_target_pairs={{0,1},{1,0},{2,3},{3,2},{4,5},{5,4},{6,7},{7,6},{8,9},{9,8},{10,11... | collective-permute-start | bytes 184328 | tf_op jit(solution)/shard_map/ppermute | solution.py:256
  12.7 1.4 collective-permute-start.10
  15.0 60.6 %collective-permute-start = (bf16[512,768]{1,0:T(8,128)(2,1)S(1)}, bf16[512,768]{1,0:T(8,128)(2,1)}, u32[]{:S(2)}, u32[]{:S(2)}) collective-permute-start(bf16[512,768]{1,0:T(8,128)(2,1)S(1)} %dynamic-slice_bitcast_fusion.4), channel_id=1, source_target_pairs={{0,2},{2,0},{1,3},{3,1},{4,6},{6,4},{5,7},{7,5},{8,10},{10,8},{9,1... | collective-permute-start | bytes 2359304 | tf_op jit(solution)/shard_map/ppermute | solution.py:256
  19.8 130.1 %collective-permute-start.14 = (bf16[512,768]{1,0:T(8,128)(2,1)}, bf16[512,768]{1,0:T(8,128)(2,1)}, u32[]{:S(2)}, u32[]{:S(2)}) collective-permute-start(bf16[512,768]{1,0:T(8,128)(2,1)} %dynamic-slice_bitcast_fusion.2), channel_id=1, source_target_pairs={{0,2},{2,0},{1,3},{3,1},{4,6},{6,4},{5,7},{7,5},{8,10},{10,8},{9,1... | collective-permute-start | bytes 2359304 | tf_op jit(solution)/shard_map/ppermute | solution.py:256
  20.3 6.7 %collective-permute-start.3 = (bf16[48,1280]{1,0:T(8,128)(2,1)S(1)}, bf16[48,1280]{1,0:T(8,128)(2,1)S(1)}, u32[]{:S(2)}, u32[]{:S(2)}) collective-permute-start(bf16[48,1280]{1,0:T(8,128)(2,1)S(1)} %concatenate.54), channel_id=1, source_target_pairs={{0,8},{4,12},{8,0},{12,4},{16,24},{20,28},{24,16},{28,20},{1,9},{5... | collective-permute-start | bytes 368648 | tf_op jit(solution)/shard_map/ppermute | solution.py:285
  22.4 15.6 %collective-permute-start.4 = (bf16[48,1280]{1,0:T(8,128)(2,1)S(1)}, bf16[48,1280]{1,0:T(8,128)(2,1)S(1)}, u32[]{:S(2)}, u32[]{:S(2)}) collective-permute-start(bf16[48,1280]{1,0:T(8,128)(2,1)S(1)} %concatenate.54), channel_id=1, source_target_pairs={{0,16},{4,20},{8,24},{12,28},{16,0},{20,4},{24,8},{28,12},{1,17},{... | collective-permute-start | bytes 368648 | tf_op jit(solution)/shard_map/ppermute | solution.py:285
  25.0 13.0 %collective-permute-start.5 = (bf16[48,1280]{1,0:T(8,128)(2,1)S(1)}, bf16[48,1280]{1,0:T(8,128)(2,1)S(1)}, u32[]{:S(2)}, u32[]{:S(2)}) collective-permute-start(bf16[48,1280]{1,0:T(8,128)(2,1)S(1)} %concatenate.54), channel_id=1, source_target_pairs={{0,24},{4,28},{8,16},{12,20},{16,8},{20,12},{24,0},{28,4},{1,25},{... | collective-permute-start | bytes 368648 | tf_op jit(solution)/shard_map/ppermute | solution.py:285
  38.2 37.4 %copy-start.18 = (bf16[2,512,768]{2,1,0:T(8,128)(2,1)S(1)}, bf16[2,512,768]{2,1,0:T(8,128)(2,1)}, u32[]{:S(2)}) copy-start(bf16[2,512,768]{2,1,0:T(8,128)(2,1)} %param.17) | copy-start | bytes 4718596
  38.2 31.8 %collective-permute-start.6 = (bf16[4,48,640]{2,1,0:T(8,128)(2,1)S(1)}, bf16[4,48,640]{2,1,0:T(8,128)(2,1)S(1)}, u32[]{:S(2)}, u32[]{:S(2)}) collective-permute-start(bf16[4,48,640]{2,1,0:T(8,128)(2,1)S(1)} %get-tuple-element.86), channel_id=1, source_target_pairs={{0,2},{2,0},{1,3},{3,1},{4,6},{6,4},{5,7},{7,5},{8,10},{10,8},{9,1... | collective-permute-start | bytes 737288 | tf_op jit(solution)/shard_map/ppermute | solution.py:256
  39.8 30.2 %collective-permute-start.8 = (bf16[4,48,640]{2,1,0:T(8,128)(2,1)S(1)}, bf16[4,48,640]{2,1,0:T(8,128)(2,1)S(1)}, u32[]{:S(2)}, u32[]{:S(2)}) collective-permute-start(bf16[4,48,640]{2,1,0:T(8,128)(2,1)S(1)} %get-tuple-element.85), channel_id=1, source_target_pairs={{0,4},{4,0},{8,12},{12,8},{16,20},{20,16},{24,28},{28,24},{1,5},{5... | collective-permute-start | bytes 737288 | tf_op jit(solution)/shard_map/ppermute | solution.py:285
  70.9 12.7 %collective-permute-start.9 = (bf16[4,2,48,640]{3,2,0,1:T(8,128)(2,1)}, bf16[4,2,48,640]{3,2,0,1:T(8,128)(2,1)}, u32[]{:S(2)}, u32[]{:S(2)}) collective-permute-start(bf16[4,2,48,640]{3,2,0,1:T(8,128)(2,1)} %pad_maximum_fusion.18), channel_id=1, source_target_pairs={{0,2},{2,0},{1,3},{3,1},{4,6},{6,4},{5,7},{7,5},{8,10},{10,8},{9,1... | collective-permute-start | bytes 1474568 | tf_op jit(solution)/shard_map/ppermute | solution.py:256
  74.2 11.7 %collective-permute-start.7 = (bf16[4,2,48,640]{3,2,1,0:T(8,128)(2,1)}, bf16[4,2,48,640]{3,2,1,0:T(8,128)(2,1)}, u32[]{:S(2)}, u32[]{:S(2)}) collective-permute-start(bf16[4,2,48,640]{3,2,1,0:T(8,128)(2,1)} %pad_maximum_fusion.17), channel_id=1, source_target_pairs={{0,4},{4,0},{8,12},{12,8},{16,20},{20,16},{24,28},{28,24},{1,5},{5... | collective-permute-start | bytes 1474568 | tf_op jit(solution)/shard_map/ppermute | solution.py:285
  79.0 10.7 %collective-permute-start.1 = (bf16[2,512,768]{2,1,0:T(8,128)(2,1)}, bf16[2,512,768]{2,1,0:T(8,128)(2,1)}, u32[]{:S(2)}, u32[]{:S(2)}) collective-permute-start(bf16[2,512,768]{2,1,0:T(8,128)(2,1)} %pad_maximum_fusion.6), channel_id=1, source_target_pairs={{0,1},{1,0},{2,3},{3,2},{4,5},{5,4},{6,7},{7,6},{8,9},{9,8},{10,11... | collective-permute-start | bytes 4718600 | tf_op jit(solution)/shard_map/ppermute | solution.py:256
  149.8 15.2 %collective-permute-start.11 = (bf16[2048,768]{1,0:T(8,128)(2,1)}, bf16[2048,768]{1,0:T(8,128)(2,1)}, u32[]{:S(2)}, u32[]{:S(2)}) collective-permute-start(bf16[2048,768]{1,0:T(8,128)(2,1)} %convolution_convert_fusion.1), channel_id=1, source_target_pairs={{0,1},{1,0},{2,3},{3,2},{4,5},{5,4},{6,7},{7,6},{8,9},{9,8},{10,11... | collective-permute-start | bytes 9437192 | tf_op jit(solution)/shard_map/ppermute | solution.py:256
  153.3 4.8 collective-permute-start.15
  224.5 30.0 %collective-permute-start.19 = (bf16[4,2,48,1536]{3,2,0,1:T(8,128)(2,1)}, bf16[4,2,48,1536]{3,2,0,1:T(8,128)(2,1)S(1)}, u32[]{:S(2)}, u32[]{:S(2)}) collective-permute-start(bf16[4,2,48,1536]{3,2,0,1:T(8,128)(2,1)} %bitcast.383), channel_id=1, source_target_pairs={{0,4},{4,0},{8,12},{12,8},{16,20},{20,16},{24,28},{28,24},{1,5},{5... | collective-permute-start | bytes 3538952 | tf_op jit(solution)/shard_map/ppermute | solution.py:285
  226.3 27.8 %collective-permute-start.17 = (bf16[2,4,2,48,768]{4,3,0,1,2:T(8,128)(2,1)S(1)}, bf16[2,4,2,48,768]{4,3,0,1,2:T(8,128)(2,1)S(1)}, u32[]{:S(2)}, u32[]{:S(2)}) collective-permute-start(bf16[2,4,2,48,768]{4,3,0,1,2:T(8,128)(2,1)S(1)} %bitcast.418), channel_id=1, source_target_pairs={{0,2},{2,0},{1,3},{3,1},{4,6},{6,4},{5,7},{7,5},{8,10},{10,8},{9,1... | collective-permute-start | bytes 3538952 | tf_op jit(solution)/shard_map/ppermute | solution.py:256
  235.2 62.7 %collective-permute-start.16 = (bf16[2048,768]{1,0:T(8,128)(2,1)S(1)}, bf16[2048,768]{1,0:T(8,128)(2,1)S(1)}, u32[]{:S(2)}, u32[]{:S(2)}) collective-permute-start(bf16[2048,768]{1,0:T(8,128)(2,1)S(1)} %convolution_convert_fusion.2), channel_id=1, source_target_pairs={{0,1},{1,0},{2,3},{3,2},{4,5},{5,4},{6,7},{7,6},{8,9},{9,8},{10,11... | collective-permute-start | bytes 9437192 | tf_op jit(solution)/shard_map/ppermute | solution.py:256
  237.4 20.5 %collective-permute-start.12 = (bf16[2,512,768]{2,1,0:T(8,128)(2,1)S(1)}, bf16[2,512,768]{2,1,0:T(8,128)(2,1)S(1)}, u32[]{:S(2)}, u32[]{:S(2)}) collective-permute-start(bf16[2,512,768]{2,1,0:T(8,128)(2,1)S(1)} %fusion.22), channel_id=1, source_target_pairs={{0,1},{1,0},{2,3},{3,2},{4,5},{5,4},{6,7},{7,6},{8,9},{9,8},{10,11... | collective-permute-start | bytes 4718600 | tf_op jit(solution)/shard_map/ppermute | solution.py:256
  255.0 14.3 %collective-permute-start.18 = (bf16[2,4,48,768]{3,2,0,1:T(8,128)(2,1)S(1)}, bf16[2,4,48,768]{3,2,0,1:T(8,128)(2,1)S(1)}, u32[]{:S(2)}, u32[]{:S(2)}) collective-permute-start(bf16[2,4,48,768]{3,2,0,1:T(8,128)(2,1)S(1)} %dynamic-slice_bitcast_fusion.6), channel_id=1, source_target_pairs={{0,4},{4,0},{8,12},{12,8},{16,20},{20,16},{24,28},{28,24},{1,5},{5... | collective-permute-start | bytes 1769480 | tf_op jit(solution)/shard_map/ppermute | solution.py:285
  256.1 18.0 %collective-permute-start.23 = (bf16[4,48,1536]{2,1,0:T(8,128)(2,1)S(1)}, bf16[4,48,1536]{2,1,0:T(8,128)(2,1)S(1)}, u32[]{:S(2)}, u32[]{:S(2)}) collective-permute-start(bf16[4,48,1536]{2,1,0:T(8,128)(2,1)S(1)} %dynamic-slice_bitcast_fusion.5), channel_id=1, source_target_pairs={{0,2},{2,0},{1,3},{3,1},{4,6},{6,4},{5,7},{7,5},{8,10},{10,8},{9,1... | collective-permute-start | bytes 1769480 | tf_op jit(solution)/shard_map/ppermute | solution.py:256
  260.6 35.9 %collective-permute-start.13 = (bf16[512,768]{1,0:T(8,128)(2,1)S(1)}, bf16[512,768]{1,0:T(8,128)(2,1)S(1)}, u32[]{:S(2)}, u32[]{:S(2)}) collective-permute-start(bf16[512,768]{1,0:T(8,128)(2,1)S(1)} %dynamic-slice_bitcast_fusion.3), channel_id=1, source_target_pairs={{0,2},{2,0},{1,3},{3,1},{4,6},{6,4},{5,7},{7,5},{8,10},{10,8},{9,1... | collective-permute-start | bytes 2359304 | tf_op jit(solution)/shard_map/ppermute | solution.py:256
  269.6 8.6 %collective-permute-start.20 = (bf16[2,48,768]{2,1,0:T(8,128)(2,1)S(1)}, bf16[2,48,768]{2,1,0:T(8,128)(2,1)S(1)}, u32[]{:S(2)}, u32[]{:S(2)}) collective-permute-start(bf16[2,48,768]{2,1,0:T(8,128)(2,1)S(1)} %get-tuple-element.80), channel_id=1, source_target_pairs={{0,8},{4,12},{8,0},{12,4},{16,24},{20,28},{24,16},{28,20},{1,9},{5... | collective-permute-start | bytes 442376 | tf_op jit(solution)/shard_map/ppermute | solution.py:285
  271.3 14.0 %collective-permute-start.21 = (bf16[2,48,768]{2,1,0:T(8,128)(2,1)S(1)}, bf16[2,48,768]{2,1,0:T(8,128)(2,1)S(1)}, u32[]{:S(2)}, u32[]{:S(2)}) collective-permute-start(bf16[2,48,768]{2,1,0:T(8,128)(2,1)S(1)} %get-tuple-element.82), channel_id=1, source_target_pairs={{0,16},{4,20},{8,24},{12,28},{16,0},{20,4},{24,8},{28,12},{1,17},{... | collective-permute-start | bytes 442376 | tf_op jit(solution)/shard_map/ppermute | solution.py:285
  274.1 11.3 %collective-permute-start.22 = (bf16[2,48,768]{2,1,0:T(8,128)(2,1)S(1)}, bf16[2,48,768]{2,1,0:T(8,128)(2,1)S(1)}, u32[]{:S(2)}, u32[]{:S(2)}) collective-permute-start(bf16[2,48,768]{2,1,0:T(8,128)(2,1)S(1)} %get-tuple-element.81), channel_id=1, source_target_pairs={{0,24},{4,28},{8,16},{12,20},{16,8},{20,12},{24,0},{28,4},{1,25},{... | collective-permute-start | bytes 442376 | tf_op jit(solution)/shard_map/ppermute | solution.py:285
  278.2 10.6 %collective-permute-start.48 = (bf16[48,1536]{1,0:T(8,128)(2,1)S(1)}, bf16[48,1536]{1,0:T(8,128)(2,1)S(1)}, u32[]{:S(2)}, u32[]{:S(2)}) collective-permute-start(bf16[48,1536]{1,0:T(8,128)(2,1)S(1)} %get-tuple-element.77), channel_id=1, source_target_pairs={{0,8},{4,12},{8,0},{12,4},{16,24},{20,28},{24,16},{28,20},{1,9},{5... | collective-permute-start | bytes 442376 | tf_op jit(solution)/shard_map/ppermute | solution.py:285
  285.3 11.1 %collective-permute-start.49 = (bf16[48,1536]{1,0:T(8,128)(2,1)S(1)}, bf16[48,1536]{1,0:T(8,128)(2,1)S(1)}, u32[]{:S(2)}, u32[]{:S(2)}) collective-permute-start(bf16[48,1536]{1,0:T(8,128)(2,1)S(1)} %get-tuple-element.79), channel_id=1, source_target_pairs={{0,16},{4,20},{8,24},{12,28},{16,0},{20,4},{24,8},{28,12},{1,17},{... | collective-permute-start | bytes 442376 | tf_op jit(solution)/shard_map/ppermute | solution.py:285
  285.3 11.1 %collective-permute-start.50 = (bf16[48,1536]{1,0:T(8,128)(2,1)S(1)}, bf16[48,1536]{1,0:T(8,128)(2,1)S(1)}, u32[]{:S(2)}, u32[]{:S(2)}) collective-permute-start(bf16[48,1536]{1,0:T(8,128)(2,1)S(1)} %get-tuple-element.78), channel_id=1, source_target_pairs={{0,24},{4,28},{8,16},{12,20},{16,8},{20,12},{24,0},{28,4},{1,25},{... | collective-permute-start | bytes 442376 | tf_op jit(solution)/shard_map/ppermute | solution.py:285
  310.6 45.8 %collective-permute-start.24 = (bf16[2,2,48,768]{3,2,1,0:T(8,128)(2,1)S(1)}, bf16[2,2,48,768]{3,2,1,0:T(8,128)(2,1)S(1)}, u32[]{:S(2)}, u32[]{:S(2)}) collective-permute-start(bf16[2,2,48,768]{3,2,1,0:T(8,128)(2,1)S(1)} %dynamic-slice_bitcast_fusion.10), channel_id=1, source_target_pairs={{0,2},{2,0},{1,3},{3,1},{4,6},{6,4},{5,7},{7,5},{8,10},{10,8},{9,1... | collective-permute-start | bytes 884744 | tf_op jit(solution)/shard_map/ppermute | solution.py:256
  333.9 51.9 %collective-permute-start.27 = (bf16[4,2,48,384]{3,2,1,0:T(8,128)(2,1)}, bf16[4,2,48,384]{3,2,1,0:T(8,128)(2,1)S(1)}, u32[]{:S(2)}, u32[]{:S(2)}) collective-permute-start(bf16[4,2,48,384]{3,2,1,0:T(8,128)(2,1)} %dynamic-slice_bitcast_fusion.9), channel_id=1, source_target_pairs={{0,4},{4,0},{8,12},{12,8},{16,20},{20,16},{24,28},{28,24},{1,5},{5... | collective-permute-start | bytes 884744 | tf_op jit(solution)/shard_map/ppermute | solution.py:285
  356.0 32.4 %collective-permute-start.32 = (bf16[4,2,48,384]{3,2,1,0:T(8,128)(2,1)S(1)}, bf16[4,2,48,384]{3,2,1,0:T(8,128)(2,1)S(1)}, u32[]{:S(2)}, u32[]{:S(2)}) collective-permute-start(bf16[4,2,48,384]{3,2,1,0:T(8,128)(2,1)S(1)} %dynamic-slice_bitcast_fusion.8), channel_id=1, source_target_pairs={{0,2},{2,0},{1,3},{3,1},{4,6},{6,4},{5,7},{7,5},{8,10},{10,8},{9,1... | collective-permute-start | bytes 884744 | tf_op jit(solution)/shard_map/ppermute | solution.py:256
  356.6 19.2 %copy-start.22 = (bf16[4,2,2,48,640]{4,3,2,1,0:T(8,128)(2,1)S(1)}, bf16[4,2,2,48,640]{4,3,2,1,0:T(8,128)(2,1)}, u32[]{:S(2)}) copy-start(bf16[4,2,2,48,640]{4,3,2,1,0:T(8,128)(2,1)} %copy-done.20) | copy-start | bytes 2949124
  375.3 28.8 %collective-permute-start.51 = (bf16[2,48,768]{2,1,0:T(8,128)(2,1)S(1)}, bf16[2,48,768]{2,1,0:T(8,128)(2,1)S(1)}, u32[]{:S(2)}, u32[]{:S(2)}) collective-permute-start(bf16[2,48,768]{2,1,0:T(8,128)(2,1)S(1)} %dynamic-slice_bitcast_fusion.11), channel_id=1, source_target_pairs={{0,4},{4,0},{8,12},{12,8},{16,20},{20,16},{24,28},{28,24},{1,5},{5... | collective-permute-start | bytes 442376 | tf_op jit(solution)/shard_map/ppermute | solution.py:285
  385.9 13.8 %collective-permute-start.28 = (bf16[4,48,384]{2,1,0:T(8,128)(2,1)S(1)}, bf16[4,48,384]{2,1,0:T(8,128)(2,1)}, u32[]{:S(2)}, u32[]{:S(2)}) collective-permute-start(bf16[4,48,384]{2,1,0:T(8,128)(2,1)S(1)} %dynamic-slice_bitcast_fusion.17), channel_id=1, source_target_pairs={{0,2},{2,0},{1,3},{3,1},{4,6},{6,4},{5,7},{7,5},{8,10},{10,8},{9,1... | collective-permute-start | bytes 442376 | tf_op jit(solution)/shard_map/ppermute | solution.py:256
  388.5 16.7 %collective-permute-start.33 = (bf16[4,48,384]{2,1,0:T(8,128)(2,1)S(1)}, bf16[4,48,384]{2,1,0:T(8,128)(2,1)S(1)}, u32[]{:S(2)}, u32[]{:S(2)}) collective-permute-start(bf16[4,48,384]{2,1,0:T(8,128)(2,1)S(1)} %dynamic-slice_bitcast_fusion.16), channel_id=1, source_target_pairs={{0,4},{4,0},{8,12},{12,8},{16,20},{20,16},{24,28},{28,24},{1,5},{5... | collective-permute-start | bytes 442376 | tf_op jit(solution)/shard_map/ppermute | solution.py:285
  390.7 4.7 collective-permute-start.42
  391.2 37.9 %collective-permute-start.37 = (bf16[4,2,48,384]{3,2,1,0:T(8,128)(2,1)S(1)}, bf16[4,2,48,384]{3,2,1,0:T(8,128)(2,1)S(1)}, u32[]{:S(2)}, u32[]{:S(2)}) collective-permute-start(bf16[4,2,48,384]{3,2,1,0:T(8,128)(2,1)S(1)} %dynamic-slice_bitcast_fusion.7), channel_id=1, source_target_pairs={{0,4},{4,0},{8,12},{12,8},{16,20},{20,16},{24,28},{28,24},{1,5},{5... | collective-permute-start | bytes 884744 | tf_op jit(solution)/shard_map/ppermute | solution.py:285
  395.4 4.2 collective-permute-start.43
  399.6 50.2 %collective-permute-start.25 = (bf16[2,512,768]{2,1,0:T(8,128)(2,1)}, bf16[2,512,768]{2,1,0:T(8,128)(2,1)}, u32[]{:S(2)}, u32[]{:S(2)}) collective-permute-start(bf16[2,512,768]{2,1,0:T(8,128)(2,1)} %dynamic-slice_bitcast_fusion), channel_id=1, source_target_pairs={{0,1},{1,0},{2,3},{3,2},{4,5},{5,4},{6,7},{7,6},{8,9},{9,8},{10,11... | collective-permute-start | bytes 4718600 | tf_op jit(solution)/shard_map/ppermute | solution.py:256
  399.6 7.3 %collective-permute-start.44 = (bf16[48,128]{1,0:T(8,128)(2,1)S(1)}, bf16[48,128]{1,0:T(8,128)(2,1)S(1)}, u32[]{:S(2)}, u32[]{:S(2)}) collective-permute-start(bf16[48,128]{1,0:T(8,128)(2,1)S(1)} %get-tuple-element.125), channel_id=1, source_target_pairs={{0,8},{4,12},{8,0},{12,4},{16,24},{20,28},{24,16},{28,20},{1,9},{5... | collective-permute-start | bytes 36872 | tf_op jit(solution)/shard_map/ppermute | solution.py:285
  404.1 4.7 collective-permute-start.45
  405.2 5.7 %collective-permute-start.46 = (bf16[48,128]{1,0:T(8,128)(2,1)S(1)}, bf16[48,128]{1,0:T(8,128)(2,1)S(1)}, u32[]{:S(2)}, u32[]{:S(2)}) collective-permute-start(bf16[48,128]{1,0:T(8,128)(2,1)S(1)} %get-tuple-element.126), channel_id=1, source_target_pairs={{0,24},{4,28},{8,16},{12,20},{16,8},{20,12},{24,0},{28,4},{1,25},{... | collective-permute-start | bytes 36872 | tf_op jit(solution)/shard_map/ppermute | solution.py:285
  406.9 6.3 %collective-permute-start.29 = (bf16[48,384]{1,0:T(8,128)(2,1)S(1)}, bf16[48,384]{1,0:T(8,128)(2,1)S(1)}, u32[]{:S(2)}, u32[]{:S(2)}) collective-permute-start(bf16[48,384]{1,0:T(8,128)(2,1)S(1)} %get-tuple-element.114), channel_id=1, source_target_pairs={{0,8},{4,12},{8,0},{12,4},{16,24},{20,28},{24,16},{28,20},{1,9},{5... | collective-permute-start | bytes 110600 | tf_op jit(solution)/shard_map/ppermute | solution.py:285
  408.8 4.9 %collective-permute-start.30 = (bf16[48,384]{1,0:T(8,128)(2,1)S(1)}, bf16[48,384]{1,0:T(8,128)(2,1)S(1)}, u32[]{:S(2)}, u32[]{:S(2)}) collective-permute-start(bf16[48,384]{1,0:T(8,128)(2,1)S(1)} %get-tuple-element.116), channel_id=1, source_target_pairs={{0,16},{4,20},{8,24},{12,28},{16,0},{20,4},{24,8},{28,12},{1,17},{... | collective-permute-start | bytes 110600 | tf_op jit(solution)/shard_map/ppermute | solution.py:285
  410.9 5.9 %collective-permute-start.31 = (bf16[48,384]{1,0:T(8,128)(2,1)S(1)}, bf16[48,384]{1,0:T(8,128)(2,1)S(1)}, u32[]{:S(2)}, u32[]{:S(2)}) collective-permute-start(bf16[48,384]{1,0:T(8,128)(2,1)S(1)} %get-tuple-element.115), channel_id=1, source_target_pairs={{0,24},{4,28},{8,16},{12,20},{16,8},{20,12},{24,0},{28,4},{1,25},{... | collective-permute-start | bytes 110600 | tf_op jit(solution)/shard_map/ppermute | solution.py:285
  413.2 5.7 %collective-permute-start.34 = (bf16[48,384]{1,0:T(8,128)(2,1)S(1)}, bf16[48,384]{1,0:T(8,128)(2,1)S(1)}, u32[]{:S(2)}, u32[]{:S(2)}) collective-permute-start(bf16[48,384]{1,0:T(8,128)(2,1)S(1)} %get-tuple-element.117), channel_id=1, source_target_pairs={{0,8},{4,12},{8,0},{12,4},{16,24},{20,28},{24,16},{28,20},{1,9},{5... | collective-permute-start | bytes 110600 | tf_op jit(solution)/shard_map/ppermute | solution.py:285
  413.7 5.2 %collective-permute-start.35 = (bf16[48,384]{1,0:T(8,128)(2,1)S(1)}, bf16[48,384]{1,0:T(8,128)(2,1)S(1)}, u32[]{:S(2)}, u32[]{:S(2)}) collective-permute-start(bf16[48,384]{1,0:T(8,128)(2,1)S(1)} %get-tuple-element.119), channel_id=1, source_target_pairs={{0,16},{4,20},{8,24},{12,28},{16,0},{20,4},{24,8},{28,12},{1,17},{... | collective-permute-start | bytes 110600 | tf_op jit(solution)/shard_map/ppermute | solution.py:285
  416.8 5.9 %collective-permute-start.36 = (bf16[48,384]{1,0:T(8,128)(2,1)S(1)}, bf16[48,384]{1,0:T(8,128)(2,1)S(1)}, u32[]{:S(2)}, u32[]{:S(2)}) collective-permute-start(bf16[48,384]{1,0:T(8,128)(2,1)S(1)} %get-tuple-element.118), channel_id=1, source_target_pairs={{0,24},{4,28},{8,16},{12,20},{16,8},{20,12},{24,0},{28,4},{1,25},{... | collective-permute-start | bytes 110600 | tf_op jit(solution)/shard_map/ppermute | solution.py:285
  418.9 6.2 %collective-permute-start.52 = (bf16[48,768]{1,0:T(8,128)(2,1)S(1)}, bf16[48,768]{1,0:T(8,128)(2,1)S(1)}, u32[]{:S(2)}, u32[]{:S(2)}) collective-permute-start(bf16[48,768]{1,0:T(8,128)(2,1)S(1)} %get-tuple-element.103), channel_id=1, source_target_pairs={{0,8},{4,12},{8,0},{12,4},{16,24},{20,28},{24,16},{28,20},{1,9},{5... | collective-permute-start | bytes 221192 | tf_op jit(solution)/shard_map/ppermute | solution.py:285
  418.9 6.9 %collective-permute-start.53 = (bf16[48,768]{1,0:T(8,128)(2,1)S(1)}, bf16[48,768]{1,0:T(8,128)(2,1)S(1)}, u32[]{:S(2)}, u32[]{:S(2)}) collective-permute-start(bf16[48,768]{1,0:T(8,128)(2,1)S(1)} %get-tuple-element.104), channel_id=1, source_target_pairs={{0,16},{4,20},{8,24},{12,28},{16,0},{20,4},{24,8},{28,12},{1,17},{... | collective-permute-start | bytes 221192 | tf_op jit(solution)/shard_map/ppermute | solution.py:285
  422.7 6.2 %collective-permute-start.54 = (bf16[48,768]{1,0:T(8,128)(2,1)S(1)}, bf16[48,768]{1,0:T(8,128)(2,1)S(1)}, u32[]{:S(2)}, u32[]{:S(2)}) collective-permute-start(bf16[48,768]{1,0:T(8,128)(2,1)S(1)} %get-tuple-element.105), channel_id=1, source_target_pairs={{0,24},{4,28},{8,16},{12,20},{16,8},{20,12},{24,0},{28,4},{1,25},{... | collective-permute-start | bytes 221192 | tf_op jit(solution)/shard_map/ppermute | solution.py:285
  429.0 1.5 collective-permute-start.55
  429.2 20.6 %copy-start.8 = (bf16[2048,768]{1,0:T(8,128)(2,1)S(1)}, bf16[2048,768]{1,0:T(8,128)(2,1)}, u32[]{:S(2)}) copy-start(bf16[2048,768]{1,0:T(8,128)(2,1)} %get-tuple-element.49) | copy-start | bytes 9437188
  429.2 20.6 %copy-start.34 = (f32[2,512]{1,0:T(2,128)S(1)}, f32[2,512]{1,0:T(2,128)}, u32[]{:S(2)}) copy-start(f32[2,512]{1,0:T(2,128)} %copy-done.33) | copy-start | bytes 12292
  429.2 20.6 %copy-start.36 = (f32[768]{0:T(1024)S(1)}, f32[768]{0:T(1024)}, u32[]{:S(2)}) copy-start(f32[768]{0:T(1024)} %copy-done.35) | copy-start | bytes 9220
  429.2 20.6 %copy-start.37 = (f32[2,512]{1,0:T(2,128)S(1)}, f32[2,512]{1,0:T(2,128)}, u32[]{:S(2)}) copy-start(f32[2,512]{1,0:T(2,128)} %add_rsqrt_fusion.2) | copy-start | bytes 12292
  429.9 6.6 %collective-permute-start.38 = (bf16[4,48,384]{2,1,0:T(8,128)(2,1)}, bf16[4,48,384]{2,1,0:T(8,128)(2,1)}, u32[]{:S(2)}, u32[]{:S(2)}) collective-permute-start(bf16[4,48,384]{2,1,0:T(8,128)(2,1)} %dynamic-slice_bitcast_fusion.15), channel_id=1, source_target_pairs={{0,2},{2,0},{1,3},{3,1},{4,6},{6,4},{5,7},{7,5},{8,10},{10,8},{9,1... | collective-permute-start | bytes 442376 | tf_op jit(solution)/shard_map/ppermute | solution.py:256
  437.5 9.9 %collective-permute-start.39 = (bf16[48,384]{1,0:T(8,128)(2,1)S(1)}, bf16[48,384]{1,0:T(8,128)(2,1)S(1)}, u32[]{:S(2)}, u32[]{:S(2)}) collective-permute-start(bf16[48,384]{1,0:T(8,128)(2,1)S(1)} %get-tuple-element.120), channel_id=1, source_target_pairs={{0,8},{4,12},{8,0},{12,4},{16,24},{20,28},{24,16},{28,20},{1,9},{5... | collective-permute-start | bytes 110600 | tf_op jit(solution)/shard_map/ppermute | solution.py:285
  437.5 9.8 %collective-permute-start.40 = (bf16[48,384]{1,0:T(8,128)(2,1)S(1)}, bf16[48,384]{1,0:T(8,128)(2,1)S(1)}, u32[]{:S(2)}, u32[]{:S(2)}) collective-permute-start(bf16[48,384]{1,0:T(8,128)(2,1)S(1)} %get-tuple-element.122), channel_id=1, source_target_pairs={{0,16},{4,20},{8,24},{12,28},{16,0},{20,4},{24,8},{28,12},{1,17},{... | collective-permute-start | bytes 110600 | tf_op jit(solution)/shard_map/ppermute | solution.py:285
  439.9 7.5 %collective-permute-start.41 = (bf16[48,384]{1,0:T(8,128)(2,1)S(1)}, bf16[48,384]{1,0:T(8,128)(2,1)S(1)}, u32[]{:S(2)}, u32[]{:S(2)}) collective-permute-start(bf16[48,384]{1,0:T(8,128)(2,1)S(1)} %get-tuple-element.121), channel_id=1, source_target_pairs={{0,24},{4,28},{8,16},{12,20},{16,8},{20,12},{24,0},{28,4},{1,25},{... | collective-permute-start | bytes 110600 | tf_op jit(solution)/shard_map/ppermute | solution.py:285
  449.0 10.2 %collective-permute-start.47 = (bf16[24,1280]{1,0:T(8,128)(2,1)S(1)}, bf16[24,1280]{1,0:T(8,128)(2,1)S(1)}, u32[]{:S(2)}, u32[]{:S(2)}) collective-permute-start(bf16[24,1280]{1,0:T(8,128)(2,1)S(1)} %constant_dynamic-slice_fusion), channel_id=1, source_target_pairs={{0,1},{1,0},{2,3},{3,2},{4,5},{5,4},{6,7},{7,6},{8,9},{9,8},{10,11... | collective-permute-start | bytes 184328 | tf_op jit(solution)/shard_map/ppermute | solution.py:256
  458.5 20.0 %collective-permute-start.26 = (bf16[512,768]{1,0:T(8,128)(2,1)S(1)}, bf16[512,768]{1,0:T(8,128)(2,1)S(1)}, u32[]{:S(2)}, u32[]{:S(2)}) collective-permute-start(bf16[512,768]{1,0:T(8,128)(2,1)S(1)} %dynamic-slice_bitcast_fusion.1), channel_id=1, source_target_pairs={{0,2},{2,0},{1,3},{3,1},{4,6},{6,4},{5,7},{7,5},{8,10},{10,8},{9,1... | collective-permute-start | bytes 2359304 | tf_op jit(solution)/shard_map/ppermute | solution.py:256
  460.3 20.8 %copy-start.1 = (s32[2,2048]{1,0:T(2,128)S(1)}, s32[2,2048]{1,0:T(2,128)}, u32[]{:S(2)}) copy-start(s32[2,2048]{1,0:T(2,128)} %param.18) | copy-start | bytes 49156
  (47 other events, 257.8 us)
Sparse Core Ops, SparseCore 0:
  15.0 108.3 all-gather.1

commit v3 on v2

--- a/solution.py
+++ b/solution.py
@@ -44,7 +44,9 @@
     return jnp.where(key_at <= query_at, scores, NEG)
 
 
-def attention_forward_kernel(qkv_ref, qs_ref, ks_ref, o_ref, lse_ref, qx, kx, vt, acc):
+def attention_forward_kernel(qkv_ref, qs_ref, ks_ref, *rest):
+    o_ref, lse_ref, tick_ref, qx, kx, vt, acc = rest[-7:]
+    tick_ref[...] = jnp.zeros_like(tick_ref)
     length = qkv_ref.shape[0]
     blocks = length // BLK
 
@@ -91,7 +93,8 @@
 
 
 def attention_backward_kernel(qkv_ref, qs_ref, ks_ref, o_ref, do_ref, lse_ref, *rest):
-    d_ref, qx, kx, qm, dm, kt, delta, dqt, dk, dv = rest[-10:]
+    d_ref, tick_ref, qx, kx, qm, dm, kt, delta, dqt, dk, dv = rest[-11:]
+    tick_ref[...] = jnp.zeros_like(tick_ref)
     length = qkv_ref.shape[0]
     blocks = length // BLK
 
@@ -154,25 +157,118 @@
 VMEM_LIMIT = 48 * 1024 * 1024
 
 
-def attention_forward(qkv, query_code, key_code):
-    length, width = qkv.shape
-    pairs = width // (3 * PAIR)
-    tiles = pairs * 2 * length * length
+SMALL_COST = pl.CostEstimate(flops=10**8, bytes_accessed=10**6, transcendentals=0)
+
+
+TICK = jax.ShapeDtypeStruct((8, 128), F32)
+TICK_SPEC = pl.BlockSpec((8, 128), lambda i: (0, 0))
+ANY_SPEC = pl.BlockSpec(memory_space=pl.ANY)
+
+
+def gate_kernel(*refs):
+    refs[-1][...] = jnp.zeros_like(refs[-1])
+
+
+def gate(after):
+    return pl.pallas_call(
+        gate_kernel,
+        grid=(1,),
+        in_specs=[ANY_SPEC] * len(after),
+        out_specs=TICK_SPEC,
+        out_shape=TICK,
+        cost_estimate=SMALL_COST,
+    )(*after)
+
+
+def qkv_kernel(x_ref, w_ref, vec_ref, col_ref, a_ref, qkv_ref, tick_ref):
+    normal, _ = norm_forward(x_ref[...].astype(F32))
+    normed = (normal * vec_ref[0:1, :] + vec_ref[1:2, :]).astype(BF16)
+    a_ref[...] = normed
+    qkv_ref[...] = ((mm(normed, w_ref[...]) + col_ref[0:1, :]) * col_ref[1:2, :]).astype(BF16)
+    tick_ref[...] = jnp.zeros_like(tick_ref)
+
+
+def qkv_projection(inputs, weight, vectors, columns):
+    length, width = inputs.shape
+    cols = weight.shape[1]
+    return pl.pallas_call(
+        qkv_kernel,
+        grid=(length // ROWS,),
+        in_specs=[
+            pl.BlockSpec((ROWS, width), lambda i: (i, 0)),
+            pl.BlockSpec((width, cols), lambda i: (0, 0)),
+            pl.BlockSpec(vectors.shape, lambda i: (0, 0)),
+            pl.BlockSpec(columns.shape, lambda i: (0, 0)),
+        ],
+        out_specs=[
+            pl.BlockSpec((ROWS, width), lambda i: (i, 0)),
+            pl.BlockSpec((ROWS, cols), lambda i: (i, 0)),
+            TICK_SPEC,
+        ],
+        out_shape=[
+            jax.ShapeDtypeStruct((length, width), BF16),
+            jax.ShapeDtypeStruct((length, cols), BF16),
+            TICK,
+        ],
+        compiler_params=pltpu.CompilerParams(vmem_limit_bytes=VMEM_LIMIT),
+        cost_estimate=SMALL_COST,
+    )(inputs, weight, vectors, columns)
+
+
+ROWS = 256
+
+
+def norm_one_input_kernel(core_ref, mine_ref, come_ref, x_ref, mid_ref, vec_ref, out_ref, tick_ref):
+    grad = (mine_ref[...].astype(F32) + come_ref[...].astype(F32)) * vec_ref[0:1, :]
+    normal, scale = norm_forward(x_ref[...].astype(F32))
+    out_ref[...] = (mid_ref[...] + norm_backward(normal, scale, grad)).astype(BF16)
+    tick_ref[...] = jnp.zeros_like(tick_ref)
+
+
+def norm_one_input(core, partial, come, inputs, grad_middle, vectors):
+    length, width = inputs.shape
+    count = come.shape[0] // ROWS
+    per = count // 2
+
+    def own_block(i, core_ref):
+        return ((i // per) * 2 + core_ref[0]) * per + i % per, 0
+
+    own = pl.BlockSpec((ROWS, width), own_block)
+    plain = pl.BlockSpec((ROWS, width), lambda i, core_ref: (i, 0))
+    return pl.pallas_call(
+        norm_one_input_kernel,
+        grid_spec=pltpu.PrefetchScalarGridSpec(
+            num_scalar_prefetch=1,
+            grid=(count,),
+            in_specs=[own, plain, own, own, pl.BlockSpec(vectors.shape, lambda i, core_ref: (0, 0))],
+            out_specs=[plain, pl.BlockSpec((8, 128), lambda i, core_ref: (0, 0))],
+        ),
+        out_shape=[jax.ShapeDtypeStruct((count * ROWS, width), BF16), TICK],
+        compiler_params=pltpu.CompilerParams(vmem_limit_bytes=VMEM_LIMIT),
+        cost_estimate=SMALL_COST,
+    )(core.reshape(1).astype(jnp.int32), partial, come, inputs, grad_middle, vectors)
+
+
+def attention_forward(pair, qkv, query_code, key_code, after):
+    length = qkv.shape[0]
     return pl.pallas_call(
         attention_forward_kernel,
-        grid=(pairs,),
+        grid=(1,),
         in_specs=[
-            pl.BlockSpec((length, 3 * PAIR), lambda p: (0, p)),
+            pl.BlockSpec((length, 3 * PAIR), lambda p: (0, pair)),
             pl.BlockSpec((length, PAIR), lambda p: (0, 0)),
             pl.BlockSpec((length, PAIR), lambda p: (0, 0)),
-        ],
+        ]
+        + [pl.BlockSpec(memory_space=pl.ANY)] * len(after),
         out_specs=[
-            pl.BlockSpec((length, PAIR), lambda p: (0, p)),
-            pl.BlockSpec((1, 8, length), lambda p: (p, 0, 0)),
+            pl.BlockSpec((length, PAIR), lambda p: (0, 0)),
+            pl.BlockSpec((1, 8, length), lambda p: (0, 0, 0)),
+            TICK_SPEC,
         ],
         out_shape=[
-            jax.ShapeDtypeStruct((length, pairs * PAIR), BF16),
-            jax.ShapeDtypeStruct((pairs, 8, length), F32),
+            jax.ShapeDtypeStruct((length, PAIR), BF16),
+            jax.ShapeDtypeStruct((1, 8, length), F32),
+            TICK,
         ],
         scratch_shapes=[
             pltpu.VMEM((2, length, PAIR), BF16),
@@ -181,15 +277,64 @@
             pltpu.VMEM((2, HEAD_DIM + 16, BLK), F32),
         ],
         compiler_params=pltpu.CompilerParams(vmem_limit_bytes=VMEM_LIMIT),
-        cost_estimate=pl.CostEstimate(
-            flops=tiles * 1024, bytes_accessed=length * width * 3, transcendentals=tiles // 2
-        ),
-    )(qkv, query_code, key_code)
+        cost_estimate=SMALL_COST,
+    )(qkv, query_code, key_code, *after)
+
+
+def norm_one_grad_kernel(d0_ref, d1_ref, d2_ref, w_ref, x_ref, *rest):
+    out_ref, sums_ref, bias_ref, tick_ref = rest[-4:]
+
+    @pl.when(pl.program_id(0) == 0)
+    def _():
+        sums_ref[...] = jnp.zeros_like(sums_ref)
+        bias_ref[...] = jnp.zeros_like(bias_ref)
+        tick_ref[...] = jnp.zeros_like(tick_ref)
+
+    total = None
+    for i, ref in enumerate((d0_ref, d1_ref, d2_ref)):
+        cols = slice(i * 3 * PAIR, (i + 1) * 3 * PAIR)
+        grad = ref[...]
+        part = mm(grad, w_ref[:, cols], NT)
+        total = part if i == 0 else total + part
+        bias_ref[0:1, cols] += jnp.sum(grad.astype(F32), axis=0, keepdims=True)
+    normal, _ = norm_forward(x_ref[...].astype(F32))
+    sums_ref[0:1, :] += jnp.sum(total * normal, axis=0, keepdims=True)
+    sums_ref[1:2, :] += jnp.sum(total, axis=0, keepdims=True)
+    out_ref[...] = total.astype(BF16)
+
+
+def norm_one_grad(grads, weight, inputs, after):
+    length, width = inputs.shape
+    cols = weight.shape[1]
+    block = pl.BlockSpec((ROWS, 3 * PAIR), lambda i: (i, 0))
+    return pl.pallas_call(
+        norm_one_grad_kernel,
+        grid=(length // ROWS,),
+        in_specs=[block] * 3
+        + [
+            pl.BlockSpec((width, cols), lambda i: (0, 0)),
+            pl.BlockSpec((ROWS, width), lambda i: (i, 0)),
+        ]
+        + [pl.BlockSpec(memory_space=pl.ANY)] * len(after),
+        out_specs=[
+            pl.BlockSpec((ROWS, width), lambda i: (i, 0)),
+            pl.BlockSpec((8, width), lambda i: (0, 0)),
+            pl.BlockSpec((8, cols), lambda i: (0, 0)),
+            TICK_SPEC,
+        ],
+        out_shape=[
+            jax.ShapeDtypeStruct((length, width), BF16),
+            jax.ShapeDtypeStruct((8, width), F32),
+            jax.ShapeDtypeStruct((8, cols), F32),
+            TICK,
+        ],
+        compiler_params=pltpu.CompilerParams(vmem_limit_bytes=VMEM_LIMIT),
+        cost_estimate=SMALL_COST,
+    )(*grads, weight, inputs, *after)
 
 
 def attention_backward(pair, qkv, query_code, key_code, attended, grad_attended, log_total, after):
     length = qkv.shape[0]
-    tiles = 2 * length * length
     return pl.pallas_call(
         attention_backward_kernel,
         grid=(1,),
@@ -197,13 +342,13 @@
             pl.BlockSpec((length, 3 * PAIR), lambda p: (0, pair)),
             pl.BlockSpec((length, PAIR), lambda p: (0, 0)),
             pl.BlockSpec((length, PAIR), lambda p: (0, 0)),
+            pl.BlockSpec((length, PAIR), lambda p: (0, 0)),
             pl.BlockSpec((length, PAIR), lambda p: (0, pair)),
-            pl.BlockSpec((length, PAIR), lambda p: (0, pair)),
-            pl.BlockSpec((1, 8, length), lambda p: (pair, 0, 0)),
+            pl.BlockSpec((1, 8, length), lambda p: (0, 0, 0)),
         ]
         + [pl.BlockSpec(memory_space=pl.ANY)] * len(after),
-        out_specs=pl.BlockSpec((length, 3 * PAIR), lambda p: (0, 0)),
-        out_shape=jax.ShapeDtypeStruct((length, 3 * PAIR), BF16),
+        out_specs=[pl.BlockSpec((length, 3 * PAIR), lambda p: (0, 0)), TICK_SPEC],
+        out_shape=[jax.ShapeDtypeStruct((length, 3 * PAIR), BF16), TICK],
         scratch_shapes=[
             pltpu.VMEM((2, length, PAIR), BF16),
             pltpu.VMEM((2, length, PAIR), BF16),
@@ -216,9 +361,7 @@
             pltpu.VMEM((BLK, PAIR), F32),
         ],
         compiler_params=pltpu.CompilerParams(vmem_limit_bytes=VMEM_LIMIT),
-        cost_estimate=pl.CostEstimate(
-            flops=tiles * 2560, bytes_accessed=length * PAIR * 24, transcendentals=tiles // 2
-        ),
+        cost_estimate=SMALL_COST,
     )(qkv, query_code, key_code, attended, grad_attended, log_total, *after)
 
 
@@ -287,16 +430,18 @@
     def place(self, d):
         return self.side if d == "x" else self.groups[d][2]
 
-    def reduce(self, state, d):
+    def reduce(self, state, d, tick=None):
         array, dims = state
         axis, at = dims.index(d), self.place(d)
         total = lax.dynamic_index_in_dim(array, at, axis, keepdims=False).astype(F32)
         for mask in range(1, array.shape[axis]):
             block = lax.dynamic_index_in_dim(array, at ^ mask, axis, keepdims=False)
             total = total + self.send(block, d, mask).astype(F32)
+        if tick is not None:
+            total = total + tick[0, 0]
         return total.astype(BF16), [other for other in dims if other != d]
 
-    def gather(self, state, d):
+    def gather(self, state, d, tick=None):
         array, dims = state
         parts = [array] + [self.send(array, d, mask) for mask in range(1, self.counts([d])[0])]
         for bit in range(len(parts).bit_length() - 1):
@@ -306,7 +451,10 @@
                     high = low | (1 << bit)
                     parts[low], parts[high] = pick(flag, parts[low], parts[high])
         dims = [other for other in self.dims if other in dims or other == d]
-        return jnp.stack(parts, axis=dims.index(d)), dims
+        joined = jnp.stack(parts, axis=dims.index(d))
+        if tick is not None:
+            joined = joined + tick[0, 0].astype(joined.dtype)
+        return joined, dims
 
     def rows(self, array, lead=()):
         shape = list(lead) + self.counts(self.dims)
@@ -352,14 +500,17 @@
     def at_index(array, index):
         return lax.dynamic_index_in_dim(array, index, 0, keepdims=False)
 
-    def to_sequence(array):
+    def to_sequence(array, tick=None):
         kept = at_index(array, side)
-        come = swap(at_index(array, 1 - side), "xx")
+        sent = at_index(array, 1 - side)
+        if tick is not None:
+            sent = sent + tick[0, 0].astype(sent.dtype)
+        come = swap(sent, "xx")
         low, high = pick(side, kept, come)
         mine = jnp.stack([low, high])
         other = swap(mine, "core")
         even, odd = pick(core, mine, other)
-        return jnp.stack([even, odd], axis=1).reshape(length, width)
+        return jnp.stack([even, odd], axis=1).reshape(length, width), come
 
     def own_rows(array):
         return lax.dynamic_index_in_dim(
@@ -374,7 +525,7 @@
     def from_sequence(mine):
         come = swap(at_index(mine, 1 - side), "xx")
         first, second = pick(side, at_index(mine, side), come)
-        return jnp.stack([first, second])
+        return jnp.stack([first, second]), come
 
     qkv_cols = qkv_weight.reshape(own, 3, 2, pairs, PAIR).transpose(2, 0, 3, 1, 4).reshape(2, own, cols)
     up_cols = (
@@ -403,38 +554,41 @@
         ],
         axis=1,
     )
+    links = Links()
+
+    def gather_rest(array, tick=None):
+        state = (array, [])
+        for d in links.rest:
+            state = links.gather(state, d, tick if d == links.rest[-1] else None)
+        return state
+
+    def halves_of(state):
+        middle = state[0].shape[-1] // 2
+        return [(state[0][..., :middle], state[1]), (state[0][..., middle:], state[1])]
+
+    def joined(halves):
+        return [half_state[0].reshape(width, -1) for half_state in halves]
+
+    inputs_low, come = to_sequence(tokens)
+    grad_out_low, _ = to_sequence(cotangent, gate([come]))
+    early_halves = [
+        links.gather(links.gather(piece, order[0]), order[1])
+        for piece, order in zip(halves_of(gather_rest(early)), ("yx", "xy"))
+    ]
+    early = jnp.concatenate(joined(early_halves), axis=1)
     late = with_partner(
         jnp.concatenate([up_cols, jnp.broadcast_to(out_weight, (2, own, width))], axis=2)
     )
     down_own = down_weight.reshape(splits, pair_row, width)
     late = jnp.concatenate([late] + [down_own[i] for i in range(splits)], axis=1)
-    links = Links()
-    state = (early, [])
-    for d in links.rest:
-        state = links.gather(state, d)
-    middle_col = early.shape[1] // 2
-    halves = []
-    for order, part in (("yx", slice(0, middle_col)), ("xy", slice(middle_col, None))):
-        piece = (state[0][..., part], state[1])
-        for d in order:
-            piece = links.gather(piece, d)
-        halves.append(piece[0].reshape(width, middle_col))
-    early = jnp.concatenate(halves, axis=1)
-    late = lax.all_gather(late, ("dp", "xx"), axis=0, tiled=True)
     proj_qkv = early[:, :cols]
     small = early[:, cols:].astype(F32).T
     gain_one, shift_one, query_shift, value_shift, out_shift, gain_two, shift_two, down_shift = (
         small[i] for i in range(8)
     )
     up_shift = small[8 : 8 + splits].reshape(hidden)
-    proj_up = late[:, :hidden]
-    proj_out = lax.dynamic_slice_in_dim(late[:, hidden : hidden + width], core * half, half, 0)
-    proj_down = jnp.concatenate(
-        [late[:, hidden + (1 + i) * width : hidden + (2 + i) * width] for i in range(splits)], axis=0
-    )
-
-    inputs = to_sequence(tokens).astype(F32)
-    grad_out_low = to_sequence(cotangent)
+
+    inputs = inputs_low.astype(F32)
     seg = at_index(segments, side)
     numbers = jnp.arange(PAIR, dtype=jnp.int32) % HEAD_DIM
     same = seg[:, None] == numbers[None, :]
@@ -442,9 +596,6 @@
     query_code = jnp.where(same & coded, 1.0, 0.0).astype(BF16)
     key_code = jnp.where(same | ~coded, 0.0, NEG).astype(BF16)
 
-    normal_one, scale_one = norm_forward(inputs)
-    normed_low = (normal_one * gain_one + shift_one).astype(BF16)
-
     def head_cols(vector):
         return lax.dynamic_slice_in_dim(vector, core * half, half, 0).reshape(pairs, 1, PAIR)
 
@@ -453,8 +604,34 @@
         [head_cols(query_shift), zeros, head_cols(value_shift)], axis=1
     ).reshape(1, cols)
     qkv_scale = jnp.tile(jnp.repeat(jnp.array([0.125, 1.0, 1.0], F32), PAIR), pairs)[None]
-    qkv = ((mm(normed_low, proj_qkv) + qkv_shift) * qkv_scale).astype(BF16)
-    attended, log_total = attention_forward(qkv, query_code, key_code)
+    normed_low, qkv, tick = qkv_projection(
+        inputs_low,
+        proj_qkv,
+        jnp.pad(jnp.stack([gain_one, shift_one]), ((0, 6), (0, 0))),
+        jnp.pad(jnp.concatenate([qkv_shift, qkv_scale]), ((0, 6), (0, 0))),
+    )
+    attended_pairs, log_totals = [], []
+    late_halves = halves_of(gather_rest(late, tick))
+    for pair in range(pairs):
+        if pair == 0:
+            after = [piece[0] for piece in late_halves]
+        else:
+            after = [attended_pairs[-1]]
+        if pair == 1:
+            late_halves = [links.gather(piece, d, tick) for piece, d in zip(late_halves, "xy")]
+            after += [piece[0] for piece in late_halves]
+        one_pair = attention_forward(pair, qkv, query_code, key_code, after)
+        attended_pairs.append(one_pair[0])
+        log_totals.append(one_pair[1])
+        tick = one_pair[2]
+    attended = jnp.concatenate(attended_pairs, axis=1)
+    late_halves = joined([links.gather(piece, d, tick) for piece, d in zip(late_halves, "yx")])
+    late = jnp.concatenate(late_halves, axis=1)
+    proj_up = late[:, :hidden]
+    proj_out = lax.dynamic_slice_in_dim(late[:, hidden : hidden + width], core * half, half, 0)
+    proj_down = jnp.concatenate(
+        [late[:, hidden + (1 + i) * width : hidden + (2 + i) * width] for i in range(splits)], axis=0
+    )
 
     branch = mm(attended, proj_out).astype(BF16)
     middle = inputs + (branch.astype(F32) + swap(branch, "core").astype(F32)) + out_shift
@@ -464,7 +641,7 @@
     hidden_low = hidden_value.astype(BF16)
     ffn = mm(hidden_low, proj_down)
     ffn_own = own_rows(ffn) + swap(other_rows(ffn).astype(BF16), "core").astype(F32)
-    mixed = from_sequence((own_rows(middle) + ffn_own + down_shift).astype(BF16))
+    mixed, _ = from_sequence((own_rows(middle) + ffn_own + down_shift).astype(BF16))
 
     grad_mixed = grad_out_low.astype(F32)
     grad_hidden = mm(grad_out_low, proj_down, NT)
@@ -503,64 +680,52 @@
         jnp.concatenate([part.astype(BF16) for part in grad_proj_down], axis=0), (splits,)
     )
     up_piece = links.rows(grad_proj_up.astype(BF16))
-    out_piece = (
-        grad_proj_out.astype(BF16).reshape(chips // 8, 2, 2, pair_row, width),
-        ["rest", "y", "x"],
-    )
-
-    def reduce_rest(piece):
+    out_low = grad_proj_out.astype(BF16)
+    grad_out_rows = jnp.concatenate(
+        [only_mine(core == 0, out_low), only_mine(core == 1, out_low)], axis=0
+    )
+
+    def reduce_rest(piece, tick=None):
         for d in links.rest:
-            piece = links.reduce(piece, d)
+            piece = links.reduce(piece, d, tick if d == links.rest[0] else None)
         return piece
 
-    def pair_backward(pair, after):
-        grad = attention_backward(
-            pair, qkv, query_code, key_code, attended, grad_attended, log_total, after
+    grads, weight_grads, tick = [], [grad_out_rows], None
+    after = [mixed]
+    for pair in range(pairs):
+        grad, tick = attention_backward(
+            pair,
+            qkv,
+            query_code,
+            key_code,
+            attended_pairs[pair],
+            grad_attended,
+            log_totals[pair],
+            after + grads[-1:],
         )
-        return grad, links.rows(mm(normed_low, grad, TN).astype(BF16))
-
-    down_piece = links.reduce(down_piece, "x")
-    grads, pieces = [], []
-    for pair in range(pairs):
+        grads.append(grad)
         if pair == 0:
-            after = [down_piece[0], mixed]
+            down_piece = links.reduce(down_piece, "x", tick)
+            up_piece = links.reduce(up_piece, "y", tick)
+            after = [down_piece[0], up_piece[0]]
         elif pair == 1:
-            down_piece = links.reduce(down_piece, "y")
-            up_piece = links.reduce(up_piece, "y")
+            down_piece = links.reduce(down_piece, "y", tick)
+            up_piece = links.reduce(up_piece, "x", tick)
             after = [down_piece[0], up_piece[0]]
-        else:
-            down_piece = reduce_rest(down_piece)
-            up_piece = links.reduce(up_piece, "x")
-            out_piece = links.reduce(out_piece, "x")
-            after = [down_piece[0], up_piece[0], out_piece[0]]
-        grad, piece = pair_backward(pair, after)
-        grads.append(grad)
-        pieces.append(piece)
-    grad_qkv = jnp.concatenate(grads, axis=1)
-    up_piece = reduce_rest(up_piece)
-    out_part = links.reduce(out_piece, "y")[0]
-    empty = jnp.zeros_like(out_part)
-    out_part = jnp.concatenate(pick(core, out_part, empty), axis=0)
-    out_piece = reduce_rest(
-        (out_part.reshape(links.counts(links.rest) + [pair_row, width]), links.rest)
-    )
-    qkv_own = jnp.concatenate(
-        [
-            reduce_rest(links.reduce(links.reduce(piece, order[0]), order[1]))[0]
-            for piece, order in zip(pieces, ("yx", "xy", "yx"))
-        ],
-        axis=1,
-    )
-    partial_one_wide = mm(grad_qkv, proj_qkv, NT)
-    partial_one = partial_one_wide.astype(BF16)
-    grad_normed = own_rows(partial_one).astype(F32) + swap(other_rows(partial_one), "core").astype(F32)
-    normal_own, scale_own = norm_forward(own_rows(inputs))
-    token_grad = from_sequence(
-        (
-            own_rows(grad_middle) + norm_backward(normal_own, scale_own, grad_normed * gain_one)
-        ).astype(BF16)
-    )
-    grad_by_pair = jnp.sum(grad_qkv.astype(F32), axis=0).reshape(pairs, 3, PAIR)
+        if pair < pairs - 1:
+            weight_grads.append(mm(normed_low, grad, TN).astype(BF16))
+    first_piece = links.rows(jnp.concatenate(weight_grads, axis=1))
+    partial_one, norm_sums, bias_sums, tick = norm_one_grad(grads, proj_qkv, inputs_low, [])
+    first_piece = links.reduce(first_piece, "x", tick)
+    come = swap(other_rows(partial_one), "core").reshape(2 * quarter, width)
+    norm_vectors = jnp.pad(jnp.stack([gain_one, shift_one]), ((0, 6), (0, 0)))
+    token_own, tick = norm_one_input(
+        core, partial_one, come, inputs_low, grad_middle, norm_vectors
+    )
+    down_piece = reduce_rest(down_piece, tick)
+    up_piece = reduce_rest(up_piece, tick)
+    token_grad, come = from_sequence(token_own.reshape(2, quarter, width))
+    grad_by_pair = bias_sums[0].reshape(pairs, 3, PAIR)
 
     def padded(vector):
         vector = vector.reshape(half)
@@ -568,14 +733,19 @@
 
     small = as_column(
         [
-            jnp.sum(partial_one_wide * normal_one, axis=0),
-            jnp.sum(partial_one_wide, axis=0),
+            norm_sums[0],
+            norm_sums[1],
             padded(grad_by_pair[:, 0]),
             padded(grad_by_pair[:, 2]),
         ]
         + small_two
     )
-    small_own = reduce_rest(links.reduce(links.reduce(links.rows(small.astype(BF16)), "y"), "x"))[0]
+    last_piece = links.rows(
+        jnp.concatenate([mm(normed_low, grads[-1], TN).astype(BF16), small.astype(BF16)], axis=1)
+    )
+    last_piece = links.reduce(links.reduce(last_piece, "y", tick), "x")
+    last_own = reduce_rest(last_piece, gate([come]))[0]
+    first_own = reduce_rest(links.reduce(first_piece, "y", tick))[0]
 
     def rows_of(array, index):
         return lax.dynamic_slice_in_dim(array, index * own, own, 0)
@@ -586,27 +756,30 @@
     def shared(array):
         return rows_of(array, core), swap(rows_of(array, 1 - core), "core")
 
-    late_mine, late_come = shared(jnp.concatenate([up_piece[0], out_piece[0]], axis=1))
-    early_mine, early_come = shared(jnp.concatenate([qkv_own, small_own], axis=1))
-    out_grad = late_mine[:, hidden:].astype(F32) + late_come[:, hidden:].astype(F32)
+    late_mine, late_come = shared(up_piece[0])
+    early_mine, early_come = shared(jnp.concatenate([first_own, last_own], axis=1))
+    out_grad = early_mine[:, :width].astype(F32) + early_come[:, :width].astype(F32)
     up_grad = (
-        by_core(late_mine[:, :hidden], late_come[:, :hidden])
+        by_core(late_mine, late_come)
         .reshape(2, own, splits, chips, pair_row)
         .transpose(1, 3, 0, 2, 4)
         .reshape(own, 2 * hidden)
         .astype(F32)
     )
     down_grad = down_piece[0].reshape(hidden_own, width).astype(F32)
-    up_shift_grad = small_own[:, 8 : 8 + splits].T.reshape(hidden_own).astype(F32)
     qkv_grad = (
-        by_core(early_mine[:, :cols], early_come[:, :cols])
+        by_core(early_mine[:, width : width + cols], early_come[:, width : width + cols])
         .reshape(2, own, pairs, 3, PAIR)
         .transpose(1, 3, 0, 2, 4)
         .reshape(own, 2 * cols)
         .astype(F32)
     )
-    small_mine = early_mine[:, cols : cols + 8].astype(F32)
-    one = small_mine[:, :4] + early_come[:, cols : cols + 4].astype(F32)
+    tail = width + cols
+    small_mine = early_mine[:, tail : tail + 8].astype(F32)
+    one = small_mine[:, :4] + early_come[:, tail : tail + 4].astype(F32)
+    up_shift_grad = (
+        last_own[:, cols // pairs + 8 : cols // pairs + 8 + splits].T.reshape(hidden_own).astype(F32)
+    )
     two = small_mine[:, 4:]
     return (
         mixed,

time: 492 us -> 470 us (0.955)
  waiting for transfers between devices: 119 us -> 85 us
  Pallas kernels: 93.6 us -> 125 us
  starting transfers between devices: 66.3 us -> 49.1 us
  between operations: 15.8 us -> 2.71 us
  other arithmetic: 60.3 us -> 71.9 us
  matrix products: 84.3 us -> 73.6 us
  local copies, waits for them, and re-layouts: 49.2 us -> 55.5 us
    ppermute x23 -> x22, waiting for transfers between devices: 70.7 us -> 38.7 us  [swap(): return lax.ppermute(value, axis, [(0, 1), (1, 0)])]
    pallas_call x1 -> x8, Pallas kernels: 37.4 us -> 67.9 us  [the longest x3 40.4 us: attention_forward(): pl.pallas_call(attention_forward_kernel, grid=(1,), in_specs=[pl.BlockSpe...]
    ppermute x33 -> x26, starting transfers between devices: 48 us -> 31.7 us  [send(): return lax.ppermute(value, 'dp', [(i, i ^ move) for i in range(self.size)])]
    dot_general x15 -> x13, matrix products: 84.3 us -> 73.6 us  [mm(): return lax.dot_general(left, right, dims, preferred_element_type=F32)]
    convert_element_type x20 -> x12, other arithmetic: 5.61 us -> 14.9 us  [reduce(): return (total.astype(BF16), [other for other in dims if other != d])]
    add x2 -> x8, other arithmetic: 1.43 us -> 10.3 us  [the longest x5 6.9 us: gather(): joined = joined + tick[0, 0].astype(joined.dtype)]
    convert_element_type x7 -> x4, other arithmetic: 7.22 us -> 0.28 us  [the longest x1 0.11 us: body(): up_grad = by_core(late_mine, late_come).reshape(2, own, splits, chips, pa...]
    slice x1 -> x13, local copies, waits for them, and re-layouts: 0.04 us -> 6.26 us  [the longest x5 3.29 us: reduce(): total = total + tick[0, 0]]
  transfers between devices with their start and end apart: 57 -> 48, of which waited for: 22 -> 18; matrix products, arithmetic and copies ran while one was open for 23% -> 26% of each run, Pallas kernels for 19% -> 25%
where the time goes in v3:
time: 470 us; the launch traced here: 463 us
  Pallas kernels  125 us (27%)
  waiting for transfers between devices  85 us (18%)
  matrix products  73.6 us (16%)
  other arithmetic  71.9 us (15%)
  local copies, waits for them, and re-layouts  55.5 us (12%)
  starting transfers between devices  49.1 us (10%)
    dot_general x13, matrix products, mm(): return lax.dot_general(left, right, dims, preferred_element_type=F32)  73.6 us
    pallas_call x3, Pallas kernels, attention_backward(): pl.pallas_call(attention_backward_kernel, grid=(1,), in_specs=[pl.BlockSp...  57.2 us
    ppermute x26, waiting for transfers between devices, send(): return lax.ppermute(value, 'dp', [(i, i ^ move) for i in range(self.size)])  46.3 us
    pallas_call x3, Pallas kernels, attention_forward(): pl.pallas_call(attention_forward_kernel, grid=(1,), in_specs=[pl.BlockSpe...  40.4 us
    ppermute x22, waiting for transfers between devices, swap(): return lax.ppermute(value, axis, [(0, 1), (1, 0)])  38.7 us
    ppermute x26, starting transfers between devices, send(): return lax.ppermute(value, 'dp', [(i, i ^ move) for i in range(self.size)])  31.7 us
    ppermute x22, starting transfers between devices, swap(): return lax.ppermute(value, axis, [(0, 1), (1, 0)])  17.4 us
    unnamed x160, local copies, waits for them, and re-layouts  15.2 us
  transfers between devices with their start and end apart: 48, of which 18 were waited for; matrix products, arithmetic and copies ran while one was open for 26% of the time, Pallas kernels for 25%

profile of v3, /device:TPU:0, one launch (start us, length us, event | category | flops | bytes accessed | tf_op | source)
XLA Modules:
  0.0 462.9 jit_solution(14689213380108684744)
XLA Ops:
  6.1 3.0 collective-permute-start
  11.6 3.7 collective-permute-start.5
  16.1 3.6 collective-permute-done.5
  19.7 5.8 %collective-permute-done.4 = bf16[48,1280]{1,0:T(8,128)(2,1)S(1)} collective-permute-done((bf16[48,1280]{1,0:T(8,128)(2,1)S(1)}, bf16[48,1280]{1,0:T(8,128)(2,1)S(1)}, u32[]{:S(2)}, u32[]{:S(2)}) %collective-permute-start.4) | collective-permute-done | bytes 122912 | tf_op jit(solution)/shard_map/ppermute | solution.py:428
  25.7 1.6 collective-permute-start.6
  28.1 2.4 collective-permute-start.13
  30.5 2.3 collective-permute-done.6
  34.9 18.6 %collective-permute-done.12 = bf16[48,3840]{1,0:T(8,128)(2,1)S(1)} collective-permute-done((bf16[48,3840]{1,0:T(8,128)(2,1)S(1)}, bf16[48,3840]{1,0:T(8,128)(2,1)S(1)}, u32[]{:S(2)}, u32[]{:S(2)}) %collective-permute-start.12) | collective-permute-done | bytes 368672 | tf_op jit(solution)/shard_map/ppermute | solution.py:428
  54.9 2.3 collective-permute-done.11
  61.0 5.5 %collective-permute-done.7 = bf16[4,2,48,640]{3,2,0,1:T(8,128)(2,1)S(1)} collective-permute-done((bf16[4,2,48,640]{3,2,0,1:T(8,128)(2,1)S(1)}, bf16[4,2,48,640]{3,2,0,1:T(8,128)(2,1)S(1)}, u32[]{:S(2)}, u32[]{:S(2)}) %collective-permute-start.7) | collective-permute-done | bytes 491552 | tf_op jit(solution)/shard_map/ppermute | solution.py:399
  67.6 1.7 copy.125
  74.9 2.3 select_bitcast_fusion.1
  77.5 1.8 copy.90
  79.3 10.4 %shard_map.280 = (bf16[2048,768]{1,0:T(8,128)(2,1)S(1)}, bf16[2048,1152]{1,0:T(8,128)(2,1)}, f32[8,128]{1,0:T(8,128)S(1)}) custom-call(bf16[2048,768]{1,0:T(8,128)(2,1)} %bitcast.320, bf16[768,1152]{1,0:T(8,128)(2,1)S(1)} %pad_maximum_fusion.5.w_ref, f32[8,768]{1,0:T(8,128)S(1)} %slice_select_fusion.vec_ref, f32[8,1152]{1,0:T(8,128)S(1)} %select_maximum_fusion.col_ref), custom_call_target="tpu_custom_call" | custom-call | flops 100000000 | bytes 1000000 | tf_op jit(solution)/shard_map/pallas_call | solution.py:194
  94.1 13.3 %shard_map.281 = (bf16[2048,128]{1,0:T(8,128)(2,1)S(1)}, f32[1,8,2048]{2,1,0:T(8,128)S(1)}, f32[8,128]{1,0:T(8,128)S(1)}) custom-call(bf16[2048,1152]{1,0:T(8,128)(2,1)} %get-tuple-element.37.qkv_ref, bf16[2048,128]{1,0:T(8,128)(2,1)S(1)} %get-tuple-element.165.qs_ref, bf16[2048,128]{1,0:T(8,128)(2,1)S(1)} %get-tuple-element.164.ks_ref, ...), custom_call_target="tpu_custom_call" | custom-call | flops 100000000 | bytes 1000000 | tf_op jit(solution)/shard_map/pallas_call | solution.py:254
  111.2 1.9 maximum_add_fusion.3
  116.4 2.7 add_bitcast_fusion
  120.6 2.0 copy_add_fusion.rest_2_
  124.8 13.7 %shard_map.282 = (bf16[2048,128]{1,0:T(8,128)(2,1)S(1)}, f32[1,8,2048]{2,1,0:T(8,128)S(1)}, f32[8,128]{1,0:T(8,128)}) custom-call(bf16[2048,1152]{1,0:T(8,128)(2,1)} %get-tuple-element.37.qkv_ref, bf16[2048,128]{1,0:T(8,128)(2,1)S(1)} %get-tuple-element.165.qs_ref, bf16[2048,128]{1,0:T(8,128)(2,1)S(1)} %get-tuple-element.164.ks_ref, ...), custom_call_target="tpu_custom_call" | custom-call | flops 100000000 | bytes 1000000 | tf_op jit(solution)/shard_map/pallas_call | solution.py:254
  138.6 13.4 %shard_map.283 = (bf16[2048,128]{1,0:T(8,128)(2,1)S(1)}, f32[1,8,2048]{2,1,0:T(8,128)S(1)}, f32[8,128]{1,0:T(8,128)S(1)}) custom-call(bf16[2048,1152]{1,0:T(8,128)(2,1)} %get-tuple-element.37.qkv_ref, bf16[2048,128]{1,0:T(8,128)(2,1)S(1)} %get-tuple-element.165.qs_ref, bf16[2048,128]{1,0:T(8,128)(2,1)S(1)} %get-tuple-element.164.ks_ref, ...), custom_call_target="tpu_custom_call" | custom-call | flops 100000000 | bytes 1000000 | tf_op jit(solution)/shard_map/pallas_call | solution.py:254
  153.6 2.4 select_bitcast_fusion.5
  157.2 10.9 %collective-permute-done.17 = bf16[4,2,48,1920]{3,2,1,0:T(8,128)(2,1)} collective-permute-done((bf16[4,2,48,1920]{3,2,1,0:T(8,128)(2,1)S(1)}, bf16[4,2,48,1920]{3,2,1,0:T(8,128)(2,1)}, u32[]{:S(2)}, u32[]{:S(2)}) %collective-permute-start.17) | collective-permute-done | bytes 1474592 | tf_op jit(solution)/shard_map/ppermute | solution.py:399
  168.1 2.6 select_bitcast_fusion.3
  172.0 3.5 convolution_convert_fusion.1
  178.3 5.4 %collective-permute-done.22 = bf16[2,512,768]{2,1,0:T(8,128)(2,1)} collective-permute-done((bf16[2,512,768]{2,1,0:T(8,128)(2,1)}, bf16[2,512,768]{2,1,0:T(8,128)(2,1)}, u32[]{:S(2)}, u32[]{:S(2)}) %collective-permute-start.22) | collective-permute-done | bytes 1572896 | tf_op jit(solution)/shard_map/ppermute | solution.py:399
  183.7 2.4 fusion.47
  186.7 1.6 copy-done.25
  189.5 2.3 copy-done.23
  191.7 4.3 fusion.93
  197.9 11.7 %multiply_convert_fusion.1 = (bf16[2048,1536]{1,0:T(8,128)(2,1)}, f32[2048,1536]{1,0:T(8,128)}) fusion(f32[1536]{0:T(1024)S(1)} %add.405, bf16[768,1920]{1,0:T(8,128)(2,1)S(1)} %bitcast.327, f32[2048,768]{1,0:T(8,128)S(1)} %get-tuple-element.82, f32[768]{0:T(1024)S(1)} %copy-done.68, f32[768]{0:T(1024)S(1)} %copy-done.62, f32[2048]{0:T(1024)S(1)} %add_rsqrt_fusion, ...), kind=kOutput, calls=%fused_computation.1 | convolution fusion | flops 4871159808 | bytes 27557888 | tf_op jit(solution)/shard_map/dot_general | solution.py:24
  209.7 4.8 %fusion.24 = bf16[768,768]{1,0:T(8,128)(2,1)S(1)} fusion(bf16[2048,768]{1,0:T(8,128)(2,1)S(1)} %bitcast.330, bf16[2048,1536]{1,0:T(8,128)(2,1)} %get-tuple-element.172), kind=kOutput, calls=%fused_computation.62 | convolution fusion | flops 2416508928 | bytes 7471104 | tf_op jit(solution)/shard_map/dot_general | solution.py:24
  214.5 6.8 %fusion.27 = f32[2048,768]{1,0:T(8,128)} fusion(bf16[2048,1536]{1,0:T(8,128)(2,1)S(1)} %copy-done.74, bf16[768,768]{1,0:T(8,128)(2,1)S(1)} %copy-done.58, bf16[768,768]{1,0:T(8,128)(2,1)S(1)} %get-tuple-element.87), kind=kOutput, calls=%fused_computation.63 | convolution fusion | flops 4836556800 | bytes 14942208 | tf_op jit(solution)/shard_map/dot_general | solution.py:24
  221.4 17.1 %multiply_convert_fusion = bf16[2048,1536]{1,0:T(8,128)(2,1)} fusion(f32[2048,1536]{1,0:T(8,128)} %get-tuple-element.173, bf16[2048,768]{1,0:T(8,128)(2,1)S(1)} %bitcast.331, f32[1536]{0:T(1024)S(1)} %add.405, bf16[768,768]{1,0:T(8,128)(2,1)S(1)} %copy-done.58, bf16[768,768]{1,0:T(8,128)(2,1)S(1)} %get-tuple-element.87), kind=kOutput, calls=%fused_computation | convolution fusion | flops 4896325632 | bytes 24385536 | tf_op jit(solution)/shard_map/dot_general | solution.py:24
  238.4 2.2 fusion.19
  240.8 8.6 %convolution_convert_fusion.2 = bf16[2048,768]{1,0:T(8,128)(2,1)S(1)} fusion(bf16[2048,1536]{1,0:T(8,128)(2,1)} %multiply_convert_fusion, bf16[768,1920]{1,0:T(8,128)(2,1)S(1)} %bitcast.328), kind=kOutput, calls=%fused_computation.16 | convolution fusion | flops 4833411072 | bytes 11796480 | tf_op jit(solution)/shard_map/dot_general | solution.py:24
  249.5 3.8 fusion.21
  253.7 6.7 %convolution_convert_fusion = bf16[768,1536]{1,0:T(8,128)(2,1)} fusion(bf16[2048,1536]{1,0:T(8,128)(2,1)S(1)} %copy-done.41, f32[2048,768]{1,0:T(8,128)S(1)} %get-tuple-element.82, f32[768]{0:T(1024)S(1)} %copy-done.68, f32[768]{0:T(1024)S(1)} %copy-done.62, f32[2048]{0:T(1024)S(1)} %add_rsqrt_fusion, f32[2048]{0:T(1024)S(1)} %broadcast_multiply_fusion.2), kind=kOutput, calls=%fused_computation.14 | convolution fusion | flops 4840882176 | bytes 14964736 | tf_op jit(solution)/shard_map/dot_general | solution.py:24
  260.5 2.7 fusion.9
  263.3 1.6 collective-permute-start.20
  271.1 12.6 %collective-permute-done.20 = bf16[512,768]{1,0:T(8,128)(2,1)S(1)} collective-permute-done((bf16[512,768]{1,0:T(8,128)(2,1)S(1)}, bf16[512,768]{1,0:T(8,128)(2,1)S(1)}, u32[]{:S(2)}, u32[]{:S(2)}) %collective-permute-start.20) | collective-permute-done | bytes 786464 | tf_op jit(solution)/shard_map/ppermute | solution.py:399
  285.1 3.5 multiply_reduce_fusion
  288.7 5.0 %convert_reduce_fusion = (bf16[768]{0:T(1024)(128)(2,1)S(1)}, f32[2048,768]{1,0:T(8,128)S(1)}) fusion(f32[2048]{0:T(1024)S(1)} %broadcast_multiply_fusion, f32[2048,768]{1,0:T(8,128)S(1)} %get-tuple-element.82, f32[2048]{0:T(1024)S(1)} %broadcast_multiply_fusion.2, f32[2048]{0:T(1024)S(1)} %broadcast_multiply_fusion.1, f32[768]{0:T(1024)S(1)} %copy-done.62, ...), kind=kLoop, calls=%fused_computation.299 | loop fusion | flops 22019328 | bytes 22057472 | tf_op jit(solution)/shard_map/reduce_sum | solution.py:669
  293.7 1.9 convolution_convert_fusion.3.do_ref
  296.3 19.2 %shard_map.285 = (bf16[2048,384]{1,0:T(8,128)(2,1)S(1)}, f32[8,128]{1,0:T(8,128)S(1)}) custom-call(bf16[2048,1152]{1,0:T(8,128)(2,1)} %get-tuple-element.37.qkv_ref, bf16[2048,128]{1,0:T(8,128)(2,1)S(1)} %get-tuple-element.165.qs_ref, bf16[2048,128]{1,0:T(8,128)(2,1)S(1)} %get-tuple-element.164.ks_ref, ...), custom_call_target="tpu_custom_call" | custom-call | flops 100000000 | bytes 1000000 | tf_op jit(solution)/shard_map/pallas_call | solution.py:338
  316.1 2.4 fusion.15
  319.8 2.5 fusion.13
  326.5 1.8 convolution_convert_fusion.6
  328.3 18.6 %shard_map.286 = (bf16[2048,384]{1,0:T(8,128)(2,1)S(1)}, f32[8,128]{1,0:T(8,128)S(1)}) custom-call(bf16[2048,1152]{1,0:T(8,128)(2,1)} %get-tuple-element.37.qkv_ref, bf16[2048,128]{1,0:T(8,128)(2,1)S(1)} %get-tuple-element.165.qs_ref, bf16[2048,128]{1,0:T(8,128)(2,1)S(1)} %get-tuple-element.164.ks_ref, ...), custom_call_target="tpu_custom_call" | custom-call | flops 100000000 | bytes 1000000 | tf_op jit(solution)/shard_map/pallas_call | solution.py:338
  346.9 1.8 convolution_convert_fusion.5
  354.3 19.4 %shard_map.287 = (bf16[2048,384]{1,0:T(8,128)(2,1)S(1)}, f32[8,128]{1,0:T(8,128)}) custom-call(bf16[2048,1152]{1,0:T(8,128)(2,1)} %get-tuple-element.37.qkv_ref, bf16[2048,128]{1,0:T(8,128)(2,1)S(1)} %get-tuple-element.165.qs_ref, bf16[2048,128]{1,0:T(8,128)(2,1)S(1)} %get-tuple-element.164.ks_ref, bf16[2048,128]{1,0:T(8,128)(2,1)S(1)} %copy-done.17, ...), custom_call_target="tpu_custom_call" | custom-call | flops 100000000 | bytes 1000000 | tf_op jit(solution)/shard_map/pallas_call | solution.py:338
  373.7 10.6 %shard_map.288 = (bf16[2048,768]{1,0:T(8,128)(2,1)}, f32[8,768]{1,0:T(8,128)S(1)}, f32[8,1152]{1,0:T(8,128)S(1)}, f32[8,128]{1,0:T(8,128)S(1)}) custom-call(bf16[2048,384]{1,0:T(8,128)(2,1)S(1)} %copy-done.6, bf16[2048,384]{1,0:T(8,128)(2,1)S(1)} %copy-done.8, bf16[2048,384]{1,0:T(8,128)(2,1)S(1)} %get-tuple-element.51.d2_ref, bf16[768,1152]{1,0:T(8,128)(2,1)} %copy-done.4, ...), custom_call_target="tpu_custom_call" | custom-call | flops 100000000 | bytes 1000000 | tf_op jit(solution)/shard_map/pallas_call | solution.py:310
  385.0 2.9 dynamic-slice_bitcast_fusion
  388.0 3.6 convolution_convert_fusion.4
  391.7 2.1 fusion.34
  396.9 2.2 collective-permute-start.41
  400.8 2.3 fusion.11
  403.1 2.9 collective-permute-start.45
  406.0 5.2 %shard_map.289 = (bf16[1024,768]{1,0:T(8,128)(2,1)S(1)}, f32[8,128]{1,0:T(8,128)S(1)}) custom-call(s32[1]{0:T(128)} %bitcast.66.core_ref, bf16[2048,768]{1,0:T(8,128)(2,1)} %get-tuple-element.52.mine_ref, bf16[1024,768]{1,0:T(8,128)(2,1)} %bitcast.89.come_ref, bf16[2048,768]{1,0:T(8,128)(2,1)} %bitcast.322, f32[2048,768]{1,0:T(8,128)} %copy-done.21, ...), custom_call_target="tpu_custom_call" | custom-call | flops 100000000 | bytes 1000000 | tf_op jit(solution)/shard_map/pallas_call | solution.py:238
  420.1 6.6 %collective-permute-done.46 = bf16[2,48,768]{2,1,0:T(8,128)(2,1)S(1)} collective-permute-done((bf16[2,48,768]{2,1,0:T(8,128)(2,1)S(1)}, bf16[2,48,768]{2,1,0:T(8,128)(2,1)S(1)}, u32[]{:S(2)}, u32[]{:S(2)}) %collective-permute-start.46) | collective-permute-done | bytes 147488 | tf_op jit(solution)/shard_map/ppermute | solution.py:428
  437.3 1.8 reshape.259
  440.2 2.2 collective-permute-start.37
  443.7 1.9 collective-permute-start.38
  445.6 3.0 collective-permute-done.33
  449.8 2.8 collective-permute-done.29.refs_0_
  (403 shorter events, 107.8 us)
Async XLA Ops:
  0.6 92.9 %copy-start = (s32[2,2048]{1,0:T(2,128)S(1)}, s32[2,2048]{1,0:T(2,128)}, u32[]{:S(2)}) copy-start(s32[2,2048]{1,0:T(2,128)} %param.18) | copy-start | bytes 49156
  3.5 7.0 %collective-permute-start.2 = (bf16[24,1280]{1,0:T(8,128)(2,1)}, bf16[24,1280]{1,0:T(8,128)(2,1)}, u32[]{:S(2)}, u32[]{:S(2)}) collective-permute-start(bf16[24,1280]{1,0:T(8,128)(2,1)} %fusion.73), channel_id=1, source_target_pairs={{0,1},{1,0},{2,3},{3,2},{4,5},{5,4},{6,7},{7,6},{8,9},{9,8},{10,11... | collective-permute-start | bytes 184328 | tf_op jit(solution)/shard_map/ppermute | solution.py:399
  5.9 10.1 %collective-permute-start.10 = (bf16[24,2304]{1,0:T(8,128)(2,1)S(1)}, bf16[24,2304]{1,0:T(8,128)(2,1)S(1)}, u32[]{:S(2)}, u32[]{:S(2)}) collective-permute-start(bf16[24,2304]{1,0:T(8,128)(2,1)S(1)} %fusion.63), channel_id=1, source_target_pairs={{0,1},{1,0},{2,3},{3,2},{4,5},{5,4},{6,7},{7,6},{8,9},{9,8},{10,11... | collective-permute-start | bytes 331784 | tf_op jit(solution)/shard_map/ppermute | solution.py:399
  6.1 53.5 %collective-permute-start = (bf16[512,768]{1,0:T(8,128)(2,1)S(1)}, bf16[512,768]{1,0:T(8,128)(2,1)S(1)}, u32[]{:S(2)}, u32[]{:S(2)}) collective-permute-start(bf16[512,768]{1,0:T(8,128)(2,1)S(1)} %dynamic-slice_bitcast_fusion.3), channel_id=1, source_target_pairs={{0,2},{2,0},{1,3},{3,1},{4,6},{6,4},{5,7},{7,5},{8,10},{10,8},{9,1... | collective-permute-start | bytes 2359304 | tf_op jit(solution)/shard_map/ppermute | solution.py:399
  11.6 8.1 %collective-permute-start.5 = (bf16[48,1280]{1,0:T(8,128)(2,1)S(1)}, bf16[48,1280]{1,0:T(8,128)(2,1)S(1)}, u32[]{:S(2)}, u32[]{:S(2)}) collective-permute-start(bf16[48,1280]{1,0:T(8,128)(2,1)S(1)} %concatenate.63), channel_id=1, source_target_pairs={{0,24},{4,28},{8,16},{12,20},{16,8},{20,12},{24,0},{28,4},{1,25},{... | collective-permute-start | bytes 368648 | tf_op jit(solution)/shard_map/ppermute | solution.py:428
  15.3 10.3 %collective-permute-start.4 = (bf16[48,1280]{1,0:T(8,128)(2,1)S(1)}, bf16[48,1280]{1,0:T(8,128)(2,1)S(1)}, u32[]{:S(2)}, u32[]{:S(2)}) collective-permute-start(bf16[48,1280]{1,0:T(8,128)(2,1)S(1)} %concatenate.63), channel_id=1, source_target_pairs={{0,16},{4,20},{8,24},{12,28},{16,0},{20,4},{24,8},{28,12},{1,17},{... | collective-permute-start | bytes 368648 | tf_op jit(solution)/shard_map/ppermute | solution.py:428
  15.3 10.3 %collective-permute-start.3 = (bf16[48,1280]{1,0:T(8,128)(2,1)S(1)}, bf16[48,1280]{1,0:T(8,128)(2,1)S(1)}, u32[]{:S(2)}, u32[]{:S(2)}) collective-permute-start(bf16[48,1280]{1,0:T(8,128)(2,1)S(1)} %concatenate.63), channel_id=1, source_target_pairs={{0,8},{4,12},{8,0},{12,4},{16,24},{20,28},{24,16},{28,20},{1,9},{5... | collective-permute-start | bytes 368648 | tf_op jit(solution)/shard_map/ppermute | solution.py:428
  25.7 7.1 %collective-permute-start.6 = (bf16[4,48,640]{2,1,0:T(8,128)(2,1)S(1)}, bf16[4,48,640]{2,1,0:T(8,128)(2,1)S(1)}, u32[]{:S(2)}, u32[]{:S(2)}) collective-permute-start(bf16[4,48,640]{2,1,0:T(8,128)(2,1)S(1)} %get-tuple-element.139), channel_id=1, source_target_pairs={{0,4},{4,0},{8,12},{12,8},{16,20},{20,16},{24,28},{28,24},{1,5},{5... | collective-permute-start | bytes 737288 | tf_op jit(solution)/shard_map/ppermute | solution.py:428
  27.3 6.7 %collective-permute-start.8 = (bf16[4,48,640]{2,1,0:T(8,128)(2,1)S(1)}, bf16[4,48,640]{2,1,0:T(8,128)(2,1)S(1)}, u32[]{:S(2)}, u32[]{:S(2)}) collective-permute-start(bf16[4,48,640]{2,1,0:T(8,128)(2,1)S(1)} %get-tuple-element.140), channel_id=1, source_target_pairs={{0,2},{2,0},{1,3},{3,1},{4,6},{6,4},{5,7},{7,5},{8,10},{10,8},{9,1... | collective-permute-start | bytes 737288 | tf_op jit(solution)/shard_map/ppermute | solution.py:399
  27.9 25.5 %collective-permute-start.12 = (bf16[48,3840]{1,0:T(8,128)(2,1)S(1)}, bf16[48,3840]{1,0:T(8,128)(2,1)S(1)}, u32[]{:S(2)}, u32[]{:S(2)}) collective-permute-start(bf16[48,3840]{1,0:T(8,128)(2,1)S(1)} %pad_maximum_fusion.18), channel_id=1, source_target_pairs={{0,16},{4,20},{8,24},{12,28},{16,0},{20,4},{24,8},{28,12},{1,17},{... | collective-permute-start | bytes 1105928 | tf_op jit(solution)/shard_map/ppermute | solution.py:428
  28.1 26.8 %collective-permute-start.13 = (bf16[48,3840]{1,0:T(8,128)(2,1)S(1)}, bf16[48,3840]{1,0:T(8,128)(2,1)S(1)}, u32[]{:S(2)}, u32[]{:S(2)}) collective-permute-start(bf16[48,3840]{1,0:T(8,128)(2,1)S(1)} %pad_maximum_fusion.18), channel_id=1, source_target_pairs={{0,24},{4,28},{8,16},{12,20},{16,8},{20,12},{24,0},{28,4},{1,25},{... | collective-permute-start | bytes 1105928 | tf_op jit(solution)/shard_map/ppermute | solution.py:428
  32.8 24.4 %collective-permute-start.11 = (bf16[48,3840]{1,0:T(8,128)(2,1)S(1)}, bf16[48,3840]{1,0:T(8,128)(2,1)S(1)}, u32[]{:S(2)}, u32[]{:S(2)}) collective-permute-start(bf16[48,3840]{1,0:T(8,128)(2,1)S(1)} %pad_maximum_fusion.18), channel_id=1, source_target_pairs={{0,8},{4,12},{8,0},{12,4},{16,24},{20,28},{24,16},{28,20},{1,9},{5... | collective-permute-start | bytes 1105928 | tf_op jit(solution)/shard_map/ppermute | solution.py:428
  34.2 26.8 %collective-permute-start.9 = (bf16[4,2,48,640]{3,2,0,1:T(8,128)(2,1)S(1)}, bf16[4,2,48,640]{3,2,0,1:T(8,128)(2,1)S(1)}, u32[]{:S(2)}, u32[]{:S(2)}) collective-permute-start(bf16[4,2,48,640]{3,2,0,1:T(8,128)(2,1)S(1)} %pad_maximum_fusion.17), channel_id=1, source_target_pairs={{0,4},{4,0},{8,12},{12,8},{16,20},{20,16},{24,28},{28,24},{1,5},{5... | collective-permute-start | bytes 1474568 | tf_op jit(solution)/shard_map/ppermute | solution.py:428
  34.9 24.8 %copy-start.49 = (bf16[2,512,768]{2,1,0:T(8,128)(2,1)S(1)}, bf16[2,512,768]{2,1,0:T(8,128)(2,1)}, u32[]{:S(2)}) copy-start(bf16[2,512,768]{2,1,0:T(8,128)(2,1)} %param.17) | copy-start | bytes 4718596
  53.4 13.0 %collective-permute-start.7 = (bf16[4,2,48,640]{3,2,0,1:T(8,128)(2,1)S(1)}, bf16[4,2,48,640]{3,2,0,1:T(8,128)(2,1)S(1)}, u32[]{:S(2)}, u32[]{:S(2)}) collective-permute-start(bf16[4,2,48,640]{3,2,0,1:T(8,128)(2,1)S(1)} %pad_maximum_fusion.16), channel_id=1, source_target_pairs={{0,2},{2,0},{1,3},{3,1},{4,6},{6,4},{5,7},{7,5},{8,10},{10,8},{9,1... | collective-permute-start | bytes 1474568 | tf_op jit(solution)/shard_map/ppermute | solution.py:399
  61.0 13.9 %collective-permute-start.1 = (bf16[2,512,768]{2,1,0:T(8,128)(2,1)}, bf16[2,512,768]{2,1,0:T(8,128)(2,1)}, u32[]{:S(2)}, u32[]{:S(2)}) collective-permute-start(bf16[2,512,768]{2,1,0:T(8,128)(2,1)} %pad_maximum_fusion.6), channel_id=1, source_target_pairs={{0,1},{1,0},{2,3},{3,2},{4,5},{5,4},{6,7},{7,6},{8,9},{9,8},{10,11... | collective-permute-start | bytes 4718600 | tf_op jit(solution)/shard_map/ppermute | solution.py:399
  79.3 11.0 %copy-start.53 = (bf16[1,48,3840]{2,1,0:T(8,128)(2,1)S(1)}, bf16[1,48,3840]{2,1,0:T(8,128)(2,1)}, u32[]{:S(2)}) copy-start(bf16[1,48,3840]{2,1,0:T(8,128)(2,1)} %get-tuple-element.115) | copy-start | bytes 1105924
  79.3 11.0 %copy-start.54 = (bf16[1,48,3840]{2,1,0:T(8,128)(2,1)S(1)}, bf16[1,48,3840]{2,1,0:T(8,128)(2,1)}, u32[]{:S(2)}) copy-start(bf16[1,48,3840]{2,1,0:T(8,128)(2,1)} %get-tuple-element.116) | copy-start | bytes 1105924
  79.3 11.0 %copy-start.55 = (bf16[1,48,3840]{2,1,0:T(8,128)(2,1)S(1)}, bf16[1,48,3840]{2,1,0:T(8,128)(2,1)}, u32[]{:S(2)}) copy-start(bf16[1,48,3840]{2,1,0:T(8,128)(2,1)} %get-tuple-element.117) | copy-start | bytes 1105924
  91.5 17.5 %collective-permute-start.15 = (bf16[4,48,1920]{2,1,0:T(8,128)(2,1)S(1)}, bf16[4,48,1920]{2,1,0:T(8,128)(2,1)S(1)}, u32[]{:S(2)}, u32[]{:S(2)}) collective-permute-start(bf16[4,48,1920]{2,1,0:T(8,128)(2,1)S(1)} %get-tuple-element.113.rest_1_), channel_id=1, source_target_pairs={{0,4},{4,0},{8,12},{12,8},{16,20},{20,16},{24,28},{28,24},{1,5},{5... | collective-permute-start | bytes 2211848 | tf_op jit(solution)/shard_map/ppermute | solution.py:428
  92.0 17.2 %collective-permute-start.14 = (bf16[4,48,1920]{2,1,0:T(8,128)(2,1)S(1)}, bf16[4,48,1920]{2,1,0:T(8,128)(2,1)S(1)}, u32[]{:S(2)}, u32[]{:S(2)}) collective-permute-start(bf16[4,48,1920]{2,1,0:T(8,128)(2,1)S(1)} %get-tuple-element.114.rest_0_), channel_id=1, source_target_pairs={{0,2},{2,0},{1,3},{3,1},{4,6},{6,4},{5,7},{7,5},{8,10},{10,8},{9,1... | collective-permute-start | bytes 2211848 | tf_op jit(solution)/shard_map/ppermute | solution.py:399
  113.1 39.7 %collective-permute-start.16 = (bf16[4,2,48,1920]{3,2,0,1:T(8,128)(2,1)}, bf16[4,2,48,1920]{3,2,0,1:T(8,128)(2,1)}, u32[]{:S(2)}, u32[]{:S(2)}) collective-permute-start(bf16[4,2,48,1920]{3,2,0,1:T(8,128)(2,1)} %maximum_add_fusion.3), channel_id=1, source_target_pairs={{0,4},{4,0},{8,12},{12,8},{16,20},{20,16},{24,28},{28,24},{1,5},{5... | collective-permute-start | bytes 4423688 | tf_op jit(solution)/shard_map/ppermute | solution.py:428
  119.2 56.3 %collective-permute-start.21 = (bf16[512,768]{1,0:T(8,128)(2,1)}, bf16[512,768]{1,0:T(8,128)(2,1)S(1)}, u32[]{:S(2)}, u32[]{:S(2)}) collective-permute-start(bf16[512,768]{1,0:T(8,128)(2,1)} %add_bitcast_fusion), channel_id=1, source_target_pairs={{0,2},{2,0},{1,3},{3,1},{4,6},{6,4},{5,7},{7,5},{8,10},{10,8},{9,1... | collective-permute-start | bytes 2359304 | tf_op jit(solution)/shard_map/ppermute | solution.py:399
  122.7 45.4 %collective-permute-start.17 = (bf16[4,2,48,1920]{3,2,1,0:T(8,128)(2,1)S(1)}, bf16[4,2,48,1920]{3,2,1,0:T(8,128)(2,1)}, u32[]{:S(2)}, u32[]{:S(2)}) collective-permute-start(bf16[4,2,48,1920]{3,2,1,0:T(8,128)(2,1)S(1)} %copy_add_fusion.rest_2_), channel_id=1, source_target_pairs={{0,2},{2,0},{1,3},{3,1},{4,6},{6,4},{5,7},{7,5},{8,10},{10,8},{9,1... | collective-permute-start | bytes 4423688 | tf_op jit(solution)/shard_map/ppermute | solution.py:399
  152.8 19.1 %copy-start.33 = (bf16[2048,384]{1,0:T(8,128)(2,1)}, bf16[2048,384]{1,0:T(8,128)(2,1)S(1)}, u32[]{:S(2)}) copy-start(bf16[2048,384]{1,0:T(8,128)(2,1)S(1)} %constant_dynamic-update-slice_fusion) | copy-start | bytes 4718596
  157.0 11.1 %copy-start.36 = (bf16[4,1,48,1920]{3,2,0,1:T(8,128)(2,1)S(1)}, bf16[4,1,48,1920]{3,2,0,1:T(8,128)(2,1)}, u32[]{:S(2)}) copy-start(bf16[4,1,48,1920]{3,2,0,1:T(8,128)(2,1)} %get-tuple-element.108) | copy-start | bytes 2211844
  157.2 14.8 %copy-start.27 = (bf16[4,2,2,48,1920]{4,3,2,1,0:T(8,128)(2,1)}, bf16[4,2,2,48,1920]{4,3,2,1,0:T(8,128)(2,1)S(1)}, u32[]{:S(2)}) copy-start(bf16[4,2,2,48,1920]{4,3,2,1,0:T(8,128)(2,1)S(1)} %copy.103) | copy-start | bytes 8847364
  175.5 14.0 %collective-permute-start.18 = (bf16[2048,768]{1,0:T(8,128)(2,1)}, bf16[2048,768]{1,0:T(8,128)(2,1)}, u32[]{:S(2)}, u32[]{:S(2)}) collective-permute-start(bf16[2048,768]{1,0:T(8,128)(2,1)} %convolution_convert_fusion.1), channel_id=1, source_target_pairs={{0,1},{1,0},{2,3},{3,2},{4,5},{5,4},{6,7},{7,6},{8,9},{9,8},{10,11... | collective-permute-start | bytes 9437192 | tf_op jit(solution)/shard_map/ppermute | solution.py:399
  177.8 6.0 %collective-permute-start.22 = (bf16[2,512,768]{2,1,0:T(8,128)(2,1)}, bf16[2,512,768]{2,1,0:T(8,128)(2,1)}, u32[]{:S(2)}, u32[]{:S(2)}) collective-permute-start(bf16[2,512,768]{2,1,0:T(8,128)(2,1)} %pad_maximum_fusion.8), channel_id=1, source_target_pairs={{0,1},{1,0},{2,3},{3,2},{4,5},{5,4},{6,7},{7,6},{8,9},{9,8},{10,11... | collective-permute-start | bytes 4718600 | tf_op jit(solution)/shard_map/ppermute | solution.py:399
  188.3 61.2 %copy-start.30 = (bf16[2,2,512,768]{3,2,1,0:T(8,128)(2,1)}, bf16[2,2,512,768]{3,2,1,0:T(8,128)(2,1)S(1)}, u32[]{:S(2)}) copy-start(bf16[2,2,512,768]{3,2,1,0:T(8,128)(2,1)S(1)} %copy.106) | copy-start | bytes 9437188
  238.4 11.0 %slice-start.1 = ((s8[6291456]{0:T(1024)(128)(4,1)}), s8[4194304]{0:T(1024)(128)(4,1)S(1)}, s32[]{:S(2)}) async-start(s8[6291456]{0:T(1024)(128)(4,1)} %bitcast.359), calls=%async_computation.1 | async-start | bytes 8388608
  240.6 19.8 %collective-permute-start.19 = (bf16[2,512,768]{2,1,0:T(8,128)(2,1)S(1)}, bf16[2,512,768]{2,1,0:T(8,128)(2,1)S(1)}, u32[]{:S(2)}, u32[]{:S(2)}) collective-permute-start(bf16[2,512,768]{2,1,0:T(8,128)(2,1)S(1)} %fusion.19), channel_id=1, source_target_pairs={{0,1},{1,0},{2,3},{3,2},{4,5},{5,4},{6,7},{7,6},{8,9},{9,8},{10,11... | collective-permute-start | bytes 4718600 | tf_op jit(solution)/shard_map/ppermute | solution.py:399
  253.3 31.8 %collective-permute-start.23 = (bf16[2048,768]{1,0:T(8,128)(2,1)S(1)}, bf16[2048,768]{1,0:T(8,128)(2,1)S(1)}, u32[]{:S(2)}, u32[]{:S(2)}) collective-permute-start(bf16[2048,768]{1,0:T(8,128)(2,1)S(1)} %convolution_convert_fusion.2), channel_id=1, source_target_pairs={{0,1},{1,0},{2,3},{3,2},{4,5},{5,4},{6,7},{7,6},{8,9},{9,8},{10,11... | collective-permute-start | bytes 9437192 | tf_op jit(solution)/shard_map/ppermute | solution.py:399
  263.3 20.5 %collective-permute-start.20 = (bf16[512,768]{1,0:T(8,128)(2,1)S(1)}, bf16[512,768]{1,0:T(8,128)(2,1)S(1)}, u32[]{:S(2)}, u32[]{:S(2)}) collective-permute-start(bf16[512,768]{1,0:T(8,128)(2,1)S(1)} %dynamic-slice_bitcast_fusion.2), channel_id=1, source_target_pairs={{0,2},{2,0},{1,3},{3,1},{4,6},{6,4},{5,7},{7,5},{8,10},{10,8},{9,1... | collective-permute-start | bytes 2359304 | tf_op jit(solution)/shard_map/ppermute | solution.py:399
  267.3 48.8 %collective-permute-start.24 = (bf16[2,4,2,48,768]{4,3,1,0,2:T(8,128)(2,1)}, bf16[2,4,2,48,768]{4,3,1,0,2:T(8,128)(2,1)}, u32[]{:S(2)}, u32[]{:S(2)}) collective-permute-start(bf16[2,4,2,48,768]{4,3,1,0,2:T(8,128)(2,1)} %bitcast.316), channel_id=1, source_target_pairs={{0,2},{2,0},{1,3},{3,1},{4,6},{6,4},{5,7},{7,5},{8,10},{10,8},{9,1... | collective-permute-start | bytes 3538952 | tf_op jit(solution)/shard_map/ppermute | solution.py:399
  270.6 48.1 %collective-permute-start.25 = (bf16[4,2,48,1536]{3,2,0,1:T(8,128)(2,1)}, bf16[4,2,48,1536]{3,2,0,1:T(8,128)(2,1)}, u32[]{:S(2)}, u32[]{:S(2)}) collective-permute-start(bf16[4,2,48,1536]{3,2,0,1:T(8,128)(2,1)} %bitcast.315), channel_id=1, source_target_pairs={{0,4},{4,0},{8,12},{12,8},{16,20},{20,16},{24,28},{28,24},{1,5},{5... | collective-permute-start | bytes 3538952 | tf_op jit(solution)/shard_map/ppermute | solution.py:428
  296.3 19.2 %copy-start.2 = (bf16[2048,384]{1,0:T(8,128)(2,1)}, bf16[2048,384]{1,0:T(8,128)(2,1)S(1)}, u32[]{:S(2)}) copy-start(bf16[2048,384]{1,0:T(8,128)(2,1)S(1)} %convolution_convert_fusion.3.do_ref) | copy-start | bytes 4718596
  324.4 28.1 %collective-permute-start.27 = (bf16[4,48,1536]{2,1,0:T(8,128)(2,1)S(1)}, bf16[4,48,1536]{2,1,0:T(8,128)(2,1)S(1)}, u32[]{:S(2)}, u32[]{:S(2)}) collective-permute-start(bf16[4,48,1536]{2,1,0:T(8,128)(2,1)S(1)} %dynamic-slice_bitcast_fusion.5), channel_id=1, source_target_pairs={{0,2},{2,0},{1,3},{3,1},{4,6},{6,4},{5,7},{7,5},{8,10},{10,8},{9,1... | collective-permute-start | bytes 1769480 | tf_op jit(solution)/shard_map/ppermute | solution.py:399
  326.0 27.4 %collective-permute-start.26 = (bf16[2,4,48,768]{3,2,1,0:T(8,128)(2,1)S(1)}, bf16[2,4,48,768]{3,2,1,0:T(8,128)(2,1)S(1)}, u32[]{:S(2)}, u32[]{:S(2)}) collective-permute-start(bf16[2,4,48,768]{3,2,1,0:T(8,128)(2,1)S(1)} %dynamic-slice_bitcast_fusion.6), channel_id=1, source_target_pairs={{0,4},{4,0},{8,12},{12,8},{16,20},{20,16},{24,28},{28,24},{1,5},{5... | collective-permute-start | bytes 1769480 | tf_op jit(solution)/shard_map/ppermute | solution.py:428
  351.9 48.6 %collective-permute-start.30 = (bf16[4,2,48,1536]{3,2,0,1:T(8,128)(2,1)}, bf16[4,2,48,1536]{3,2,0,1:T(8,128)(2,1)}, u32[]{:S(2)}, u32[]{:S(2)}) collective-permute-start(bf16[4,2,48,1536]{3,2,0,1:T(8,128)(2,1)} %bitcast.314), channel_id=1, source_target_pairs={{0,2},{2,0},{1,3},{3,1},{4,6},{6,4},{5,7},{7,5},{8,10},{10,8},{9,1... | collective-permute-start | bytes 3538952 | tf_op jit(solution)/shard_map/ppermute | solution.py:399
  353.4 20.3 %copy-start.14 = (bf16[4,48,1536]{2,1,0:T(8,128)(2,1)}, bf16[4,48,1536]{2,1,0:T(8,128)(2,1)S(1)}, u32[]{:S(2)}) copy-start(bf16[4,48,1536]{2,1,0:T(8,128)(2,1)S(1)} %fusion.31.rest_1_) | copy-start | bytes 1769476
  354.3 19.5 %copy-start.12 = (bf16[2,4,48,768]{3,2,1,0:T(8,128)(2,1)}, bf16[2,4,48,768]{3,2,1,0:T(8,128)(2,1)S(1)}, u32[]{:S(2)}) copy-start(bf16[2,4,48,768]{3,2,1,0:T(8,128)(2,1)S(1)} %fusion.33.rest_0_) | copy-start | bytes 1769476
  354.3 19.4 %copy-start.6 = (bf16[2048,384]{1,0:T(8,128)(2,1)S(1)}, bf16[2048,384]{1,0:T(8,128)(2,1)}, u32[]{:S(2)}) copy-start(bf16[2048,384]{1,0:T(8,128)(2,1)} %copy-done.5) | copy-start | bytes 4718596
  354.3 19.4 %copy-start.8 = (bf16[2048,384]{1,0:T(8,128)(2,1)S(1)}, bf16[2048,384]{1,0:T(8,128)(2,1)}, u32[]{:S(2)}) copy-start(bf16[2048,384]{1,0:T(8,128)(2,1)} %copy-done.7) | copy-start | bytes 4718596
  388.0 15.1 %collective-permute-start.28 = (bf16[2,512,768]{2,1,0:T(8,128)(2,1)}, bf16[2,512,768]{2,1,0:T(8,128)(2,1)}, u32[]{:S(2)}, u32[]{:S(2)}) collective-permute-start(bf16[2,512,768]{2,1,0:T(8,128)(2,1)} %dynamic-slice_bitcast_fusion), channel_id=1, source_target_pairs={{0,1},{1,0},{2,3},{3,2},{4,5},{5,4},{6,7},{7,6},{8,9},{9,8},{10,11... | collective-permute-start | bytes 4718600 | tf_op jit(solution)/shard_map/ppermute | solution.py:399
  395.4 20.8 %collective-permute-start.35 = (bf16[4,2,48,512]{3,2,1,0:T(8,128)(2,1)S(1)}, bf16[4,2,48,512]{3,2,1,0:T(8,128)(2,1)S(1)}, u32[]{:S(2)}, u32[]{:S(2)}) collective-permute-start(bf16[4,2,48,512]{3,2,1,0:T(8,128)(2,1)S(1)} %dynamic-slice_bitcast_fusion.7), channel_id=1, source_target_pairs={{0,4},{4,0},{8,12},{12,8},{16,20},{20,16},{24,28},{28,24},{1,5},{5... | collective-permute-start | bytes 1179656 | tf_op jit(solution)/shard_map/ppermute | solution.py:428
  396.9 14.8 %collective-permute-start.41 = (bf16[48,1536]{1,0:T(8,128)(2,1)S(1)}, bf16[48,1536]{1,0:T(8,128)(2,1)S(1)}, u32[]{:S(2)}, u32[]{:S(2)}) collective-permute-start(bf16[48,1536]{1,0:T(8,128)(2,1)S(1)} %get-tuple-element.129), channel_id=1, source_target_pairs={{0,8},{4,12},{8,0},{12,4},{16,24},{20,28},{24,16},{28,20},{1,9},{5... | collective-permute-start | bytes 442376 | tf_op jit(solution)/shard_map/ppermute | solution.py:428
  399.1 14.0 %collective-permute-start.43 = (bf16[48,1536]{1,0:T(8,128)(2,1)S(1)}, bf16[48,1536]{1,0:T(8,128)(2,1)S(1)}, u32[]{:S(2)}, u32[]{:S(2)}) collective-permute-start(bf16[48,1536]{1,0:T(8,128)(2,1)S(1)} %get-tuple-element.130), channel_id=1, source_target_pairs={{0,24},{4,28},{8,16},{12,20},{16,8},{20,12},{24,0},{28,4},{1,25},{... | collective-permute-start | bytes 442376 | tf_op jit(solution)/shard_map/ppermute | solution.py:428
  400.5 14.3 %collective-permute-start.42 = (bf16[48,1536]{1,0:T(8,128)(2,1)S(1)}, bf16[48,1536]{1,0:T(8,128)(2,1)S(1)}, u32[]{:S(2)}, u32[]{:S(2)}) collective-permute-start(bf16[48,1536]{1,0:T(8,128)(2,1)S(1)} %get-tuple-element.131), channel_id=1, source_target_pairs={{0,16},{4,20},{8,24},{12,28},{16,0},{20,4},{24,8},{28,12},{1,17},{... | collective-permute-start | bytes 442376 | tf_op jit(solution)/shard_map/ppermute | solution.py:428
  403.1 14.7 %collective-permute-start.45 = (bf16[2,48,768]{2,1,0:T(8,128)(2,1)S(1)}, bf16[2,48,768]{2,1,0:T(8,128)(2,1)S(1)}, u32[]{:S(2)}, u32[]{:S(2)}) collective-permute-start(bf16[2,48,768]{2,1,0:T(8,128)(2,1)S(1)} %get-tuple-element.126), channel_id=1, source_target_pairs={{0,8},{4,12},{8,0},{12,4},{16,24},{20,28},{24,16},{28,20},{1,9},{5... | collective-permute-start | bytes 442376 | tf_op jit(solution)/shard_map/ppermute | solution.py:428
  411.8 8.3 %collective-permute-start.47 = (bf16[2,48,768]{2,1,0:T(8,128)(2,1)S(1)}, bf16[2,48,768]{2,1,0:T(8,128)(2,1)S(1)}, u32[]{:S(2)}, u32[]{:S(2)}) collective-permute-start(bf16[2,48,768]{2,1,0:T(8,128)(2,1)S(1)} %get-tuple-element.127), channel_id=1, source_target_pairs={{0,24},{4,28},{8,16},{12,20},{16,8},{20,12},{24,0},{28,4},{1,25},{... | collective-permute-start | bytes 442376 | tf_op jit(solution)/shard_map/ppermute | solution.py:428
  413.1 13.6 %collective-permute-start.46 = (bf16[2,48,768]{2,1,0:T(8,128)(2,1)S(1)}, bf16[2,48,768]{2,1,0:T(8,128)(2,1)S(1)}, u32[]{:S(2)}, u32[]{:S(2)}) collective-permute-start(bf16[2,48,768]{2,1,0:T(8,128)(2,1)S(1)} %get-tuple-element.128), channel_id=1, source_target_pairs={{0,16},{4,20},{8,24},{12,28},{16,0},{20,4},{24,8},{28,12},{1,17},{... | collective-permute-start | bytes 442376 | tf_op jit(solution)/shard_map/ppermute | solution.py:428
  414.8 13.9 %collective-permute-start.31 = (bf16[4,48,1536]{2,1,0:T(8,128)(2,1)S(1)}, bf16[4,48,1536]{2,1,0:T(8,128)(2,1)S(1)}, u32[]{:S(2)}, u32[]{:S(2)}) collective-permute-start(bf16[4,48,1536]{2,1,0:T(8,128)(2,1)S(1)} %dynamic-slice_bitcast_fusion.4), channel_id=1, source_target_pairs={{0,4},{4,0},{8,12},{12,8},{16,20},{20,16},{24,28},{28,24},{1,5},{5... | collective-permute-start | bytes 1769480 | tf_op jit(solution)/shard_map/ppermute | solution.py:428
  416.2 18.7 %collective-permute-start.44 = (bf16[24,1536]{1,0:T(8,128)(2,1)S(1)}, bf16[24,1536]{1,0:T(8,128)(2,1)S(1)}, u32[]{:S(2)}, u32[]{:S(2)}) collective-permute-start(bf16[24,1536]{1,0:T(8,128)(2,1)S(1)} %constant_dynamic-slice_fusion), channel_id=1, source_target_pairs={{0,1},{1,0},{2,3},{3,2},{4,5},{5,4},{6,7},{7,6},{8,9},{9,8},{10,11... | collective-permute-start | bytes 221192 | tf_op jit(solution)/shard_map/ppermute | solution.py:399
  417.0 17.8 %copy-start.51 = (bf16[4,2,48,512]{3,2,1,0:T(8,128)(2,1)}, bf16[4,2,48,512]{3,2,1,0:T(8,128)(2,1)S(1)}, u32[]{:S(2)}) copy-start(bf16[4,2,48,512]{3,2,1,0:T(8,128)(2,1)S(1)} %fusion.36) | copy-start | bytes 1179652
  417.8 21.4 %collective-permute-start.36 = (bf16[4,48,512]{2,1,0:T(8,128)(2,1)}, bf16[4,48,512]{2,1,0:T(8,128)(2,1)}, u32[]{:S(2)}, u32[]{:S(2)}) collective-permute-start(bf16[4,48,512]{2,1,0:T(8,128)(2,1)} %dynamic-slice_bitcast_fusion.8), channel_id=1, source_target_pairs={{0,2},{2,0},{1,3},{3,1},{4,6},{6,4},{5,7},{7,5},{8,10},{10,8},{9,1... | collective-permute-start | bytes 589832 | tf_op jit(solution)/shard_map/ppermute | solution.py:399
  430.4 11.9 %collective-permute-start.32 = (bf16[48,1536]{1,0:T(8,128)(2,1)}, bf16[48,1536]{1,0:T(8,128)(2,1)}, u32[]{:S(2)}, u32[]{:S(2)}) collective-permute-start(bf16[48,1536]{1,0:T(8,128)(2,1)} %get-tuple-element.132), channel_id=1, source_target_pairs={{0,8},{4,12},{8,0},{12,4},{16,24},{20,28},{24,16},{28,20},{1,9},{5... | collective-permute-start | bytes 442376 | tf_op jit(solution)/shard_map/ppermute | solution.py:428
  431.6 12.1 %collective-permute-start.34 = (bf16[48,1536]{1,0:T(8,128)(2,1)}, bf16[48,1536]{1,0:T(8,128)(2,1)}, u32[]{:S(2)}, u32[]{:S(2)}) collective-permute-start(bf16[48,1536]{1,0:T(8,128)(2,1)} %get-tuple-element.133), channel_id=1, source_target_pairs={{0,24},{4,28},{8,16},{12,20},{16,8},{20,12},{24,0},{28,4},{1,25},{... | collective-permute-start | bytes 442376 | tf_op jit(solution)/shard_map/ppermute | solution.py:428
  432.9 15.6 %collective-permute-start.33 = (bf16[48,1536]{1,0:T(8,128)(2,1)}, bf16[48,1536]{1,0:T(8,128)(2,1)}, u32[]{:S(2)}, u32[]{:S(2)}) collective-permute-start(bf16[48,1536]{1,0:T(8,128)(2,1)} %get-tuple-element.134), channel_id=1, source_target_pairs={{0,16},{4,20},{8,24},{12,28},{16,0},{20,4},{24,8},{28,12},{1,17},{... | collective-permute-start | bytes 442376 | tf_op jit(solution)/shard_map/ppermute | solution.py:428
  434.8 17.7 %collective-permute-start.29 = (bf16[512,768]{1,0:T(8,128)(2,1)}, bf16[512,768]{1,0:T(8,128)(2,1)S(1)}, u32[]{:S(2)}, u32[]{:S(2)}) collective-permute-start(bf16[512,768]{1,0:T(8,128)(2,1)} %dynamic-slice_bitcast_fusion.1), channel_id=1, source_target_pairs={{0,2},{2,0},{1,3},{3,1},{4,6},{6,4},{5,7},{7,5},{8,10},{10,8},{9,1... | collective-permute-start | bytes 2359304 | tf_op jit(solution)/shard_map/ppermute | solution.py:399
  440.2 15.0 %collective-permute-start.37 = (bf16[48,512]{1,0:T(8,128)(2,1)S(1)}, bf16[48,512]{1,0:T(8,128)(2,1)S(1)}, u32[]{:S(2)}, u32[]{:S(2)}) collective-permute-start(bf16[48,512]{1,0:T(8,128)(2,1)S(1)} %get-tuple-element.155), channel_id=1, source_target_pairs={{0,8},{4,12},{8,0},{12,4},{16,24},{20,28},{24,16},{28,20},{1,9},{5... | collective-permute-start | bytes 147464 | tf_op jit(solution)/shard_map/ppermute | solution.py:428
  442.3 12.9 %collective-permute-start.39 = (bf16[48,512]{1,0:T(8,128)(2,1)S(1)}, bf16[48,512]{1,0:T(8,128)(2,1)S(1)}, u32[]{:S(2)}, u32[]{:S(2)}) collective-permute-start(bf16[48,512]{1,0:T(8,128)(2,1)S(1)} %get-tuple-element.156), channel_id=1, source_target_pairs={{0,24},{4,28},{8,16},{12,20},{16,8},{20,12},{24,0},{28,4},{1,25},{... | collective-permute-start | bytes 147464 | tf_op jit(solution)/shard_map/ppermute | solution.py:428
  443.7 11.5 %collective-permute-start.38 = (bf16[48,512]{1,0:T(8,128)(2,1)S(1)}, bf16[48,512]{1,0:T(8,128)(2,1)S(1)}, u32[]{:S(2)}, u32[]{:S(2)}) collective-permute-start(bf16[48,512]{1,0:T(8,128)(2,1)S(1)} %get-tuple-element.157), channel_id=1, source_target_pairs={{0,16},{4,20},{8,24},{12,28},{16,0},{20,4},{24,8},{28,12},{1,17},{... | collective-permute-start | bytes 147464 | tf_op jit(solution)/shard_map/ppermute | solution.py:428
  456.7 3.3 collective-permute-start.40
  (62 other events, 242.2 us)

commit v4 on v3

--- a/solution.py
+++ b/solution.py
@@ -92,8 +92,8 @@
         o_ref[rows, :] = jnp.concatenate(parts, axis=0).T.astype(BF16)
 
 
-def attention_backward_kernel(qkv_ref, qs_ref, ks_ref, o_ref, do_ref, lse_ref, *rest):
-    d_ref, tick_ref, qx, kx, qm, dm, kt, delta, dqt, dk, dv = rest[-11:]
+def attention_backward_kernel(qkv_ref, qs_ref, ks_ref, o_ref, do_ref, lse_ref, at_ref, *rest):
+    d_ref, dw_ref, tick_ref, qx, kx, qm, dm, kt, delta, dqt, dk, dv = rest[-12:]
     tick_ref[...] = jnp.zeros_like(tick_ref)
     length = qkv_ref.shape[0]
     blocks = length // BLK
@@ -153,6 +153,11 @@
         rows = pl.ds(pl.multiple_of(i * BLK, BLK), BLK)
         d_ref[rows, 0:PAIR] = (dqt[:, rows].T.astype(BF16).astype(F32) * 0.125).astype(BF16)
 
+    @pl.loop(0, dw_ref.shape[0] // ROWS)
+    def _(i):
+        rows = pl.ds(pl.multiple_of(i * ROWS, ROWS), ROWS)
+        dw_ref[rows, :] = mm(at_ref[rows, :], d_ref[...]).astype(BF16)
+
 
 VMEM_LIMIT = 48 * 1024 * 1024
 
@@ -180,73 +185,165 @@
     )(*after)
 
 
-def qkv_kernel(x_ref, w_ref, vec_ref, col_ref, a_ref, qkv_ref, tick_ref):
-    normal, _ = norm_forward(x_ref[...].astype(F32))
-    normed = (normal * vec_ref[0:1, :] + vec_ref[1:2, :]).astype(BF16)
-    a_ref[...] = normed
-    qkv_ref[...] = ((mm(normed, w_ref[...]) + col_ref[0:1, :]) * col_ref[1:2, :]).astype(BF16)
+def qkv_kernel(x_ref, wa_ref, wb_ref, vec_ref, col_ref, *rest_refs):
+    a_ref, qkv_ref, tick_ref = rest_refs[-3:]
+    split = wa_ref.shape[1]
+    rest = qkv_ref.shape[1] - split
+    for part in range(2):
+        rows = slice(part * ROWS, (part + 1) * ROWS)
+        normal, _ = norm_forward(x_ref[rows, :].astype(F32))
+        normed = (normal * vec_ref[0:1, :] + vec_ref[1:2, :]).astype(BF16)
+        a_ref[:, rows] = normed.astype(F32).T.astype(BF16)
+        for w, cols in ((wa_ref[...], slice(0, split)), (wb_ref[:, :rest], slice(split, None))):
+            shift, scale = col_ref[0:1, cols], col_ref[1:2, cols]
+            qkv_ref[rows, cols] = ((mm(normed, w) + shift) * scale).astype(BF16)
     tick_ref[...] = jnp.zeros_like(tick_ref)
 
 
-def qkv_projection(inputs, weight, vectors, columns):
+def qkv_projection(inputs, weight_a, weight_b, vectors, columns, after):
     length, width = inputs.shape
-    cols = weight.shape[1]
+    cols = columns.shape[1]
     return pl.pallas_call(
         qkv_kernel,
-        grid=(length // ROWS,),
+        grid=(length // (2 * ROWS),),
         in_specs=[
-            pl.BlockSpec((ROWS, width), lambda i: (i, 0)),
-            pl.BlockSpec((width, cols), lambda i: (0, 0)),
+            pl.BlockSpec((2 * ROWS, width), lambda i: (i, 0)),
+            pl.BlockSpec(weight_a.shape, lambda i: (0, 0)),
+            pl.BlockSpec(weight_b.shape, lambda i: (0, 0)),
             pl.BlockSpec(vectors.shape, lambda i: (0, 0)),
             pl.BlockSpec(columns.shape, lambda i: (0, 0)),
-        ],
+        ]
+        + [ANY_SPEC] * len(after),
         out_specs=[
-            pl.BlockSpec((ROWS, width), lambda i: (i, 0)),
-            pl.BlockSpec((ROWS, cols), lambda i: (i, 0)),
+            pl.BlockSpec((width, 2 * ROWS), lambda i: (0, i)),
+            pl.BlockSpec((2 * ROWS, cols), lambda i: (i, 0)),
             TICK_SPEC,
         ],
+        out_shape=[
+            jax.ShapeDtypeStruct((width, length), BF16),
+            jax.ShapeDtypeStruct((length, cols), BF16),
+            TICK,
+        ],
+        compiler_params=pltpu.CompilerParams(vmem_limit_bytes=VMEM_LIMIT),
+        cost_estimate=SMALL_COST,
+    )(inputs, weight_a, weight_b, vectors, columns, *after)
+
+
+def feed_forward_kernel(
+    x_ref, b0_ref, b1_ref, dy_ref, up_ref, down_ref, vec_ref, shift_ref,
+    a_ref, g_ref, du_ref, ffn_ref, dh_ref, sums_ref,
+):
+    @pl.when(pl.program_id(0) == 0)
+    def _():
+        sums_ref[...] = jnp.zeros_like(sums_ref)
+
+    middle = x_ref[...].astype(F32) + (b0_ref[...].astype(F32) + b1_ref[...].astype(F32)) + vec_ref[0:1, :]
+    normal, _ = norm_forward(middle)
+    normed = (normal * vec_ref[1:2, :] + vec_ref[2:3, :]).astype(BF16)
+    a_ref[...] = normed
+    dy = dy_ref[...]
+    ffn, dh = None, None
+    for at in range(0, up_ref.shape[1], HIDDEN):
+        cols = slice(at, at + HIDDEN)
+        up, down = up_ref[:, cols], down_ref[cols, :]
+        value, slope = gelu_parts(mm(normed, up) + shift_ref[0:1, cols])
+        du = slope * mm(dy, down, NT)
+        value, du = value.astype(BF16), du.astype(BF16)
+        g_ref[:, cols] = value
+        du_ref[:, cols] = du
+        sums_ref[0:1, cols] += jnp.sum(du.astype(F32), axis=0, keepdims=True)
+        ffn_part, dh_part = mm(value, down), mm(du, up, NT)
+        ffn = ffn_part if at == 0 else ffn + ffn_part
+        dh = dh_part if at == 0 else dh + dh_part
+    ffn_ref[...] = ffn.astype(BF16)
+    dh_ref[...] = dh.astype(BF16)
+
+
+HIDDEN = 512
+
+
+def feed_forward(inputs, branch, branch_come, grad_out, up, down, vectors, up_shift):
+    length, width = inputs.shape
+    hidden = up.shape[1]
+    narrow = pl.BlockSpec((ROWS, width), lambda i: (i, 0))
+    wide = pl.BlockSpec((ROWS, hidden), lambda i: (i, 0))
+
+    def whole(array):
+        return pl.BlockSpec(array.shape, lambda i: (0, 0))
+
+    return pl.pallas_call(
+        feed_forward_kernel,
+        grid=(length // ROWS,),
+        in_specs=[narrow] * 4 + [whole(up), whole(down), whole(vectors), whole(up_shift)],
+        out_specs=[narrow, wide, wide, narrow, narrow, pl.BlockSpec((8, hidden), lambda i: (0, 0))],
         out_shape=[
             jax.ShapeDtypeStruct((length, width), BF16),
-            jax.ShapeDtypeStruct((length, cols), BF16),
-            TICK,
+            jax.ShapeDtypeStruct((length, hidden), BF16),
+            jax.ShapeDtypeStruct((length, hidden), BF16),
+            jax.ShapeDtypeStruct((length, width), BF16),
+            jax.ShapeDtypeStruct((length, width), BF16),
+            jax.ShapeDtypeStruct((8, hidden), F32),
         ],
         compiler_params=pltpu.CompilerParams(vmem_limit_bytes=VMEM_LIMIT),
         cost_estimate=SMALL_COST,
-    )(inputs, weight, vectors, columns)
-
-
-ROWS = 256
-
-
-def norm_one_input_kernel(core_ref, mine_ref, come_ref, x_ref, mid_ref, vec_ref, out_ref, tick_ref):
-    grad = (mine_ref[...].astype(F32) + come_ref[...].astype(F32)) * vec_ref[0:1, :]
-    normal, scale = norm_forward(x_ref[...].astype(F32))
-    out_ref[...] = (mid_ref[...] + norm_backward(normal, scale, grad)).astype(BF16)
-    tick_ref[...] = jnp.zeros_like(tick_ref)
-
-
-def norm_one_input(core, partial, come, inputs, grad_middle, vectors):
+    )(inputs, branch, branch_come, grad_out, up, down, vectors, up_shift)
+
+
+def norm_two_kernel(
+    x_ref, b0_ref, b1_ref, dy_ref, p0_ref, p1_ref, w_ref, vec_ref, *rest
+):
+    mid_ref, low_ref, do_ref, sums_ref, tick_ref = rest[-5:]
+
+    @pl.when(pl.program_id(0) == 0)
+    def _():
+        sums_ref[...] = jnp.zeros_like(sums_ref)
+        tick_ref[...] = jnp.zeros_like(tick_ref)
+
+    middle = x_ref[...].astype(F32) + (b0_ref[...].astype(F32) + b1_ref[...].astype(F32)) + vec_ref[0:1, :]
+    normal, scale = norm_forward(middle)
+    grad = p0_ref[...].astype(F32) + p1_ref[...].astype(F32)
+    dy = dy_ref[...].astype(F32)
+    mid = dy + norm_backward(normal, scale, grad * vec_ref[1:2, :])
+    low = mid.astype(BF16)
+    mid_ref[...] = mid
+    low_ref[...] = low
+    do_ref[...] = mm(low, w_ref[...], NT).astype(BF16)
+    for i, value in enumerate((low.astype(F32), grad * normal, grad, dy)):
+        sums_ref[i : i + 1, :] += jnp.sum(value, axis=0, keepdims=True)
+
+
+def norm_two(inputs, branch, branch_come, grad_out, partial, partial_come, weight, vectors, after):
     length, width = inputs.shape
-    count = come.shape[0] // ROWS
-    per = count // 2
-
-    def own_block(i, core_ref):
-        return ((i // per) * 2 + core_ref[0]) * per + i % per, 0
-
-    own = pl.BlockSpec((ROWS, width), own_block)
-    plain = pl.BlockSpec((ROWS, width), lambda i, core_ref: (i, 0))
+    cols = weight.shape[0]
+    narrow = pl.BlockSpec((ROWS, width), lambda i: (i, 0))
+
+    def whole(array):
+        return pl.BlockSpec(array.shape, lambda i: (0, 0))
+
     return pl.pallas_call(
-        norm_one_input_kernel,
-        grid_spec=pltpu.PrefetchScalarGridSpec(
-            num_scalar_prefetch=1,
-            grid=(count,),
-            in_specs=[own, plain, own, own, pl.BlockSpec(vectors.shape, lambda i, core_ref: (0, 0))],
-            out_specs=[plain, pl.BlockSpec((8, 128), lambda i, core_ref: (0, 0))],
-        ),
-        out_shape=[jax.ShapeDtypeStruct((count * ROWS, width), BF16), TICK],
+        norm_two_kernel,
+        grid=(length // ROWS,),
+        in_specs=[narrow] * 6 + [whole(weight), whole(vectors)] + [ANY_SPEC] * len(after),
+        out_specs=[
+            narrow,
+            narrow,
+            pl.BlockSpec((ROWS, cols), lambda i: (i, 0)),
+            pl.BlockSpec((8, width), lambda i: (0, 0)),
+            TICK_SPEC,
+        ],
+        out_shape=[
+            jax.ShapeDtypeStruct((length, width), F32),
+            jax.ShapeDtypeStruct((length, width), BF16),
+            jax.ShapeDtypeStruct((length, cols), BF16),
+            jax.ShapeDtypeStruct((8, width), F32),
+            TICK,
+        ],
         compiler_params=pltpu.CompilerParams(vmem_limit_bytes=VMEM_LIMIT),
         cost_estimate=SMALL_COST,
-    )(core.reshape(1).astype(jnp.int32), partial, come, inputs, grad_middle, vectors)
+    )(inputs, branch, branch_come, grad_out, partial, partial_come, weight, vectors, *after)
+
+
+ROWS = 256
 
 
 def attention_forward(pair, qkv, query_code, key_code, after):
@@ -281,59 +378,94 @@
     )(qkv, query_code, key_code, *after)
 
 
-def norm_one_grad_kernel(d0_ref, d1_ref, d2_ref, w_ref, x_ref, *rest):
-    out_ref, sums_ref, bias_ref, tick_ref = rest[-4:]
+def norm_one_kernel(own, core_ref, d0_ref, d1_ref, d2_ref, wa_ref, wb_ref, x_ref, *rest):
+    if own:
+        come_ref, mid_ref, vec_ref, out_ref, sums_ref, bias_ref, tick_ref, w = rest
+    else:
+        out_ref, sums_ref, bias_ref, tick_ref, w = rest
+    split = wa_ref.shape[1]
 
     @pl.when(pl.program_id(0) == 0)
     def _():
         sums_ref[...] = jnp.zeros_like(sums_ref)
         bias_ref[...] = jnp.zeros_like(bias_ref)
+        w[:, :split] = wa_ref[...]
+        w[:, split:] = wb_ref[:, : w.shape[1] - split]
         tick_ref[...] = jnp.zeros_like(tick_ref)
 
     total = None
     for i, ref in enumerate((d0_ref, d1_ref, d2_ref)):
         cols = slice(i * 3 * PAIR, (i + 1) * 3 * PAIR)
         grad = ref[...]
-        part = mm(grad, w_ref[:, cols], NT)
+        part = mm(grad, w[:, cols], NT)
         total = part if i == 0 else total + part
         bias_ref[0:1, cols] += jnp.sum(grad.astype(F32), axis=0, keepdims=True)
-    normal, _ = norm_forward(x_ref[...].astype(F32))
+    normal, scale = norm_forward(x_ref[...].astype(F32))
     sums_ref[0:1, :] += jnp.sum(total * normal, axis=0, keepdims=True)
     sums_ref[1:2, :] += jnp.sum(total, axis=0, keepdims=True)
-    out_ref[...] = total.astype(BF16)
-
-
-def norm_one_grad(grads, weight, inputs, after):
+    if own:
+        grad = (total + come_ref[...].astype(F32)) * vec_ref[0:1, :]
+        out_ref[...] = (mid_ref[...] + norm_backward(normal, scale, grad)).astype(BF16)
+    else:
+        out_ref[...] = total.astype(BF16)
+
+
+def norm_one(own, core, grads, weight_a, weight_b, cols, inputs, extra, after):
     length, width = inputs.shape
-    cols = weight.shape[1]
-    block = pl.BlockSpec((ROWS, 3 * PAIR), lambda i: (i, 0))
+    count = length // (2 * ROWS)
+    per = count // 2
+
+    def block(i, core_ref):
+        which = core_ref[0] if own else 1 - core_ref[0]
+        return ((i // per) * 2 + which) * per + i % per, 0
+
+    def at_zero(i, core_ref):
+        return 0, 0
+
+    plain = pl.BlockSpec((ROWS, width), lambda i, core_ref: (i, 0))
+    rows = pl.BlockSpec((ROWS, width), block)
+    in_specs = [pl.BlockSpec((ROWS, 3 * PAIR), block)] * 3 + [
+        pl.BlockSpec(weight_a.shape, at_zero),
+        pl.BlockSpec(weight_b.shape, at_zero),
+        rows,
+    ]
+    out_specs = [
+        plain,
+        pl.BlockSpec((8, width), at_zero),
+        pl.BlockSpec((8, cols), at_zero),
+        pl.BlockSpec((8, 128), at_zero),
+    ]
+    out_shape = [
+        jax.ShapeDtypeStruct((count * ROWS, width), BF16),
+        jax.ShapeDtypeStruct((8, width), F32),
+        jax.ShapeDtypeStruct((8, cols), F32),
+        TICK,
+    ]
+    if own:
+        in_specs += [plain, rows, pl.BlockSpec(extra[2].shape, at_zero)]
+
+    def kernel(*refs):
+        inner = refs[: 1 + len(in_specs)] + refs[1 + len(in_specs) + len(after) :]
+        norm_one_kernel(own, *inner)
+
     return pl.pallas_call(
-        norm_one_grad_kernel,
-        grid=(length // ROWS,),
-        in_specs=[block] * 3
-        + [
-            pl.BlockSpec((width, cols), lambda i: (0, 0)),
-            pl.BlockSpec((ROWS, width), lambda i: (i, 0)),
-        ]
-        + [pl.BlockSpec(memory_space=pl.ANY)] * len(after),
-        out_specs=[
-            pl.BlockSpec((ROWS, width), lambda i: (i, 0)),
-            pl.BlockSpec((8, width), lambda i: (0, 0)),
-            pl.BlockSpec((8, cols), lambda i: (0, 0)),
-            TICK_SPEC,
-        ],
-        out_shape=[
-            jax.ShapeDtypeStruct((length, width), BF16),
-            jax.ShapeDtypeStruct((8, width), F32),
-            jax.ShapeDtypeStruct((8, cols), F32),
-            TICK,
-        ],
+        kernel,
+        grid_spec=pltpu.PrefetchScalarGridSpec(
+            num_scalar_prefetch=1,
+            grid=(count,),
+            in_specs=in_specs + [ANY_SPEC] * len(after),
+            out_specs=out_specs,
+            scratch_shapes=[pltpu.VMEM((width, cols), BF16)],
+        ),
+        out_shape=out_shape,
         compiler_params=pltpu.CompilerParams(vmem_limit_bytes=VMEM_LIMIT),
         cost_estimate=SMALL_COST,
-    )(*grads, weight, inputs, *after)
-
-
-def attention_backward(pair, qkv, query_code, key_code, attended, grad_attended, log_total, after):
+    )(core.reshape(1).astype(jnp.int32), *grads, weight_a, weight_b, inputs, *extra, *after)
+
+
+def attention_backward(
+    pair, qkv, query_code, key_code, attended, grad_attended, log_total, normed_t, after
+):
     length = qkv.shape[0]
     return pl.pallas_call(
         attention_backward_kernel,
@@ -345,10 +477,19 @@
             pl.BlockSpec((length, PAIR), lambda p: (0, 0)),
             pl.BlockSpec((length, PAIR), lambda p: (0, pair)),
             pl.BlockSpec((1, 8, length), lambda p: (0, 0, 0)),
+            pl.BlockSpec(normed_t.shape, lambda p: (0, 0)),
         ]
         + [pl.BlockSpec(memory_space=pl.ANY)] * len(after),
-        out_specs=[pl.BlockSpec((length, 3 * PAIR), lambda p: (0, 0)), TICK_SPEC],
-        out_shape=[jax.ShapeDtypeStruct((length, 3 * PAIR), BF16), TICK],
+        out_specs=[
+            pl.BlockSpec((length, 3 * PAIR), lambda p: (0, 0)),
+            pl.BlockSpec((normed_t.shape[0], 3 * PAIR), lambda p: (0, 0)),
+            TICK_SPEC,
+        ],
+        out_shape=[
+            jax.ShapeDtypeStruct((length, 3 * PAIR), BF16),
+            jax.ShapeDtypeStruct((normed_t.shape[0], 3 * PAIR), BF16),
+            TICK,
+        ],
         scratch_shapes=[
             pltpu.VMEM((2, length, PAIR), BF16),
             pltpu.VMEM((2, length, PAIR), BF16),
@@ -362,7 +503,7 @@
         ],
         compiler_params=pltpu.CompilerParams(vmem_limit_bytes=VMEM_LIMIT),
         cost_estimate=SMALL_COST,
-    )(qkv, query_code, key_code, attended, grad_attended, log_total, *after)
+    )(qkv, query_code, key_code, attended, grad_attended, log_total, normed_t, *after)
 
 
 def norm_forward(source):
@@ -430,20 +571,36 @@
     def place(self, d):
         return self.side if d == "x" else self.groups[d][2]
 
-    def reduce(self, state, d, tick=None):
+    def begin_reduce(self, state, d):
         array, dims = state
         axis, at = dims.index(d), self.place(d)
-        total = lax.dynamic_index_in_dim(array, at, axis, keepdims=False).astype(F32)
-        for mask in range(1, array.shape[axis]):
-            block = lax.dynamic_index_in_dim(array, at ^ mask, axis, keepdims=False)
-            total = total + self.send(block, d, mask).astype(F32)
+        kept = lax.dynamic_index_in_dim(array, at, axis, keepdims=False)
+        come = [
+            self.send(lax.dynamic_index_in_dim(array, at ^ mask, axis, keepdims=False), d, mask)
+            for mask in range(1, array.shape[axis])
+        ]
+        return kept, come, [other for other in dims if other != d]
+
+    def end_reduce(self, begun, tick=None):
+        kept, come, dims = begun
+        total = kept.astype(F32)
+        for block in come:
+            total = total + block.astype(F32)
         if tick is not None:
             total = total + tick[0, 0]
-        return total.astype(BF16), [other for other in dims if other != d]
-
-    def gather(self, state, d, tick=None):
+        return total.astype(BF16), dims
+
+    def reduce(self, state, d, tick=None):
+        return self.end_reduce(self.begin_reduce(state, d), tick)
+
+    def begin_gather(self, state, d):
         array, dims = state
-        parts = [array] + [self.send(array, d, mask) for mask in range(1, self.counts([d])[0])]
+        come = [self.send(array, d, mask) for mask in range(1, self.counts([d])[0])]
+        return array, come, dims, d
+
+    def end_gather(self, begun, tick=None):
+        array, come, dims, d = begun
+        parts = [array] + come
         for bit in range(len(parts).bit_length() - 1):
             flag = (self.place(d) >> bit) & 1
             for low in range(len(parts)):
@@ -455,6 +612,12 @@
         if tick is not None:
             joined = joined + tick[0, 0].astype(joined.dtype)
         return joined, dims
+
+    def gather(self, state, d, tick=None):
+        return self.end_gather(self.begin_gather(state, d), tick)
+
+    def settle(self, tick, *stages):
+        return gate([tick] + [block for stage in stages for block in stage[1]])
 
     def rows(self, array, lead=()):
         shape = list(lead) + self.counts(self.dims)
@@ -510,7 +673,7 @@
         mine = jnp.stack([low, high])
         other = swap(mine, "core")
         even, odd = pick(core, mine, other)
-        return jnp.stack([even, odd], axis=1).reshape(length, width), come
+        return jnp.stack([even, odd], axis=1).reshape(length, width), come, other
 
     def own_rows(array):
         return lax.dynamic_index_in_dim(
@@ -524,8 +687,13 @@
 
     def from_sequence(mine):
         come = swap(at_index(mine, 1 - side), "xx")
-        first, second = pick(side, at_index(mine, side), come)
-        return jnp.stack([first, second]), come
+        return merged(at_index(mine, side), come), come
+
+    def merged(kept, come, tick=None):
+        if tick is not None:
+            kept = kept + tick[0, 0].astype(kept.dtype)
+        first, second = pick(side, kept, come)
+        return jnp.stack([first, second])
 
     qkv_cols = qkv_weight.reshape(own, 3, 2, pairs, PAIR).transpose(2, 0, 3, 1, 4).reshape(2, own, cols)
     up_cols = (
@@ -569,20 +737,26 @@
     def joined(halves):
         return [half_state[0].reshape(width, -1) for half_state in halves]
 
-    inputs_low, come = to_sequence(tokens)
-    grad_out_low, _ = to_sequence(cotangent, gate([come]))
-    early_halves = [
-        links.gather(links.gather(piece, order[0]), order[1])
-        for piece, order in zip(halves_of(gather_rest(early)), ("yx", "xy"))
+    inputs_low, come, other = to_sequence(tokens)
+    grad_out_low, _, _ = to_sequence(cotangent, gate([come]))
+    begun = [
+        links.begin_gather(piece, d) for piece, d in zip(halves_of(gather_rest(early)), "yx")
     ]
-    early = jnp.concatenate(joined(early_halves), axis=1)
+    late_tick = gate([block for piece in begun for block in piece[1]] + [other])
+    early_halves = [links.end_gather(piece, late_tick) for piece in begun]
+    early_a, early_b = joined(
+        [links.gather(piece, d) for piece, d in zip(early_halves, "xy")]
+    )
+    split = early_a.shape[1]
     late = with_partner(
         jnp.concatenate([up_cols, jnp.broadcast_to(out_weight, (2, own, width))], axis=2)
     )
     down_own = down_weight.reshape(splits, pair_row, width)
     late = jnp.concatenate([late] + [down_own[i] for i in range(splits)], axis=1)
-    proj_qkv = early[:, :cols]
-    small = early[:, cols:].astype(F32).T
+    late = late + late_tick[0, 0].astype(BF16)
+    late_one, late_two = halves_of((late, []))
+    late_one = gather_rest(late_one[0])
+    small = early_b[:, cols - split :].astype(F32).T
     gain_one, shift_one, query_shift, value_shift, out_shift, gain_two, shift_two, down_shift = (
         small[i] for i in range(8)
     )
@@ -604,28 +778,37 @@
         [head_cols(query_shift), zeros, head_cols(value_shift)], axis=1
     ).reshape(1, cols)
     qkv_scale = jnp.tile(jnp.repeat(jnp.array([0.125, 1.0, 1.0], F32), PAIR), pairs)[None]
-    normed_low, qkv, tick = qkv_projection(
+    normed_t, qkv, tick = qkv_projection(
         inputs_low,
-        proj_qkv,
+        early_a,
+        early_b,
         jnp.pad(jnp.stack([gain_one, shift_one]), ((0, 6), (0, 0))),
         jnp.pad(jnp.concatenate([qkv_shift, qkv_scale]), ((0, 6), (0, 0))),
+        [late_one[0]],
     )
     attended_pairs, log_totals = [], []
-    late_halves = halves_of(gather_rest(late, tick))
+    for d in links.rest[:-1]:
+        late_two = links.gather(late_two, d)
+    begun = links.begin_gather(late_two, links.rest[-1])
+    stage_one = links.begin_gather(late_one, "x")
+    late_two = links.end_gather(begun, links.settle(tick, begun))
+    stage_two = links.begin_gather(late_two, "y")
+    after = [late_two[0]]
     for pair in range(pairs):
-        if pair == 0:
-            after = [piece[0] for piece in late_halves]
-        else:
-            after = [attended_pairs[-1]]
-        if pair == 1:
-            late_halves = [links.gather(piece, d, tick) for piece, d in zip(late_halves, "xy")]
-            after += [piece[0] for piece in late_halves]
         one_pair = attention_forward(pair, qkv, query_code, key_code, after)
         attended_pairs.append(one_pair[0])
         log_totals.append(one_pair[1])
         tick = one_pair[2]
+        after = [one_pair[0]]
+        if pair == 0:
+            tick = links.settle(tick, stage_one, stage_two)
+            late_one, late_two = links.end_gather(stage_one, tick), links.end_gather(stage_two, tick)
+            after += [late_one[0], late_two[0]]
+            stage_one = links.begin_gather(late_one, "y")
+            stage_two = links.begin_gather(late_two, "x")
     attended = jnp.concatenate(attended_pairs, axis=1)
-    late_halves = joined([links.gather(piece, d, tick) for piece, d in zip(late_halves, "yx")])
+    tick = links.settle(tick, stage_one, stage_two)
+    late_halves = joined([links.end_gather(stage, tick) for stage in (stage_one, stage_two)])
     late = jnp.concatenate(late_halves, axis=1)
     proj_up = late[:, :hidden]
     proj_out = lax.dynamic_slice_in_dim(late[:, hidden : hidden + width], core * half, half, 0)
@@ -634,28 +817,40 @@
     )
 
     branch = mm(attended, proj_out).astype(BF16)
-    middle = inputs + (branch.astype(F32) + swap(branch, "core").astype(F32)) + out_shift
-    normal_two, scale_two = norm_forward(middle)
-    normed_two_low = (normal_two * gain_two + shift_two).astype(BF16)
-    hidden_value, hidden_slope = gelu_parts(mm(normed_two_low, proj_up) + up_shift)
-    hidden_low = hidden_value.astype(BF16)
-    ffn = mm(hidden_low, proj_down)
-    ffn_own = own_rows(ffn) + swap(other_rows(ffn).astype(BF16), "core").astype(F32)
-    mixed, _ = from_sequence((own_rows(middle) + ffn_own + down_shift).astype(BF16))
-
-    grad_mixed = grad_out_low.astype(F32)
-    grad_hidden = mm(grad_out_low, proj_down, NT)
-    grad_pre_low = (hidden_slope * grad_hidden).astype(BF16)
+    branch_come = swap(branch, "core")
+    mid_vectors = jnp.pad(jnp.stack([out_shift, gain_two, shift_two]), ((0, 5), (0, 0)))
+    normed_two_low, hidden_low, grad_pre_low, ffn, partial_two, up_sums = feed_forward(
+        inputs_low,
+        branch,
+        branch_come,
+        grad_out_low,
+        proj_up,
+        proj_down,
+        mid_vectors,
+        jnp.pad(up_shift[None], ((0, 7), (0, 0))),
+    )
+    partial_come = swap(partial_two, "core")
+    middle_own = own_rows(inputs_low).astype(F32) + (
+        own_rows(branch).astype(F32) + own_rows(branch_come).astype(F32)
+    )
+
     grad_proj_down = [
-        mm(hidden_low[:, i * width : (i + 1) * width], grad_out_low, TN) for i in range(splits)
+        mm(hidden_low[:, i * width : (i + 1) * width], grad_out_low, TN).astype(BF16)
+        for i in range(splits)
     ]
-    grad_proj_up = mm(normed_two_low, grad_pre_low, TN)
-    partial_two = mm(grad_pre_low, proj_up, NT).astype(BF16)
-    grad_normed_two = partial_two.astype(F32) + swap(partial_two, "core").astype(F32)
-    grad_middle = grad_mixed + norm_backward(normal_two, scale_two, grad_normed_two * gain_two)
-    branch_low = grad_middle.astype(BF16)
+    grad_proj_up = mm(normed_two_low, grad_pre_low, TN).astype(BF16)
+    grad_middle, branch_low, grad_attended, mid_sums, tick = norm_two(
+        inputs_low,
+        branch,
+        branch_come,
+        grad_out_low,
+        partial_two,
+        partial_come,
+        proj_out,
+        mid_vectors,
+        [*grad_proj_down, grad_proj_up],
+    )
     grad_proj_out = mm(attended, branch_low, TN)
-    grad_attended = mm(branch_low, proj_out, NT).astype(BF16)
 
     def as_column(vectors):
         table = jnp.stack(vectors, axis=1)
@@ -664,36 +859,27 @@
     def only_mine(flag, array):
         return jnp.where(flag, array, jnp.zeros_like(array))
 
-    small_two = (
-        [
-            jnp.sum(branch_low.astype(F32), axis=0),
-            jnp.sum(grad_normed_two * normal_two, axis=0),
-            jnp.sum(grad_normed_two, axis=0),
-            jnp.sum(grad_mixed, axis=0),
-        ]
-        + [
-            jnp.sum(grad_pre_low[:, i * width : (i + 1) * width].astype(F32), axis=0)
-            for i in range(splits)
-        ]
-    )
+    small_two = [mid_sums[i] for i in range(4)] + [
+        up_sums[0, i * width : (i + 1) * width] for i in range(splits)
+    ]
     down_piece = links.rows(
-        jnp.concatenate([part.astype(BF16) for part in grad_proj_down], axis=0), (splits,)
-    )
-    up_piece = links.rows(grad_proj_up.astype(BF16))
+        jnp.concatenate(grad_proj_down, axis=0) + tick[0, 0].astype(BF16), (splits,)
+    )
+    up_piece = links.rows(grad_proj_up + tick[0, 0].astype(BF16))
+    ffn_come = swap(other_rows(ffn) + tick[0, 0].astype(BF16), "core")
     out_low = grad_proj_out.astype(BF16)
     grad_out_rows = jnp.concatenate(
         [only_mine(core == 0, out_low), only_mine(core == 1, out_low)], axis=0
     )
 
-    def reduce_rest(piece, tick=None):
-        for d in links.rest:
-            piece = links.reduce(piece, d, tick if d == links.rest[0] else None)
+    def reduce_rest(piece, start=0):
+        for d in links.rest[start:]:
+            piece = links.reduce(piece, d)
         return piece
 
-    grads, weight_grads, tick = [], [grad_out_rows], None
-    after = [mixed]
+    grads, weight_grads, after = [], [], [down_piece[0], up_piece[0]]
     for pair in range(pairs):
-        grad, tick = attention_backward(
+        grad, weight_grad, tick = attention_backward(
             pair,
             qkv,
             query_code,
@@ -701,29 +887,65 @@
             attended_pairs[pair],
             grad_attended,
             log_totals[pair],
+            normed_t,
             after + grads[-1:],
         )
         grads.append(grad)
+        weight_grads.append(weight_grad)
         if pair == 0:
-            down_piece = links.reduce(down_piece, "x", tick)
-            up_piece = links.reduce(up_piece, "y", tick)
+            begun = [links.begin_reduce(down_piece, "x"), links.begin_reduce(up_piece, "y")]
+            tick = links.settle(tick, *begun, (None, [ffn_come]))
+            down_piece, up_piece = [links.end_reduce(piece, tick) for piece in begun]
+            first_piece = links.rows(
+                jnp.concatenate([grad_out_rows, weight_grad], axis=1) + tick[0, 0].astype(BF16)
+            )
+            after = [down_piece[0], up_piece[0], first_piece[0]]
+        elif pair == 1:
+            begun = [
+                links.begin_reduce(down_piece, links.rest[0]),
+                links.begin_reduce(up_piece, "x"),
+                links.begin_reduce(first_piece, "y"),
+            ]
+            tick = links.settle(tick, *begun)
+            ffn_own = own_rows(ffn).astype(F32) + ffn_come.astype(F32)
+            mixed_own = (middle_own + out_shift + ffn_own + down_shift + tick[0, 0]).astype(BF16)
+            mixed_come = swap(at_index(mixed_own, 1 - side), "xx")
+            down_piece, up_piece, first_piece = [links.end_reduce(piece, tick) for piece in begun]
+            down_piece = reduce_rest(down_piece, 1)
+            after = [down_piece[0], up_piece[0], first_piece[0]]
+        else:
+            begun = [
+                links.begin_reduce(down_piece, "y"),
+                links.begin_reduce(up_piece, links.rest[0]),
+            ]
+            tick = links.settle(tick, *begun, (None, [mixed_come]))
+            mixed = merged(at_index(mixed_own, side), mixed_come, tick)
+            down_piece, up_piece = [links.end_reduce(piece, tick) for piece in begun]
+            up_piece = reduce_rest(up_piece, 1)
             after = [down_piece[0], up_piece[0]]
-        elif pair == 1:
-            down_piece = links.reduce(down_piece, "y", tick)
-            up_piece = links.reduce(up_piece, "x", tick)
-            after = [down_piece[0], up_piece[0]]
-        if pair < pairs - 1:
-            weight_grads.append(mm(normed_low, grad, TN).astype(BF16))
-    first_piece = links.rows(jnp.concatenate(weight_grads, axis=1))
-    partial_one, norm_sums, bias_sums, tick = norm_one_grad(grads, proj_qkv, inputs_low, [])
-    first_piece = links.reduce(first_piece, "x", tick)
-    come = swap(other_rows(partial_one), "core").reshape(2 * quarter, width)
+    first_piece = (first_piece[0] + tick[0, 0].astype(BF16), first_piece[1])
+    begun = [
+        links.begin_reduce(first_piece, "x"),
+        links.begin_reduce(links.rows(weight_grads[1] + tick[0, 0].astype(BF16)), "y"),
+    ]
     norm_vectors = jnp.pad(jnp.stack([gain_one, shift_one]), ((0, 6), (0, 0)))
-    token_own, tick = norm_one_input(
-        core, partial_one, come, inputs_low, grad_middle, norm_vectors
-    )
-    down_piece = reduce_rest(down_piece, tick)
-    up_piece = reduce_rest(up_piece, tick)
+    partial_one, norm_sums, bias_sums, _ = norm_one(
+        False, core, grads, early_a, early_b, cols, inputs_low, [], after
+    )
+    come = swap(partial_one, "core")
+    token_own, norm_sums_own, bias_sums_own, tick = norm_one(
+        True,
+        core,
+        grads,
+        early_a,
+        early_b,
+        cols,
+        inputs_low,
+        [come, grad_middle, norm_vectors],
+        [],
+    )
+    norm_sums = norm_sums + norm_sums_own
+    bias_sums = bias_sums + bias_sums_own
     token_grad, come = from_sequence(token_own.reshape(2, quarter, width))
     grad_by_pair = bias_sums[0].reshape(pairs, 3, PAIR)
 
@@ -740,12 +962,17 @@
         ]
         + small_two
     )
-    last_piece = links.rows(
-        jnp.concatenate([mm(normed_low, grads[-1], TN).astype(BF16), small.astype(BF16)], axis=1)
-    )
-    last_piece = links.reduce(links.reduce(last_piece, "y", tick), "x")
-    last_own = reduce_rest(last_piece, gate([come]))[0]
-    first_own = reduce_rest(links.reduce(first_piece, "y", tick))[0]
+    tick = links.settle(tick, *begun)
+    first_piece, middle_piece = [links.end_reduce(piece, tick) for piece in begun]
+    begun = links.begin_reduce(first_piece, links.rest[0])
+    first_own = reduce_rest(links.end_reduce(begun), 1)[0]
+    last_piece = links.reduce(
+        links.rows(jnp.concatenate([weight_grads[2], small.astype(BF16)], axis=1)), "y"
+    )
+    last_piece = (jnp.concatenate([middle_piece[0], last_piece[0]], axis=-1), last_piece[1])
+    begun = links.begin_reduce(links.reduce(last_piece, "x"), links.rest[0])
+    tick = links.settle(tick, begun, (None, [come]))
+    last_own = reduce_rest(links.end_reduce(begun, tick), 1)[0]
 
     def rows_of(array, index):
         return lax.dynamic_slice_in_dim(array, index * own, own, 0)
@@ -774,11 +1001,11 @@
         .reshape(own, 2 * cols)
         .astype(F32)
     )
-    tail = width + cols
-    small_mine = early_mine[:, tail : tail + 8].astype(F32)
-    one = small_mine[:, :4] + early_come[:, tail : tail + 4].astype(F32)
+    tail, first = width + cols + 8, first_own.shape[1]
+    small_mine = early_mine[:, tail - 8 : tail].astype(F32)
+    one = small_mine[:, :4] + early_come[:, tail - 8 : tail - 4].astype(F32)
     up_shift_grad = (
-        last_own[:, cols // pairs + 8 : cols // pairs + 8 + splits].T.reshape(hidden_own).astype(F32)
+        last_own[:, tail - first : tail - first + splits].T.reshape(hidden_own).astype(F32)
     )
     two = small_mine[:, 4:]
     return (

time: 470 us -> 498 us (1.060)
  matrix products: 73.6 us -> 20.2 us
  Pallas kernels: 125 us -> 178 us
  local copies, waits for them, and re-layouts: 55.5 us -> 89.2 us
  waiting for transfers between devices: 85 us -> 55.8 us
  other arithmetic: 71.9 us -> 83.5 us
  starting transfers between devices: 49.1 us -> 58.5 us
    dot_general x13 -> x5, matrix products: 73.6 us -> 20.2 us  [mm(): return lax.dot_general(left, right, dims, preferred_element_type=F32)]
    pallas_call x3 -> x5, Pallas kernels: 26.3 us -> 66.2 us  [the longest x1 31 us: feed_forward(): pl.pallas_call(feed_forward_kernel, grid=(length // ROWS,), in_specs=[nar...]
    ppermute x26 -> x30, waiting for transfers between devices: 46.3 us -> 29.2 us  [send(): return lax.ppermute(value, 'dp', [(i, i ^ move) for i in range(self.size)])]
    reduce_sum x7 -> x0, other arithmetic: 17.1 us -> none  [the longest x1 5.03 us: body(): jnp.sum(branch_low.astype(F32), axis=0)]
    unnamed x160 -> x310, local copies, waits for them, and re-layouts: 15.2 us -> 29.2 us
    ppermute x0 -> x8, local copies, waits for them, and re-layouts: none -> 13.1 us  [the longest x7 10.7 us: send(): return lax.ppermute(value, 'dp', [(i, i ^ move) for i in range(self.size)])]
    add x6 -> x15, other arithmetic: 6.91 us -> 19.1 us  [the longest x7 12.7 us: end_gather(): joined = joined + tick[0, 0].astype(joined.dtype)]
    ppermute x22, waiting for transfers between devices: 38.7 us -> 26.6 us  [swap(): return lax.ppermute(value, axis, [(0, 1), (1, 0)])]
  transfers between devices with their start and end apart: 48 -> 52, of which waited for: 18 -> 12; matrix products, arithmetic and copies ran while one was open for 26% -> 27% of each run, Pallas kernels for 25% -> 26%
where the time goes in v4:
time: 498 us; the launch traced here: 490 us
  Pallas kernels  178 us (36%)
  local copies, waits for them, and re-layouts  89.2 us (18%)
  other arithmetic  83.5 us (17%)
  starting transfers between devices  58.5 us (12%)
  waiting for transfers between devices  55.8 us (11%)
  matrix products  20.2 us (4%)
    pallas_call x3, Pallas kernels, attention_backward(): pl.pallas_call(attention_backward_kernel, grid=(1,), in_specs=[pl.BlockSp...  65.5 us
    ppermute x30, starting transfers between devices, send(): return lax.ppermute(value, 'dp', [(i, i ^ move) for i in range(self.size)])  42.5 us
    pallas_call x3, Pallas kernels, attention_forward(): pl.pallas_call(attention_forward_kernel, grid=(1,), in_specs=[pl.BlockSpe...  40.3 us
    pallas_call x1, Pallas kernels, feed_forward(): pl.pallas_call(feed_forward_kernel, grid=(length // ROWS,), in_specs=[nar...  31 us
    unnamed x310, local copies, waits for them, and re-layouts  29.2 us
    ppermute x30, waiting for transfers between devices, send(): return lax.ppermute(value, 'dp', [(i, i ^ move) for i in range(self.size)])  29.2 us
    ppermute x22, waiting for transfers between devices, swap(): return lax.ppermute(value, axis, [(0, 1), (1, 0)])  26.6 us
    dot_general x5, matrix products, mm(): return lax.dot_general(left, right, dims, preferred_element_type=F32)  20.2 us
  transfers between devices with their start and end apart: 52, of which 12 were waited for; matrix products, arithmetic and copies ran while one was open for 27% of the time, Pallas kernels for 26%

profile of v4, /device:TPU:0, one launch (start us, length us, event | category | flops | bytes accessed | tf_op | source)
XLA Modules:
  0.0 489.6 jit_solution(931763719512724861)
XLA Ops:
  4.5 2.6 collective-permute-start
  12.4 1.6 collective-permute-start.3
  14.0 2.6 collective-permute-start.4
  16.8 8.5 %collective-permute-done.refs_0_ = bf16[512,768]{1,0:T(8,128)(2,1)S(1)} collective-permute-done((bf16[512,768]{1,0:T(8,128)(2,1)S(1)}, bf16[512,768]{1,0:T(8,128)(2,1)S(1)}, u32[]{:S(2)}, u32[]{:S(2)}) %collective-permute-start) | collective-permute-done | bytes 786464 | tf_op jit(solution)/shard_map/ppermute | solution.py:540
  27.3 1.8 collective-permute-start.6
  32.2 3.5 collective-permute-done.6.refs_0_
  42.0 1.6 collective-permute-start.14
  43.7 2.6 collective-permute-start.15
  46.5 1.8 maximum_add_fusion.7
  52.1 8.0 %collective-permute-done.15.refs_2_ = bf16[48,1920]{1,0:T(8,128)(2,1)S(1)} collective-permute-done((bf16[48,1920]{1,0:T(8,128)(2,1)S(1)}, bf16[48,1920]{1,0:T(8,128)(2,1)S(1)}, u32[]{:S(2)}, u32[]{:S(2)}) %collective-permute-start.15) | collective-permute-done | bytes 184352 | tf_op jit(solution)/shard_map/ppermute | solution.py:569
  60.2 2.7 collective-permute-start.11
  65.7 1.9 copy.193
  68.7 9.6 %collective-permute-done.12 = bf16[48,1920]{1,0:T(8,128)(2,1)S(1)} collective-permute-done((bf16[48,1920]{1,0:T(8,128)(2,1)S(1)}, bf16[48,1920]{1,0:T(8,128)(2,1)S(1)}, u32[]{:S(2)}, u32[]{:S(2)}) %collective-permute-start.12) | collective-permute-done | bytes 184352 | tf_op jit(solution)/shard_map/ppermute | solution.py:569
  82.7 1.8 select_bitcast_fusion.14
  85.2 8.7 %shard_map.281 = (bf16[768,2048]{1,0:T(8,128)(2,1)S(1)}, bf16[2048,1152]{1,0:T(8,128)(2,1)}, f32[8,128]{1,0:T(8,128)S(1)}) custom-call(bf16[2048,768]{1,0:T(8,128)(2,1)} %bitcast.357, bf16[768,640]{1,0:T(8,128)(2,1)S(1)} %bitcast.351, bf16[768,640]{1,0:T(8,128)(2,1)S(1)} %bitcast.348, f32[8,768]{1,0:T(8,128)S(1)} %slice_select_fusion.vec_ref.refs_9_, ...), custom_call_target="tpu_custom_call" | custom-call | flops 100000000 | bytes 1000000 | tf_op jit(solution)/shard_map/pallas_call | solution.py:206
  93.9 1.7 copy-done.2
  100.3 13.3 %shard_map.283 = (bf16[2048,128]{1,0:T(8,128)(2,1)S(1)}, f32[1,8,2048]{2,1,0:T(8,128)S(1)}, f32[8,128]{1,0:T(8,128)S(1)}) custom-call(bf16[2048,1152]{1,0:T(8,128)(2,1)} %get-tuple-element.53.qkv_ref, bf16[2048,128]{1,0:T(8,128)(2,1)S(1)} %get-tuple-element.191.qs_ref, bf16[2048,128]{1,0:T(8,128)(2,1)S(1)} %get-tuple-element.190.ks_ref, ...), custom_call_target="tpu_custom_call" | custom-call | flops 100000000 | bytes 1000000 | tf_op jit(solution)/shard_map/pallas_call | solution.py:351
  113.7 2.6 select_bitcast_fusion.10
  119.1 3.3 maximum_add_fusion.3
  128.9 2.8 add_bitcast_fusion
  134.9 13.7 %shard_map.285 = (bf16[2048,128]{1,0:T(8,128)(2,1)S(1)}, f32[1,8,2048]{2,1,0:T(8,128)S(1)}, f32[8,128]{1,0:T(8,128)}) custom-call(bf16[2048,1152]{1,0:T(8,128)(2,1)} %get-tuple-element.53.qkv_ref, bf16[2048,128]{1,0:T(8,128)(2,1)S(1)} %get-tuple-element.191.qs_ref, bf16[2048,128]{1,0:T(8,128)(2,1)S(1)} %get-tuple-element.190.ks_ref, ...), custom_call_target="tpu_custom_call" | custom-call | flops 100000000 | bytes 1000000 | tf_op jit(solution)/shard_map/pallas_call | solution.py:351
  148.6 13.3 %shard_map.286 = (bf16[2048,128]{1,0:T(8,128)(2,1)S(1)}, f32[1,8,2048]{2,1,0:T(8,128)S(1)}, f32[8,128]{1,0:T(8,128)S(1)}) custom-call(bf16[2048,1152]{1,0:T(8,128)(2,1)} %get-tuple-element.53.qkv_ref, bf16[2048,128]{1,0:T(8,128)(2,1)S(1)} %get-tuple-element.191.qs_ref, bf16[2048,128]{1,0:T(8,128)(2,1)S(1)} %get-tuple-element.190.ks_ref, ...), custom_call_target="tpu_custom_call" | custom-call | flops 100000000 | bytes 1000000 | tf_op jit(solution)/shard_map/pallas_call | solution.py:351
  162.2 3.2 copy.206.refs_1_
  167.2 3.0 select_bitcast_fusion.4
  170.2 3.5 maximum_add_fusion.1
  175.1 2.4 select_bitcast_fusion.6
  180.1 1.8 convolution_convert_fusion.1.b0_ref
  182.0 1.8 fusion.34
  185.6 4.3 collective-permute-done.23
  190.4 1.8 copy.215
  194.4 31.0 %shard_map.289 = (bf16[2048,768]{1,0:T(8,128)(2,1)}, bf16[2048,1536]{1,0:T(8,128)(2,1)}, bf16[2048,1536]{1,0:T(8,128)(2,1)}, bf16[2048,768]{1,0:T(8,128)(2,1)}, ...) custom-call(bf16[2048,768]{1,0:T(8,128)(2,1)} %bitcast.358, bf16[2048,768]{1,0:T(8,128)(2,1)} %copy-done.50, ...), custom_call_target="tpu_custom_call" | custom-call | flops 100000000 | bytes 1000000 | tf_op jit(solution)/shard_map/pallas_call | solution.py:274
  226.2 5.7 %fusion.20.rest_1_ = bf16[768,768]{1,0:T(8,128)(2,1)S(1)} fusion(bf16[2048,768]{1,0:T(8,128)(2,1)} %bitcast.363, bf16[2048,1536]{1,0:T(8,128)(2,1)} %get-tuple-element.62), kind=kOutput, calls=%fused_computation.45 | convolution fusion | flops 2416508928 | bytes 7471104 | tf_op jit(solution)/shard_map/dot_general | solution.py:24
  231.8 4.7 fusion.17.rest_0_
  236.6 6.6 %convolution_convert_fusion.rest_2_ = bf16[768,1536]{1,0:T(8,128)(2,1)} fusion(bf16[2048,768]{1,0:T(8,128)(2,1)S(1)} %copy-done.147, bf16[2048,1536]{1,0:T(8,128)(2,1)S(1)} %bitcast.399), kind=kOutput, calls=%fused_computation.3 | convolution fusion | flops 4833017856 | bytes 11796480 | tf_op jit(solution)/shard_map/dot_general | solution.py:24
  243.3 14.3 %shard_map.290 = (f32[2048,768]{1,0:T(8,128)}, bf16[2048,768]{1,0:T(8,128)(2,1)}, bf16[2048,384]{1,0:T(8,128)(2,1)S(1)}, f32[8,768]{1,0:T(8,128)S(1)}, f32[8,128]{1,0:T(8,128)S(1)}) custom-call(bf16[2048,768]{1,0:T(8,128)(2,1)} %bitcast.359, bf16[2048,768]{1,0:T(8,128)(2,1)} %copy-done.50, bf16[2048,768]{1,0:T(8,128)(2,1)} %copy-done.51, ...), custom_call_target="tpu_custom_call" | custom-call | flops 100000000 | bytes 1000000 | tf_op jit(solution)/shard_map/pallas_call | solution.py:323
  262.7 1.9 fusion.15
  273.5 21.9 %shard_map.291 = (bf16[2048,384]{1,0:T(8,128)(2,1)S(1)}, bf16[768,384]{1,0:T(8,128)(2,1)S(1)}, f32[8,128]{1,0:T(8,128)S(1)}) custom-call(bf16[2048,1152]{1,0:T(8,128)(2,1)} %get-tuple-element.53.qkv_ref, bf16[2048,128]{1,0:T(8,128)(2,1)S(1)} %get-tuple-element.191.qs_ref, bf16[2048,128]{1,0:T(8,128)(2,1)S(1)} %get-tuple-element.190.ks_ref, ...), custom_call_target="tpu_custom_call" | custom-call | flops 100000000 | bytes 1000000 | tf_op jit(solution)/shard_map/pallas_call | solution.py:470
  298.1 2.4 copy.222.refs_2_
  300.5 2.4 copy.221.refs_1_
  305.3 1.8 copy_add_fusion
  309.0 2.4 fusion.9
  311.4 2.0 collective-permute-start.31
  313.5 2.3 fusion.11
  315.9 2.6 collective-permute-start.28
  325.7 21.9 %shard_map.293 = (bf16[2048,384]{1,0:T(8,128)(2,1)S(1)}, bf16[768,384]{1,0:T(8,128)(2,1)S(1)}, f32[8,128]{1,0:T(8,128)S(1)}) custom-call(bf16[2048,1152]{1,0:T(8,128)(2,1)} %get-tuple-element.53.qkv_ref, bf16[2048,128]{1,0:T(8,128)(2,1)S(1)} %get-tuple-element.191.qs_ref, bf16[2048,128]{1,0:T(8,128)(2,1)S(1)} %get-tuple-element.190.ks_ref, ...), custom_call_target="tpu_custom_call" | custom-call | flops 100000000 | bytes 1000000 | tf_op jit(solution)/shard_map/pallas_call | solution.py:470
  354.0 2.1 fusion.25.rest_1_
  356.8 2.4 collective-permute-start.35
  360.6 5.3 %fusion.3 = bf16[2,512,768]{2,1,0:T(8,128)(2,1)S(1)} fusion(bf16[2,512,768]{2,1,0:T(8,128)(2,1)} %collective-permute-done.25.refs_3_, s32[]{:T(128)S(6)} %select_n.489, bf16[2,1,512,768]{3,2,0,1:T(8,128)(2,1)S(1)} %copy-done.55, bf16[2,1,512,768]{3,2,0,1:T(8,128)(2,1)} %copy-done.56, f32[]{:T(128)} %bitcast.91, f32[768]{0:T(1024)S(1)} %get-tuple-element.92, ...), kind=kLoop, calls=%fused_computation.10 | loop fusion | flops 11010048 | bytes 11016200 | tf_op jit(solution)/shard_map/convert_element_type | solution.py:911
  366.2 2.5 fusion.45
  372.2 21.7 %shard_map.295 = (bf16[2048,384]{1,0:T(8,128)(2,1)S(1)}, bf16[768,384]{1,0:T(8,128)(2,1)S(1)}, f32[8,128]{1,0:T(8,128)S(1)}) custom-call(bf16[2048,1152]{1,0:T(8,128)(2,1)} %get-tuple-element.53.qkv_ref, bf16[2048,128]{1,0:T(8,128)(2,1)S(1)} %get-tuple-element.191.qs_ref, bf16[2048,128]{1,0:T(8,128)(2,1)S(1)} %get-tuple-element.190.ks_ref, ...), custom_call_target="tpu_custom_call" | custom-call | flops 100000000 | bytes 1000000 | tf_op jit(solution)/shard_map/pallas_call | solution.py:470
  399.8 1.9 fusion.53.refs_8_
  403.6 5.2 %shard_map.297 = (bf16[1024,768]{1,0:T(8,128)(2,1)S(1)}, f32[8,768]{1,0:T(8,128)S(1)}, f32[8,1152]{1,0:T(8,128)S(1)}, f32[8,128]{1,0:T(8,128)}) custom-call(s32[1]{0:T(128)} %bitcast.104.refs_0_, bf16[2048,384]{1,0:T(8,128)(2,1)S(1)} %copy-done.4, bf16[2048,384]{1,0:T(8,128)(2,1)} %copy-done.8, bf16[2048,384]{1,0:T(8,128)(2,1)} %copy-done.9, ...), custom_call_target="tpu_custom_call" | custom-call | flops 100000000 | bytes 1000000 | tf_op jit(solution)/shard_map/pallas_call | solution.py:451
  417.4 1.8 stack.304
  419.1 1.8 stack.305
  423.3 3.0 reshape.256
  426.3 1.7 copy.236.refs_2_
  430.2 7.1 %shard_map.298 = (bf16[1024,768]{1,0:T(8,128)(2,1)S(1)}, f32[8,768]{1,0:T(8,128)S(1)}, f32[8,1152]{1,0:T(8,128)S(1)}, f32[8,128]{1,0:T(8,128)S(1)}) custom-call(s32[1]{0:T(128)} %bitcast.104.refs_0_, bf16[2048,384]{1,0:T(8,128)(2,1)S(1)} %copy-done.5, bf16[2048,384]{1,0:T(8,128)(2,1)} %copy-done.8, bf16[2048,384]{1,0:T(8,128)(2,1)} %copy-done.9, ...), custom_call_target="tpu_custom_call" | custom-call | flops 100000000 | bytes 1000000 | tf_op jit(solution)/shard_map/pallas_call | solution.py:451
  445.9 1.8 fusion.27
  447.8 3.0 collective-permute-start.43
  452.2 1.7 fusion.41
  455.8 3.3 collective-permute-done.43
  459.1 12.4 %collective-permute-done.46 = bf16[4,48,896]{2,1,0:T(8,128)(2,1)S(1)} collective-permute-done((bf16[4,48,896]{2,1,0:T(8,128)(2,1)S(1)}, bf16[4,48,896]{2,1,0:T(8,128)(2,1)S(1)}, u32[]{:S(2)}, u32[]{:S(2)}) %collective-permute-start.46) | collective-permute-done | bytes 344096 | tf_op jit(solution)/shard_map/ppermute | solution.py:540
  471.7 3.0 collective-permute-start.48
  483.5 1.7 fusion.62
  (577 shorter events, 146.6 us)
Async XLA Ops:
  2.8 9.4 %collective-permute-start.2 = (bf16[24,1280]{1,0:T(8,128)(2,1)S(1)}, bf16[24,1280]{1,0:T(8,128)(2,1)S(1)}, u32[]{:S(2)}, u32[]{:S(2)}) collective-permute-start(bf16[24,1280]{1,0:T(8,128)(2,1)S(1)} %fusion.70), channel_id=1, source_target_pairs={{0,1},{1,0},{2,3},{3,2},{4,5},{5,4},{6,7},{7,6},{8,9},{9,8},{10,11... | collective-permute-start | bytes 184328 | tf_op jit(solution)/shard_map/ppermute | solution.py:540
  4.5 20.8 %collective-permute-start = (bf16[512,768]{1,0:T(8,128)(2,1)S(1)}, bf16[512,768]{1,0:T(8,128)(2,1)S(1)}, u32[]{:S(2)}, u32[]{:S(2)}) collective-permute-start(bf16[512,768]{1,0:T(8,128)(2,1)S(1)} %dynamic-slice_bitcast_fusion.3), channel_id=1, source_target_pairs={{0,2},{2,0},{1,3},{3,1},{4,6},{6,4},{5,7},{7,5},{8,10},{10,8},{9,1... | collective-permute-start | bytes 2359304 | tf_op jit(solution)/shard_map/ppermute | solution.py:540
  8.8 21.8 %collective-permute-start.10 = (bf16[24,2304]{1,0:T(8,128)(2,1)}, bf16[24,2304]{1,0:T(8,128)(2,1)}, u32[]{:S(2)}, u32[]{:S(2)}) collective-permute-start(bf16[24,2304]{1,0:T(8,128)(2,1)} %fusion.64), channel_id=1, source_target_pairs={{0,1},{1,0},{2,3},{3,2},{4,5},{5,4},{6,7},{7,6},{8,9},{9,8},{10,11... | collective-permute-start | bytes 331784 | tf_op jit(solution)/shard_map/ppermute | solution.py:540
  12.4 14.7 %collective-permute-start.3 = (bf16[48,1280]{1,0:T(8,128)(2,1)S(1)}, bf16[48,1280]{1,0:T(8,128)(2,1)S(1)}, u32[]{:S(2)}, u32[]{:S(2)}) collective-permute-start(bf16[48,1280]{1,0:T(8,128)(2,1)S(1)} %concatenate.68), channel_id=1, source_target_pairs={{0,8},{4,12},{8,0},{12,4},{16,24},{20,28},{24,16},{28,20},{1,9},{5... | collective-permute-start | bytes 368648 | tf_op jit(solution)/shard_map/ppermute | solution.py:569
  14.0 13.0 %collective-permute-start.4 = (bf16[48,1280]{1,0:T(8,128)(2,1)S(1)}, bf16[48,1280]{1,0:T(8,128)(2,1)S(1)}, u32[]{:S(2)}, u32[]{:S(2)}) collective-permute-start(bf16[48,1280]{1,0:T(8,128)(2,1)S(1)} %concatenate.68), channel_id=1, source_target_pairs={{0,16},{4,20},{8,24},{12,28},{16,0},{20,4},{24,8},{28,12},{1,17},{... | collective-permute-start | bytes 368648 | tf_op jit(solution)/shard_map/ppermute | solution.py:569
  16.6 10.5 %collective-permute-start.5 = (bf16[48,1280]{1,0:T(8,128)(2,1)S(1)}, bf16[48,1280]{1,0:T(8,128)(2,1)S(1)}, u32[]{:S(2)}, u32[]{:S(2)}) collective-permute-start(bf16[48,1280]{1,0:T(8,128)(2,1)S(1)} %concatenate.68), channel_id=1, source_target_pairs={{0,24},{4,28},{8,16},{12,20},{16,8},{20,12},{24,0},{28,4},{1,25},{... | collective-permute-start | bytes 368648 | tf_op jit(solution)/shard_map/ppermute | solution.py:569
  27.0 11.2 %collective-permute-start.1 = (bf16[2,512,768]{2,1,0:T(8,128)(2,1)S(1)}, bf16[2,512,768]{2,1,0:T(8,128)(2,1)S(1)}, u32[]{:S(2)}, u32[]{:S(2)}) collective-permute-start(bf16[2,512,768]{2,1,0:T(8,128)(2,1)S(1)} %pad_maximum_fusion.4), channel_id=1, source_target_pairs={{0,1},{1,0},{2,3},{3,2},{4,5},{5,4},{6,7},{7,6},{8,9},{9,8},{10,11... | collective-permute-start | bytes 4718600 | tf_op jit(solution)/shard_map/ppermute | solution.py:540
  27.3 8.4 %collective-permute-start.6 = (bf16[4,48,640]{2,1,0:T(8,128)(2,1)S(1)}, bf16[4,48,640]{2,1,0:T(8,128)(2,1)S(1)}, u32[]{:S(2)}, u32[]{:S(2)}) collective-permute-start(bf16[4,48,640]{2,1,0:T(8,128)(2,1)S(1)} %get-tuple-element.156), channel_id=1, source_target_pairs={{0,4},{4,0},{8,12},{12,8},{16,20},{20,16},{24,28},{28,24},{1,5},{5... | collective-permute-start | bytes 737288 | tf_op jit(solution)/shard_map/ppermute | solution.py:569
  29.1 8.1 %collective-permute-start.7 = (bf16[4,48,640]{2,1,0:T(8,128)(2,1)S(1)}, bf16[4,48,640]{2,1,0:T(8,128)(2,1)S(1)}, u32[]{:S(2)}, u32[]{:S(2)}) collective-permute-start(bf16[4,48,640]{2,1,0:T(8,128)(2,1)S(1)} %get-tuple-element.155), channel_id=1, source_target_pairs={{0,2},{2,0},{1,3},{3,1},{4,6},{6,4},{5,7},{7,5},{8,10},{10,8},{9,1... | collective-permute-start | bytes 737288 | tf_op jit(solution)/shard_map/ppermute | solution.py:540
  42.0 10.0 %collective-permute-start.14 = (bf16[48,1920]{1,0:T(8,128)(2,1)S(1)}, bf16[48,1920]{1,0:T(8,128)(2,1)S(1)}, u32[]{:S(2)}, u32[]{:S(2)}) collective-permute-start(bf16[48,1920]{1,0:T(8,128)(2,1)S(1)} %slice.291), channel_id=1, source_target_pairs={{0,8},{4,12},{8,0},{12,4},{16,24},{20,28},{24,16},{28,20},{1,9},{5... | collective-permute-start | bytes 552968 | tf_op jit(solution)/shard_map/ppermute | solution.py:569
  43.7 16.4 %collective-permute-start.15 = (bf16[48,1920]{1,0:T(8,128)(2,1)S(1)}, bf16[48,1920]{1,0:T(8,128)(2,1)S(1)}, u32[]{:S(2)}, u32[]{:S(2)}) collective-permute-start(bf16[48,1920]{1,0:T(8,128)(2,1)S(1)} %slice.291), channel_id=1, source_target_pairs={{0,16},{4,20},{8,24},{12,28},{16,0},{20,4},{24,8},{28,12},{1,17},{... | collective-permute-start | bytes 552968 | tf_op jit(solution)/shard_map/ppermute | solution.py:569
  46.3 13.8 %collective-permute-start.16 = (bf16[48,1920]{1,0:T(8,128)(2,1)S(1)}, bf16[48,1920]{1,0:T(8,128)(2,1)S(1)}, u32[]{:S(2)}, u32[]{:S(2)}) collective-permute-start(bf16[48,1920]{1,0:T(8,128)(2,1)S(1)} %slice.291), channel_id=1, source_target_pairs={{0,24},{4,28},{8,16},{12,20},{16,8},{20,12},{24,0},{28,4},{1,25},{... | collective-permute-start | bytes 552968 | tf_op jit(solution)/shard_map/ppermute | solution.py:569
  48.3 32.8 %collective-permute-start.9 = (bf16[4,2,48,640]{3,2,0,1:T(8,128)(2,1)S(1)}, bf16[4,2,48,640]{3,2,0,1:T(8,128)(2,1)S(1)}, u32[]{:S(2)}, u32[]{:S(2)}) collective-permute-start(bf16[4,2,48,640]{3,2,0,1:T(8,128)(2,1)S(1)} %maximum_add_fusion.7), channel_id=1, source_target_pairs={{0,4},{4,0},{8,12},{12,8},{16,20},{20,16},{24,28},{28,24},{1,5},{5... | collective-permute-start | bytes 1474568 | tf_op jit(solution)/shard_map/ppermute | solution.py:569
  50.2 32.5 %collective-permute-start.8 = (bf16[4,2,48,640]{3,2,0,1:T(8,128)(2,1)}, bf16[4,2,48,640]{3,2,0,1:T(8,128)(2,1)}, u32[]{:S(2)}, u32[]{:S(2)}) collective-permute-start(bf16[4,2,48,640]{3,2,0,1:T(8,128)(2,1)} %maximum_add_fusion.6), channel_id=1, source_target_pairs={{0,2},{2,0},{1,3},{3,1},{4,6},{6,4},{5,7},{7,5},{8,10},{10,8},{9,1... | collective-permute-start | bytes 1474568 | tf_op jit(solution)/shard_map/ppermute | solution.py:540
  52.0 13.6 %copy-start.54 = (bf16[2,1,512,768]{3,2,0,1:T(8,128)(2,1)}, bf16[2,1,512,768]{3,2,0,1:T(8,128)(2,1)S(1)}, u32[]{:S(2)}) copy-start(bf16[2,1,512,768]{3,2,0,1:T(8,128)(2,1)S(1)} %get-tuple-element.103) | copy-start | bytes 4718596
  52.0 13.6 %copy-start.56 = (bf16[2,1,512,768]{3,2,0,1:T(8,128)(2,1)}, bf16[2,1,512,768]{3,2,0,1:T(8,128)(2,1)S(1)}, u32[]{:S(2)}) copy-start(bf16[2,1,512,768]{3,2,0,1:T(8,128)(2,1)S(1)} %get-tuple-element.104) | copy-start | bytes 4718596
  60.2 37.9 %copy-start.98 = (bf16[1,48,1920]{2,1,0:T(8,128)(2,1)}, bf16[1,48,1920]{2,1,0:T(8,128)(2,1)S(1)}, u32[]{:S(2)}) copy-start(bf16[1,48,1920]{2,1,0:T(8,128)(2,1)S(1)} %get-tuple-element.132) | copy-start | bytes 552964
  60.2 37.8 %copy-start.100 = (bf16[1,48,1920]{2,1,0:T(8,128)(2,1)}, bf16[1,48,1920]{2,1,0:T(8,128)(2,1)S(1)}, u32[]{:S(2)}) copy-start(bf16[1,48,1920]{2,1,0:T(8,128)(2,1)S(1)} %get-tuple-element.133) | copy-start | bytes 552964
  60.2 37.8 %copy-start.102 = (bf16[1,48,1920]{2,1,0:T(8,128)(2,1)}, bf16[1,48,1920]{2,1,0:T(8,128)(2,1)S(1)}, u32[]{:S(2)}) copy-start(bf16[1,48,1920]{2,1,0:T(8,128)(2,1)S(1)} %get-tuple-element.134) | copy-start | bytes 552964
  60.2 37.8 %copy-start.104 = (bf16[1,48,1920]{2,1,0:T(8,128)(2,1)}, bf16[1,48,1920]{2,1,0:T(8,128)(2,1)S(1)}, u32[]{:S(2)}) copy-start(bf16[1,48,1920]{2,1,0:T(8,128)(2,1)S(1)} %get-tuple-element.135) | copy-start | bytes 552964
  60.2 8.5 %collective-permute-start.11 = (bf16[48,1920]{1,0:T(8,128)(2,1)S(1)}, bf16[48,1920]{1,0:T(8,128)(2,1)S(1)}, u32[]{:S(2)}, u32[]{:S(2)}) collective-permute-start(bf16[48,1920]{1,0:T(8,128)(2,1)S(1)} %get-tuple-element.166), channel_id=1, source_target_pairs={{0,8},{4,12},{8,0},{12,4},{16,24},{20,28},{24,16},{28,20},{1,9},{5... | collective-permute-start | bytes 552968 | tf_op jit(solution)/shard_map/ppermute | solution.py:569
  62.9 15.4 %collective-permute-start.12 = (bf16[48,1920]{1,0:T(8,128)(2,1)S(1)}, bf16[48,1920]{1,0:T(8,128)(2,1)S(1)}, u32[]{:S(2)}, u32[]{:S(2)}) collective-permute-start(bf16[48,1920]{1,0:T(8,128)(2,1)S(1)} %get-tuple-element.166), channel_id=1, source_target_pairs={{0,16},{4,20},{8,24},{12,28},{16,0},{20,4},{24,8},{28,12},{1,17},{... | collective-permute-start | bytes 552968 | tf_op jit(solution)/shard_map/ppermute | solution.py:569
  64.0 14.3 %collective-permute-start.13 = (bf16[48,1920]{1,0:T(8,128)(2,1)S(1)}, bf16[48,1920]{1,0:T(8,128)(2,1)S(1)}, u32[]{:S(2)}, u32[]{:S(2)}) collective-permute-start(bf16[48,1920]{1,0:T(8,128)(2,1)S(1)} %get-tuple-element.166), channel_id=1, source_target_pairs={{0,24},{4,28},{8,16},{12,20},{16,8},{20,12},{24,0},{28,4},{1,25},{... | collective-permute-start | bytes 552968 | tf_op jit(solution)/shard_map/ppermute | solution.py:569
  79.5 34.1 %collective-permute-start.17 = (bf16[4,48,1920]{2,1,0:T(8,128)(2,1)}, bf16[4,48,1920]{2,1,0:T(8,128)(2,1)}, u32[]{:S(2)}, u32[]{:S(2)}) collective-permute-start(bf16[4,48,1920]{2,1,0:T(8,128)(2,1)} %pad_maximum_fusion.11.rest_refs_0_), channel_id=1, source_target_pairs={{0,2},{2,0},{1,3},{3,1},{4,6},{6,4},{5,7},{7,5},{8,10},{10,8},{9,1... | collective-permute-start | bytes 2211848 | tf_op jit(solution)/shard_map/ppermute | solution.py:540
  98.8 17.4 %collective-permute-start.18 = (bf16[4,48,1920]{2,1,0:T(8,128)(2,1)S(1)}, bf16[4,48,1920]{2,1,0:T(8,128)(2,1)S(1)}, u32[]{:S(2)}, u32[]{:S(2)}) collective-permute-start(bf16[4,48,1920]{2,1,0:T(8,128)(2,1)S(1)} %maximum_add_fusion.5.rest_0_), channel_id=1, source_target_pairs={{0,4},{4,0},{8,12},{12,8},{16,20},{20,16},{24,28},{28,24},{1,5},{5... | collective-permute-start | bytes 2211848 | tf_op jit(solution)/shard_map/ppermute | solution.py:569
  113.6 19.6 %copy-start.11 = (bf16[2048,128]{1,0:T(8,128)(2,1)}, bf16[2048,128]{1,0:T(8,128)(2,1)S(1)}, u32[]{:S(2)}) copy-start(bf16[2048,128]{1,0:T(8,128)(2,1)S(1)} %get-tuple-element.55.rest_0_.o_ref) | copy-start | bytes 1572868
  122.3 39.9 %collective-permute-start.19 = (bf16[4,2,48,1920]{3,2,0,1:T(8,128)(2,1)}, bf16[4,2,48,1920]{3,2,0,1:T(8,128)(2,1)}, u32[]{:S(2)}, u32[]{:S(2)}) collective-permute-start(bf16[4,2,48,1920]{3,2,0,1:T(8,128)(2,1)} %maximum_add_fusion.3), channel_id=1, source_target_pairs={{0,4},{4,0},{8,12},{12,8},{16,20},{20,16},{24,28},{28,24},{1,5},{5... | collective-permute-start | bytes 4423688 | tf_op jit(solution)/shard_map/ppermute | solution.py:569
  126.6 38.8 %collective-permute-start.20 = (bf16[4,2,48,1920]{3,2,1,0:T(8,128)(2,1)}, bf16[4,2,48,1920]{3,2,1,0:T(8,128)(2,1)}, u32[]{:S(2)}, u32[]{:S(2)}) collective-permute-start(bf16[4,2,48,1920]{3,2,1,0:T(8,128)(2,1)} %copy.203.rest_2_), channel_id=1, source_target_pairs={{0,2},{2,0},{1,3},{3,1},{4,6},{6,4},{5,7},{7,5},{8,10},{10,8},{9,1... | collective-permute-start | bytes 4423688 | tf_op jit(solution)/shard_map/ppermute | solution.py:540
  131.7 50.3 %collective-permute-start.22 = (bf16[512,768]{1,0:T(8,128)(2,1)}, bf16[512,768]{1,0:T(8,128)(2,1)}, u32[]{:S(2)}, u32[]{:S(2)}) collective-permute-start(bf16[512,768]{1,0:T(8,128)(2,1)} %add_bitcast_fusion), channel_id=1, source_target_pairs={{0,2},{2,0},{1,3},{3,1},{4,6},{6,4},{5,7},{7,5},{8,10},{10,8},{9,1... | collective-permute-start | bytes 2359304 | tf_op jit(solution)/shard_map/ppermute | solution.py:540
  181.9 10.8 %collective-permute-start.21 = (bf16[2048,768]{1,0:T(8,128)(2,1)S(1)}, bf16[2048,768]{1,0:T(8,128)(2,1)S(1)}, u32[]{:S(2)}, u32[]{:S(2)}) collective-permute-start(bf16[2048,768]{1,0:T(8,128)(2,1)S(1)} %convolution_convert_fusion.1.b0_ref), channel_id=1, source_target_pairs={{0,1},{1,0},{2,3},{3,2},{4,5},{5,4},{6,7},{7,6},{8,9},{9,8},{10,11... | collective-permute-start | bytes 9437192 | tf_op jit(solution)/shard_map/ppermute | solution.py:540
  184.0 5.9 %collective-permute-start.23 = (bf16[2,512,768]{2,1,0:T(8,128)(2,1)S(1)}, bf16[2,512,768]{2,1,0:T(8,128)(2,1)S(1)}, u32[]{:S(2)}, u32[]{:S(2)}) collective-permute-start(bf16[2,512,768]{2,1,0:T(8,128)(2,1)S(1)} %pad_maximum_fusion.5), channel_id=1, source_target_pairs={{0,1},{1,0},{2,3},{3,2},{4,5},{5,4},{6,7},{7,6},{8,9},{9,8},{10,11... | collective-permute-start | bytes 4718600 | tf_op jit(solution)/shard_map/ppermute | solution.py:540
  226.0 17.2 %collective-permute-start.24 = (bf16[2048,768]{1,0:T(8,128)(2,1)}, bf16[2048,768]{1,0:T(8,128)(2,1)}, u32[]{:S(2)}, u32[]{:S(2)}) collective-permute-start(bf16[2048,768]{1,0:T(8,128)(2,1)} %get-tuple-element.61.p0_ref), channel_id=1, source_target_pairs={{0,1},{1,0},{2,3},{3,2},{4,5},{5,4},{6,7},{7,6},{8,9},{9,8},{10,11... | collective-permute-start | bytes 9437192 | tf_op jit(solution)/shard_map/ppermute | solution.py:540
  243.2 14.9 %copy-start.63 = (bf16[768,1536]{1,0:T(8,128)(2,1)S(1)}, bf16[768,1536]{1,0:T(8,128)(2,1)}, u32[]{:S(2)}) copy-start(bf16[768,1536]{1,0:T(8,128)(2,1)} %convolution_convert_fusion.rest_2_) | copy-start | bytes 7077892
  261.9 36.2 %collective-permute-start.27 = (bf16[4,2,48,1536]{3,2,0,1:T(8,128)(2,1)}, bf16[4,2,48,1536]{3,2,0,1:T(8,128)(2,1)}, u32[]{:S(2)}, u32[]{:S(2)}) collective-permute-start(bf16[4,2,48,1536]{3,2,0,1:T(8,128)(2,1)} %bitcast.343), channel_id=1, source_target_pairs={{0,4},{4,0},{8,12},{12,8},{16,20},{20,16},{24,28},{28,24},{1,5},{5... | collective-permute-start | bytes 3538952 | tf_op jit(solution)/shard_map/ppermute | solution.py:569
  264.6 38.2 %collective-permute-start.25 = (bf16[2,512,768]{2,1,0:T(8,128)(2,1)}, bf16[2,512,768]{2,1,0:T(8,128)(2,1)}, u32[]{:S(2)}, u32[]{:S(2)}) collective-permute-start(bf16[2,512,768]{2,1,0:T(8,128)(2,1)} %fusion.15), channel_id=1, source_target_pairs={{0,1},{1,0},{2,3},{3,2},{4,5},{5,4},{6,7},{7,6},{8,9},{9,8},{10,11... | collective-permute-start | bytes 4718600 | tf_op jit(solution)/shard_map/ppermute | solution.py:540
  268.8 31.7 %collective-permute-start.26 = (bf16[2,4,2,48,768]{4,3,0,2,1:T(8,128)(2,1)}, bf16[2,4,2,48,768]{4,3,0,2,1:T(8,128)(2,1)}, u32[]{:S(2)}, u32[]{:S(2)}) collective-permute-start(bf16[2,4,2,48,768]{4,3,0,2,1:T(8,128)(2,1)} %bitcast.344), channel_id=1, source_target_pairs={{0,2},{2,0},{1,3},{3,1},{4,6},{6,4},{5,7},{7,5},{8,10},{10,8},{9,1... | collective-permute-start | bytes 3538952 | tf_op jit(solution)/shard_map/ppermute | solution.py:540
  273.5 21.9 %copy-start.134 = (bf16[2048,384]{1,0:T(8,128)(2,1)S(1)}, bf16[2048,384]{1,0:T(8,128)(2,1)}, u32[]{:S(2)}) copy-start(bf16[2048,384]{1,0:T(8,128)(2,1)} %copy-done.132) | copy-start | bytes 4718596
  273.5 21.9 %copy-start.146 = (bf16[2048,768]{1,0:T(8,128)(2,1)S(1)}, bf16[2048,768]{1,0:T(8,128)(2,1)}, u32[]{:S(2)}) copy-start(bf16[2048,768]{1,0:T(8,128)(2,1)} %get-tuple-element.71) | copy-start | bytes 9437188
  307.1 16.2 %copy-start.52 = (bf16[4,2,2,48,1152]{4,3,0,2,1:T(8,128)(2,1)}, bf16[4,2,2,48,1152]{4,3,0,2,1:T(8,128)(2,1)S(1)}, u32[]{:S(2)}) copy-start(bf16[4,2,2,48,1152]{4,3,0,2,1:T(8,128)(2,1)S(1)} %copy_add_fusion) | copy-start | bytes 5308420
  307.2 42.9 %collective-permute-start.32 = (bf16[4,2,48,1152]{3,2,0,1:T(8,128)(2,1)S(1)}, bf16[4,2,48,1152]{3,2,0,1:T(8,128)(2,1)S(1)}, u32[]{:S(2)}, u32[]{:S(2)}) collective-permute-start(bf16[4,2,48,1152]{3,2,0,1:T(8,128)(2,1)S(1)} %dynamic-slice_bitcast_fusion), channel_id=1, source_target_pairs={{0,4},{4,0},{8,12},{12,8},{16,20},{20,16},{24,28},{28,24},{1,5},{5... | collective-permute-start | bytes 2654216 | tf_op jit(solution)/shard_map/ppermute | solution.py:569
  311.4 39.7 %collective-permute-start.31 = (bf16[4,48,1536]{2,1,0:T(8,128)(2,1)S(1)}, bf16[4,48,1536]{2,1,0:T(8,128)(2,1)S(1)}, u32[]{:S(2)}, u32[]{:S(2)}) collective-permute-start(bf16[4,48,1536]{2,1,0:T(8,128)(2,1)S(1)} %dynamic-slice_bitcast_fusion.4), channel_id=1, source_target_pairs={{0,2},{2,0},{1,3},{3,1},{4,6},{6,4},{5,7},{7,5},{8,10},{10,8},{9,1... | collective-permute-start | bytes 1769480 | tf_op jit(solution)/shard_map/ppermute | solution.py:540
  315.9 31.8 %collective-permute-start.28 = (bf16[2,2,48,768]{3,2,0,1:T(8,128)(2,1)S(1)}, bf16[2,2,48,768]{3,2,0,1:T(8,128)(2,1)S(1)}, u32[]{:S(2)}, u32[]{:S(2)}) collective-permute-start(bf16[2,2,48,768]{3,2,0,1:T(8,128)(2,1)S(1)} %get-tuple-element.127), channel_id=1, source_target_pairs={{0,8},{4,12},{8,0},{12,4},{16,24},{20,28},{24,16},{28,20},{1,9},{5... | collective-permute-start | bytes 884744 | tf_op jit(solution)/shard_map/ppermute | solution.py:569
  318.5 30.1 %collective-permute-start.29 = (bf16[2,2,48,768]{3,2,0,1:T(8,128)(2,1)S(1)}, bf16[2,2,48,768]{3,2,0,1:T(8,128)(2,1)S(1)}, u32[]{:S(2)}, u32[]{:S(2)}) collective-permute-start(bf16[2,2,48,768]{3,2,0,1:T(8,128)(2,1)S(1)} %get-tuple-element.126), channel_id=1, source_target_pairs={{0,16},{4,20},{8,24},{12,28},{16,0},{20,4},{24,8},{28,12},{1,17},{... | collective-permute-start | bytes 884744 | tf_op jit(solution)/shard_map/ppermute | solution.py:569
  319.9 29.4 %collective-permute-start.30 = (bf16[2,2,48,768]{3,2,0,1:T(8,128)(2,1)S(1)}, bf16[2,2,48,768]{3,2,0,1:T(8,128)(2,1)S(1)}, u32[]{:S(2)}, u32[]{:S(2)}) collective-permute-start(bf16[2,2,48,768]{3,2,0,1:T(8,128)(2,1)S(1)} %get-tuple-element.125), channel_id=1, source_target_pairs={{0,24},{4,28},{8,16},{12,20},{16,8},{20,12},{24,0},{28,4},{1,25},{... | collective-permute-start | bytes 884744 | tf_op jit(solution)/shard_map/ppermute | solution.py:569
  356.1 15.6 %copy-start.10 = (bf16[4,48,1536]{2,1,0:T(8,128)(2,1)}, bf16[4,48,1536]{2,1,0:T(8,128)(2,1)S(1)}, u32[]{:S(2)}) copy-start(bf16[4,48,1536]{2,1,0:T(8,128)(2,1)S(1)} %fusion.25.rest_1_) | copy-start | bytes 1769476
  356.1 40.3 %collective-permute-start.34 = (bf16[48,1536]{1,0:T(8,128)(2,1)S(1)}, bf16[48,1536]{1,0:T(8,128)(2,1)S(1)}, u32[]{:S(2)}, u32[]{:S(2)}) collective-permute-start(bf16[48,1536]{1,0:T(8,128)(2,1)S(1)} %get-tuple-element.150), channel_id=1, source_target_pairs={{0,8},{4,12},{8,0},{12,4},{16,24},{20,28},{24,16},{28,20},{1,9},{5... | collective-permute-start | bytes 442376 | tf_op jit(solution)/shard_map/ppermute | solution.py:569
  356.8 39.7 %collective-permute-start.35 = (bf16[48,1536]{1,0:T(8,128)(2,1)S(1)}, bf16[48,1536]{1,0:T(8,128)(2,1)S(1)}, u32[]{:S(2)}, u32[]{:S(2)}) collective-permute-start(bf16[48,1536]{1,0:T(8,128)(2,1)S(1)} %get-tuple-element.149), channel_id=1, source_target_pairs={{0,16},{4,20},{8,24},{12,28},{16,0},{20,4},{24,8},{28,12},{1,17},{... | collective-permute-start | bytes 442376 | tf_op jit(solution)/shard_map/ppermute | solution.py:569
  359.2 37.3 %collective-permute-start.36 = (bf16[48,1536]{1,0:T(8,128)(2,1)S(1)}, bf16[48,1536]{1,0:T(8,128)(2,1)S(1)}, u32[]{:S(2)}, u32[]{:S(2)}) collective-permute-start(bf16[48,1536]{1,0:T(8,128)(2,1)S(1)} %get-tuple-element.148), channel_id=1, source_target_pairs={{0,24},{4,28},{8,16},{12,20},{16,8},{20,12},{24,0},{28,4},{1,25},{... | collective-permute-start | bytes 442376 | tf_op jit(solution)/shard_map/ppermute | solution.py:569
  366.0 30.6 %collective-permute-start.37 = (bf16[512,768]{1,0:T(8,128)(2,1)S(1)}, bf16[512,768]{1,0:T(8,128)(2,1)}, u32[]{:S(2)}, u32[]{:S(2)}) collective-permute-start(bf16[512,768]{1,0:T(8,128)(2,1)S(1)} %dynamic-slice_bitcast_fusion.2), channel_id=1, source_target_pairs={{0,2},{2,0},{1,3},{3,1},{4,6},{6,4},{5,7},{7,5},{8,10},{10,8},{9,1... | collective-permute-start | bytes 2359304 | tf_op jit(solution)/shard_map/ppermute | solution.py:540
  368.7 27.8 %collective-permute-start.33 = (bf16[2,48,768]{2,1,0:T(8,128)(2,1)S(1)}, bf16[2,48,768]{2,1,0:T(8,128)(2,1)S(1)}, u32[]{:S(2)}, u32[]{:S(2)}) collective-permute-start(bf16[2,48,768]{2,1,0:T(8,128)(2,1)S(1)} %dynamic-slice_bitcast_fusion.12), channel_id=1, source_target_pairs={{0,4},{4,0},{8,12},{12,8},{16,20},{20,16},{24,28},{28,24},{1,5},{5... | collective-permute-start | bytes 442376 | tf_op jit(solution)/shard_map/ppermute | solution.py:569
  401.7 15.0 %collective-permute-start.51 = (bf16[24,1536]{1,0:T(8,128)(2,1)S(1)}, bf16[24,1536]{1,0:T(8,128)(2,1)S(1)}, u32[]{:S(2)}, u32[]{:S(2)}) collective-permute-start(bf16[24,1536]{1,0:T(8,128)(2,1)S(1)} %constant_dynamic-slice_fusion), channel_id=1, source_target_pairs={{0,1},{1,0},{2,3},{3,2},{4,5},{5,4},{6,7},{7,6},{8,9},{9,8},{10,11... | collective-permute-start | bytes 221192 | tf_op jit(solution)/shard_map/ppermute | solution.py:540
  408.8 19.2 %collective-permute-start.38 = (bf16[1024,768]{1,0:T(8,128)(2,1)S(1)}, bf16[1024,768]{1,0:T(8,128)(2,1)}, u32[]{:S(2)}, u32[]{:S(2)}) collective-permute-start(bf16[1024,768]{1,0:T(8,128)(2,1)S(1)} %get-tuple-element.79), channel_id=1, source_target_pairs={{0,1},{1,0},{2,3},{3,2},{4,5},{5,4},{6,7},{7,6},{8,9},{9,8},{10,11... | collective-permute-start | bytes 4718600 | tf_op jit(solution)/shard_map/ppermute | solution.py:540
  410.4 15.9 %collective-permute-start.41 = (bf16[4,2,48,384]{3,2,0,1:T(8,128)(2,1)}, bf16[4,2,48,384]{3,2,0,1:T(8,128)(2,1)}, u32[]{:S(2)}, u32[]{:S(2)}) collective-permute-start(bf16[4,2,48,384]{3,2,0,1:T(8,128)(2,1)} %bitcast.346), channel_id=1, source_target_pairs={{0,4},{4,0},{8,12},{12,8},{16,20},{20,16},{24,28},{28,24},{1,5},{5... | collective-permute-start | bytes 884744 | tf_op jit(solution)/shard_map/ppermute | solution.py:569
  412.2 26.9 %collective-permute-start.40 = (bf16[4,48,1152]{2,1,0:T(8,128)(2,1)}, bf16[4,48,1152]{2,1,0:T(8,128)(2,1)}, u32[]{:S(2)}, u32[]{:S(2)}) collective-permute-start(bf16[4,48,1152]{2,1,0:T(8,128)(2,1)} %dynamic-slice_bitcast_fusion.5), channel_id=1, source_target_pairs={{0,2},{2,0},{1,3},{3,1},{4,6},{6,4},{5,7},{7,5},{8,10},{10,8},{9,1... | collective-permute-start | bytes 1327112 | tf_op jit(solution)/shard_map/ppermute | solution.py:540
  443.7 11.0 %collective-permute-start.45 = (bf16[4,2,48,512]{3,2,0,1:T(8,128)(2,1)S(1)}, bf16[4,2,48,512]{3,2,0,1:T(8,128)(2,1)S(1)}, u32[]{:S(2)}, u32[]{:S(2)}) collective-permute-start(bf16[4,2,48,512]{3,2,0,1:T(8,128)(2,1)S(1)} %bitcast.383), channel_id=1, source_target_pairs={{0,4},{4,0},{8,12},{12,8},{16,20},{20,16},{24,28},{28,24},{1,5},{5... | collective-permute-start | bytes 1179656 | tf_op jit(solution)/shard_map/ppermute | solution.py:569
  445.0 31.1 %collective-permute-start.39 = (bf16[512,768]{1,0:T(8,128)(2,1)S(1)}, bf16[512,768]{1,0:T(8,128)(2,1)S(1)}, u32[]{:S(2)}, u32[]{:S(2)}) collective-permute-start(bf16[512,768]{1,0:T(8,128)(2,1)S(1)} %dynamic-slice_bitcast_fusion.1), channel_id=1, source_target_pairs={{0,2},{2,0},{1,3},{3,1},{4,6},{6,4},{5,7},{7,5},{8,10},{10,8},{9,1... | collective-permute-start | bytes 2359304 | tf_op jit(solution)/shard_map/ppermute | solution.py:540
  447.7 8.1 %collective-permute-start.42 = (bf16[48,1152]{1,0:T(8,128)(2,1)S(1)}, bf16[48,1152]{1,0:T(8,128)(2,1)S(1)}, u32[]{:S(2)}, u32[]{:S(2)}) collective-permute-start(bf16[48,1152]{1,0:T(8,128)(2,1)S(1)} %get-tuple-element.161), channel_id=1, source_target_pairs={{0,8},{4,12},{8,0},{12,4},{16,24},{20,28},{24,16},{28,20},{1,9},{5... | collective-permute-start | bytes 331784 | tf_op jit(solution)/shard_map/ppermute | solution.py:569
  447.8 11.3 %collective-permute-start.43 = (bf16[48,1152]{1,0:T(8,128)(2,1)S(1)}, bf16[48,1152]{1,0:T(8,128)(2,1)S(1)}, u32[]{:S(2)}, u32[]{:S(2)}) collective-permute-start(bf16[48,1152]{1,0:T(8,128)(2,1)S(1)} %get-tuple-element.163), channel_id=1, source_target_pairs={{0,16},{4,20},{8,24},{12,28},{16,0},{20,4},{24,8},{28,12},{1,17},{... | collective-permute-start | bytes 331784 | tf_op jit(solution)/shard_map/ppermute | solution.py:569
  450.8 8.3 %collective-permute-start.44 = (bf16[48,1152]{1,0:T(8,128)(2,1)S(1)}, bf16[48,1152]{1,0:T(8,128)(2,1)S(1)}, u32[]{:S(2)}, u32[]{:S(2)}) collective-permute-start(bf16[48,1152]{1,0:T(8,128)(2,1)S(1)} %get-tuple-element.162), channel_id=1, source_target_pairs={{0,24},{4,28},{8,16},{12,20},{16,8},{20,12},{24,0},{28,4},{1,25},{... | collective-permute-start | bytes 331784 | tf_op jit(solution)/shard_map/ppermute | solution.py:569
  454.9 16.6 %collective-permute-start.46 = (bf16[4,48,896]{2,1,0:T(8,128)(2,1)S(1)}, bf16[4,48,896]{2,1,0:T(8,128)(2,1)S(1)}, u32[]{:S(2)}, u32[]{:S(2)}) collective-permute-start(bf16[4,48,896]{2,1,0:T(8,128)(2,1)S(1)} %fusion.47), channel_id=1, source_target_pairs={{0,2},{2,0},{1,3},{3,1},{4,6},{6,4},{5,7},{7,5},{8,10},{10,8},{9,1... | collective-permute-start | bytes 1032200 | tf_op jit(solution)/shard_map/ppermute | solution.py:540
  471.6 6.6 %collective-permute-start.47 = (bf16[48,896]{1,0:T(8,128)(2,1)S(1)}, bf16[48,896]{1,0:T(8,128)(2,1)S(1)}, u32[]{:S(2)}, u32[]{:S(2)}) collective-permute-start(bf16[48,896]{1,0:T(8,128)(2,1)S(1)} %get-tuple-element.167), channel_id=1, source_target_pairs={{0,8},{4,12},{8,0},{12,4},{16,24},{20,28},{24,16},{28,20},{1,9},{5... | collective-permute-start | bytes 258056 | tf_op jit(solution)/shard_map/ppermute | solution.py:569
  471.7 8.0 %collective-permute-start.48 = (bf16[48,896]{1,0:T(8,128)(2,1)S(1)}, bf16[48,896]{1,0:T(8,128)(2,1)S(1)}, u32[]{:S(2)}, u32[]{:S(2)}) collective-permute-start(bf16[48,896]{1,0:T(8,128)(2,1)S(1)} %get-tuple-element.169), channel_id=1, source_target_pairs={{0,16},{4,20},{8,24},{12,28},{16,0},{20,4},{24,8},{28,12},{1,17},{... | collective-permute-start | bytes 258056 | tf_op jit(solution)/shard_map/ppermute | solution.py:569
  474.7 6.4 %collective-permute-start.49 = (bf16[48,896]{1,0:T(8,128)(2,1)S(1)}, bf16[48,896]{1,0:T(8,128)(2,1)S(1)}, u32[]{:S(2)}, u32[]{:S(2)}) collective-permute-start(bf16[48,896]{1,0:T(8,128)(2,1)S(1)} %get-tuple-element.168), channel_id=1, source_target_pairs={{0,24},{4,28},{8,16},{12,20},{16,8},{20,12},{24,0},{28,4},{1,25},{... | collective-permute-start | bytes 258056 | tf_op jit(solution)/shard_map/ppermute | solution.py:569
  485.4 1.5 collective-permute-start.50
  (139 other events, 591.8 us)

commit v5 on v4

--- a/solution.py
+++ b/solution.py
@@ -170,6 +170,52 @@
 ANY_SPEC = pl.BlockSpec(memory_space=pl.ANY)
 
 
+def pack_kernel(count, refs):
+    refs[-1][...] = jnp.concatenate([ref[...] for ref in refs[:count]], axis=-1)
+
+
+def pack(parts, after):
+    rows = parts[0].shape[0]
+    width = sum(part.shape[1] for part in parts)
+    return pl.pallas_call(
+        lambda *refs: pack_kernel(len(parts), refs),
+        grid=(1,),
+        in_specs=[pl.BlockSpec(part.shape, lambda i: (0, 0)) for part in parts]
+        + [ANY_SPEC] * len(after),
+        out_specs=pl.BlockSpec((rows, width), lambda i: (0, 0)),
+        out_shape=jax.ShapeDtypeStruct((rows, width), BF16),
+        compiler_params=pltpu.CompilerParams(vmem_limit_bytes=VMEM_LIMIT),
+        cost_estimate=SMALL_COST,
+    )(*parts, *after)
+
+
+def widen(source, width, after):
+    rows, cols = source.shape
+    count = cols // width - 2
+
+    def kernel(source_ref, *refs):
+        up_ref, down_ref = refs[-2:]
+        up_ref[...] = source_ref[:, : 2 * width].astype(F32)
+        for i in range(count):
+            down_ref[i] = source_ref[:, (2 + i) * width : (3 + i) * width].astype(F32)
+
+    return pl.pallas_call(
+        kernel,
+        grid=(1,),
+        in_specs=[pl.BlockSpec((rows, cols), lambda i: (0, 0))] + [ANY_SPEC] * len(after),
+        out_specs=[
+            pl.BlockSpec((rows, 2 * width), lambda i: (0, 0)),
+            pl.BlockSpec((count, rows, width), lambda i: (0, 0, 0)),
+        ],
+        out_shape=[
+            jax.ShapeDtypeStruct((rows, 2 * width), F32),
+            jax.ShapeDtypeStruct((count, rows, width), F32),
+        ],
+        compiler_params=pltpu.CompilerParams(vmem_limit_bytes=VMEM_LIMIT),
+        cost_estimate=SMALL_COST,
+    )(source, *after)
+
+
 def gate_kernel(*refs):
     refs[-1][...] = jnp.zeros_like(refs[-1])
 
@@ -183,6 +229,58 @@
         out_shape=TICK,
         cost_estimate=SMALL_COST,
     )(*after)
+
+
+def fold_kernel(counts, refs):
+    parts, comes, outs = counts
+    first = refs[1 : 1 + parts * outs]
+    second = refs[1 + parts * outs : 1 + (parts + comes) * outs]
+    for m in range(outs):
+        value = jnp.concatenate([ref[0] for ref in first[m * parts : (m + 1) * parts]], axis=-1)
+        if comes:
+            value = value.astype(F32)
+            for ref in second[m * comes : (m + 1) * comes]:
+                value = value + ref[0].astype(F32)
+            value = value.astype(BF16)
+        refs[len(refs) - outs + m][0] = value
+
+
+def fold(parts, comes, sizes, axis, at, after):
+    blocks, rows = parts[0].shape[:2]
+    width = sum(part.shape[2] for part in parts)
+    outs = sizes[axis] if axis is not None else 1
+    inner = 1
+    if axis is not None:
+        for size in sizes[axis + 1 :]:
+            inner *= size
+
+    def spec(array, m):
+        def index(j, at_ref):
+            if axis is None:
+                return j, 0, 0
+            return (j // inner) * (outs * inner) + (at_ref[0] ^ m) * inner + j % inner, 0, 0
+
+        return pl.BlockSpec((1, rows, array.shape[2]), index)
+
+    def kernel(*refs):
+        ins = 1 + (len(parts) + len(comes)) * outs
+        fold_kernel((len(parts), len(comes), outs), refs[:ins] + refs[ins + len(after) :])
+
+    out = pl.BlockSpec((1, rows, width), lambda j, at_ref: (j, 0, 0))
+    return pl.pallas_call(
+        kernel,
+        grid_spec=pltpu.PrefetchScalarGridSpec(
+            num_scalar_prefetch=1,
+            grid=(blocks // outs,),
+            in_specs=[spec(part, m) for m in range(outs) for part in parts]
+            + [spec(come, m) for m in range(outs) for come in comes]
+            + [ANY_SPEC] * len(after),
+            out_specs=[out] * outs,
+        ),
+        out_shape=[jax.ShapeDtypeStruct((blocks // outs, rows, width), BF16)] * outs,
+        compiler_params=pltpu.CompilerParams(vmem_limit_bytes=VMEM_LIMIT),
+        cost_estimate=SMALL_COST,
+    )(at.reshape(1).astype(jnp.int32), *(list(parts) * outs), *(list(comes) * outs), *after)
 
 
 def qkv_kernel(x_ref, wa_ref, wb_ref, vec_ref, col_ref, *rest_refs):
@@ -346,25 +444,25 @@
 ROWS = 256
 
 
-def attention_forward(pair, qkv, query_code, key_code, after):
-    length = qkv.shape[0]
+def attention_forward(qkv, query_code, key_code):
+    length, width = qkv.shape
+    pairs = width // (3 * PAIR)
     return pl.pallas_call(
         attention_forward_kernel,
-        grid=(1,),
+        grid=(pairs,),
         in_specs=[
-            pl.BlockSpec((length, 3 * PAIR), lambda p: (0, pair)),
+            pl.BlockSpec((length, 3 * PAIR), lambda p: (0, p)),
             pl.BlockSpec((length, PAIR), lambda p: (0, 0)),
             pl.BlockSpec((length, PAIR), lambda p: (0, 0)),
-        ]
-        + [pl.BlockSpec(memory_space=pl.ANY)] * len(after),
+        ],
         out_specs=[
-            pl.BlockSpec((length, PAIR), lambda p: (0, 0)),
-            pl.BlockSpec((1, 8, length), lambda p: (0, 0, 0)),
+            pl.BlockSpec((length, PAIR), lambda p: (0, p)),
+            pl.BlockSpec((1, 8, length), lambda p: (p, 0, 0)),
             TICK_SPEC,
         ],
         out_shape=[
-            jax.ShapeDtypeStruct((length, PAIR), BF16),
-            jax.ShapeDtypeStruct((1, 8, length), F32),
+            jax.ShapeDtypeStruct((length, pairs * PAIR), BF16),
+            jax.ShapeDtypeStruct((pairs, 8, length), F32),
             TICK,
         ],
         scratch_shapes=[
@@ -375,10 +473,10 @@
         ],
         compiler_params=pltpu.CompilerParams(vmem_limit_bytes=VMEM_LIMIT),
         cost_estimate=SMALL_COST,
-    )(qkv, query_code, key_code, *after)
-
-
-def norm_one_kernel(own, core_ref, d0_ref, d1_ref, d2_ref, wa_ref, wb_ref, x_ref, *rest):
+    )(qkv, query_code, key_code)
+
+
+def norm_one_kernel(own, core_ref, d0_ref, d1_ref, wa_ref, wb_ref, x_ref, *rest):
     if own:
         come_ref, mid_ref, vec_ref, out_ref, sums_ref, bias_ref, tick_ref, w = rest
     else:
@@ -394,8 +492,8 @@
         tick_ref[...] = jnp.zeros_like(tick_ref)
 
     total = None
-    for i, ref in enumerate((d0_ref, d1_ref, d2_ref)):
-        cols = slice(i * 3 * PAIR, (i + 1) * 3 * PAIR)
+    for i, ref in enumerate((d0_ref, d1_ref)):
+        cols = slice(0, ref.shape[1]) if i == 0 else slice(d0_ref.shape[1], None)
         grad = ref[...]
         part = mm(grad, w[:, cols], NT)
         total = part if i == 0 else total + part
@@ -424,7 +522,7 @@
 
     plain = pl.BlockSpec((ROWS, width), lambda i, core_ref: (i, 0))
     rows = pl.BlockSpec((ROWS, width), block)
-    in_specs = [pl.BlockSpec((ROWS, 3 * PAIR), block)] * 3 + [
+    in_specs = [pl.BlockSpec((ROWS, grad.shape[1]), block) for grad in grads] + [
         pl.BlockSpec(weight_a.shape, at_zero),
         pl.BlockSpec(weight_b.shape, at_zero),
         rows,
@@ -464,30 +562,31 @@
 
 
 def attention_backward(
-    pair, qkv, query_code, key_code, attended, grad_attended, log_total, normed_t, after
+    first, count, qkv, query_code, key_code, attended, grad_attended, log_total, normed_t, after
 ):
     length = qkv.shape[0]
+    width = normed_t.shape[0]
     return pl.pallas_call(
         attention_backward_kernel,
-        grid=(1,),
+        grid=(count,),
         in_specs=[
-            pl.BlockSpec((length, 3 * PAIR), lambda p: (0, pair)),
+            pl.BlockSpec((length, 3 * PAIR), lambda p: (0, first + p)),
             pl.BlockSpec((length, PAIR), lambda p: (0, 0)),
             pl.BlockSpec((length, PAIR), lambda p: (0, 0)),
-            pl.BlockSpec((length, PAIR), lambda p: (0, 0)),
-            pl.BlockSpec((length, PAIR), lambda p: (0, pair)),
-            pl.BlockSpec((1, 8, length), lambda p: (0, 0, 0)),
+            pl.BlockSpec((length, PAIR), lambda p: (0, first + p)),
+            pl.BlockSpec((length, PAIR), lambda p: (0, first + p)),
+            pl.BlockSpec((1, 8, length), lambda p: (first + p, 0, 0)),
             pl.BlockSpec(normed_t.shape, lambda p: (0, 0)),
         ]
-        + [pl.BlockSpec(memory_space=pl.ANY)] * len(after),
+        + [ANY_SPEC] * len(after),
         out_specs=[
-            pl.BlockSpec((length, 3 * PAIR), lambda p: (0, 0)),
-            pl.BlockSpec((normed_t.shape[0], 3 * PAIR), lambda p: (0, 0)),
+            pl.BlockSpec((length, 3 * PAIR), lambda p: (0, p)),
+            pl.BlockSpec((width, 3 * PAIR), lambda p: (0, p)),
             TICK_SPEC,
         ],
         out_shape=[
-            jax.ShapeDtypeStruct((length, 3 * PAIR), BF16),
-            jax.ShapeDtypeStruct((normed_t.shape[0], 3 * PAIR), BF16),
+            jax.ShapeDtypeStruct((length, count * 3 * PAIR), BF16),
+            jax.ShapeDtypeStruct((width, count * 3 * PAIR), BF16),
             TICK,
         ],
         scratch_shapes=[
@@ -571,27 +670,23 @@
     def place(self, d):
         return self.side if d == "x" else self.groups[d][2]
 
-    def begin_reduce(self, state, d):
-        array, dims = state
-        axis, at = dims.index(d), self.place(d)
-        kept = lax.dynamic_index_in_dim(array, at, axis, keepdims=False)
-        come = [
-            self.send(lax.dynamic_index_in_dim(array, at ^ mask, axis, keepdims=False), d, mask)
-            for mask in range(1, array.shape[axis])
-        ]
-        return kept, come, [other for other in dims if other != d]
-
-    def end_reduce(self, begun, tick=None):
-        kept, come, dims = begun
-        total = kept.astype(F32)
-        for block in come:
-            total = total + block.astype(F32)
-        if tick is not None:
-            total = total + tick[0, 0]
-        return total.astype(BF16), dims
-
-    def reduce(self, state, d, tick=None):
-        return self.end_reduce(self.begin_reduce(state, d), tick)
+    def scatter(self, parts, comes, dims, d, after=()):
+        axis = dims.index(d)
+        shares = fold(parts, comes, self.counts(dims), axis, self.place(d), list(after))
+        come = [self.send(share, d, mask) for mask, share in enumerate(shares) if mask > 0]
+        return [shares[0]], come, [other for other in dims if other != d]
+
+    def scatter_rest(self, state):
+        for d in self.rest:
+            state = self.scatter(*state, d)
+        return self.total(state)
+
+    def total(self, state):
+        parts, comes, dims = state
+        total = parts[0].astype(F32)
+        for come in comes:
+            total = total + come.astype(F32)
+        return total[0]
 
     def begin_gather(self, state, d):
         array, dims = state
@@ -615,18 +710,6 @@
 
     def gather(self, state, d, tick=None):
         return self.end_gather(self.begin_gather(state, d), tick)
-
-    def settle(self, tick, *stages):
-        return gate([tick] + [block for stage in stages for block in stage[1]])
-
-    def rows(self, array, lead=()):
-        shape = list(lead) + self.counts(self.dims)
-        count = 1
-        for size in shape:
-            count *= size
-        names = ["lead"] * len(lead) + self.dims
-        return array.reshape(shape + [array.shape[0] // count, array.shape[1]]), names
-
 
 def body(
     tokens,
@@ -742,8 +825,7 @@
     begun = [
         links.begin_gather(piece, d) for piece, d in zip(halves_of(gather_rest(early)), "yx")
     ]
-    late_tick = gate([block for piece in begun for block in piece[1]] + [other])
-    early_halves = [links.end_gather(piece, late_tick) for piece in begun]
+    early_halves = [links.end_gather(piece) for piece in begun]
     early_a, early_b = joined(
         [links.gather(piece, d) for piece, d in zip(early_halves, "xy")]
     )
@@ -752,10 +834,12 @@
         jnp.concatenate([up_cols, jnp.broadcast_to(out_weight, (2, own, width))], axis=2)
     )
     down_own = down_weight.reshape(splits, pair_row, width)
-    late = jnp.concatenate([late] + [down_own[i] for i in range(splits)], axis=1)
-    late = late + late_tick[0, 0].astype(BF16)
-    late_one, late_two = halves_of((late, []))
-    late_one = gather_rest(late_one[0])
+    late = lax.all_gather(
+        pack([late, *(down_own[i] for i in range(splits))], [begun[0][1][0], begun[1][1][0], other]),
+        ("dp", "xx"),
+        axis=0,
+        tiled=True,
+    )
     small = early_b[:, cols - split :].astype(F32).T
     gain_one, shift_one, query_shift, value_shift, out_shift, gain_two, shift_two, down_shift = (
         small[i] for i in range(8)
@@ -784,32 +868,9 @@
         early_b,
         jnp.pad(jnp.stack([gain_one, shift_one]), ((0, 6), (0, 0))),
         jnp.pad(jnp.concatenate([qkv_shift, qkv_scale]), ((0, 6), (0, 0))),
-        [late_one[0]],
-    )
-    attended_pairs, log_totals = [], []
-    for d in links.rest[:-1]:
-        late_two = links.gather(late_two, d)
-    begun = links.begin_gather(late_two, links.rest[-1])
-    stage_one = links.begin_gather(late_one, "x")
-    late_two = links.end_gather(begun, links.settle(tick, begun))
-    stage_two = links.begin_gather(late_two, "y")
-    after = [late_two[0]]
-    for pair in range(pairs):
-        one_pair = attention_forward(pair, qkv, query_code, key_code, after)
-        attended_pairs.append(one_pair[0])
-        log_totals.append(one_pair[1])
-        tick = one_pair[2]
-        after = [one_pair[0]]
-        if pair == 0:
-            tick = links.settle(tick, stage_one, stage_two)
-            late_one, late_two = links.end_gather(stage_one, tick), links.end_gather(stage_two, tick)
-            after += [late_one[0], late_two[0]]
-            stage_one = links.begin_gather(late_one, "y")
-            stage_two = links.begin_gather(late_two, "x")
-    attended = jnp.concatenate(attended_pairs, axis=1)
-    tick = links.settle(tick, stage_one, stage_two)
-    late_halves = joined([links.end_gather(stage, tick) for stage in (stage_one, stage_two)])
-    late = jnp.concatenate(late_halves, axis=1)
+        [],
+    )
+    attended, log_total, _ = attention_forward(qkv, query_code, key_code)
     proj_up = late[:, :hidden]
     proj_out = lax.dynamic_slice_in_dim(late[:, hidden : hidden + width], core * half, half, 0)
     proj_down = jnp.concatenate(
@@ -830,15 +891,20 @@
         jnp.pad(up_shift[None], ((0, 7), (0, 0))),
     )
     partial_come = swap(partial_two, "core")
+    ffn_own = own_rows(ffn).astype(F32) + swap(other_rows(ffn), "core").astype(F32)
     middle_own = own_rows(inputs_low).astype(F32) + (
         own_rows(branch).astype(F32) + own_rows(branch_come).astype(F32)
     )
+
+    mixed, _ = from_sequence((middle_own + out_shift + ffn_own + down_shift).astype(BF16))
 
     grad_proj_down = [
         mm(hidden_low[:, i * width : (i + 1) * width], grad_out_low, TN).astype(BF16)
         for i in range(splits)
     ]
     grad_proj_up = mm(normed_two_low, grad_pre_low, TN).astype(BF16)
+    late_grads = jnp.concatenate([grad_proj_up, *grad_proj_down], axis=1)
+    late_own = lax.psum_scatter(late_grads, ("dp", "xx"), scatter_dimension=0, tiled=True)
     grad_middle, branch_low, grad_attended, mid_sums, tick = norm_two(
         inputs_low,
         branch,
@@ -848,7 +914,7 @@
         partial_come,
         proj_out,
         mid_vectors,
-        [*grad_proj_down, grad_proj_up],
+        [late_grads],
     )
     grad_proj_out = mm(attended, branch_low, TN)
 
@@ -862,75 +928,29 @@
     small_two = [mid_sums[i] for i in range(4)] + [
         up_sums[0, i * width : (i + 1) * width] for i in range(splits)
     ]
-    down_piece = links.rows(
-        jnp.concatenate(grad_proj_down, axis=0) + tick[0, 0].astype(BF16), (splits,)
-    )
-    up_piece = links.rows(grad_proj_up + tick[0, 0].astype(BF16))
-    ffn_come = swap(other_rows(ffn) + tick[0, 0].astype(BF16), "core")
     out_low = grad_proj_out.astype(BF16)
     grad_out_rows = jnp.concatenate(
         [only_mine(core == 0, out_low), only_mine(core == 1, out_low)], axis=0
     )
 
-    def reduce_rest(piece, start=0):
-        for d in links.rest[start:]:
-            piece = links.reduce(piece, d)
-        return piece
-
-    grads, weight_grads, after = [], [], [down_piece[0], up_piece[0]]
-    for pair in range(pairs):
-        grad, weight_grad, tick = attention_backward(
-            pair,
-            qkv,
-            query_code,
-            key_code,
-            attended_pairs[pair],
-            grad_attended,
-            log_totals[pair],
-            normed_t,
-            after + grads[-1:],
+    def blocks(array):
+        return array.reshape(chips, pair_row, array.shape[1])
+
+    def pairs_backward(first, count, after):
+        return attention_backward(
+            first, count, qkv, query_code, key_code, attended, grad_attended, log_total, normed_t, after
         )
-        grads.append(grad)
-        weight_grads.append(weight_grad)
-        if pair == 0:
-            begun = [links.begin_reduce(down_piece, "x"), links.begin_reduce(up_piece, "y")]
-            tick = links.settle(tick, *begun, (None, [ffn_come]))
-            down_piece, up_piece = [links.end_reduce(piece, tick) for piece in begun]
-            first_piece = links.rows(
-                jnp.concatenate([grad_out_rows, weight_grad], axis=1) + tick[0, 0].astype(BF16)
-            )
-            after = [down_piece[0], up_piece[0], first_piece[0]]
-        elif pair == 1:
-            begun = [
-                links.begin_reduce(down_piece, links.rest[0]),
-                links.begin_reduce(up_piece, "x"),
-                links.begin_reduce(first_piece, "y"),
-            ]
-            tick = links.settle(tick, *begun)
-            ffn_own = own_rows(ffn).astype(F32) + ffn_come.astype(F32)
-            mixed_own = (middle_own + out_shift + ffn_own + down_shift + tick[0, 0]).astype(BF16)
-            mixed_come = swap(at_index(mixed_own, 1 - side), "xx")
-            down_piece, up_piece, first_piece = [links.end_reduce(piece, tick) for piece in begun]
-            down_piece = reduce_rest(down_piece, 1)
-            after = [down_piece[0], up_piece[0], first_piece[0]]
-        else:
-            begun = [
-                links.begin_reduce(down_piece, "y"),
-                links.begin_reduce(up_piece, links.rest[0]),
-            ]
-            tick = links.settle(tick, *begun, (None, [mixed_come]))
-            mixed = merged(at_index(mixed_own, side), mixed_come, tick)
-            down_piece, up_piece = [links.end_reduce(piece, tick) for piece in begun]
-            up_piece = reduce_rest(up_piece, 1)
-            after = [down_piece[0], up_piece[0]]
-    first_piece = (first_piece[0] + tick[0, 0].astype(BF16), first_piece[1])
-    begun = [
-        links.begin_reduce(first_piece, "x"),
-        links.begin_reduce(links.rows(weight_grads[1] + tick[0, 0].astype(BF16)), "y"),
-    ]
+
+    grad_a, weight_grad_a, tick = pairs_backward(0, pairs - 1, [])
+    first_piece = links.scatter(
+        [blocks(grad_out_rows), blocks(weight_grad_a)], [], links.dims, "y", [tick]
+    )
+    grad_b, weight_grad_b, tick = pairs_backward(pairs - 1, 1, [first_piece[0][0], tick, mixed])
+    grads = [grad_a, grad_b]
+    first_piece = links.scatter(*first_piece, "x", [tick])
     norm_vectors = jnp.pad(jnp.stack([gain_one, shift_one]), ((0, 6), (0, 0)))
     partial_one, norm_sums, bias_sums, _ = norm_one(
-        False, core, grads, early_a, early_b, cols, inputs_low, [], after
+        False, core, grads, early_a, early_b, cols, inputs_low, [], [first_piece[0][0]]
     )
     come = swap(partial_one, "core")
     token_own, norm_sums_own, bias_sums_own, tick = norm_one(
@@ -962,17 +982,12 @@
         ]
         + small_two
     )
-    tick = links.settle(tick, *begun)
-    first_piece, middle_piece = [links.end_reduce(piece, tick) for piece in begun]
-    begun = links.begin_reduce(first_piece, links.rest[0])
-    first_own = reduce_rest(links.end_reduce(begun), 1)[0]
-    last_piece = links.reduce(
-        links.rows(jnp.concatenate([weight_grads[2], small.astype(BF16)], axis=1)), "y"
-    )
-    last_piece = (jnp.concatenate([middle_piece[0], last_piece[0]], axis=-1), last_piece[1])
-    begun = links.begin_reduce(links.reduce(last_piece, "x"), links.rest[0])
-    tick = links.settle(tick, begun, (None, [come]))
-    last_own = reduce_rest(links.end_reduce(begun, tick), 1)[0]
+    last_piece = links.scatter(
+        [blocks(weight_grad_b), blocks(small.astype(BF16))], [], links.dims, "y", [tick]
+    )
+    first_own = links.scatter_rest(first_piece)
+    last_piece = links.scatter(*last_piece, "x", [come])
+    last_own = links.scatter_rest(last_piece)
 
     def rows_of(array, index):
         return lax.dynamic_slice_in_dim(array, index * own, own, 0)
@@ -983,8 +998,9 @@
     def shared(array):
         return rows_of(array, core), swap(rows_of(array, 1 - core), "core")
 
-    late_mine, late_come = shared(up_piece[0])
-    early_mine, early_come = shared(jnp.concatenate([first_own, last_own], axis=1))
+    up_own, down_grad = widen(late_own, width, [last_own])
+    late_mine, late_come = shared(up_own)
+    early_mine, early_come = shared(jnp.concatenate([first_own, last_own], axis=1).astype(BF16))
     out_grad = early_mine[:, :width].astype(F32) + early_come[:, :width].astype(F32)
     up_grad = (
         by_core(late_mine, late_come)
@@ -993,7 +1009,7 @@
         .reshape(own, 2 * hidden)
         .astype(F32)
     )
-    down_grad = down_piece[0].reshape(hidden_own, width).astype(F32)
+    down_grad = down_grad.reshape(hidden_own, width)
     qkv_grad = (
         by_core(early_mine[:, width : width + cols], early_come[:, width : width + cols])
         .reshape(2, own, pairs, 3, PAIR)

time: 498 us -> 401 us (0.81)
  other arithmetic: 83.5 us -> 27.7 us
  local copies, waits for them, and re-layouts: 89.2 us -> 40.7 us
  waiting for transfers between devices: 55.8 us -> 93.8 us
  starting transfers between devices: 58.5 us -> 32 us
  between operations: 4.47 us -> 15.4 us
  Pallas kernels: 178 us -> 171 us
    ppermute x30 -> x13, starting transfers between devices: 42.5 us -> 17.8 us  [send(): return lax.ppermute(value, 'dp', [(i, i ^ move) for i in range(self.size)])]
    ppermute x22 -> x18, waiting for transfers between devices: 26.6 us -> 51.2 us  [swap(): return lax.ppermute(value, axis, [(0, 1), (1, 0)])]
    convert_element_type x17 -> x1, other arithmetic: 25.4 us -> 4.88 us  [body(): (middle_own + out_shift + ffn_own + down_shift).astype(BF16)]
    all_gather x0 -> x1, waiting for transfers between devices: none -> 19.3 us  [body(): lax.all_gather(pack([late, *(down_own[i] for i in range(splits))], [begun...]
    add x14 -> x0, other arithmetic: 19.1 us -> none  [the longest x7 12.7 us: end_gather(): joined = joined + tick[0, 0].astype(joined.dtype)]
    unnamed x310 -> x113, local copies, waits for them, and re-layouts: 29.2 us -> 14.9 us
    ppermute x8 -> x0, local copies, waits for them, and re-layouts: 13.1 us -> none  [the longest x7 10.7 us: send(): return lax.ppermute(value, 'dp', [(i, i ^ move) for i in range(self.size)])]
    another operation x14 -> x8, other arithmetic: 14.1 us -> 3.3 us  [end_gather(): joined = jnp.stack(parts, axis=dims.index(d))]
  transfers between devices with their start and end apart: 52 -> 33, of which waited for: 12 -> 14; matrix products, arithmetic and copies ran while one was open for 27% -> 17% of each run, Pallas kernels for 26% -> 35%
where the time goes in v5:
time: 401 us; the launch traced here: 397 us
  Pallas kernels  171 us (43%)
  waiting for transfers between devices  93.8 us (23%)
  local copies, waits for them, and re-layouts  40.7 us (10%)
  starting transfers between devices  32 us (8%)
  other arithmetic  27.7 us (7%)
  matrix products  17.1 us (4%)
  between operations  15.4 us (4%)
    pallas_call x2, Pallas kernels, attention_backward(): pl.pallas_call(attention_backward_kernel, grid=(count,), in_specs=[pl.Blo...  64.2 us
    ppermute x18, waiting for transfers between devices, swap(): return lax.ppermute(value, axis, [(0, 1), (1, 0)])  51.2 us
    pallas_call x1, Pallas kernels, attention_forward(): pl.pallas_call(attention_forward_kernel, grid=(pairs,), in_specs=[pl.Bloc...  37.8 us
    pallas_call x1, Pallas kernels, feed_forward(): pl.pallas_call(feed_forward_kernel, grid=(length // ROWS,), in_specs=[nar...  29.8 us
    ppermute x13, waiting for transfers between devices, send(): return lax.ppermute(value, 'dp', [(i, i ^ move) for i in range(self.size)])  23.3 us
    all_gather x1, waiting for transfers between devices, body(): lax.all_gather(pack([late, *(down_own[i] for i in range(splits))], [begun...  19.3 us
    ppermute x13, starting transfers between devices, send(): return lax.ppermute(value, 'dp', [(i, i ^ move) for i in range(self.size)])  17.8 us
    dot_general x5, matrix products, mm(): return lax.dot_general(left, right, dims, preferred_element_type=F32)  17.1 us
  transfers between devices with their start and end apart: 33, of which 14 were waited for; matrix products, arithmetic and copies ran while one was open for 17% of the time, Pallas kernels for 35%

profile of v5, /device:TPU:0, one launch (start us, length us, event | category | flops | bytes accessed | tf_op | source)
XLA Modules:
  0.0 397.5 jit_solution(16731212833353840857)
XLA Ops:
  10.5 1.3 reshape.195
  13.5 2.9 collective-permute-start
  17.8 1.6 collective-permute-start.3
  19.4 2.6 collective-permute-start.4
  22.2 12.2 %collective-permute-done.refs_0_ = bf16[512,768]{1,0:T(8,128)(2,1)S(1)} collective-permute-done((bf16[512,768]{1,0:T(8,128)(2,1)}, bf16[512,768]{1,0:T(8,128)(2,1)S(1)}, u32[]{:S(2)}, u32[]{:S(2)}) %collective-permute-start) | collective-permute-done | bytes 786464 | tf_op jit(solution)/shard_map/ppermute | solution.py:639
  37.6 1.8 collective-permute-start.6
  39.4 1.5 collective-permute-start.8
  41.0 5.1 %collective-permute-done.6.refs_3_ = bf16[4,48,640]{2,1,0:T(8,128)(2,1)S(1)} collective-permute-done((bf16[4,48,640]{2,1,0:T(8,128)(2,1)S(1)}, bf16[4,48,640]{2,1,0:T(8,128)(2,1)S(1)}, u32[]{:S(2)}, u32[]{:S(2)}) %collective-permute-start.6) | collective-permute-done | bytes 245792 | tf_op jit(solution)/shard_map/ppermute | solution.py:668
  46.1 1.5 collective-permute-done.8.refs_4_
  48.3 1.1 copy-done.3
  51.2 1.5 collective-permute-start.7
  56.3 2.8 add_bitcast_fusion
  59.4 8.8 %collective-permute-done.7 = bf16[4,2,48,640]{3,2,0,1:T(8,128)(2,1)S(1)} collective-permute-done((bf16[4,2,48,640]{3,2,0,1:T(8,128)(2,1)}, bf16[4,2,48,640]{3,2,0,1:T(8,128)(2,1)S(1)}, u32[]{:S(2)}, u32[]{:S(2)}) %collective-permute-start.7) | collective-permute-done | bytes 491552 | tf_op jit(solution)/shard_map/ppermute | solution.py:639
  68.6 1.2 select_bitcast_fusion.5
  71.8 1.1 slice_select_fusion.vec_ref.refs_8_
  74.8 1.9 copy.67
  76.7 8.5 %shard_map.280 = (bf16[768,2048]{1,0:T(8,128)(2,1)S(1)}, bf16[2048,1152]{1,0:T(8,128)(2,1)}, f32[8,128]{1,0:T(8,128)}) custom-call(bf16[2048,768]{1,0:T(8,128)(2,1)} %bitcast.221, bf16[768,640]{1,0:T(8,128)(2,1)S(1)} %bitcast.208, bf16[768,640]{1,0:T(8,128)(2,1)S(1)} %bitcast.205, f32[8,768]{1,0:T(8,128)S(1)} %slice_select_fusion.vec_ref.refs_8_, ...), custom_call_target="tpu_custom_call" | custom-call | flops 100000000 | bytes 1000000 | tf_op jit(solution)/shard_map/pallas_call | solution.py:304
  85.2 1.7 copy-done.2
  86.9 37.8 %shard_map.281 = (bf16[2048,384]{1,0:T(8,128)(2,1)S(1)}, f32[3,8,2048]{2,1,0:T(8,128)S(1)}, f32[8,128]{1,0:T(8,128)}) custom-call(bf16[2048,1152]{1,0:T(8,128)(2,1)} %get-tuple-element.60.qkv_ref, bf16[2048,128]{1,0:T(8,128)(2,1)S(1)} %get-tuple-element.173.qs_ref, bf16[2048,128]{1,0:T(8,128)(2,1)S(1)} %get-tuple-element.172.ks_ref), custom_call_target="tpu_custom_call" | custom-call | flops 100000000 | bytes 1000000 | tf_op jit(solution)/shard_map/pallas_call | solution.py:450
  124.7 1.1 copy-done.5
  125.8 19.3 %all-gather.2.cloned.1.call-done = bf16[768,3840]{1,0:T(8,128)(2,1)} async-done(((bf16[48,3840]{1,0:T(8,128)(2,1)}), bf16[768,3840]{1,0:T(8,128)(2,1)}) %all-gather.2.cloned.1.call-update) | async-done | bytes 5898256 | tf_op jit(solution)/shard_map/all_gather | solution.py:837
  145.1 2.3 fusion.46
  147.6 1.8 convolution_convert_fusion.1.b0_ref
  149.5 1.8 fusion.18
  153.1 4.3 %collective-permute-done.13 = bf16[2,512,768]{2,1,0:T(8,128)(2,1)S(1)} collective-permute-done((bf16[2,512,768]{2,1,0:T(8,128)(2,1)S(1)}, bf16[2,512,768]{2,1,0:T(8,128)(2,1)S(1)}, u32[]{:S(2)}, u32[]{:S(2)}) %collective-permute-start.13) | collective-permute-done | bytes 1572896 | tf_op jit(solution)/shard_map/ppermute | solution.py:639
  157.9 2.0 copy.78
  159.9 1.8 slice.223.up_ref
  161.9 1.6 copy-done.27
  163.5 29.8 %shard_map.284 = (bf16[2048,768]{1,0:T(8,128)(2,1)}, bf16[2048,1536]{1,0:T(8,128)(2,1)}, bf16[2048,1536]{1,0:T(8,128)(2,1)}, bf16[2048,768]{1,0:T(8,128)(2,1)}, ...) custom-call(bf16[2048,768]{1,0:T(8,128)(2,1)} %bitcast.222, bf16[2048,768]{1,0:T(8,128)(2,1)} %copy-done.26, ...), custom_call_target="tpu_custom_call" | custom-call | flops 100000000 | bytes 1000000 | tf_op jit(solution)/shard_map/pallas_call | solution.py:372
  193.4 2.8 dynamic-slice_bitcast_fusion
  196.6 8.4 %convolution_convert_fusion = bf16[768,1536]{1,0:T(8,128)(2,1)S(1)} fusion(bf16[2048,768]{1,0:T(8,128)(2,1)} %get-tuple-element.64, bf16[2048,1536]{1,0:T(8,128)(2,1)} %get-tuple-element.65), kind=kOutput, calls=%fused_computation.4 | convolution fusion | flops 4833017856 | bytes 11796480 | tf_op jit(solution)/shard_map/dot_general | solution.py:24
  205.0 2.8 fusion.8
  207.8 2.7 fusion.11
  210.5 2.7 pad_maximum_fusion.rest_0_
  213.2 4.9 %fusion.2 = bf16[2,512,768]{2,1,0:T(8,128)(2,1)S(1)} fusion(bf16[2,512,768]{2,1,0:T(8,128)(2,1)} %collective-permute-done.14, s32[]{:T(128)S(6)} %select_n.314, bf16[2,1,512,768]{3,2,0,1:T(8,128)(2,1)} %copy-done.28, bf16[2,1,512,768]{3,2,0,1:T(8,128)(2,1)} %copy-done.29, f32[768]{0:T(1024)S(1)} %get-tuple-element.106, ...), kind=kLoop, calls=%fused_computation.10 | loop fusion | flops 10223616 | bytes 11016196 | tf_op jit(solution)/shard_map/convert_element_type | solution.py:899
  218.2 1.4 collective-permute-start.15
  219.6 13.3 %shard_map.285 = (f32[2048,768]{1,0:T(8,128)}, bf16[2048,768]{1,0:T(8,128)(2,1)S(1)}, bf16[2048,384]{1,0:T(8,128)(2,1)S(1)}, f32[8,768]{1,0:T(8,128)S(1)}, f32[8,128]{1,0:T(8,128)}) custom-call(bf16[2048,768]{1,0:T(8,128)(2,1)} %bitcast.223, bf16[2048,768]{1,0:T(8,128)(2,1)} %copy-done.26, bf16[2048,768]{1,0:T(8,128)(2,1)} %copy-done.27, ...), custom_call_target="tpu_custom_call" | custom-call | flops 100000000 | bytes 1000000 | tf_op jit(solution)/shard_map/pallas_call | solution.py:421
  233.0 1.4 broadcast_select_fusion.1
  234.5 42.2 %shard_map.286 = (bf16[2048,768]{1,0:T(8,128)(2,1)}, bf16[768,768]{1,0:T(8,128)(2,1)S(1)}, f32[8,128]{1,0:T(8,128)S(1)}) custom-call(bf16[2048,1152]{1,0:T(8,128)(2,1)} %get-tuple-element.60.qkv_ref, bf16[2048,128]{1,0:T(8,128)(2,1)S(1)} %get-tuple-element.173.qs_ref, bf16[2048,128]{1,0:T(8,128)(2,1)S(1)} %get-tuple-element.172.ks_ref, ...), custom_call_target="tpu_custom_call" | custom-call | flops 100000000 | bytes 1000000 | tf_op jit(solution)/shard_map/pallas_call | solution.py:569
  277.0 1.2 collective-permute-start.17
  278.3 1.3 pad_maximum_fusion.6.rest_2_
  279.6 22.0 %shard_map.288 = (bf16[2048,384]{1,0:T(8,128)(2,1)S(1)}, bf16[768,384]{1,0:T(8,128)(2,1)S(1)}, f32[8,128]{1,0:T(8,128)S(1)}) custom-call(bf16[2048,1152]{1,0:T(8,128)(2,1)} %get-tuple-element.60.qkv_ref, bf16[2048,128]{1,0:T(8,128)(2,1)S(1)} %get-tuple-element.173.qs_ref, bf16[2048,128]{1,0:T(8,128)(2,1)S(1)} %get-tuple-element.172.ks_ref, ...), custom_call_target="tpu_custom_call" | custom-call | flops 100000000 | bytes 1000000 | tf_op jit(solution)/shard_map/pallas_call | solution.py:569
  302.5 7.4 %collective-permute-done.17.refs_3_.refs_4_ = bf16[8,48,1536]{2,1,0:T(8,128)(2,1)S(1)} collective-permute-done((bf16[8,48,1536]{2,1,0:T(8,128)(2,1)S(1)}, bf16[8,48,1536]{2,1,0:T(8,128)(2,1)S(1)}, u32[]{:S(2)}, u32[]{:S(2)}) %collective-permute-start.17) | collective-permute-done | bytes 1179680 | tf_op jit(solution)/shard_map/ppermute | solution.py:668
  309.9 1.5 shard_map.289
  311.3 5.6 %shard_map.290 = (bf16[1024,768]{1,0:T(8,128)(2,1)}, f32[8,768]{1,0:T(8,128)S(1)}, f32[8,1152]{1,0:T(8,128)S(1)}, f32[8,128]{1,0:T(8,128)}) custom-call(s32[1]{0:T(128)} %bitcast.57.refs_0_, bf16[2048,768]{1,0:T(8,128)(2,1)} %get-tuple-element.70.refs_1_, bf16[2048,384]{1,0:T(8,128)(2,1)S(1)} %get-tuple-element.75.refs_2_, bf16[768,640]{1,0:T(8,128)(2,1)S(1)} %bitcast.209, ...), custom_call_target="tpu_custom_call" | custom-call | flops 100000000 | bytes 1000000 | tf_op jit(solution)/shard_map/pallas_call | solution.py:549
  318.1 1.3 collective-permute-start.20
  320.7 13.4 %collective-permute-done.20.refs_5_.refs_6_.refs_7_.refs_8_ = bf16[4,48,1536]{2,1,0:T(8,128)(2,1)S(1)} collective-permute-done((bf16[4,48,1536]{2,1,0:T(8,128)(2,1)}, bf16[4,48,1536]{2,1,0:T(8,128)(2,1)S(1)}, u32[]{:S(2)}, u32[]{:S(2)}) %collective-permute-start.20) | collective-permute-done | bytes 589856 | tf_op jit(solution)/shard_map/ppermute | solution.py:639
  334.9 1.2 collective-permute-start.21
  336.1 1.3 collective-permute-start.22
  337.4 1.9 collective-permute-start.23
  339.3 6.4 %shard_map.291 = (bf16[1024,768]{1,0:T(8,128)(2,1)S(1)}, f32[8,768]{1,0:T(8,128)S(1)}, f32[8,1152]{1,0:T(8,128)S(1)}, f32[8,128]{1,0:T(8,128)S(1)}) custom-call(s32[1]{0:T(128)} %bitcast.57.refs_0_, bf16[2048,768]{1,0:T(8,128)(2,1)} %get-tuple-element.70.refs_1_, bf16[2048,384]{1,0:T(8,128)(2,1)S(1)} %copy-done.10, bf16[768,640]{1,0:T(8,128)(2,1)S(1)} %bitcast.210, ...), custom_call_target="tpu_custom_call" | custom-call | flops 100000000 | bytes 1000000 | tf_op jit(solution)/shard_map/pallas_call | solution.py:549
  348.3 1.3 collective-permute-start.19
  350.3 1.0 collective-permute-start.24
  351.3 4.8 %collective-permute-done.22 = bf16[1,48,1536]{2,1,0:T(8,128)(2,1)} collective-permute-done((bf16[1,48,1536]{2,1,0:T(8,128)(2,1)}, bf16[1,48,1536]{2,1,0:T(8,128)(2,1)}, u32[]{:S(2)}, u32[]{:S(2)}) %collective-permute-start.22) | collective-permute-done | bytes 147488 | tf_op jit(solution)/shard_map/ppermute | solution.py:668
  356.0 1.1 fusion.22
  357.2 2.8 collective-permute-done.24.refs_3_.refs_4_
  360.0 6.8 %collective-permute-done.19.refs_5_ = bf16[512,768]{1,0:T(8,128)(2,1)S(1)} collective-permute-done((bf16[512,768]{1,0:T(8,128)(2,1)}, bf16[512,768]{1,0:T(8,128)(2,1)S(1)}, u32[]{:S(2)}, u32[]{:S(2)}) %collective-permute-start.19) | collective-permute-done | bytes 786464 | tf_op jit(solution)/shard_map/ppermute | solution.py:639
  367.0 1.4 collective-permute-start.25
  368.5 4.2 %collective-permute-done.25.refs_5_.refs_6_.refs_7_.refs_8_ = bf16[4,48,512]{2,1,0:T(8,128)(2,1)S(1)} collective-permute-done((bf16[4,48,512]{2,1,0:T(8,128)(2,1)S(1)}, bf16[4,48,512]{2,1,0:T(8,128)(2,1)S(1)}, u32[]{:S(2)}, u32[]{:S(2)}) %collective-permute-start.25) | collective-permute-done | bytes 196640 | tf_op jit(solution)/shard_map/ppermute | solution.py:639
  373.3 2.1 collective-permute-start.27
  375.4 1.8 collective-permute-start.28
  377.2 1.3 pad_maximum_fusion.7
  378.5 2.8 collective-permute-done.28
  388.5 1.8 reshape.210
  (260 shorter events, 39.0 us)
Async XLA Ops:
  7.2 43.0 %copy-start = (s32[2,2048]{1,0:T(2,128)S(1)}, s32[2,2048]{1,0:T(2,128)}, u32[]{:S(2)}) copy-start(s32[2,2048]{1,0:T(2,128)} %param.18) | copy-start | bytes 49156
  7.2 5.2 %copy-start.41 = (bf16[24,768]{1,0:T(8,128)(2,1)S(1)}, bf16[24,768]{1,0:T(8,128)(2,1)}, u32[]{:S(2)}) copy-start(bf16[24,768]{1,0:T(8,128)(2,1)} %param.24) | copy-start | bytes 110596
  7.2 137.9 %all-gather.2.cloned.1.call-start = ((), (), s32[]{:S(2)}) async-start(), calls=%async_computation.1 | async-start | bytes 6266880 | tf_op jit(solution)/shard_map/all_gather | solution.py:837
  8.2 4.4 %copy-start.37 = (bf16[2,512,768]{2,1,0:T(8,128)(2,1)S(1)}, bf16[2,512,768]{2,1,0:T(8,128)(2,1)}, u32[]{:S(2)}) copy-start(bf16[2,512,768]{2,1,0:T(8,128)(2,1)} %param.17) | copy-start | bytes 4718596
  10.0 6.7 %collective-permute-start.2 = (bf16[24,1280]{1,0:T(8,128)(2,1)}, bf16[24,1280]{1,0:T(8,128)(2,1)}, u32[]{:S(2)}, u32[]{:S(2)}) collective-permute-start(bf16[24,1280]{1,0:T(8,128)(2,1)} %fusion.30), channel_id=1, source_target_pairs={{0,1},{1,0},{2,3},{3,2},{4,5},{5,4},{6,7},{7,6},{8,9},{9,8},{10,11... | collective-permute-start | bytes 184328 | tf_op jit(solution)/shard_map/ppermute | solution.py:639
  11.8 4.7 %copy-start.40 = (bf16[96,768]{1,0:T(8,128)(2,1)S(1)}, bf16[96,768]{1,0:T(8,128)(2,1)}, u32[]{:S(2)}) copy-start(bf16[96,768]{1,0:T(8,128)(2,1)} %param.30) | copy-start | bytes 442372
  11.9 4.6 %copy-start.50 = (bf16[96]{0:T(256)(128)(2,1)S(1)}, bf16[96]{0:T(256)(128)(2,1)}, u32[]{:S(2)}) copy-start(bf16[96]{0:T(256)(128)(2,1)} %param.29) | copy-start | bytes 580
  12.5 24.0 %collective-permute-start.10 = (bf16[24,2304]{1,0:T(8,128)(2,1)S(1)}, bf16[24,2304]{1,0:T(8,128)(2,1)}, u32[]{:S(2)}, u32[]{:S(2)}) collective-permute-start(bf16[24,2304]{1,0:T(8,128)(2,1)S(1)} %fusion.24), channel_id=1, source_target_pairs={{0,1},{1,0},{2,3},{3,2},{4,5},{5,4},{6,7},{7,6},{8,9},{9,8},{10,11... | collective-permute-start | bytes 331784 | tf_op jit(solution)/shard_map/ppermute | solution.py:639
  13.5 20.9 %collective-permute-start = (bf16[512,768]{1,0:T(8,128)(2,1)}, bf16[512,768]{1,0:T(8,128)(2,1)S(1)}, u32[]{:S(2)}, u32[]{:S(2)}) collective-permute-start(bf16[512,768]{1,0:T(8,128)(2,1)} %dynamic-slice_bitcast_fusion.3), channel_id=1, source_target_pairs={{0,2},{2,0},{1,3},{3,1},{4,6},{6,4},{5,7},{7,5},{8,10},{10,8},{9,1... | collective-permute-start | bytes 2359304 | tf_op jit(solution)/shard_map/ppermute | solution.py:639
  17.8 19.6 %collective-permute-start.3 = (bf16[48,1280]{1,0:T(8,128)(2,1)S(1)}, bf16[48,1280]{1,0:T(8,128)(2,1)S(1)}, u32[]{:S(2)}, u32[]{:S(2)}) collective-permute-start(bf16[48,1280]{1,0:T(8,128)(2,1)S(1)} %concatenate.46), channel_id=1, source_target_pairs={{0,8},{4,12},{8,0},{12,4},{16,24},{20,28},{24,16},{28,20},{1,9},{5... | collective-permute-start | bytes 368648 | tf_op jit(solution)/shard_map/ppermute | solution.py:668
  19.4 18.0 %collective-permute-start.4 = (bf16[48,1280]{1,0:T(8,128)(2,1)S(1)}, bf16[48,1280]{1,0:T(8,128)(2,1)S(1)}, u32[]{:S(2)}, u32[]{:S(2)}) collective-permute-start(bf16[48,1280]{1,0:T(8,128)(2,1)S(1)} %concatenate.46), channel_id=1, source_target_pairs={{0,16},{4,20},{8,24},{12,28},{16,0},{20,4},{24,8},{28,12},{1,17},{... | collective-permute-start | bytes 368648 | tf_op jit(solution)/shard_map/ppermute | solution.py:668
  22.0 15.4 %collective-permute-start.5 = (bf16[48,1280]{1,0:T(8,128)(2,1)S(1)}, bf16[48,1280]{1,0:T(8,128)(2,1)S(1)}, u32[]{:S(2)}, u32[]{:S(2)}) collective-permute-start(bf16[48,1280]{1,0:T(8,128)(2,1)S(1)} %concatenate.46), channel_id=1, source_target_pairs={{0,24},{4,28},{8,16},{12,20},{16,8},{20,12},{24,0},{28,4},{1,25},{... | collective-permute-start | bytes 368648 | tf_op jit(solution)/shard_map/ppermute | solution.py:668
  36.4 11.1 %collective-permute-start.1 = (bf16[2,512,768]{2,1,0:T(8,128)(2,1)S(1)}, bf16[2,512,768]{2,1,0:T(8,128)(2,1)S(1)}, u32[]{:S(2)}, u32[]{:S(2)}) collective-permute-start(bf16[2,512,768]{2,1,0:T(8,128)(2,1)S(1)} %pad_maximum_fusion.4), channel_id=1, source_target_pairs={{0,1},{1,0},{2,3},{3,2},{4,5},{5,4},{6,7},{7,6},{8,9},{9,8},{10,11... | collective-permute-start | bytes 4718600 | tf_op jit(solution)/shard_map/ppermute | solution.py:639
  37.6 8.5 %collective-permute-start.6 = (bf16[4,48,640]{2,1,0:T(8,128)(2,1)S(1)}, bf16[4,48,640]{2,1,0:T(8,128)(2,1)S(1)}, u32[]{:S(2)}, u32[]{:S(2)}) collective-permute-start(bf16[4,48,640]{2,1,0:T(8,128)(2,1)S(1)} %get-tuple-element.145), channel_id=1, source_target_pairs={{0,4},{4,0},{8,12},{12,8},{16,20},{20,16},{24,28},{28,24},{1,5},{5... | collective-permute-start | bytes 737288 | tf_op jit(solution)/shard_map/ppermute | solution.py:668
  39.4 8.1 %collective-permute-start.8 = (bf16[4,48,640]{2,1,0:T(8,128)(2,1)S(1)}, bf16[4,48,640]{2,1,0:T(8,128)(2,1)S(1)}, u32[]{:S(2)}, u32[]{:S(2)}) collective-permute-start(bf16[4,48,640]{2,1,0:T(8,128)(2,1)S(1)} %get-tuple-element.144), channel_id=1, source_target_pairs={{0,2},{2,0},{1,3},{3,1},{4,6},{6,4},{5,7},{7,5},{8,10},{10,8},{9,1... | collective-permute-start | bytes 737288 | tf_op jit(solution)/shard_map/ppermute | solution.py:639
  47.5 2.5 copy-start.49
  49.5 334.2 %reduce-scatter.2.cloned.1.call-start = ((), (), s32[]{:S(2)}) async-start(), calls=%async_computation.2 | async-start | bytes 5013504 | tf_op jit(solution)/shard_map/reduce_scatter | solution.py:907
  51.2 17.0 %collective-permute-start.7 = (bf16[4,2,48,640]{3,2,0,1:T(8,128)(2,1)}, bf16[4,2,48,640]{3,2,0,1:T(8,128)(2,1)S(1)}, u32[]{:S(2)}, u32[]{:S(2)}) collective-permute-start(bf16[4,2,48,640]{3,2,0,1:T(8,128)(2,1)} %pad_maximum_fusion.12), channel_id=1, source_target_pairs={{0,2},{2,0},{1,3},{3,1},{4,6},{6,4},{5,7},{7,5},{8,10},{10,8},{9,1... | collective-permute-start | bytes 1474568 | tf_op jit(solution)/shard_map/ppermute | solution.py:639
  53.5 15.1 %collective-permute-start.9 = (bf16[4,2,48,640]{3,2,0,1:T(8,128)(2,1)}, bf16[4,2,48,640]{3,2,0,1:T(8,128)(2,1)S(1)}, u32[]{:S(2)}, u32[]{:S(2)}) collective-permute-start(bf16[4,2,48,640]{3,2,0,1:T(8,128)(2,1)} %pad_maximum_fusion.13), channel_id=1, source_target_pairs={{0,4},{4,0},{8,12},{12,8},{16,20},{20,16},{24,28},{28,24},{1,5},{5... | collective-permute-start | bytes 1474568 | tf_op jit(solution)/shard_map/ppermute | solution.py:668
  59.1 90.4 %collective-permute-start.12 = (bf16[512,768]{1,0:T(8,128)(2,1)}, bf16[512,768]{1,0:T(8,128)(2,1)}, u32[]{:S(2)}, u32[]{:S(2)}) collective-permute-start(bf16[512,768]{1,0:T(8,128)(2,1)} %add_bitcast_fusion), channel_id=1, source_target_pairs={{0,2},{2,0},{1,3},{3,1},{4,6},{6,4},{5,7},{7,5},{8,10},{10,8},{9,1... | collective-permute-start | bytes 2359304 | tf_op jit(solution)/shard_map/ppermute | solution.py:639
  71.1 1.8 copy-start.33
  72.9 3.8 copy-start.16
  145.1 2.5 copy-start.6
  147.5 1.9 copy-start.11
  147.6 1.9 copy-start.38
  149.4 1.9 copy-start.26
  149.4 12.4 %collective-permute-start.11 = (bf16[2048,768]{1,0:T(8,128)(2,1)S(1)}, bf16[2048,768]{1,0:T(8,128)(2,1)S(1)}, u32[]{:S(2)}, u32[]{:S(2)}) collective-permute-start(bf16[2048,768]{1,0:T(8,128)(2,1)S(1)} %convolution_convert_fusion.1.b0_ref), channel_id=1, source_target_pairs={{0,1},{1,0},{2,3},{3,2},{4,5},{5,4},{6,7},{7,6},{8,9},{9,8},{10,11... | collective-permute-start | bytes 9437192 | tf_op jit(solution)/shard_map/ppermute | solution.py:639
  151.5 5.9 %collective-permute-start.13 = (bf16[2,512,768]{2,1,0:T(8,128)(2,1)S(1)}, bf16[2,512,768]{2,1,0:T(8,128)(2,1)S(1)}, u32[]{:S(2)}, u32[]{:S(2)}) collective-permute-start(bf16[2,512,768]{2,1,0:T(8,128)(2,1)S(1)} %pad_maximum_fusion.5), channel_id=1, source_target_pairs={{0,1},{1,0},{2,3},{3,2},{4,5},{5,4},{6,7},{7,6},{8,9},{9,8},{10,11... | collective-permute-start | bytes 4718600 | tf_op jit(solution)/shard_map/ppermute | solution.py:639
  193.3 26.3 %collective-permute-start.16 = (bf16[2048,768]{1,0:T(8,128)(2,1)}, bf16[2048,768]{1,0:T(8,128)(2,1)}, u32[]{:S(2)}, u32[]{:S(2)}) collective-permute-start(bf16[2048,768]{1,0:T(8,128)(2,1)} %get-tuple-element.63.p0_ref), channel_id=1, source_target_pairs={{0,1},{1,0},{2,3},{3,2},{4,5},{5,4},{6,7},{7,6},{8,9},{9,8},{10,11... | collective-permute-start | bytes 9437192 | tf_op jit(solution)/shard_map/ppermute | solution.py:639
  193.4 11.5 %slice-start = ((s8[6291456]{0:T(1024)(128)(4,1)}), s8[4194304]{0:T(1024)(128)(4,1)S(1)}, s32[]{:S(2)}) async-start(s8[6291456]{0:T(1024)(128)(4,1)} %bitcast.250), calls=%async_computation.3 | async-start | bytes 8388608
  196.2 17.0 %collective-permute-start.14 = (bf16[2,512,768]{2,1,0:T(8,128)(2,1)}, bf16[2,512,768]{2,1,0:T(8,128)(2,1)}, u32[]{:S(2)}, u32[]{:S(2)}) collective-permute-start(bf16[2,512,768]{2,1,0:T(8,128)(2,1)} %dynamic-slice_bitcast_fusion), channel_id=1, source_target_pairs={{0,1},{1,0},{2,3},{3,2},{4,5},{5,4},{6,7},{7,6},{8,9},{9,8},{10,11... | collective-permute-start | bytes 4718600 | tf_op jit(solution)/shard_map/ppermute | solution.py:639
  196.6 8.4 %copy-start.25 = (bf16[2,2,512,768]{3,2,1,0:T(8,128)(2,1)S(1)}, bf16[2,2,512,768]{3,2,1,0:T(8,128)(2,1)}, u32[]{:S(2)}) copy-start(bf16[2,2,512,768]{3,2,1,0:T(8,128)(2,1)} %copy.78) | copy-start | bytes 9437188
  196.6 8.4 %slice-start.1 = ((s8[6291456]{0:T(1024)(128)(4,1)}), s8[2097152]{0:T(1024)(128)(4,1)S(1)}, s32[]{:S(2)}) async-start(s8[6291456]{0:T(1024)(128)(4,1)} %bitcast.250), calls=%async_computation.4 | async-start | bytes 4194304
  218.2 14.8 %copy-start.7 = (bf16[2048,384]{1,0:T(8,128)(2,1)S(1)}, bf16[2048,384]{1,0:T(8,128)(2,1)}, u32[]{:S(2)}) copy-start(bf16[2048,384]{1,0:T(8,128)(2,1)} %copy-done.5) | copy-start | bytes 4718596
  218.2 60.0 %collective-permute-start.15 = (bf16[512,768]{1,0:T(8,128)(2,1)S(1)}, bf16[512,768]{1,0:T(8,128)(2,1)S(1)}, u32[]{:S(2)}, u32[]{:S(2)}) collective-permute-start(bf16[512,768]{1,0:T(8,128)(2,1)S(1)} %dynamic-slice_bitcast_fusion.2), channel_id=1, source_target_pairs={{0,2},{2,0},{1,3},{3,1},{4,6},{6,4},{5,7},{7,5},{8,10},{10,8},{9,1... | collective-permute-start | bytes 2359304 | tf_op jit(solution)/shard_map/ppermute | solution.py:639
  277.0 32.9 %collective-permute-start.17 = (bf16[8,48,1536]{2,1,0:T(8,128)(2,1)S(1)}, bf16[8,48,1536]{2,1,0:T(8,128)(2,1)S(1)}, u32[]{:S(2)}, u32[]{:S(2)}) collective-permute-start(bf16[8,48,1536]{2,1,0:T(8,128)(2,1)S(1)} %get-tuple-element.76), channel_id=1, source_target_pairs={{0,4},{4,0},{8,12},{12,8},{16,20},{20,16},{24,28},{28,24},{1,5},{5... | collective-permute-start | bytes 3538952 | tf_op jit(solution)/shard_map/ppermute | solution.py:668
  302.5 8.9 %copy-start.9 = (bf16[2048,384]{1,0:T(8,128)(2,1)}, bf16[2048,384]{1,0:T(8,128)(2,1)S(1)}, u32[]{:S(2)}) copy-start(bf16[2048,384]{1,0:T(8,128)(2,1)S(1)} %get-tuple-element.75.refs_2_) | copy-start | bytes 4718596
  318.1 21.1 %collective-permute-start.18 = (bf16[1024,768]{1,0:T(8,128)(2,1)}, bf16[1024,768]{1,0:T(8,128)(2,1)}, u32[]{:S(2)}, u32[]{:S(2)}) collective-permute-start(bf16[1024,768]{1,0:T(8,128)(2,1)} %get-tuple-element.79), channel_id=1, source_target_pairs={{0,1},{1,0},{2,3},{3,2},{4,5},{5,4},{6,7},{7,6},{8,9},{9,8},{10,11... | collective-permute-start | bytes 4718600 | tf_op jit(solution)/shard_map/ppermute | solution.py:639
  318.1 16.0 %collective-permute-start.20 = (bf16[4,48,1536]{2,1,0:T(8,128)(2,1)}, bf16[4,48,1536]{2,1,0:T(8,128)(2,1)S(1)}, u32[]{:S(2)}, u32[]{:S(2)}) collective-permute-start(bf16[4,48,1536]{2,1,0:T(8,128)(2,1)} %get-tuple-element.82), channel_id=1, source_target_pairs={{0,2},{2,0},{1,3},{3,1},{4,6},{6,4},{5,7},{7,5},{8,10},{10,8},{9,1... | collective-permute-start | bytes 1769480 | tf_op jit(solution)/shard_map/ppermute | solution.py:639
  334.1 5.2 %copy-start.10 = (bf16[2048,384]{1,0:T(8,128)(2,1)S(1)}, bf16[2048,384]{1,0:T(8,128)(2,1)}, u32[]{:S(2)}) copy-start(bf16[2048,384]{1,0:T(8,128)(2,1)} %copy-done.9) | copy-start | bytes 4718596
  334.1 5.2 %copy-start.17 = (f32[8,768]{1,0:T(8,128)S(1)}, f32[8,768]{1,0:T(8,128)}, u32[]{:S(2)}) copy-start(f32[8,768]{1,0:T(8,128)} %copy-done.16) | copy-start | bytes 73732
  334.9 10.8 %copy-start.18 = (bf16[1,48,1536]{2,1,0:T(8,128)(2,1)}, bf16[1,48,1536]{2,1,0:T(8,128)(2,1)S(1)}, u32[]{:S(2)}) copy-start(bf16[1,48,1536]{2,1,0:T(8,128)(2,1)S(1)} %get-tuple-element.83) | copy-start | bytes 442372
  334.9 16.4 %collective-permute-start.21 = (bf16[1,48,1536]{2,1,0:T(8,128)(2,1)}, bf16[1,48,1536]{2,1,0:T(8,128)(2,1)}, u32[]{:S(2)}, u32[]{:S(2)}) collective-permute-start(bf16[1,48,1536]{2,1,0:T(8,128)(2,1)} %get-tuple-element.84), channel_id=1, source_target_pairs={{0,8},{4,12},{8,0},{12,4},{16,24},{20,28},{24,16},{28,20},{1,9},{5... | collective-permute-start | bytes 442376 | tf_op jit(solution)/shard_map/ppermute | solution.py:668
  336.1 19.9 %collective-permute-start.22 = (bf16[1,48,1536]{2,1,0:T(8,128)(2,1)}, bf16[1,48,1536]{2,1,0:T(8,128)(2,1)}, u32[]{:S(2)}, u32[]{:S(2)}) collective-permute-start(bf16[1,48,1536]{2,1,0:T(8,128)(2,1)} %get-tuple-element.85), channel_id=1, source_target_pairs={{0,16},{4,20},{8,24},{12,28},{16,0},{20,4},{24,8},{28,12},{1,17},{... | collective-permute-start | bytes 442376 | tf_op jit(solution)/shard_map/ppermute | solution.py:668
  337.4 18.7 %collective-permute-start.23 = (bf16[1,48,1536]{2,1,0:T(8,128)(2,1)}, bf16[1,48,1536]{2,1,0:T(8,128)(2,1)}, u32[]{:S(2)}, u32[]{:S(2)}) collective-permute-start(bf16[1,48,1536]{2,1,0:T(8,128)(2,1)} %get-tuple-element.86), channel_id=1, source_target_pairs={{0,24},{4,28},{8,16},{12,20},{16,8},{20,12},{24,0},{28,4},{1,25},{... | collective-permute-start | bytes 442376 | tf_op jit(solution)/shard_map/ppermute | solution.py:668
  346.3 3.2 copy-start.21
  346.3 3.3 copy-start.42
  346.3 3.3 copy-start.43
  346.3 3.3 copy-start.44
  346.3 3.3 copy-start.45
  346.3 3.3 copy-start.46
  346.4 3.3 copy-start.47
  346.4 3.6 copy-start.14
  346.4 3.2 copy-start.23
  348.3 7.8 %copy-start.19 = (bf16[1,48,1536]{2,1,0:T(8,128)(2,1)S(1)}, bf16[1,48,1536]{2,1,0:T(8,128)(2,1)}, u32[]{:S(2)}) copy-start(bf16[1,48,1536]{2,1,0:T(8,128)(2,1)} %copy-done.18) | copy-start | bytes 442372
  348.3 18.5 %collective-permute-start.19 = (bf16[512,768]{1,0:T(8,128)(2,1)}, bf16[512,768]{1,0:T(8,128)(2,1)S(1)}, u32[]{:S(2)}, u32[]{:S(2)}) collective-permute-start(bf16[512,768]{1,0:T(8,128)(2,1)} %dynamic-slice_bitcast_fusion.1), channel_id=1, source_target_pairs={{0,2},{2,0},{1,3},{3,1},{4,6},{6,4},{5,7},{7,5},{8,10},{10,8},{9,1... | collective-permute-start | bytes 2359304 | tf_op jit(solution)/shard_map/ppermute | solution.py:639
  350.3 9.7 %collective-permute-start.24 = (bf16[8,48,512]{2,1,0:T(8,128)(2,1)S(1)}, bf16[8,48,512]{2,1,0:T(8,128)(2,1)S(1)}, u32[]{:S(2)}, u32[]{:S(2)}) collective-permute-start(bf16[8,48,512]{2,1,0:T(8,128)(2,1)S(1)} %get-tuple-element.96), channel_id=1, source_target_pairs={{0,4},{4,0},{8,12},{12,8},{16,20},{20,16},{24,28},{28,24},{1,5},{5... | collective-permute-start | bytes 1179656 | tf_op jit(solution)/shard_map/ppermute | solution.py:668
  367.0 5.7 %collective-permute-start.25 = (bf16[4,48,512]{2,1,0:T(8,128)(2,1)S(1)}, bf16[4,48,512]{2,1,0:T(8,128)(2,1)S(1)}, u32[]{:S(2)}, u32[]{:S(2)}) collective-permute-start(bf16[4,48,512]{2,1,0:T(8,128)(2,1)S(1)} %get-tuple-element.98), channel_id=1, source_target_pairs={{0,2},{2,0},{1,3},{3,1},{4,6},{6,4},{5,7},{7,5},{8,10},{10,8},{9,1... | collective-permute-start | bytes 589832 | tf_op jit(solution)/shard_map/ppermute | solution.py:639
  372.7 5.7 %collective-permute-start.26 = (bf16[1,48,512]{2,1,0:T(8,128)(2,1)S(1)}, bf16[1,48,512]{2,1,0:T(8,128)(2,1)S(1)}, u32[]{:S(2)}, u32[]{:S(2)}) collective-permute-start(bf16[1,48,512]{2,1,0:T(8,128)(2,1)S(1)} %get-tuple-element.100), channel_id=1, source_target_pairs={{0,8},{4,12},{8,0},{12,4},{16,24},{20,28},{24,16},{28,20},{1,9},{5... | collective-permute-start | bytes 147464 | tf_op jit(solution)/shard_map/ppermute | solution.py:668
  373.3 5.2 %collective-permute-start.27 = (bf16[1,48,512]{2,1,0:T(8,128)(2,1)S(1)}, bf16[1,48,512]{2,1,0:T(8,128)(2,1)S(1)}, u32[]{:S(2)}, u32[]{:S(2)}) collective-permute-start(bf16[1,48,512]{2,1,0:T(8,128)(2,1)S(1)} %get-tuple-element.101), channel_id=1, source_target_pairs={{0,16},{4,20},{8,24},{12,28},{16,0},{20,4},{24,8},{28,12},{1,17},{... | collective-permute-start | bytes 147464 | tf_op jit(solution)/shard_map/ppermute | solution.py:668
  375.4 5.9 %collective-permute-start.28 = (bf16[1,48,512]{2,1,0:T(8,128)(2,1)S(1)}, bf16[1,48,512]{2,1,0:T(8,128)(2,1)S(1)}, u32[]{:S(2)}, u32[]{:S(2)}) collective-permute-start(bf16[1,48,512]{2,1,0:T(8,128)(2,1)S(1)} %get-tuple-element.102), channel_id=1, source_target_pairs={{0,24},{4,28},{8,16},{12,20},{16,8},{20,12},{24,0},{28,4},{1,25},{... | collective-permute-start | bytes 147464 | tf_op jit(solution)/shard_map/ppermute | solution.py:668
  381.3 1.6 collective-permute-start.29
  385.3 2.3 collective-permute-start.30
  388.0 2.3 copy-start.1
  (22 other events, 25.2 us)
Sparse Core Ops, SparseCore 0:
  49.6 95.4 all-gather.1
  213.3 144.3 reduce-scatter.1
